TPU v7x, 512 devices: a whole 4x4x16 slice. The times are simulated.
512 devices in a mesh: pipe: 8 (over y, core), tp: 64 (over x, z).
Axes of the slice: x: 4, y: 4, z: 16, core: 2. Of those that a mesh axis runs over, the one named last changes fastest.
Arguments:
- in_flight: bfloat16 [8, 128, 3072], P('pipe', 'tp'), may hold values from -6 to 6
- w_qkv: bfloat16 [8, 3, 3072, 3072], P('pipe', None, 'tp'), may hold values from -0.109375 to 0.109375
- w_mlp: bfloat16 [8, 12288, 3072], P('pipe', 'tp'), may hold values from -0.109375 to 0.109375
- w_attn_out: bfloat16 [8, 3072, 3072], P('pipe', 'tp'), may hold values from -0.109375 to 0.109375
- w_mlp_out: bfloat16 [8, 12288, 3072], P('pipe', 'tp'), may hold values from -0.0546875 to 0.0546875
- modulation: float32 [8, 3, 3072], P('pipe'), may hold values from -3 to 3
- qk_gain: float32 [8, 2, 128], P('pipe'), may hold values from 0.25 to 1.75
- context_kv: bfloat16 [8, 2, 1536, 3072], P('pipe', None, 'tp'), may hold values from -8 to 8
- text_len: int32 [1], replicated, may hold values from 1 to 512
Outputs:
- leaving: bfloat16 [8, 128, 3072], P('pipe', 'tp')
All inputs are finite; a program needn't handle non-finite values.
Results may differ from a plain program's by a relative error of at most 0.017.
Values may be sent and summed in bfloat16 or wider, within the bound.
No kernel may reach another device: no remote copies, remote signals or barrier semaphores. Data moves between devices by JAX's collectives and lax.ppermute only.
A program may use at most 64 MiB of HBM per device.

v0:
```python
import jax
import jax.numpy as jnp
from jax import lax
from jax.sharding import PartitionSpec as P

HEADS = 24
HEAD_DIM = 128
TICKS = 2


eps_norm = 1e-06


def shifted(block, axis, distance):
    devices = range(lax.axis_size(axis))
    route = [((i - distance) % len(devices), i) for i in devices]
    return lax.ppermute(block, axis, route)


def modulated(hidden_state, shift_scale):
    x_float = hidden_state.astype(jnp.float32)
    row_mean = jnp.mean(x_float, axis=-1, keepdims=True)
    row_var = jnp.mean(jnp.square(x_float - row_mean), axis=-1, keepdims=True)
    normed = (x_float - row_mean) * lax.rsqrt(row_var + eps_norm)
    return (normed * (1.0 + shift_scale[1]) + shift_scale[0]).astype(jnp.bfloat16)


def head_norm(values_in, gain_vector):
    mean_square = jnp.mean(values_in * values_in, axis=-1, keepdims=True)
    return values_in * lax.rsqrt(mean_square + eps_norm) * gain_vector


def project_rows(normed, weight_rows):
    return lax.dot_general(
        normed, weight_rows, (((1,), (1,)), ((), ())), preferred_element_type=jnp.float32
    )


def local(
    in_flight, w_qkv, w_mlp, w_attn_out, w_mlp_out, modulation, qk_gain, context_kv, text_len
):
    tp_count = lax.axis_size("tp")
    tp_index = lax.axis_index("tp")
    local_rows = in_flight.shape[1]
    patch_len = local_rows * tp_count
    model_width = w_attn_out.shape[2]
    shard_width = w_attn_out.shape[1]
    ctx_local = context_kv.shape[2]
    shift_scale = modulation[0]
    gains = qk_gain[0]
    cached_keys = context_kv[0, 0].reshape(ctx_local, HEADS, HEAD_DIM)
    cached_values = context_kv[0, 1].reshape(ctx_local, HEADS, HEAD_DIM)
    positions = tp_index * ctx_local + jnp.arange(ctx_local, dtype=jnp.int32)
    text_span = ctx_local * tp_count // 3
    key_mask = (positions >= text_span) | (positions < text_len[0])
    full_mask = jnp.concatenate([key_mask, jnp.ones((local_rows,), dtype=bool)])
    weight_qkv = w_qkv[0].reshape(3 * shard_width, model_width)
    weight_mlp = w_mlp[0]
    weight_attn = w_attn_out[0]
    weight_down = w_mlp_out[0]
    current_rows = in_flight[0]
    whole_patch = lax.all_gather(current_rows, "tp", axis=0, tiled=True)
    for tick_number in range(TICKS):
        own_rows = lax.dynamic_slice_in_dim(whole_patch, tp_index * local_rows, local_rows, 0)
        normed = modulated(whole_patch, shift_scale)
        local_proj = project_rows(normed, weight_qkv).astype(jnp.bfloat16)
        local_proj = local_proj.reshape(patch_len, 3, shard_width)
        projected = lax.all_gather(local_proj, "tp", axis=2, tiled=True).reshape(
            patch_len, 3, HEADS, HEAD_DIM
        )
        queries = (
            head_norm(projected[:, 0].astype(jnp.float32), gains[0]) * HEAD_DIM ** (-0.5)
        ).astype(jnp.bfloat16)
        own_keys = head_norm(
            lax.dynamic_slice_in_dim(projected[:, 1], tp_index * local_rows, local_rows, 0).astype(
                jnp.float32
            ),
            gains[1],
        ).astype(jnp.bfloat16)
        own_values = lax.dynamic_slice_in_dim(projected[:, 2], tp_index * local_rows, local_rows, 0)
        keys_here = jnp.concatenate([cached_keys, own_keys], axis=0)
        values_here = jnp.concatenate([cached_values, own_values], axis=0)
        scores = jnp.einsum("qhd,khd->qhk", queries, keys_here, preferred_element_type=jnp.float32)
        scores = jnp.where(full_mask[None, None, :], scores, -1e30)
        probs = jnp.exp(scores)
        totals = jnp.sum(probs, axis=-1)
        weighted = jnp.einsum(
            "qhk,khd->qhd",
            probs.astype(jnp.bfloat16),
            values_here,
            preferred_element_type=jnp.float32,
        )
        total_all, weighted_all = lax.psum((totals, weighted), "tp")
        attention = (
            (weighted_all / total_all[..., None])
            .reshape(patch_len, model_width)
            .astype(jnp.bfloat16)
        )
        attention_mine = lax.dynamic_slice_in_dim(attention, tp_index * shard_width, shard_width, 1)
        hidden = jax.nn.gelu(project_rows(normed, weight_mlp), approximate=True).astype(
            jnp.bfloat16
        )
        branch = lax.psum_scatter(
            jnp.dot(attention_mine, weight_attn, preferred_element_type=jnp.float32)
            + jnp.dot(hidden, weight_down, preferred_element_type=jnp.float32),
            "tp",
            scatter_dimension=0,
            tiled=True,
        )
        finished = lax.all_gather(
            (own_rows.astype(jnp.float32) + shift_scale[2] * branch).astype(jnp.bfloat16),
            "tp",
            axis=0,
            tiled=True,
        )
        whole_patch = shifted(finished, "pipe", 1)
    current_rows = lax.dynamic_slice_in_dim(whole_patch, tp_index * local_rows, local_rows, 0)
    return current_rows[None]


def solution(mesh):
    placed = (
        P("pipe", "tp", None),
        P("pipe", None, "tp", None),
        P("pipe", "tp", None),
        P("pipe", "tp", None),
        P("pipe", "tp", None),
        P("pipe", None, None),
        P("pipe", None, None),
        P("pipe", None, "tp", None),
        P(),
    )
    return jax.shard_map(
        local, mesh=mesh, in_specs=placed, out_specs=P("pipe", "tp", None), check_vma=False
    )
```

profile of v0, /device:TPU:1, one launch (start us, length us, event | category | flops | bytes accessed | tf_op | source)
XLA Modules:
  0.0 1755.2 jit_solution(2946614097308410465)
XLA Ops:
  6.5 0.8 copy.20
  7.4 83.5 %all-gather = bf16[1,128,3072]{2,0,1:T(2,128)(2,1)S(1)} all-gather(bf16[1,2,3072]{2,0,1:T(2,128)(2,1)S(1)} %copy.20), channel_id=2, replica_groups=mesh['pipe'=8,'tp'=64] {'tp'}, dimensions={1}, use_global_device_ids=true | all-gather | bytes 798720 | tf_op jit(solution)/shard_map/all_gather | solution.py:62
  92.1 1.2 convolution_convert_fusion.1
  94.2 0.7 copy.25
  94.9 0.7 copy.23
  96.6 151.5 %all-gather.6.cloned.1.call-done = bf16[128,3,3072]{0,2,1:T(8,128)(2,1)} async-done(((bf16[128,3,48]{0,2,1:T(8,128)(2,1)}), bf16[128,3,3072]{0,2,1:T(8,128)(2,1)}) %all-gather.6.cloned.1.call-update) | async-done | bytes 2359312 | tf_op jit(solution)/shard_map/all_gather | solution.py:68
  248.0 1.5 fusion.121
  249.6 1.9 fusion.13
  251.5 1.4 constant_dynamic-slice_fusion.2
  252.9 2.0 copy.36
  254.9 0.8 fusion.85
  256.3 1.3 add_rsqrt_fusion.2
  257.7 0.9 copy.22
  258.6 0.8 fusion.87
  259.4 1.7 fusion.123
  261.1 1.6 convolution_bitcast_fusion.1
  262.8 221.2 %psum.29 = f32[128,24]{0,1:T(8,128)S(1)} all-reduce(f32[128,24]{0,1:T(8,128)S(1)} %get-tuple-element.16), channel_id=1, replica_groups=mesh['pipe'=8,'tp'=64] {'tp'}, use_global_device_ids=true, to_apply=%region_6.7 | all-reduce | flops 3072 | bytes 24576 | tf_op jit(solution)/shard_map/psum | solution.py:93
  484.0 50.9 %all-reduce.8.cloned.1.call-done = f32[128,24,128]{0,2,1:T(8,128)} async-done(((f32[128,24,128]{0,2,1:T(8,128)}), f32[128,24,128]{0,2,1:T(8,128)}) %all-reduce.8.cloned.1.call-update) | async-done | bytes 1572880 | tf_op jit(solution)/shard_map/psum | solution.py:93
  534.9 1.6 divide_convert_fusion.1
  536.5 1.6 fusion.41
  538.1 4.3 convolution_add_fusion.1
  542.4 1.3 dynamic-slice.5
  544.4 269.3 %all-reduce.12.cloned.1.call-done = f32[128,3072]{1,0:T(8,128)} async-done(((f32[128,3072]{1,0:T(8,128)}), f32[128,3072]{1,0:T(8,128)}) %all-reduce.12.cloned.1.call-update) | async-done | bytes 1572880
  813.7 0.9 fusion.97
  814.6 73.6 %all-gather.1 = bf16[64,2,3072]{2,1,0:T(2,128)(2,1)S(1)} all-gather(bf16[1,2,3072]{2,1,0:T(2,128)(2,1)S(1)} %fusion.97), channel_id=1, replica_groups=mesh['pipe'=8,'tp'=64] {'tp'}, dimensions={0}, use_global_device_ids=true | all-gather | bytes 798720 | tf_op jit(solution)/shard_map/all_gather | solution.py:110
  888.5 36.3 %collective-permute-start = (bf16[128,3072]{1,0:T(8,128)(2,1)S(1)}, bf16[128,3072]{1,0:T(8,128)(2,1)S(1)}, u32[]{:S(2)}, u32[]{:S(2)}) collective-permute-start(bf16[128,3072]{1,0:T(8,128)(2,1)S(1)} %reshape.117), channel_id=1, source_target_pairs={{448,0},{0,64},{64,128},{128,192},{192,256},{256,320},{320,384},{3... | collective-permute-start | bytes 2359304 | tf_op jit(solution)/shard_map/ppermute | solution.py:17
  924.8 8.9 collective-permute-done
  934.3 1.2 convolution_convert_fusion
  935.6 129.8 %all-gather.8.cloned.1.call-done = bf16[128,3,3072]{0,2,1:T(8,128)(2,1)} async-done(((bf16[128,3,48]{0,2,1:T(8,128)(2,1)}), bf16[128,3,3072]{0,2,1:T(8,128)(2,1)}) %all-gather.8.cloned.1.call-update) | async-done | bytes 2359312 | tf_op jit(solution)/shard_map/all_gather | solution.py:68
  1065.3 1.5 fusion.120
  1066.8 1.9 fusion.17
  1069.0 0.9 copy.38
  1069.9 0.8 fusion.88
  1070.8 1.4 fusion.90
  1072.2 1.3 add_rsqrt_fusion
  1074.1 1.7 fusion.124
  1075.8 1.6 convolution_bitcast_fusion
  1077.5 221.2 %psum.31 = f32[128,24]{0,1:T(8,128)S(1)} all-reduce(f32[128,24]{0,1:T(8,128)S(1)} %get-tuple-element.18), channel_id=1, replica_groups=mesh['pipe'=8,'tp'=64] {'tp'}, use_global_device_ids=true, to_apply=%region_14.15 | all-reduce | flops 3072 | bytes 24576 | tf_op jit(solution)/shard_map/psum | solution.py:93
  1298.6 50.8 %all-reduce.10.cloned.1.call-done = f32[128,24,128]{0,2,1:T(8,128)} async-done(((f32[128,24,128]{0,2,1:T(8,128)}), f32[128,24,128]{0,2,1:T(8,128)}) %all-reduce.10.cloned.1.call-update) | async-done | bytes 1572880 | tf_op jit(solution)/shard_map/psum | solution.py:93
  1349.4 1.6 divide_convert_fusion
  1351.1 1.4 fusion.39
  1352.4 3.8 convolution_add_fusion
  1356.3 271.3 %all-reduce.14.cloned.1.call-done = f32[128,3072]{1,0:T(8,128)} async-done(((f32[128,3072]{1,0:T(8,128)}), f32[128,3072]{1,0:T(8,128)}) %all-reduce.14.cloned.1.call-update) | async-done | bytes 1572880
  1627.6 0.9 fusion.96
  1628.5 73.6 %all-gather.2 = bf16[64,2,3072]{2,1,0:T(2,128)(2,1)S(1)} all-gather(bf16[1,2,3072]{2,1,0:T(2,128)(2,1)S(1)} %fusion.96), channel_id=1, replica_groups=mesh['pipe'=8,'tp'=64] {'tp'}, dimensions={0}, use_global_device_ids=true | all-gather | bytes 798720 | tf_op jit(solution)/shard_map/all_gather | solution.py:110
  1702.4 36.4 %collective-permute-start.1 = (bf16[128,3072]{1,0:T(8,128)(2,1)S(1)}, bf16[128,3072]{1,0:T(8,128)(2,1)S(1)}, u32[]{:S(2)}, u32[]{:S(2)}) collective-permute-start(bf16[128,3072]{1,0:T(8,128)(2,1)S(1)} %reshape.119), channel_id=1, source_target_pairs={{448,0},{0,64},{64,128},{128,192},{192,256},{256,320},{320,384},{3... | collective-permute-start | bytes 2359304 | tf_op jit(solution)/shard_map/ppermute | solution.py:17
  1738.8 8.9 collective-permute-done.1
  1747.7 0.6 dynamic-slice_bitcast_fusion
  (77 shorter events, 5.4 us)
Async XLA Ops:
  6.5 531.5 %copy-start = (bf16[1,192,3072]{2,1,0:T(8,128)(2,1)S(1)}, bf16[1,192,3072]{2,1,0:T(8,128)(2,1)}, u32[]{:S(2)}) copy-start(bf16[1,192,3072]{2,1,0:T(8,128)(2,1)} %param.13) | copy-start | bytes 3538948
  6.5 241.5 %all-gather.6.cloned.1.call-start = ((), (), s32[]{:S(2)}) async-start(), calls=%async_computation | async-start | bytes 2396160 | tf_op jit(solution)/shard_map/all_gather | solution.py:68
  90.9 0.8 copy-start.10
  90.9 1.3 copy-start.19
  91.2 2.2 copy-start.11
  91.7 0.5 copy-start.16
  91.7 1.7 copy-start.5
  91.7 1.7 copy-start.7
  92.1 1.9 copy-start.4
  93.4 2.7 copy-start.15
  93.4 441.5 %all-reduce.8.cloned.1.call-start = ((), (), s32[]{:S(2)}) async-start(), calls=%async_computation.1 | async-start | bytes 3145728 | tf_op jit(solution)/shard_map/psum | solution.py:93
  258.6 2.5 copy-start.1
  258.6 2.5 copy-start.9
  262.7 273.8 %copy-start.3 = (bf16[1,48,3072]{2,1,0:T(8,128)(2,1)S(1)}, bf16[1,48,3072]{2,1,0:T(8,128)(2,1)}, u32[]{:S(2)}) copy-start(bf16[1,48,3072]{2,1,0:T(8,128)(2,1)} %param.12) | copy-start | bytes 884740
  262.7 551.0 %all-reduce.12.cloned.1.call-start = ((), (), s32[]{:S(2)}) async-start(), calls=%async_computation.4 | async-start | bytes 3145728
  484.0 54.1 %copy-start.6 = (f32[1,1,3072]{2,0,1:T(1,128)S(1)}, f32[1,1,3072]{2,0,1:T(1,128)}, u32[]{:S(2)}) copy-start(f32[1,1,3072]{2,0,1:T(1,128)} %copy-done.5) | copy-start | bytes 36868
  484.0 54.1 %copy-start.8 = (f32[1,1,3072]{2,0,1:T(1,128)S(1)}, f32[1,1,3072]{2,0,1:T(1,128)}, u32[]{:S(2)}) copy-start(f32[1,1,3072]{2,0,1:T(1,128)} %copy-done.7) | copy-start | bytes 36868
  484.0 54.1 %copy-start.12 = (f32[128]{0:T(128)S(1)}, f32[128]{0:T(128)}, u32[]{:S(2)}) copy-start(f32[128]{0:T(128)} %copy-done.11) | copy-start | bytes 1540
  484.0 54.1 %copy-start.17 = (f32[128]{0:T(128)S(1)}, f32[128]{0:T(128)}, u32[]{:S(2)}) copy-start(f32[128]{0:T(128)} %copy-done.16) | copy-start | bytes 1540
  542.4 523.0 %all-gather.8.cloned.1.call-start = ((), (), s32[]{:S(2)}) async-start(), calls=%async_computation.2 | async-start | bytes 2396160 | tf_op jit(solution)/shard_map/all_gather | solution.py:68
  888.5 45.8 %copy-start.20 = (bf16[1,3,48,3072]{3,2,1,0:T(8,128)(2,1)S(1)}, bf16[1,3,48,3072]{3,2,1,0:T(8,128)(2,1)}, u32[]{:S(2)}) copy-start(bf16[1,3,48,3072]{3,2,1,0:T(8,128)(2,1)} %param.10) | copy-start | bytes 2654212
  888.5 45.2 %collective-permute-start = (bf16[128,3072]{1,0:T(8,128)(2,1)S(1)}, bf16[128,3072]{1,0:T(8,128)(2,1)S(1)}, u32[]{:S(2)}, u32[]{:S(2)}) collective-permute-start(bf16[128,3072]{1,0:T(8,128)(2,1)S(1)} %reshape.117), channel_id=1, source_target_pairs={{448,0},{0,64},{64,128},{128,192},{192,256},{256,320},{320,384},{3... | collective-permute-start | bytes 2359304 | tf_op jit(solution)/shard_map/ppermute | solution.py:17
  933.9 1.6 copy-start.13
  934.3 131.0 %copy-start.18 = (f32[128]{0:T(128)}, f32[128]{0:T(128)S(1)}, u32[]{:S(2)}) copy-start(f32[128]{0:T(128)S(1)} %add_rsqrt_fusion.4) | copy-start | bytes 1540
  935.5 413.9 %all-reduce.10.cloned.1.call-start = ((), (), s32[]{:S(2)}) async-start(), calls=%async_computation.3 | async-start | bytes 3145728 | tf_op jit(solution)/shard_map/psum | solution.py:93
  1073.8 2.0 copy-start.2
  1077.4 550.2 %all-reduce.14.cloned.1.call-start = ((), (), s32[]{:S(2)}) async-start(), calls=%async_computation.5 | async-start | bytes 3145728
  1298.6 53.8 %copy-start.14 = (f32[128]{0:T(128)S(1)}, f32[128]{0:T(128)}, u32[]{:S(2)}) copy-start(f32[128]{0:T(128)} %copy-done.13) | copy-start | bytes 1540
  1702.4 45.3 %collective-permute-start.1 = (bf16[128,3072]{1,0:T(8,128)(2,1)S(1)}, bf16[128,3072]{1,0:T(8,128)(2,1)S(1)}, u32[]{:S(2)}, u32[]{:S(2)}) collective-permute-start(bf16[128,3072]{1,0:T(8,128)(2,1)S(1)} %reshape.119), channel_id=1, source_target_pairs={{448,0},{0,64},{64,128},{128,192},{192,256},{256,320},{320,384},{3... | collective-permute-start | bytes 2359304 | tf_op jit(solution)/shard_map/ppermute | solution.py:17
Sparse Core Ops, SparseCore 0:
  93.5 154.4 all-gather.5
  262.8 272.0 all-reduce.7
  542.5 271.1 all-reduce.11
  935.6 129.6 all-gather.7
  1077.5 271.8 all-reduce.9
  1356.4 271.1 all-reduce.13
where the time goes:
time: 1760 us
  waiting for transfers between devices  942 us (54%)
  blocking collectives  673 us (38%)
  starting transfers between devices  72.9 us (4%)
  matrix products  19.9 us (1%)
    unnamed x8, waiting for transfers between devices  541 us
    psum x2, blocking collectives, local(): total_all, weighted_all = lax.psum((totals, weighted), 'tp')  442 us
    all_gather x2, waiting for transfers between devices, local(): lax.all_gather(local_proj, 'tp', axis=2, tiled=True)  281 us
    all_gather x2, blocking collectives, local(): lax.all_gather((own_rows.astype(jnp.float32) + shift_scale[2] * branch).a...  147 us
    psum x2, waiting for transfers between devices, local(): total_all, weighted_all = lax.psum((totals, weighted), 'tp')  102 us
    all_gather x1, blocking collectives, local(): whole_patch = lax.all_gather(current_rows, 'tp', axis=0, tiled=True)  83.5 us
    ppermute x2, starting transfers between devices, shifted(): return lax.ppermute(block, axis, route)  72.7 us
  transfers between devices with their start and end apart: 8, of which 8 were waited for; matrix products, arithmetic and copies ran while one was open for 0% of the time, Pallas kernels for 0%

commit v1 on v0

v1 whole, which is shorter than its diff:
```python
import jax
import jax.numpy as jnp
from jax import lax
from jax.sharding import PartitionSpec as P

HEADS = 24
HEAD_DIM = 128
TICKS = 2
TXT = 512
TEAM = 8
TEAM_HEADS = 3

eps_norm = 1e-06
f32 = jnp.float32
bf16 = jnp.bfloat16


def shifted(block, axis, distance):
    size = lax.axis_size(axis)
    return lax.ppermute(block, axis, [((i - distance) % size, i) for i in range(size)])


def modulated(hidden_state, shift_scale):
    x_float = hidden_state.astype(f32)
    row_mean = jnp.mean(x_float, axis=-1, keepdims=True)
    row_var = jnp.mean(jnp.square(x_float - row_mean), axis=-1, keepdims=True)
    normed = (x_float - row_mean) * lax.rsqrt(row_var + eps_norm)
    return (normed * (1.0 + shift_scale[1]) + shift_scale[0]).astype(bf16)


def head_norm(values_in, gain_vector):
    mean_square = jnp.mean(values_in * values_in, axis=-2, keepdims=True)
    return values_in * lax.rsqrt(mean_square + eps_norm) * gain_vector[:, None]


def local(
    in_flight, w_qkv, w_mlp, w_attn_out, w_mlp_out, modulation, qk_gain, context_kv, text_len
):
    tp_count = lax.axis_size("tp")
    tp_index = lax.axis_index("tp")
    rows = in_flight.shape[1]
    tokens = rows * tp_count
    width = w_attn_out.shape[2]
    shard = w_attn_out.shape[1]
    ctx_local = context_kv.shape[2]
    teams = tp_count // TEAM
    team_width = TEAM * shard
    member = tp_index % TEAM
    inside = [[TEAM * t + m for m in range(TEAM)] for t in range(teams)]
    across = [[TEAM * t + m for t in range(teams)] for m in range(TEAM)]
    shift_scale = modulation[0]
    gains = qk_gain[0]
    weight_qkv = w_qkv[0].reshape(3 * shard, width)
    weight_mlp = w_mlp[0]
    weight_attn = w_attn_out[0]
    weight_down = w_mlp_out[0]

    cached = context_kv[0].reshape(2, ctx_local, teams, team_width).transpose(2, 0, 1, 3)
    cached = lax.all_to_all(cached, "tp", 0, 0, axis_index_groups=across)
    cached = cached.transpose(1, 0, 2, 3).reshape(2, teams * ctx_local, TEAM_HEADS, HEAD_DIM)
    cached_keys, cached_values = cached[0], cached[1]
    slot = jnp.arange(teams * ctx_local, dtype=jnp.int32)
    position = ctx_local * (TEAM * (slot // ctx_local) + member) + slot % ctx_local
    cached_mask = (position >= TXT) | (position < text_len[0])
    token = jnp.arange(tokens, dtype=jnp.int32)
    fresh_mask = token // (tokens // TEAM) == member

    current = in_flight[0]
    for tick_number in range(TICKS):
        normed_rows = modulated(current, shift_scale)
        spread = jnp.broadcast_to(normed_rows[None], (tp_count, rows, width))
        normed = lax.all_to_all(spread, "tp", 0, 0).reshape(tokens, width)
        own = lax.dot_general(
            weight_qkv, normed, (((1,), (1,)), ((), ())), preferred_element_type=f32
        ).astype(bf16)
        team = lax.all_gather(own.reshape(3, shard, tokens), "tp", axis=1, tiled=True, axis_index_groups=inside)
        team = team.reshape(3, TEAM_HEADS, HEAD_DIM, tokens)
        queries = (head_norm(team[0].astype(f32), gains[0]) * HEAD_DIM ** (-0.5)).astype(bf16)
        fresh_keys = head_norm(team[1].astype(f32), gains[1]).astype(bf16)
        fresh_values = team[2]
        cached_scores = jnp.einsum("khd,hdq->hkq", cached_keys, queries, preferred_element_type=f32)
        fresh_scores = jnp.einsum("hdk,hdq->hkq", fresh_keys, queries, preferred_element_type=f32)
        cached_probs = jnp.exp(jnp.where(cached_mask[None, :, None], cached_scores, -1e30))
        fresh_probs = jnp.exp(jnp.where(fresh_mask[None, :, None], fresh_scores, -1e30))
        totals = jnp.sum(cached_probs, axis=1) + jnp.sum(fresh_probs, axis=1)
        weighted = jnp.einsum(
            "khd,hkq->hdq", cached_values, cached_probs.astype(bf16), preferred_element_type=f32
        ) + jnp.einsum(
            "hdk,hkq->hdq", fresh_values, fresh_probs.astype(bf16), preferred_element_type=f32
        )
        parts = weighted.astype(bf16).reshape(TEAM, shard, tokens)
        spread_totals = jnp.broadcast_to(totals.astype(bf16)[None], (TEAM, TEAM_HEADS, tokens))
        parts = jnp.concatenate(
            [parts, spread_totals, jnp.zeros((TEAM, 16 - TEAM_HEADS, tokens), bf16)], axis=1
        )
        parts = lax.all_to_all(parts, "tp", 0, 0, axis_index_groups=inside)
        summed = jnp.sum(parts.astype(f32), axis=0)
        feature_head = (member * shard + jnp.arange(shard, dtype=jnp.int32)) // HEAD_DIM
        total_rows = summed[shard + TEAM_HEADS - 1][None]
        for h in range(TEAM_HEADS - 1):
            total_rows = jnp.where(feature_head[:, None] == h, summed[shard + h][None], total_rows)
        attention = (summed[:shard] / total_rows).astype(bf16)
        hidden = jax.nn.gelu(
            lax.dot_general(
                normed, weight_mlp, (((1,), (1,)), ((), ())), preferred_element_type=f32
            ),
            approximate=True,
        ).astype(bf16)
        branch = lax.dot_general(
            attention, weight_attn, (((0,), (0,)), ((), ())), preferred_element_type=f32
        ) + jnp.dot(hidden, weight_down, preferred_element_type=f32)
        branch = (branch * shift_scale[2]).astype(bf16).reshape(tp_count, rows, width)
        branch = lax.all_to_all(branch, "tp", 0, 0)
        finished = (current.astype(f32) + jnp.sum(branch.astype(f32), axis=0)).astype(bf16)
        current = shifted(finished, "pipe", 1)
    return current[None]


def solution(mesh):
    placed = (
        P("pipe", "tp", None),
        P("pipe", None, "tp", None),
        P("pipe", "tp", None),
        P("pipe", "tp", None),
        P("pipe", "tp", None),
        P("pipe", None, None),
        P("pipe", None, None),
        P("pipe", None, "tp", None),
        P(),
    )
    return jax.shard_map(
        local, mesh=mesh, in_specs=placed, out_specs=P("pipe", "tp", None), check_vma=False
    )
```

time: 1760 us -> 382 us (0.22)
  waiting for transfers between devices: 942 us -> 63.3 us
  blocking collectives: 673 us -> 214 us
    unnamed x8 -> x0, waiting for transfers between devices: 541 us -> none
    psum x2 -> x0, blocking collectives: 442 us -> none  [local(): total_all, weighted_all = lax.psum((totals, weighted), 'tp')]
    all_gather x2 -> x0, waiting for transfers between devices: 281 us -> none  [local(): lax.all_gather(local_proj, 'tp', axis=2, tiled=True)]
    all_gather x3 -> x2, blocking collectives: 231 us -> 82.6 us  [local(): lax.all_gather(own.reshape(3, shard, tokens), 'tp', axis=1, tiled=True, a...]
    all_to_all x0 -> x4, blocking collectives: none -> 131 us  [the longest x2 69.7 us: local(): branch = lax.all_to_all(branch, 'tp', 0, 0)]
    psum x2 -> x0, waiting for transfers between devices: 102 us -> none  [local(): total_all, weighted_all = lax.psum((totals, weighted), 'tp')]
    all_to_all x0 -> x3, waiting for transfers between devices: none -> 61.6 us  [the longest x1 37.1 us: local(): normed = lax.all_to_all(spread, 'tp', 0, 0).reshape(tokens, width)]
    ppermute x2, starting transfers between devices: 72.7 us -> 32.4 us  [shifted(): lax.ppermute(block, axis, [((i - distance) % size, i) for i in range(size)])]
  transfers between devices with their start and end apart: 8 -> 5, of which waited for: 8 -> 5; matrix products, arithmetic and copies ran while one was open for 0% -> 0% of each run, Pallas kernels for 0% -> 0%
where the time goes in v1:
time: 382 us; the launch traced here: 380 us
  blocking collectives  214 us (56%)
  starting transfers between devices  72.4 us (19%)
  waiting for transfers between devices  63.3 us (17%)
  local copies, waits for them, and re-layouts  13.4 us (4%)
  matrix products  11.6 us (3%)
  other arithmetic  4.49 us (1%)
    all_gather x2, blocking collectives, local(): lax.all_gather(own.reshape(3, shard, tokens), 'tp', axis=1, tiled=True, a...  82.6 us
    all_to_all x2, blocking collectives, local(): branch = lax.all_to_all(branch, 'tp', 0, 0)  69.7 us
    all_to_all x1, blocking collectives, local(): normed = lax.all_to_all(spread, 'tp', 0, 0).reshape(tokens, width)  44.4 us
    all_to_all x1, waiting for transfers between devices, local(): normed = lax.all_to_all(spread, 'tp', 0, 0).reshape(tokens, width)  37.1 us
    ppermute x2, starting transfers between devices, shifted(): lax.ppermute(block, axis, [((i - distance) % size, i) for i in range(size)])  32.4 us
    all_to_all x1, starting transfers between devices, local(): cached = lax.all_to_all(cached, 'tp', 0, 0, axis_index_groups=across)  18.2 us
    all_to_all x1, blocking collectives, local(): parts = lax.all_to_all(parts, 'tp', 0, 0, axis_index_groups=inside)  17 us
    all_to_all x1, starting transfers between devices, local(): normed = lax.all_to_all(spread, 'tp', 0, 0).reshape(tokens, width)  15.2 us
  transfers between devices with their start and end apart: 5, of which 5 were waited for; matrix products, arithmetic and copies ran while one was open for 0% of the time, Pallas kernels for 0%

profile of v1, /device:TPU:1, one launch (start us, length us, event | category | flops | bytes accessed | tf_op | source)
XLA Modules:
  0.0 380.3 jit_solution(2691374943753639607)
XLA Ops:
  0.0 1.1 copy.32
  1.1 0.7 copy.23
  1.9 18.2 %all-to-all-start.1 = ((bf16[8,2,24,384]{3,2,1,0:T(8,128)(2,1)}), bf16[8,2,24,384]{3,2,1,0:T(8,128)(2,1)S(1)}, u32[]{:S(2)}, u32[]{:S(2)}) async-start(bf16[8,2,24,384]{3,2,1,0:T(8,128)(2,1)} %copy.23), calls=%async_computation.1 | async-start | bytes 589824 | tf_op jit(solution)/shard_map/all_to_all | solution.py:59
  20.1 0.1 convert_reduce_fusion.5
  20.3 0.6 fusion.143
  20.9 0.2 fusion.95
  21.2 14.8 %all-to-all-done.1 = bf16[8,2,24,384]{3,2,1,0:T(8,128)(2,1)S(1)} async-done(((bf16[8,2,24,384]{3,2,1,0:T(8,128)(2,1)}), bf16[8,2,24,384]{3,2,1,0:T(8,128)(2,1)S(1)}, u32[]{:S(2)}, u32[]{:S(2)}) %all-to-all-start.1) | async-done | bytes 294944 | tf_op jit(solution)/shard_map/all_to_all | solution.py:59
  36.0 1.3 broadcast_in_dim.154
  37.4 15.2 %all-to-all-start = ((bf16[64,2,3072]{2,1,0:T(2,128)(2,1)}), bf16[64,2,3072]{2,1,0:T(2,128)(2,1)}, u32[]{:S(2)}, u32[]{:S(2)}) async-start(bf16[64,2,3072]{2,1,0:T(2,128)(2,1)} %broadcast_in_dim.154), calls=%async_computation | async-start | bytes 1572864 | tf_op jit(solution)/shard_map/all_to_all | solution.py:72
  53.7 37.1 %all-to-all-done = bf16[64,2,3072]{2,1,0:T(2,128)(2,1)} async-done(((bf16[64,2,3072]{2,1,0:T(2,128)(2,1)}), bf16[64,2,3072]{2,1,0:T(2,128)(2,1)}, u32[]{:S(2)}, u32[]{:S(2)}) %all-to-all-start) | async-done | bytes 786464 | tf_op jit(solution)/shard_map/all_to_all | solution.py:72
  90.8 2.3 reshape.229
  93.0 0.4 convolution_convert_fusion.1
  93.4 41.3 %all_gather.6 = bf16[3,384,128]{2,1,0:T(8,128)(2,1)S(1)} all-gather(bf16[3,48,128]{2,1,0:T(8,128)(2,1)S(1)} %bitcast.139), channel_id=1, replica_groups={{0,1,2,3,4,5,6,7},{8,9,10,11,12,13,14,15},{16,17,18,19,20,21,22,23},{24..., dimensions={1}, use_global_device_ids=true | all-gather | bytes 331776 | tf_op jit(solution)/shard_map/all_gather | solution.py:76
  134.9 0.3 fusion.144
  135.2 0.3 fusion.145
  135.6 0.3 convolution_bitcast_fusion.1
  135.8 0.2 fusion.16
  136.0 0.7 maximum_maximum_fusion
  136.7 6.6 %all-to-all-start.2 = ((bf16[8,64,128]{2,1,0:T(8,128)(2,1)}), bf16[8,64,128]{2,1,0:T(8,128)(2,1)S(1)}, u32[]{:S(2)}, u32[]{:S(2)}) async-start(bf16[8,64,128]{2,1,0:T(8,128)(2,1)} %maximum_maximum_fusion), calls=%async_computation.2 | async-start | bytes 262144 | tf_op jit(solution)/shard_map/all_to_all | solution.py:96
  143.3 0.6 broadcast_compare_fusion
  143.9 9.7 %all-to-all-done.2 = bf16[8,64,128]{2,1,0:T(8,128)(2,1)S(1)} async-done(((bf16[8,64,128]{2,1,0:T(8,128)(2,1)}), bf16[8,64,128]{2,1,0:T(8,128)(2,1)S(1)}, u32[]{:S(2)}, u32[]{:S(2)}) %all-to-all-start.2) | async-done | bytes 131104 | tf_op jit(solution)/shard_map/all_to_all | solution.py:96
  153.6 1.4 fusion.20
  155.1 3.4 fusion.3
  158.5 2.2 reshape.232
  160.7 35.0 %all_to_all.35 = bf16[64,2,3072]{2,1,0:T(2,128)(2,1)S(1)} all-to-all(bf16[64,2,3072]{2,1,0:T(2,128)(2,1)S(1)} %reshape.232), channel_id=1, replica_groups=mesh['pipe'=8,'tp'=64] {'tp'}, dimensions={0} | all-to-all | bytes 1572864 | tf_op jit(solution)/shard_map/all_to_all | solution.py:113
  195.7 0.6 convert_reduce_fusion.1
  196.3 15.7 %collective-permute-start = (bf16[2,3072]{1,0:T(2,128)(2,1)S(1)}, bf16[2,3072]{1,0:T(2,128)(2,1)S(1)}, u32[]{:S(2)}, u32[]{:S(2)}) collective-permute-start(bf16[2,3072]{1,0:T(2,128)(2,1)S(1)} %fusion.96), channel_id=1, source_target_pairs={{448,0},{0,64},{64,128},{128,192},{192,256},{256,320},{320,384},{3... | collective-permute-start | bytes 36872 | tf_op jit(solution)/shard_map/ppermute | solution.py:20
  212.0 0.8 collective-permute-done
  212.8 0.1 convert_reduce_fusion.4
  213.0 0.2 fusion.90
  213.3 0.4 broadcast_in_dim.167
  213.7 44.4 %all_to_all.36 = bf16[64,2,3072]{2,1,0:T(2,128)(2,1)} all-to-all(bf16[64,2,3072]{2,1,0:T(2,128)(2,1)S(1)} %broadcast_in_dim.167), channel_id=1, replica_groups=mesh['pipe'=8,'tp'=64] {'tp'}, dimensions={0} | all-to-all | bytes 1572864 | tf_op jit(solution)/shard_map/all_to_all | solution.py:72
  258.2 2.3 reshape.233
  260.5 0.4 convolution_convert_fusion
  260.9 41.3 %all_gather.7 = bf16[3,384,128]{2,1,0:T(8,128)(2,1)S(1)} all-gather(bf16[3,48,128]{2,1,0:T(8,128)(2,1)S(1)} %bitcast.140), channel_id=1, replica_groups={{0,1,2,3,4,5,6,7},{8,9,10,11,12,13,14,15},{16,17,18,19,20,21,22,23},{24..., dimensions={1}, use_global_device_ids=true | all-gather | bytes 331776 | tf_op jit(solution)/shard_map/all_gather | solution.py:76
  302.4 0.3 fusion.146
  302.7 0.3 fusion.147
  303.0 0.3 convolution_bitcast_fusion
  303.3 0.2 fusion.17
  303.6 17.0 %all_to_all.37 = bf16[8,64,128]{2,1,0:T(8,128)(2,1)S(1)} all-to-all(bf16[8,64,128]{2,1,0:T(8,128)(2,1)S(1)} %maximum_maximum_fusion.1), channel_id=1, replica_groups={{0,1,2,3,4,5,6,7},{8,9,10,11,12,13,14,15},{16,17,18,19,20,21,22,23},{24..., dimensions={0} | all-to-all | bytes 262144 | tf_op jit(solution)/shard_map/all_to_all | solution.py:96
  320.7 0.5 fusion.18
  321.2 3.4 fusion.2
  324.6 2.2 reshape.236
  326.8 34.7 %all_to_all.38 = bf16[64,2,3072]{2,1,0:T(2,128)(2,1)S(1)} all-to-all(bf16[64,2,3072]{2,1,0:T(2,128)(2,1)S(1)} %reshape.236), channel_id=1, replica_groups=mesh['pipe'=8,'tp'=64] {'tp'}, dimensions={0} | all-to-all | bytes 1572864 | tf_op jit(solution)/shard_map/all_to_all | solution.py:113
  361.5 0.6 convert_reduce_fusion
  362.1 16.7 %collective-permute-start.1 = (bf16[2,3072]{1,0:T(2,128)(2,1)S(1)}, bf16[2,3072]{1,0:T(2,128)(2,1)S(1)}, u32[]{:S(2)}, u32[]{:S(2)}) collective-permute-start(bf16[2,3072]{1,0:T(2,128)(2,1)S(1)} %fusion.101), channel_id=1, source_target_pairs={{448,0},{0,64},{64,128},{128,192},{192,256},{256,320},{320,384},{3... | collective-permute-start | bytes 36872 | tf_op jit(solution)/shard_map/ppermute | solution.py:20
  378.9 0.8 collective-permute-done.1
  379.7 0.6 copy.47
  (85 shorter events, 1.0 us)
Async XLA Ops:
  0.0 155.1 %copy-start = (bf16[1,192,3072]{2,1,0:T(8,128)(2,1)S(1)}, bf16[1,192,3072]{2,1,0:T(8,128)(2,1)}, u32[]{:S(2)}) copy-start(bf16[1,192,3072]{2,1,0:T(8,128)(2,1)} %param.13) | copy-start | bytes 3538948
  0.0 20.1 %copy-start.8 = (bf16[1,2,3072]{2,1,0:T(2,128)(2,1)S(1)}, bf16[1,2,3072]{2,1,0:T(2,128)(2,1)}, u32[]{:S(2)}) copy-start(bf16[1,2,3072]{2,1,0:T(2,128)(2,1)} %param.9) | copy-start | bytes 36868
  0.0 20.3 %copy-start.13 = (f32[1,3,3072]{2,0,1:T(1,128)S(1)}, f32[1,3,3072]{2,0,1:T(1,128)}, u32[]{:S(2)}) copy-start(f32[1,3,3072]{2,0,1:T(1,128)} %param.14) | copy-start | bytes 110596
  1.9 51.6 %copy-start.16 = (f32[1,2,128]{2,1,0:T(2,128)S(1)}, f32[1,2,128]{2,1,0:T(2,128)}, u32[]{:S(2)}) copy-start(f32[1,2,128]{2,1,0:T(2,128)} %param.15) | copy-start | bytes 3076
  1.9 34.2 %all-to-all-start.1 = ((bf16[8,2,24,384]{3,2,1,0:T(8,128)(2,1)}), bf16[8,2,24,384]{3,2,1,0:T(8,128)(2,1)S(1)}, u32[]{:S(2)}, u32[]{:S(2)}) async-start(bf16[8,2,24,384]{3,2,1,0:T(8,128)(2,1)} %copy.23), calls=%async_computation.1 | async-start | bytes 589824 | tf_op jit(solution)/shard_map/all_to_all | solution.py:59
  20.9 32.6 %copy-start.9 = (f32[1,1,3072]{2,0,1:T(1,128)}, f32[1,1,3072]{2,0,1:T(1,128)S(1)}, u32[]{:S(2)}) copy-start(f32[1,1,3072]{2,0,1:T(1,128)S(1)} %get-tuple-element.14) | copy-start | bytes 36868
  20.9 32.6 %copy-start.11 = (f32[1,1,3072]{2,0,1:T(1,128)}, f32[1,1,3072]{2,0,1:T(1,128)S(1)}, u32[]{:S(2)}) copy-start(f32[1,1,3072]{2,0,1:T(1,128)S(1)} %get-tuple-element.15) | copy-start | bytes 36868
  37.4 53.4 %all-to-all-start = ((bf16[64,2,3072]{2,1,0:T(2,128)(2,1)}), bf16[64,2,3072]{2,1,0:T(2,128)(2,1)}, u32[]{:S(2)}, u32[]{:S(2)}) async-start(bf16[64,2,3072]{2,1,0:T(2,128)(2,1)} %broadcast_in_dim.154), calls=%async_computation | async-start | bytes 1572864 | tf_op jit(solution)/shard_map/all_to_all | solution.py:72
  52.6 40.4 %copy-start.1 = (bf16[1,3,48,3072]{3,2,1,0:T(8,128)(2,1)S(1)}, bf16[1,3,48,3072]{3,2,1,0:T(8,128)(2,1)}, u32[]{:S(2)}) copy-start(bf16[1,3,48,3072]{3,2,1,0:T(8,128)(2,1)} %param.10) | copy-start | bytes 2654212
  53.4 81.7 %copy-start.23 = (pred[128]{0:T(512)(128)(4,1)}, pred[128]{0:T(512)(128)(4,1)S(1)}, u32[]{:S(2)}) copy-start(pred[128]{0:T(512)(128)(4,1)S(1)} %fusion.127) | copy-start | bytes 388
  53.5 81.4 %copy-start.21 = (pred[192]{0:T(512)(128)(4,1)}, pred[192]{0:T(512)(128)(4,1)S(1)}, u32[]{:S(2)}) copy-start(pred[192]{0:T(512)(128)(4,1)S(1)} %compare_or_fusion) | copy-start | bytes 580
  53.5 81.7 %copy-start.17 = (f32[128]{0:T(128)}, f32[128]{0:T(128)S(1)}, u32[]{:S(2)}) copy-start(f32[128]{0:T(128)S(1)} %get-tuple-element.22) | copy-start | bytes 1540
  53.5 81.7 %copy-start.19 = (f32[128]{0:T(128)}, f32[128]{0:T(128)S(1)}, u32[]{:S(2)}) copy-start(f32[128]{0:T(128)S(1)} %get-tuple-element.23) | copy-start | bytes 1540
  53.6 81.9 %copy-start.3 = (bf16[192,3,128]{2,1,0:T(4,128)(2,1)}, bf16[192,3,128]{2,1,0:T(4,128)(2,1)S(1)}, u32[]{:S(2)}) copy-start(bf16[192,3,128]{2,1,0:T(4,128)(2,1)S(1)} %squeeze.35) | copy-start | bytes 442372
  53.7 81.2 %copy-start.6 = (bf16[192,3,128]{2,1,0:T(4,128)(2,1)}, bf16[192,3,128]{2,1,0:T(4,128)(2,1)S(1)}, u32[]{:S(2)}) copy-start(bf16[192,3,128]{2,1,0:T(4,128)(2,1)S(1)} %squeeze.34) | copy-start | bytes 442372
  136.7 16.8 %all-to-all-start.2 = ((bf16[8,64,128]{2,1,0:T(8,128)(2,1)}), bf16[8,64,128]{2,1,0:T(8,128)(2,1)S(1)}, u32[]{:S(2)}, u32[]{:S(2)}) async-start(bf16[8,64,128]{2,1,0:T(8,128)(2,1)} %maximum_maximum_fusion), calls=%async_computation.2 | async-start | bytes 262144 | tf_op jit(solution)/shard_map/all_to_all | solution.py:96
  160.6 52.6 %copy-start.10 = (f32[1,1,3072]{2,0,1:T(1,128)S(1)}, f32[1,1,3072]{2,0,1:T(1,128)}, u32[]{:S(2)}) copy-start(f32[1,1,3072]{2,0,1:T(1,128)} %copy-done.9) | copy-start | bytes 36868
  160.6 52.6 %copy-start.12 = (f32[1,1,3072]{2,0,1:T(1,128)S(1)}, f32[1,1,3072]{2,0,1:T(1,128)}, u32[]{:S(2)}) copy-start(f32[1,1,3072]{2,0,1:T(1,128)} %copy-done.11) | copy-start | bytes 36868
  196.3 16.5 %collective-permute-start = (bf16[2,3072]{1,0:T(2,128)(2,1)S(1)}, bf16[2,3072]{1,0:T(2,128)(2,1)S(1)}, u32[]{:S(2)}, u32[]{:S(2)}) collective-permute-start(bf16[2,3072]{1,0:T(2,128)(2,1)S(1)} %fusion.96), channel_id=1, source_target_pairs={{448,0},{0,64},{64,128},{128,192},{192,256},{256,320},{320,384},{3... | collective-permute-start | bytes 36872 | tf_op jit(solution)/shard_map/ppermute | solution.py:20
  213.7 46.7 %copy-start.2 = (bf16[1,3,48,3072]{3,2,1,0:T(8,128)(2,1)S(1)}, bf16[1,3,48,3072]{3,2,1,0:T(8,128)(2,1)}, u32[]{:S(2)}) copy-start(bf16[1,3,48,3072]{3,2,1,0:T(8,128)(2,1)} %param.10) | copy-start | bytes 2654212
  260.5 41.9 %copy-start.7 = (bf16[192,3,128]{2,1,0:T(4,128)(2,1)S(1)}, bf16[192,3,128]{2,1,0:T(4,128)(2,1)}, u32[]{:S(2)}) copy-start(bf16[192,3,128]{2,1,0:T(4,128)(2,1)} %copy-done.6) | copy-start | bytes 442372
  260.5 41.9 %copy-start.20 = (f32[128]{0:T(128)S(1)}, f32[128]{0:T(128)}, u32[]{:S(2)}) copy-start(f32[128]{0:T(128)} %copy-done.19) | copy-start | bytes 1540
  260.5 41.9 %copy-start.22 = (pred[192]{0:T(512)(128)(4,1)S(1)}, pred[192]{0:T(512)(128)(4,1)}, u32[]{:S(2)}) copy-start(pred[192]{0:T(512)(128)(4,1)} %copy-done.21) | copy-start | bytes 580
  260.5 42.2 %copy-start.18 = (f32[128]{0:T(128)S(1)}, f32[128]{0:T(128)}, u32[]{:S(2)}) copy-start(f32[128]{0:T(128)} %copy-done.17) | copy-start | bytes 1540
  260.5 42.2 %copy-start.24 = (pred[128]{0:T(512)(128)(4,1)S(1)}, pred[128]{0:T(512)(128)(4,1)}, u32[]{:S(2)}) copy-start(pred[128]{0:T(512)(128)(4,1)} %copy-done.23) | copy-start | bytes 388
  260.9 42.1 %copy-start.4 = (bf16[192,3,128]{2,1,0:T(4,128)(2,1)S(1)}, bf16[192,3,128]{2,1,0:T(4,128)(2,1)}, u32[]{:S(2)}) copy-start(bf16[192,3,128]{2,1,0:T(4,128)(2,1)} %copy-done.3) | copy-start | bytes 442372
  302.3 18.4 %copy-start.5 = (bf16[1,48,3072]{2,1,0:T(8,128)(2,1)S(1)}, bf16[1,48,3072]{2,1,0:T(8,128)(2,1)}, u32[]{:S(2)}) copy-start(bf16[1,48,3072]{2,1,0:T(8,128)(2,1)} %param.12) | copy-start | bytes 884740
  302.3 18.4 %copy-start.14 = (pred[48]{0:T(512)(128)(4,1)S(1)}, pred[48]{0:T(512)(128)(4,1)}, u32[]{:S(2)}) copy-start(pred[48]{0:T(512)(128)(4,1)} %get-tuple-element.34) | copy-start | bytes 148
  302.3 18.4 %copy-start.15 = (pred[48]{0:T(512)(128)(4,1)S(1)}, pred[48]{0:T(512)(128)(4,1)}, u32[]{:S(2)}) copy-start(pred[48]{0:T(512)(128)(4,1)} %get-tuple-element.35) | copy-start | bytes 148
  362.1 17.6 %collective-permute-start.1 = (bf16[2,3072]{1,0:T(2,128)(2,1)S(1)}, bf16[2,3072]{1,0:T(2,128)(2,1)S(1)}, u32[]{:S(2)}, u32[]{:S(2)}) collective-permute-start(bf16[2,3072]{1,0:T(2,128)(2,1)S(1)} %fusion.101), channel_id=1, source_target_pairs={{448,0},{0,64},{64,128},{128,192},{192,256},{256,320},{320,384},{3... | collective-permute-start | bytes 36872 | tf_op jit(solution)/shard_map/ppermute | solution.py:20

commit v2 on v1

--- a/solution.py
+++ b/solution.py
@@ -33,6 +33,20 @@
     return values_in * lax.rsqrt(mean_square + eps_norm) * gain_vector[:, None]
 
 
+def gathered(block, groups):
+    size = len(groups[0])
+    spread = jnp.broadcast_to(block[None], (size,) + block.shape)
+    spread = lax.all_to_all(spread, "tp", 0, 0, axis_index_groups=groups)
+    return spread.reshape((size * block.shape[0],) + block.shape[1:])
+
+
+def summed_over(block, groups):
+    size = len(groups[0])
+    parts = block.astype(bf16).reshape((size, block.shape[0] // size) + block.shape[1:])
+    parts = lax.all_to_all(parts, "tp", 0, 0, axis_index_groups=groups)
+    return jnp.sum(parts.astype(f32), axis=0)
+
+
 def local(
     in_flight, w_qkv, w_mlp, w_attn_out, w_mlp_out, modulation, qk_gain, context_kv, text_len
 ):
@@ -46,8 +60,15 @@
     teams = tp_count // TEAM
     team_width = TEAM * shard
     member = tp_index % TEAM
+    z_count, x_count = 2 * TEAM, tp_count // (2 * TEAM)
+    along_z = [[z_count * x + z for z in range(z_count)] for x in range(x_count)]
+    along_x = [[z_count * x + z for x in range(x_count)] for z in range(z_count)]
     inside = [[TEAM * t + m for m in range(TEAM)] for t in range(teams)]
-    across = [[TEAM * t + m for t in range(teams)] for m in range(TEAM)]
+    offset = [TEAM + TEAM // 2 if m < TEAM // 2 else TEAM // 2 for m in range(TEAM)]
+    across = [
+        [z_count * x + m + half * offset[m] for x in range(x_count) for half in range(2)]
+        for m in range(TEAM)
+    ]
     shift_scale = modulation[0]
     gains = qk_gain[0]
     weight_qkv = w_qkv[0].reshape(3 * shard, width)
@@ -59,8 +80,15 @@
     cached = lax.all_to_all(cached, "tp", 0, 0, axis_index_groups=across)
     cached = cached.transpose(1, 0, 2, 3).reshape(2, teams * ctx_local, TEAM_HEADS, HEAD_DIM)
     cached_keys, cached_values = cached[0], cached[1]
+    z_here = tp_index % z_count
+    low = jnp.where(
+        z_here < TEAM, z_here, (z_here - TEAM + TEAM // 2) % TEAM
+    )
+    high = low + jnp.where(low < TEAM // 2, TEAM + TEAM // 2, TEAM // 2)
     slot = jnp.arange(teams * ctx_local, dtype=jnp.int32)
-    position = ctx_local * (TEAM * (slot // ctx_local) + member) + slot % ctx_local
+    source = slot // ctx_local
+    source = z_count * (source // 2) + jnp.where(source % 2 == 0, low, high)
+    position = ctx_local * source + slot % ctx_local
     cached_mask = (position >= TXT) | (position < text_len[0])
     token = jnp.arange(tokens, dtype=jnp.int32)
     fresh_mask = token // (tokens // TEAM) == member
@@ -68,12 +96,11 @@
     current = in_flight[0]
     for tick_number in range(TICKS):
         normed_rows = modulated(current, shift_scale)
-        spread = jnp.broadcast_to(normed_rows[None], (tp_count, rows, width))
-        normed = lax.all_to_all(spread, "tp", 0, 0).reshape(tokens, width)
+        normed = gathered(gathered(normed_rows, along_z), along_x)
         own = lax.dot_general(
             weight_qkv, normed, (((1,), (1,)), ((), ())), preferred_element_type=f32
         ).astype(bf16)
-        team = lax.all_gather(own.reshape(3, shard, tokens), "tp", axis=1, tiled=True, axis_index_groups=inside)
+        team = gathered(own, inside).reshape(TEAM, 3, shard, tokens).transpose(1, 0, 2, 3)
         team = team.reshape(3, TEAM_HEADS, HEAD_DIM, tokens)
         queries = (head_norm(team[0].astype(f32), gains[0]) * HEAD_DIM ** (-0.5)).astype(bf16)
         fresh_keys = head_norm(team[1].astype(f32), gains[1]).astype(bf16)
@@ -109,9 +136,9 @@
         branch = lax.dot_general(
             attention, weight_attn, (((0,), (0,)), ((), ())), preferred_element_type=f32
         ) + jnp.dot(hidden, weight_down, preferred_element_type=f32)
-        branch = (branch * shift_scale[2]).astype(bf16).reshape(tp_count, rows, width)
-        branch = lax.all_to_all(branch, "tp", 0, 0)
-        finished = (current.astype(f32) + jnp.sum(branch.astype(f32), axis=0)).astype(bf16)
+        branch = summed_over(branch * shift_scale[2], along_x)
+        branch = summed_over(branch, along_z)
+        finished = (current.astype(f32) + branch).astype(bf16)
         current = shifted(finished, "pipe", 1)
     return current[None]
 

time: 382 us -> 280 us (0.73)
  blocking collectives: 214 us -> 156 us
  waiting for transfers between devices: 63.3 us -> 42.9 us
  starting transfers between devices: 72.4 us -> 55.9 us
  local copies, waits for them, and re-layouts: 13.4 us -> 4.78 us
    all_gather x2 -> x0, blocking collectives: 82.6 us -> none  [local(): lax.all_gather(own.reshape(3, shard, tokens), 'tp', axis=1, tiled=True, a...]
    all_to_all x3 -> x8, blocking collectives: 114 us -> 138 us  [the longest x4 75.9 us: gathered(): spread = lax.all_to_all(spread, 'tp', 0, 0, axis_index_groups=groups)]
    all_to_all x1 -> x2, waiting for transfers between devices: 37.1 us -> 21.4 us  [gathered(): spread = lax.all_to_all(spread, 'tp', 0, 0, axis_index_groups=groups)]
    all_to_all x1, starting transfers between devices: 18.2 us -> 6.65 us  [local(): cached = lax.all_to_all(cached, 'tp', 0, 0, axis_index_groups=across)]
    ppermute x2, starting transfers between devices: 32.4 us -> 21.7 us  [shifted(): lax.ppermute(block, axis, [((i - distance) % size, i) for i in range(size)])]
    reshape x4 -> x2, local copies, waits for them, and re-layouts: 8.85 us -> 0.16 us  [summed_over(): block.astype(bf16).reshape((size, block.shape[0] // size) + block.shape[1:])]
    all_to_all x1, waiting for transfers between devices: 14.8 us -> 10.1 us  [local(): cached = lax.all_to_all(cached, 'tp', 0, 0, axis_index_groups=across)]
    all_to_all x1 -> x2, starting transfers between devices: 15.2 us -> 19.8 us  [gathered(): spread = lax.all_to_all(spread, 'tp', 0, 0, axis_index_groups=groups)]
  transfers between devices with their start and end apart: 5 -> 6, of which waited for: 5 -> 6; matrix products, arithmetic and copies ran while one was open for 0% -> 1% of each run, Pallas kernels for 0% -> 0%
where the time goes in v2:
time: 280 us; the launch traced here: 279 us
  blocking collectives  156 us (56%)
  starting transfers between devices  55.9 us (20%)
  waiting for transfers between devices  42.9 us (15%)
  matrix products  11.6 us (4%)
  other arithmetic  6.06 us (2%)
  local copies, waits for them, and re-layouts  4.78 us (2%)
    all_to_all x4, blocking collectives, gathered(): spread = lax.all_to_all(spread, 'tp', 0, 0, axis_index_groups=groups)  75.9 us
    all_to_all x4, blocking collectives, summed_over(): parts = lax.all_to_all(parts, 'tp', 0, 0, axis_index_groups=groups)  61.8 us
    ppermute x2, starting transfers between devices, shifted(): lax.ppermute(block, axis, [((i - distance) % size, i) for i in range(size)])  21.7 us
    all_to_all x2, waiting for transfers between devices, gathered(): spread = lax.all_to_all(spread, 'tp', 0, 0, axis_index_groups=groups)  21.4 us
    all_to_all x2, starting transfers between devices, gathered(): spread = lax.all_to_all(spread, 'tp', 0, 0, axis_index_groups=groups)  19.8 us
    all_to_all x1, blocking collectives, local(): parts = lax.all_to_all(parts, 'tp', 0, 0, axis_index_groups=inside)  18.4 us
    all_to_all x1, waiting for transfers between devices, local(): cached = lax.all_to_all(cached, 'tp', 0, 0, axis_index_groups=across)  10.1 us
    all_to_all x1, waiting for transfers between devices, local(): parts = lax.all_to_all(parts, 'tp', 0, 0, axis_index_groups=inside)  9.69 us
  transfers between devices with their start and end apart: 6, of which 6 were waited for; matrix products, arithmetic and copies ran while one was open for 1% of the time, Pallas kernels for 0%

profile of v2, /device:TPU:1, one launch (start us, length us, event | category | flops | bytes accessed | tf_op | source)
XLA Modules:
  0.0 278.7 jit_solution(3466185580724021679)
XLA Ops:
  0.0 0.9 convert_reduce_fusion.5
  1.0 0.9 fusion.97
  1.9 0.8 fusion.143
  2.7 0.6 copy-done.11
  3.3 0.8 fusion.122
  4.2 28.1 %all_to_all.65 = bf16[16,2,3072]{2,1,0:T(2,128)(2,1)S(1)} all-to-all(bf16[16,2,3072]{2,1,0:T(2,128)(2,1)S(1)} %broadcast_in_dim.190), channel_id=1, replica_groups={{0,1,2,3,4,5,6,7,8,9,10,11,12,13,14,15},{16,17,18,19,20,21,22,23,24,25,..., dimensions={0} | all-to-all | bytes 393216 | tf_op jit(solution)/shard_map/all_to_all | solution.py:39
  32.4 1.0 broadcast_in_dim.192
  33.3 4.0 %all-to-all-start.1 = ((bf16[4,32,3072]{2,1,0:T(8,128)(2,1)}), bf16[4,32,3072]{2,1,0:T(8,128)(2,1)S(1)}, u32[]{:S(2)}, u32[]{:S(2)}) async-start(bf16[4,32,3072]{2,1,0:T(8,128)(2,1)} %broadcast_in_dim.192), calls=%async_computation.1 | async-start | bytes 1572864 | tf_op jit(solution)/shard_map/all_to_all | solution.py:39
  37.4 0.7 copy.55
  38.1 7.5 %all-to-all-done.1 = bf16[4,32,3072]{2,1,0:T(8,128)(2,1)S(1)} async-done(((bf16[4,32,3072]{2,1,0:T(8,128)(2,1)}), bf16[4,32,3072]{2,1,0:T(8,128)(2,1)S(1)}, u32[]{:S(2)}, u32[]{:S(2)}) %all-to-all-start.1) | async-done | bytes 786464 | tf_op jit(solution)/shard_map/all_to_all | solution.py:39
  45.7 6.7 %all-to-all-start.3 = ((bf16[8,2,24,384]{3,2,1,0:T(8,128)(2,1)}), bf16[8,2,24,384]{3,2,1,0:T(8,128)(2,1)S(1)}, u32[]{:S(2)}, u32[]{:S(2)}) async-start(bf16[8,2,24,384]{3,2,1,0:T(8,128)(2,1)} %copy.55), calls=%async_computation.3 | async-start | bytes 589824 | tf_op jit(solution)/shard_map/all_to_all | solution.py:80
  52.3 0.4 fusion.18
  52.7 10.1 %all-to-all-done.3 = bf16[8,2,24,384]{3,2,1,0:T(8,128)(2,1)S(1)} async-done(((bf16[8,2,24,384]{3,2,1,0:T(8,128)(2,1)}), bf16[8,2,24,384]{3,2,1,0:T(8,128)(2,1)S(1)}, u32[]{:S(2)}, u32[]{:S(2)}) %all-to-all-start.3) | async-done | bytes 294944 | tf_op jit(solution)/shard_map/all_to_all | solution.py:80
  62.9 0.7 broadcast_in_dim.193
  63.6 15.8 %all-to-all-start.2 = ((bf16[8,144,128]{2,1,0:T(8,128)(2,1)}), bf16[8,144,128]{2,1,0:T(8,128)(2,1)S(1)}, u32[]{:S(2)}, u32[]{:S(2)}) async-start(bf16[8,144,128]{2,1,0:T(8,128)(2,1)} %broadcast_in_dim.193), calls=%async_computation.2 | async-start | bytes 589824 | tf_op jit(solution)/shard_map/all_to_all | solution.py:39
  80.4 13.9 %all-to-all-done.2 = bf16[8,144,128]{2,1,0:T(8,128)(2,1)S(1)} async-done(((bf16[8,144,128]{2,1,0:T(8,128)(2,1)}), bf16[8,144,128]{2,1,0:T(8,128)(2,1)S(1)}, u32[]{:S(2)}, u32[]{:S(2)}) %all-to-all-start.2) | async-done | bytes 294944 | tf_op jit(solution)/shard_map/all_to_all | solution.py:39
  94.4 0.3 fusion.144
  94.8 0.3 fusion.145
  95.1 0.3 convolution_bitcast_fusion.1
  95.4 0.2 fusion.16
  95.6 0.7 maximum_maximum_fusion
  96.3 7.8 %all-to-all-start.4 = ((bf16[8,64,128]{2,1,0:T(8,128)(2,1)}), bf16[8,64,128]{2,1,0:T(8,128)(2,1)S(1)}, u32[]{:S(2)}, u32[]{:S(2)}) async-start(bf16[8,64,128]{2,1,0:T(8,128)(2,1)} %maximum_maximum_fusion), calls=%async_computation.4 | async-start | bytes 262144 | tf_op jit(solution)/shard_map/all_to_all | solution.py:123
  104.1 0.6 broadcast_compare_fusion
  104.7 9.7 %all-to-all-done.4 = bf16[8,64,128]{2,1,0:T(8,128)(2,1)S(1)} async-done(((bf16[8,64,128]{2,1,0:T(8,128)(2,1)}), bf16[8,64,128]{2,1,0:T(8,128)(2,1)S(1)}, u32[]{:S(2)}, u32[]{:S(2)}) %all-to-all-start.4) | async-done | bytes 131104 | tf_op jit(solution)/shard_map/all_to_all | solution.py:123
  114.4 1.4 fusion.22
  115.9 3.4 %fusion.3 = bf16[128,3072]{1,0:T(8,128)(2,1)} fusion(f32[128,3072]{1,0:T(8,128)S(1)} %fusion.22, bf16[1,192,3072]{2,1,0:T(8,128)(2,1)S(1)} %copy-done, f32[3072]{0:T(1024)S(1)} %bitcast.155, bf16[128,3072]{1,0:T(8,128)(2,1)S(1)} %bitcast.129, bf16[1,192,3072]{2,1,0:T(8,128)(2,1)} %param.11), kind=kOutput, calls=%fused_computation.5 | convolution fusion | flops 303390720 | bytes 5517312 | tf_op jit(solution)/shard_map/dot_general | solution.py:138
  119.3 12.8 %all_to_all.66 = bf16[4,32,3072]{2,1,0:T(8,128)(2,1)S(1)} all-to-all(bf16[4,32,3072]{2,1,0:T(8,128)(2,1)} %bitcast.135), channel_id=1, replica_groups={{0,16,32,48},{1,17,33,49},{2,18,34,50},{3,19,35,51},{4,20,36,52},{5,21,..., dimensions={0} | all-to-all | bytes 1572864 | tf_op jit(solution)/shard_map/all_to_all | solution.py:46
  132.1 0.2 reduce_sum.175
  132.4 18.8 %all_to_all.67 = bf16[16,2,3072]{2,1,0:T(2,128)(2,1)S(1)} all-to-all(bf16[16,2,3072]{2,1,0:T(2,128)(2,1)S(1)} %reshape.264), channel_id=1, replica_groups={{0,1,2,3,4,5,6,7,8,9,10,11,12,13,14,15},{16,17,18,19,20,21,22,23,24,25,..., dimensions={0} | all-to-all | bytes 393216 | tf_op jit(solution)/shard_map/all_to_all | solution.py:46
  151.3 6.8 %collective-permute-start = (bf16[2,3072]{1,0:T(2,128)(2,1)S(1)}, bf16[2,3072]{1,0:T(2,128)(2,1)S(1)}, u32[]{:S(2)}, u32[]{:S(2)}) collective-permute-start(bf16[2,3072]{1,0:T(2,128)(2,1)S(1)} %fusion.98), channel_id=1, source_target_pairs={{448,0},{0,64},{64,128},{128,192},{192,256},{256,320},{320,384},{3... | collective-permute-start | bytes 36872 | tf_op jit(solution)/shard_map/ppermute | solution.py:20
  158.1 0.8 collective-permute-done
  159.1 0.2 fusion.92
  159.5 16.2 %all_to_all.68 = bf16[16,2,3072]{2,1,0:T(2,128)(2,1)S(1)} all-to-all(bf16[16,2,3072]{2,1,0:T(2,128)(2,1)S(1)} %broadcast_in_dim.206), channel_id=1, replica_groups={{0,1,2,3,4,5,6,7,8,9,10,11,12,13,14,15},{16,17,18,19,20,21,22,23,24,25,..., dimensions={0} | all-to-all | bytes 393216 | tf_op jit(solution)/shard_map/all_to_all | solution.py:39
  175.9 10.9 %all_to_all.69 = bf16[4,32,3072]{2,1,0:T(8,128)(2,1)S(1)} all-to-all(bf16[4,32,3072]{2,1,0:T(8,128)(2,1)S(1)} %broadcast_in_dim.208), channel_id=1, replica_groups={{0,16,32,48},{1,17,33,49},{2,18,34,50},{3,19,35,51},{4,20,36,52},{5,21,..., dimensions={0} | all-to-all | bytes 1572864 | tf_op jit(solution)/shard_map/all_to_all | solution.py:39
  186.8 0.4 fusion.19
  187.3 20.7 %all_to_all.70 = bf16[8,144,128]{2,1,0:T(8,128)(2,1)S(1)} all-to-all(bf16[8,144,128]{2,1,0:T(8,128)(2,1)S(1)} %broadcast_in_dim.209), channel_id=1, replica_groups={{0,1,2,3,4,5,6,7},{8,9,10,11,12,13,14,15},{16,17,18,19,20,21,22,23},{24..., dimensions={0} | all-to-all | bytes 589824 | tf_op jit(solution)/shard_map/all_to_all | solution.py:39
  208.2 0.3 fusion.146
  208.5 0.3 fusion.147
  208.9 0.3 convolution_bitcast_fusion
  209.2 0.2 fusion.17
  209.5 18.4 %all_to_all.71 = bf16[8,64,128]{2,1,0:T(8,128)(2,1)S(1)} all-to-all(bf16[8,64,128]{2,1,0:T(8,128)(2,1)S(1)} %maximum_maximum_fusion.1), channel_id=1, replica_groups={{0,1,2,3,4,5,6,7},{8,9,10,11,12,13,14,15},{16,17,18,19,20,21,22,23},{24..., dimensions={0} | all-to-all | bytes 262144 | tf_op jit(solution)/shard_map/all_to_all | solution.py:123
  228.0 0.5 fusion.20
  228.4 3.4 %fusion.2 = bf16[128,3072]{1,0:T(8,128)(2,1)} fusion(f32[128,3072]{1,0:T(8,128)S(1)} %fusion.20, bf16[1,192,3072]{2,1,0:T(8,128)(2,1)S(1)} %copy-done, f32[3072]{0:T(1024)} %bitcast.156, bf16[128,3072]{1,0:T(8,128)(2,1)S(1)} %bitcast.131, bf16[1,192,3072]{2,1,0:T(8,128)(2,1)} %param.11), kind=kOutput, calls=%fused_computation.4 | convolution fusion | flops 303390720 | bytes 5517312 | tf_op jit(solution)/shard_map/dot_general | solution.py:138
  231.8 11.9 %all_to_all.72 = bf16[4,32,3072]{2,1,0:T(8,128)(2,1)S(1)} all-to-all(bf16[4,32,3072]{2,1,0:T(8,128)(2,1)} %bitcast.134), channel_id=1, replica_groups={{0,16,32,48},{1,17,33,49},{2,18,34,50},{3,19,35,51},{4,20,36,52},{5,21,..., dimensions={0} | all-to-all | bytes 1572864 | tf_op jit(solution)/shard_map/all_to_all | solution.py:46
  244.0 18.2 %all_to_all.73 = bf16[16,2,3072]{2,1,0:T(2,128)(2,1)S(1)} all-to-all(bf16[16,2,3072]{2,1,0:T(2,128)(2,1)S(1)} %reshape.268), channel_id=1, replica_groups={{0,1,2,3,4,5,6,7,8,9,10,11,12,13,14,15},{16,17,18,19,20,21,22,23,24,25,..., dimensions={0} | all-to-all | bytes 393216 | tf_op jit(solution)/shard_map/all_to_all | solution.py:46
  262.3 14.9 %collective-permute-start.1 = (bf16[2,3072]{1,0:T(2,128)(2,1)S(1)}, bf16[2,3072]{1,0:T(2,128)(2,1)S(1)}, u32[]{:S(2)}, u32[]{:S(2)}) collective-permute-start(bf16[2,3072]{1,0:T(2,128)(2,1)S(1)} %fusion.103), channel_id=1, source_target_pairs={{448,0},{0,64},{64,128},{128,192},{192,256},{256,320},{320,384},{3... | collective-permute-start | bytes 36872 | tf_op jit(solution)/shard_map/ppermute | solution.py:20
  277.2 0.8 collective-permute-done.1
  278.1 0.6 copy.83
  (98 shorter events, 2.1 us)
Async XLA Ops:
  0.0 115.9 %copy-start = (bf16[1,192,3072]{2,1,0:T(8,128)(2,1)S(1)}, bf16[1,192,3072]{2,1,0:T(8,128)(2,1)}, u32[]{:S(2)}) copy-start(bf16[1,192,3072]{2,1,0:T(8,128)(2,1)} %param.13) | copy-start | bytes 3538948
  2.6 0.6 copy-start.11
  2.6 0.6 copy-start.13
  2.7 113.2 %copy-start.10 = (f32[1,1,3072]{2,0,1:T(1,128)}, f32[1,1,3072]{2,0,1:T(1,128)S(1)}, u32[]{:S(2)}) copy-start(f32[1,1,3072]{2,0,1:T(1,128)S(1)} %get-tuple-element.13) | copy-start | bytes 36868
  32.3 5.0 %copy-start.6 = (bf16[1,2,24,3072]{3,2,1,0:T(8,128)(2,1)S(1)}, bf16[1,2,24,3072]{3,2,1,0:T(8,128)(2,1)}, u32[]{:S(2)}) copy-start(bf16[1,2,24,3072]{3,2,1,0:T(8,128)(2,1)} %param.16) | copy-start | bytes 884740
  33.3 12.4 %all-to-all-start.1 = ((bf16[4,32,3072]{2,1,0:T(8,128)(2,1)}), bf16[4,32,3072]{2,1,0:T(8,128)(2,1)S(1)}, u32[]{:S(2)}, u32[]{:S(2)}) async-start(bf16[4,32,3072]{2,1,0:T(8,128)(2,1)} %broadcast_in_dim.192), calls=%async_computation.1 | async-start | bytes 1572864 | tf_op jit(solution)/shard_map/all_to_all | solution.py:39
  37.3 15.0 %copy-start.1 = (bf16[1,3,48,3072]{3,2,1,0:T(8,128)(2,1)S(1)}, bf16[1,3,48,3072]{3,2,1,0:T(8,128)(2,1)}, u32[]{:S(2)}) copy-start(bf16[1,3,48,3072]{3,2,1,0:T(8,128)(2,1)} %param.10) | copy-start | bytes 2654212
  45.7 17.2 %all-to-all-start.3 = ((bf16[8,2,24,384]{3,2,1,0:T(8,128)(2,1)}), bf16[8,2,24,384]{3,2,1,0:T(8,128)(2,1)S(1)}, u32[]{:S(2)}, u32[]{:S(2)}) async-start(bf16[8,2,24,384]{3,2,1,0:T(8,128)(2,1)} %copy.55), calls=%async_computation.3 | async-start | bytes 589824 | tf_op jit(solution)/shard_map/all_to_all | solution.py:80
  52.3 27.9 %copy-start.17 = (f32[1,2,128]{2,1,0:T(2,128)S(1)}, f32[1,2,128]{2,1,0:T(2,128)}, u32[]{:S(2)}) copy-start(f32[1,2,128]{2,1,0:T(2,128)} %param.15) | copy-start | bytes 3076
  63.6 30.7 %all-to-all-start.2 = ((bf16[8,144,128]{2,1,0:T(8,128)(2,1)}), bf16[8,144,128]{2,1,0:T(8,128)(2,1)S(1)}, u32[]{:S(2)}, u32[]{:S(2)}) async-start(bf16[8,144,128]{2,1,0:T(8,128)(2,1)} %broadcast_in_dim.193), calls=%async_computation.2 | async-start | bytes 589824 | tf_op jit(solution)/shard_map/all_to_all | solution.py:39
  80.2 14.6 %copy-start.24 = (pred[128]{0:T(512)(128)(4,1)}, pred[128]{0:T(512)(128)(4,1)S(1)}, u32[]{:S(2)}) copy-start(pred[128]{0:T(512)(128)(4,1)S(1)} %fusion.127) | copy-start | bytes 388
  80.2 14.5 %copy-start.22 = (pred[192]{0:T(512)(128)(4,1)}, pred[192]{0:T(512)(128)(4,1)S(1)}, u32[]{:S(2)}) copy-start(pred[192]{0:T(512)(128)(4,1)S(1)} %compare_or_fusion) | copy-start | bytes 580
  80.2 14.5 %copy-start.18 = (f32[128]{0:T(128)}, f32[128]{0:T(128)S(1)}, u32[]{:S(2)}) copy-start(f32[128]{0:T(128)S(1)} %get-tuple-element.22) | copy-start | bytes 1540
  80.2 14.5 %copy-start.20 = (f32[128]{0:T(128)}, f32[128]{0:T(128)S(1)}, u32[]{:S(2)}) copy-start(f32[128]{0:T(128)S(1)} %get-tuple-element.23) | copy-start | bytes 1540
  80.3 14.8 %copy-start.3 = (bf16[192,3,128]{2,1,0:T(4,128)(2,1)}, bf16[192,3,128]{2,1,0:T(4,128)(2,1)S(1)}, u32[]{:S(2)}) copy-start(bf16[192,3,128]{2,1,0:T(4,128)(2,1)S(1)} %squeeze.35) | copy-start | bytes 442372
  80.4 15.0 %copy-start.7 = (bf16[192,3,128]{2,1,0:T(4,128)(2,1)}, bf16[192,3,128]{2,1,0:T(4,128)(2,1)S(1)}, u32[]{:S(2)}) copy-start(bf16[192,3,128]{2,1,0:T(4,128)(2,1)S(1)} %squeeze.34) | copy-start | bytes 442372
  96.3 18.1 %all-to-all-start.4 = ((bf16[8,64,128]{2,1,0:T(8,128)(2,1)}), bf16[8,64,128]{2,1,0:T(8,128)(2,1)S(1)}, u32[]{:S(2)}, u32[]{:S(2)}) async-start(bf16[8,64,128]{2,1,0:T(8,128)(2,1)} %maximum_maximum_fusion), calls=%async_computation.4 | async-start | bytes 262144 | tf_op jit(solution)/shard_map/all_to_all | solution.py:123
  132.1 19.2 %copy-start.9 = (bf16[1,2,3072]{2,1,0:T(2,128)(2,1)S(1)}, bf16[1,2,3072]{2,1,0:T(2,128)(2,1)}, u32[]{:S(2)}) copy-start(bf16[1,2,3072]{2,1,0:T(2,128)(2,1)} %param.9) | copy-start | bytes 36868
  132.1 27.2 %copy-start.12 = (f32[1,1,3072]{2,0,1:T(1,128)S(1)}, f32[1,1,3072]{2,0,1:T(1,128)}, u32[]{:S(2)}) copy-start(f32[1,1,3072]{2,0,1:T(1,128)} %copy-done.11) | copy-start | bytes 36868
  132.1 27.2 %copy-start.14 = (f32[1,1,3072]{2,0,1:T(1,128)S(1)}, f32[1,1,3072]{2,0,1:T(1,128)}, u32[]{:S(2)}) copy-start(f32[1,1,3072]{2,0,1:T(1,128)} %copy-done.13) | copy-start | bytes 36868
  151.3 7.6 %collective-permute-start = (bf16[2,3072]{1,0:T(2,128)(2,1)S(1)}, bf16[2,3072]{1,0:T(2,128)(2,1)S(1)}, u32[]{:S(2)}, u32[]{:S(2)}) collective-permute-start(bf16[2,3072]{1,0:T(2,128)(2,1)S(1)} %fusion.98), channel_id=1, source_target_pairs={{448,0},{0,64},{64,128},{128,192},{192,256},{256,320},{320,384},{3... | collective-permute-start | bytes 36872 | tf_op jit(solution)/shard_map/ppermute | solution.py:20
  175.8 11.0 %copy-start.2 = (bf16[1,3,48,3072]{3,2,1,0:T(8,128)(2,1)S(1)}, bf16[1,3,48,3072]{3,2,1,0:T(8,128)(2,1)}, u32[]{:S(2)}) copy-start(bf16[1,3,48,3072]{3,2,1,0:T(8,128)(2,1)} %param.10) | copy-start | bytes 2654212
  187.2 20.9 %copy-start.8 = (bf16[192,3,128]{2,1,0:T(4,128)(2,1)S(1)}, bf16[192,3,128]{2,1,0:T(4,128)(2,1)}, u32[]{:S(2)}) copy-start(bf16[192,3,128]{2,1,0:T(4,128)(2,1)} %copy-done.7) | copy-start | bytes 442372
  187.2 20.9 %copy-start.21 = (f32[128]{0:T(128)S(1)}, f32[128]{0:T(128)}, u32[]{:S(2)}) copy-start(f32[128]{0:T(128)} %copy-done.20) | copy-start | bytes 1540
  187.2 20.9 %copy-start.23 = (pred[192]{0:T(512)(128)(4,1)S(1)}, pred[192]{0:T(512)(128)(4,1)}, u32[]{:S(2)}) copy-start(pred[192]{0:T(512)(128)(4,1)} %copy-done.22) | copy-start | bytes 580
  187.2 21.2 %copy-start.19 = (f32[128]{0:T(128)S(1)}, f32[128]{0:T(128)}, u32[]{:S(2)}) copy-start(f32[128]{0:T(128)} %copy-done.18) | copy-start | bytes 1540
  187.2 21.2 %copy-start.25 = (pred[128]{0:T(512)(128)(4,1)S(1)}, pred[128]{0:T(512)(128)(4,1)}, u32[]{:S(2)}) copy-start(pred[128]{0:T(512)(128)(4,1)} %copy-done.24) | copy-start | bytes 388
  208.0 0.9 copy-start.4
  208.5 19.5 %copy-start.5 = (bf16[1,48,3072]{2,1,0:T(8,128)(2,1)S(1)}, bf16[1,48,3072]{2,1,0:T(8,128)(2,1)}, u32[]{:S(2)}) copy-start(bf16[1,48,3072]{2,1,0:T(8,128)(2,1)} %param.12) | copy-start | bytes 884740
  208.5 19.5 %copy-start.15 = (pred[48]{0:T(512)(128)(4,1)S(1)}, pred[48]{0:T(512)(128)(4,1)}, u32[]{:S(2)}) copy-start(pred[48]{0:T(512)(128)(4,1)} %get-tuple-element.34) | copy-start | bytes 148
  208.5 19.5 %copy-start.16 = (pred[48]{0:T(512)(128)(4,1)S(1)}, pred[48]{0:T(512)(128)(4,1)}, u32[]{:S(2)}) copy-start(pred[48]{0:T(512)(128)(4,1)} %get-tuple-element.35) | copy-start | bytes 148
  262.3 15.7 %collective-permute-start.1 = (bf16[2,3072]{1,0:T(2,128)(2,1)S(1)}, bf16[2,3072]{1,0:T(2,128)(2,1)S(1)}, u32[]{:S(2)}, u32[]{:S(2)}) collective-permute-start(bf16[2,3072]{1,0:T(2,128)(2,1)S(1)} %fusion.103), channel_id=1, source_target_pairs={{448,0},{0,64},{64,128},{128,192},{192,256},{256,320},{320,384},{3... | collective-permute-start | bytes 36872 | tf_op jit(solution)/shard_map/ppermute | solution.py:20

commit v3 on v2

--- a/solution.py
+++ b/solution.py
@@ -9,6 +9,7 @@
 TXT = 512
 TEAM = 8
 TEAM_HEADS = 3
+LANES = 128
 
 eps_norm = 1e-06
 f32 = jnp.float32
@@ -64,11 +65,6 @@
     along_z = [[z_count * x + z for z in range(z_count)] for x in range(x_count)]
     along_x = [[z_count * x + z for x in range(x_count)] for z in range(z_count)]
     inside = [[TEAM * t + m for m in range(TEAM)] for t in range(teams)]
-    offset = [TEAM + TEAM // 2 if m < TEAM // 2 else TEAM // 2 for m in range(TEAM)]
-    across = [
-        [z_count * x + m + half * offset[m] for x in range(x_count) for half in range(2)]
-        for m in range(TEAM)
-    ]
     shift_scale = modulation[0]
     gains = qk_gain[0]
     weight_qkv = w_qkv[0].reshape(3 * shard, width)
@@ -76,19 +72,31 @@
     weight_attn = w_attn_out[0]
     weight_down = w_mlp_out[0]
 
-    cached = context_kv[0].reshape(2, ctx_local, teams, team_width).transpose(2, 0, 1, 3)
-    cached = lax.all_to_all(cached, "tp", 0, 0, axis_index_groups=across)
-    cached = cached.transpose(1, 0, 2, 3).reshape(2, teams * ctx_local, TEAM_HEADS, HEAD_DIM)
-    cached_keys, cached_values = cached[0], cached[1]
+    half_team = TEAM // 2
+    partner = [
+        z + TEAM + half_team if z < half_team else z + half_team if z < TEAM
+        else z - half_team if z < TEAM + half_team else z - TEAM - half_team
+        for z in range(z_count)
+    ]
     z_here = tp_index % z_count
-    low = jnp.where(
-        z_here < TEAM, z_here, (z_here - TEAM + TEAM // 2) % TEAM
+    z_partner = jnp.where(
+        z_here < TEAM,
+        z_here + jnp.where(z_here < half_team, TEAM + half_team, half_team),
+        z_here - jnp.where(z_here < TEAM + half_team, half_team, TEAM + half_team),
     )
-    high = low + jnp.where(low < TEAM // 2, TEAM + TEAM // 2, TEAM // 2)
+    by_half = context_kv[0].reshape(2, ctx_local, x_count, 2, team_width)
+    upper = z_here >= TEAM
+    keep = jnp.where(upper, by_half[:, :, :, 1], by_half[:, :, :, 0])
+    give = jnp.where(upper, by_half[:, :, :, 0], by_half[:, :, :, 1])
+    got = lax.ppermute(
+        give, "tp", [(z_count * x + z, z_count * x + partner[z]) for x in range(x_count) for z in range(z_count)]
+    )
+    cached = jnp.concatenate([keep, got], axis=1).transpose(2, 1, 0, 3)
+    cached = cached.reshape(x_count, 2 * ctx_local, 2 * team_width)
     slot = jnp.arange(teams * ctx_local, dtype=jnp.int32)
-    source = slot // ctx_local
-    source = z_count * (source // 2) + jnp.where(source % 2 == 0, low, high)
-    position = ctx_local * source + slot % ctx_local
+    within = slot % (2 * ctx_local)
+    source = z_count * (slot // (2 * ctx_local)) + jnp.where(within < ctx_local, z_here, z_partner)
+    position = ctx_local * source + within % ctx_local
     cached_mask = (position >= TXT) | (position < text_len[0])
     token = jnp.arange(tokens, dtype=jnp.int32)
     fresh_mask = token // (tokens // TEAM) == member
@@ -96,7 +104,22 @@
     current = in_flight[0]
     for tick_number in range(TICKS):
         normed_rows = modulated(current, shift_scale)
-        normed = gathered(gathered(normed_rows, along_z), along_x)
+        normed = gathered(normed_rows.reshape(rows * width // LANES, LANES), along_z)
+        normed = normed.reshape(rows * z_count, width)
+        if tick_number == 0:
+            wide = 2 * team_width
+            split = width // wide
+            normed = normed.reshape(-1, split, wide).transpose(1, 0, 2).reshape(-1, wide)
+            both = jnp.concatenate(
+                [jnp.broadcast_to(normed[None], (x_count,) + normed.shape), cached], axis=1
+            )
+            both = lax.all_to_all(both, "tp", 0, 0, axis_index_groups=along_x)
+            normed = both[:, : normed.shape[0]].reshape(x_count, split, -1, wide)
+            normed = normed.transpose(0, 2, 1, 3).reshape(tokens, width)
+            cached = both[:, split * rows * z_count :].reshape(-1, 2, TEAM_HEADS, HEAD_DIM)
+            cached_keys, cached_values = cached[:, 0], cached[:, 1]
+        else:
+            normed = gathered(normed, along_x)
         own = lax.dot_general(
             weight_qkv, normed, (((1,), (1,)), ((), ())), preferred_element_type=f32
         ).astype(bf16)
@@ -133,11 +156,12 @@
             ),
             approximate=True,
         ).astype(bf16)
+        hidden = lax.optimization_barrier(hidden)
         branch = lax.dot_general(
             attention, weight_attn, (((0,), (0,)), ((), ())), preferred_element_type=f32
         ) + jnp.dot(hidden, weight_down, preferred_element_type=f32)
         branch = summed_over(branch * shift_scale[2], along_x)
-        branch = summed_over(branch, along_z)
+        branch = summed_over(branch.reshape(-1, LANES), along_z).reshape(rows, width)
         finished = (current.astype(f32) + branch).astype(bf16)
         current = shifted(finished, "pipe", 1)
     return current[None]

time: 280 us -> 271 us (0.968)
  blocking collectives: 156 us -> 126 us
  starting transfers between devices: 55.9 us -> 74.5 us
  local copies, waits for them, and re-layouts: 4.78 us -> 9.5 us
  matrix products: 11.6 us -> 7.53 us
    all_to_all x4 -> x3, blocking collectives: 75.9 us -> 47.8 us  [gathered(): spread = lax.all_to_all(spread, 'tp', 0, 0, axis_index_groups=groups)]
    ppermute x0 -> x1, waiting for transfers between devices: none -> 13.8 us  [local(): lax.ppermute(give, 'tp', [(z_count * x + z, z_count * x + partner[z]) for...]
    all_to_all x2, waiting for transfers between devices: 21.4 us -> 9.69 us  [gathered(): spread = lax.all_to_all(spread, 'tp', 0, 0, axis_index_groups=groups)]
    all_to_all x1 -> x2, starting transfers between devices: 7.79 us -> 18.7 us  [local(): parts = lax.all_to_all(parts, 'tp', 0, 0, axis_index_groups=inside)]
    all_to_all x1 -> x0, waiting for transfers between devices: 10.1 us -> none  [local(): cached = lax.all_to_all(cached, 'tp', 0, 0, axis_index_groups=across)]
    all_to_all x1 -> x2, waiting for transfers between devices: 9.69 us -> 19.5 us  [local(): parts = lax.all_to_all(parts, 'tp', 0, 0, axis_index_groups=inside)]
    ppermute x0 -> x1, starting transfers between devices: none -> 7.17 us  [local(): lax.ppermute(give, 'tp', [(z_count * x + z, z_count * x + partner[z]) for...]
    all_to_all x2, starting transfers between devices: 19.8 us -> 26.9 us  [gathered(): spread = lax.all_to_all(spread, 'tp', 0, 0, axis_index_groups=groups)]
  transfers between devices with their start and end apart: 6 -> 7, of which waited for: 6 -> 6; matrix products, arithmetic and copies ran while one was open for 1% -> 2% of each run, Pallas kernels for 0% -> 0%
where the time goes in v3:
time: 271 us; the launch traced here: 270 us
  blocking collectives  126 us (46%)
  starting transfers between devices  74.5 us (27%)
  waiting for transfers between devices  44.6 us (16%)
  local copies, waits for them, and re-layouts  9.5 us (4%)
  matrix products  7.53 us (3%)
  other arithmetic  6.81 us (3%)
    all_to_all x4, blocking collectives, summed_over(): parts = lax.all_to_all(parts, 'tp', 0, 0, axis_index_groups=groups)  59.7 us
    all_to_all x3, blocking collectives, gathered(): spread = lax.all_to_all(spread, 'tp', 0, 0, axis_index_groups=groups)  47.8 us
    all_to_all x2, starting transfers between devices, gathered(): spread = lax.all_to_all(spread, 'tp', 0, 0, axis_index_groups=groups)  26.9 us
    ppermute x2, starting transfers between devices, shifted(): lax.ppermute(block, axis, [((i - distance) % size, i) for i in range(size)])  21.8 us
    all_to_all x2, waiting for transfers between devices, local(): parts = lax.all_to_all(parts, 'tp', 0, 0, axis_index_groups=inside)  19.5 us
    all_to_all x2, starting transfers between devices, local(): parts = lax.all_to_all(parts, 'tp', 0, 0, axis_index_groups=inside)  18.7 us
    all_to_all x1, blocking collectives, local(): both = lax.all_to_all(both, 'tp', 0, 0, axis_index_groups=along_x)  18.2 us
    ppermute x1, waiting for transfers between devices, local(): lax.ppermute(give, 'tp', [(z_count * x + z, z_count * x + partner[z]) for...  13.8 us
  transfers between devices with their start and end apart: 7, of which 6 were waited for; matrix products, arithmetic and copies ran while one was open for 2% of the time, Pallas kernels for 0%

profile of v3, /device:TPU:1, one launch (start us, length us, event | category | flops | bytes accessed | tf_op | source)
XLA Modules:
  0.0 270.1 jit_solution(1344702192711728297)
XLA Ops:
  0.0 0.9 convert_reduce_fusion.5
  0.9 0.7 reshape.301
  1.7 0.9 fusion.83
  2.9 0.8 fusion.115
  3.7 0.6 copy-done.7
  4.4 0.7 broadcast_in_dim.184
  5.1 15.7 %all-to-all-start = ((bf16[16,48,128]{2,1,0:T(8,128)(2,1)}), bf16[16,48,128]{2,1,0:T(8,128)(2,1)S(1)}, u32[]{:S(2)}, u32[]{:S(2)}) async-start(bf16[16,48,128]{2,1,0:T(8,128)(2,1)} %broadcast_in_dim.184), calls=%async_computation | async-start | bytes 393216 | tf_op jit(solution)/shard_map/all_to_all | solution.py:40
  20.8 1.2 reshape_squeeze.6
  22.0 0.7 broadcast_select_fusion.1
  22.7 7.2 %collective-permute-start = (bf16[2,24,4,384]{3,1,2,0:T(8,128)(2,1)S(1)}, bf16[2,24,4,384]{3,1,2,0:T(8,128)(2,1)S(1)}, u32[]{:S(2)}, u32[]{:S(2)}) collective-permute-start(bf16[2,24,4,384]{3,1,2,0:T(8,128)(2,1)S(1)} %bitcast.166), channel_id=1, source_target_pairs={{0,12},{1,13},{2,14},{3,15},{4,8},{5,9},{6,10},{7,11},{8,4},{9,5},... | collective-permute-start | bytes 442376 | tf_op jit(solution)/shard_map/ppermute | solution.py:91
  29.9 13.8 %collective-permute-done = bf16[2,24,4,384]{3,1,2,0:T(8,128)(2,1)S(1)} collective-permute-done((bf16[2,24,4,384]{3,1,2,0:T(8,128)(2,1)S(1)}, bf16[2,24,4,384]{3,1,2,0:T(8,128)(2,1)S(1)}, u32[]{:S(2)}, u32[]{:S(2)}) %collective-permute-start) | collective-permute-done | bytes 147488 | tf_op jit(solution)/shard_map/ppermute | solution.py:91
  44.0 18.2 %all_to_all.60 = bf16[4,176,768]{2,1,0:T(8,128)(2,1)S(1)} all-to-all(bf16[4,176,768]{2,1,0:T(8,128)(2,1)S(1)} %pad_maximum_fusion), channel_id=1, replica_groups={{0,16,32,48},{1,17,33,49},{2,18,34,50},{3,19,35,51},{4,20,36,52},{5,21,..., dimensions={0} | all-to-all | bytes 2162688 | tf_op jit(solution)/shard_map/all_to_all | solution.py:116
  62.3 0.6 copy.43
  63.1 1.0 copy-done.2
  64.1 0.4 fusion.16
  64.5 0.7 broadcast_in_dim.190
  65.3 11.1 %all-to-all-start.2 = ((bf16[8,144,128]{2,1,0:T(8,128)(2,1)}), bf16[8,144,128]{2,1,0:T(8,128)(2,1)S(1)}, u32[]{:S(2)}, u32[]{:S(2)}) async-start(bf16[8,144,128]{2,1,0:T(8,128)(2,1)} %broadcast_in_dim.190), calls=%async_computation.2 | async-start | bytes 589824 | tf_op jit(solution)/shard_map/all_to_all | solution.py:40
  77.2 0.7 slice.120
  77.9 1.1 reshape.291
  79.2 9.7 %all-to-all-done.2 = bf16[8,144,128]{2,1,0:T(8,128)(2,1)S(1)} async-done(((bf16[8,144,128]{2,1,0:T(8,128)(2,1)}), bf16[8,144,128]{2,1,0:T(8,128)(2,1)S(1)}, u32[]{:S(2)}, u32[]{:S(2)}) %all-to-all-start.2) | async-done | bytes 294944 | tf_op jit(solution)/shard_map/all_to_all | solution.py:40
  89.4 0.3 fusion.117
  90.2 0.7 maximum_maximum_fusion
  90.9 10.2 %all-to-all-start.3 = ((bf16[8,64,128]{2,1,0:T(8,128)(2,1)}), bf16[8,64,128]{2,1,0:T(8,128)(2,1)S(1)}, u32[]{:S(2)}, u32[]{:S(2)}) async-start(bf16[8,64,128]{2,1,0:T(8,128)(2,1)} %maximum_maximum_fusion), calls=%async_computation.3 | async-start | bytes 262144 | tf_op jit(solution)/shard_map/all_to_all | solution.py:146
  101.1 0.5 fusion.49
  101.6 9.7 %all-to-all-done.3 = bf16[8,64,128]{2,1,0:T(8,128)(2,1)S(1)} async-done(((bf16[8,64,128]{2,1,0:T(8,128)(2,1)}), bf16[8,64,128]{2,1,0:T(8,128)(2,1)S(1)}, u32[]{:S(2)}, u32[]{:S(2)}) %all-to-all-start.3) | async-done | bytes 131104 | tf_op jit(solution)/shard_map/all_to_all | solution.py:146
  111.4 1.4 fusion.20
  112.9 0.4 fusion.3
  113.3 11.8 %all_to_all.61 = bf16[4,32,3072]{2,1,0:T(8,128)(2,1)S(1)} all-to-all(bf16[4,32,3072]{2,1,0:T(8,128)(2,1)S(1)} %bitcast.145), channel_id=1, replica_groups={{0,16,32,48},{1,17,33,49},{2,18,34,50},{3,19,35,51},{4,20,36,52},{5,21,..., dimensions={0} | all-to-all | bytes 1572864 | tf_op jit(solution)/shard_map/all_to_all | solution.py:47
  125.3 18.8 %all_to_all.62 = bf16[16,48,128]{2,1,0:T(8,128)(2,1)S(1)} all-to-all(bf16[16,48,128]{2,1,0:T(8,128)(2,1)S(1)} %convert_element_type.195), channel_id=1, replica_groups={{0,1,2,3,4,5,6,7,8,9,10,11,12,13,14,15},{16,17,18,19,20,21,22,23,24,25,..., dimensions={0} | all-to-all | bytes 393216 | tf_op jit(solution)/shard_map/all_to_all | solution.py:47
  144.2 6.8 %collective-permute-start.1 = (bf16[2,3072]{1,0:T(2,128)(2,1)S(1)}, bf16[2,3072]{1,0:T(2,128)(2,1)S(1)}, u32[]{:S(2)}, u32[]{:S(2)}) collective-permute-start(bf16[2,3072]{1,0:T(2,128)(2,1)S(1)} %fusion.84), channel_id=1, source_target_pairs={{448,0},{0,64},{64,128},{128,192},{192,256},{256,320},{320,384},{3... | collective-permute-start | bytes 36872 | tf_op jit(solution)/shard_map/ppermute | solution.py:21
  151.0 0.8 collective-permute-done.1
  152.2 0.8 fusion.77
  153.1 16.3 %all_to_all.63 = bf16[16,48,128]{2,1,0:T(8,128)(2,1)S(1)} all-to-all(bf16[16,48,128]{2,1,0:T(8,128)(2,1)S(1)} %broadcast_in_dim.204), channel_id=1, replica_groups={{0,1,2,3,4,5,6,7,8,9,10,11,12,13,14,15},{16,17,18,19,20,21,22,23,24,25,..., dimensions={0} | all-to-all | bytes 393216 | tf_op jit(solution)/shard_map/all_to_all | solution.py:40
  169.5 10.9 %all_to_all.64 = bf16[4,32,3072]{2,1,0:T(8,128)(2,1)S(1)} all-to-all(bf16[4,32,3072]{2,1,0:T(8,128)(2,1)S(1)} %broadcast_in_dim.206), channel_id=1, replica_groups={{0,16,32,48},{1,17,33,49},{2,18,34,50},{3,19,35,51},{4,20,36,52},{5,21,..., dimensions={0} | all-to-all | bytes 1572864 | tf_op jit(solution)/shard_map/all_to_all | solution.py:40
  180.4 0.4 fusion.17
  180.9 20.7 %all_to_all.65 = bf16[8,144,128]{2,1,0:T(8,128)(2,1)S(1)} all-to-all(bf16[8,144,128]{2,1,0:T(8,128)(2,1)S(1)} %broadcast_in_dim.207), channel_id=1, replica_groups={{0,1,2,3,4,5,6,7},{8,9,10,11,12,13,14,15},{16,17,18,19,20,21,22,23},{24..., dimensions={0} | all-to-all | bytes 589824 | tf_op jit(solution)/shard_map/all_to_all | solution.py:40
  202.1 0.3 fusion.119
  202.9 0.7 maximum_maximum_fusion.1
  203.6 8.5 %all-to-all-start.9 = ((bf16[8,64,128]{2,1,0:T(8,128)(2,1)}), bf16[8,64,128]{2,1,0:T(8,128)(2,1)S(1)}, u32[]{:S(2)}, u32[]{:S(2)}) async-start(bf16[8,64,128]{2,1,0:T(8,128)(2,1)} %maximum_maximum_fusion.1), calls=%async_computation.9 | async-start | bytes 262144 | tf_op jit(solution)/shard_map/all_to_all | solution.py:146
  212.1 0.5 fusion.61
  212.6 9.8 %all-to-all-done.9 = bf16[8,64,128]{2,1,0:T(8,128)(2,1)S(1)} async-done(((bf16[8,64,128]{2,1,0:T(8,128)(2,1)}), bf16[8,64,128]{2,1,0:T(8,128)(2,1)S(1)}, u32[]{:S(2)}, u32[]{:S(2)}) %all-to-all-start.9) | async-done | bytes 131104 | tf_op jit(solution)/shard_map/all_to_all | solution.py:146
  222.4 1.4 fusion.18
  223.9 0.4 fusion.2
  224.3 10.9 %all_to_all.66 = bf16[4,32,3072]{2,1,0:T(8,128)(2,1)S(1)} all-to-all(bf16[4,32,3072]{2,1,0:T(8,128)(2,1)S(1)} %bitcast.144), channel_id=1, replica_groups={{0,16,32,48},{1,17,33,49},{2,18,34,50},{3,19,35,51},{4,20,36,52},{5,21,..., dimensions={0} | all-to-all | bytes 1572864 | tf_op jit(solution)/shard_map/all_to_all | solution.py:47
  235.4 18.3 %all_to_all.67 = bf16[16,48,128]{2,1,0:T(8,128)(2,1)S(1)} all-to-all(bf16[16,48,128]{2,1,0:T(8,128)(2,1)S(1)} %convert_element_type.216), channel_id=1, replica_groups={{0,1,2,3,4,5,6,7,8,9,10,11,12,13,14,15},{16,17,18,19,20,21,22,23,24,25,..., dimensions={0} | all-to-all | bytes 393216 | tf_op jit(solution)/shard_map/all_to_all | solution.py:47
  253.7 14.9 %collective-permute-start.2 = (bf16[2,3072]{1,0:T(2,128)(2,1)S(1)}, bf16[2,3072]{1,0:T(2,128)(2,1)S(1)}, u32[]{:S(2)}, u32[]{:S(2)}) collective-permute-start(bf16[2,3072]{1,0:T(2,128)(2,1)S(1)} %fusion.78), channel_id=1, source_target_pairs={{448,0},{0,64},{64,128},{128,192},{192,256},{256,320},{320,384},{3... | collective-permute-start | bytes 36872 | tf_op jit(solution)/shard_map/ppermute | solution.py:21
  268.7 0.8 collective-permute-done.2
  269.5 0.6 copy.68
  (113 shorter events, 4.2 us)
Async XLA Ops:
  0.0 112.9 %copy-start = (bf16[1,192,3072]{2,1,0:T(8,128)(2,1)S(1)}, bf16[1,192,3072]{2,1,0:T(8,128)(2,1)}, u32[]{:S(2)}) copy-start(bf16[1,192,3072]{2,1,0:T(8,128)(2,1)} %param.13) | copy-start | bytes 3538948
  3.7 0.6 copy-start.7
  3.7 0.7 copy-start.8
  3.7 109.2 %copy-start.9 = (f32[1,1,3072]{2,0,1:T(1,128)}, f32[1,1,3072]{2,0,1:T(1,128)S(1)}, u32[]{:S(2)}) copy-start(f32[1,1,3072]{2,0,1:T(1,128)S(1)} %get-tuple-element.15) | copy-start | bytes 36868
  5.1 38.7 %all-to-all-start = ((bf16[16,48,128]{2,1,0:T(8,128)(2,1)}), bf16[16,48,128]{2,1,0:T(8,128)(2,1)S(1)}, u32[]{:S(2)}, u32[]{:S(2)}) async-start(bf16[16,48,128]{2,1,0:T(8,128)(2,1)} %broadcast_in_dim.184), calls=%async_computation | async-start | bytes 393216 | tf_op jit(solution)/shard_map/all_to_all | solution.py:40
  22.7 21.0 %collective-permute-start = (bf16[2,24,4,384]{3,1,2,0:T(8,128)(2,1)S(1)}, bf16[2,24,4,384]{3,1,2,0:T(8,128)(2,1)S(1)}, u32[]{:S(2)}, u32[]{:S(2)}) collective-permute-start(bf16[2,24,4,384]{3,1,2,0:T(8,128)(2,1)S(1)} %bitcast.166), channel_id=1, source_target_pairs={{0,12},{1,13},{2,14},{3,15},{4,8},{5,9},{6,10},{7,11},{8,4},{9,5},... | collective-permute-start | bytes 442376 | tf_op jit(solution)/shard_map/ppermute | solution.py:91
  62.9 1.2 copy-start.2
  64.1 13.1 %copy-start.15 = (f32[1,2,128]{2,1,0:T(2,128)S(1)}, f32[1,2,128]{2,1,0:T(2,128)}, u32[]{:S(2)}) copy-start(f32[1,2,128]{2,1,0:T(2,128)} %param.15) | copy-start | bytes 3076
  65.3 23.6 %all-to-all-start.2 = ((bf16[8,144,128]{2,1,0:T(8,128)(2,1)}), bf16[8,144,128]{2,1,0:T(8,128)(2,1)S(1)}, u32[]{:S(2)}, u32[]{:S(2)}) async-start(bf16[8,144,128]{2,1,0:T(8,128)(2,1)} %broadcast_in_dim.190), calls=%async_computation.2 | async-start | bytes 589824 | tf_op jit(solution)/shard_map/all_to_all | solution.py:40
  77.1 12.2 %copy-start.22 = (pred[128]{0:T(512)(128)(4,1)}, pred[128]{0:T(512)(128)(4,1)S(1)}, u32[]{:S(2)}) copy-start(pred[128]{0:T(512)(128)(4,1)S(1)} %fusion.107) | copy-start | bytes 388
  77.2 11.8 %copy-start.20 = (pred[192]{0:T(512)(128)(4,1)}, pred[192]{0:T(512)(128)(4,1)S(1)}, u32[]{:S(2)}) copy-start(pred[192]{0:T(512)(128)(4,1)S(1)} %compare_or_fusion) | copy-start | bytes 580
  77.2 12.1 %copy-start.16 = (f32[128]{0:T(128)}, f32[128]{0:T(128)S(1)}, u32[]{:S(2)}) copy-start(f32[128]{0:T(128)S(1)} %get-tuple-element.24) | copy-start | bytes 1540
  77.2 12.1 %copy-start.18 = (f32[128]{0:T(128)}, f32[128]{0:T(128)S(1)}, u32[]{:S(2)}) copy-start(f32[128]{0:T(128)S(1)} %get-tuple-element.25) | copy-start | bytes 1540
  79.2 9.8 %copy-start.5 = (bf16[192,1,3,128]{3,2,1,0:T(4,128)(2,1)}, bf16[192,1,3,128]{3,2,1,0:T(4,128)(2,1)S(1)}, u32[]{:S(2)}) copy-start(bf16[192,1,3,128]{3,2,1,0:T(4,128)(2,1)S(1)} %get-tuple-element.6) | copy-start | bytes 442372
  89.3 11.8 %copy-start.1 = (bf16[1,192,3072]{2,1,0:T(8,128)(2,1)S(1)}, bf16[1,192,3072]{2,1,0:T(8,128)(2,1)}, u32[]{:S(2)}) copy-start(bf16[1,192,3072]{2,1,0:T(8,128)(2,1)} %param.11) | copy-start | bytes 3538948
  90.9 20.5 %all-to-all-start.3 = ((bf16[8,64,128]{2,1,0:T(8,128)(2,1)}), bf16[8,64,128]{2,1,0:T(8,128)(2,1)S(1)}, u32[]{:S(2)}, u32[]{:S(2)}) async-start(bf16[8,64,128]{2,1,0:T(8,128)(2,1)} %maximum_maximum_fusion), calls=%async_computation.3 | async-start | bytes 262144 | tf_op jit(solution)/shard_map/all_to_all | solution.py:146
  101.1 11.7 %copy-start.11 = (pred[48]{0:T(512)(128)(4,1)}, pred[48]{0:T(512)(128)(4,1)S(1)}, u32[]{:S(2)}) copy-start(pred[48]{0:T(512)(128)(4,1)S(1)} %get-tuple-element.36) | copy-start | bytes 148
  101.1 11.7 %copy-start.13 = (pred[48]{0:T(512)(128)(4,1)}, pred[48]{0:T(512)(128)(4,1)S(1)}, u32[]{:S(2)}) copy-start(pred[48]{0:T(512)(128)(4,1)S(1)} %get-tuple-element.37) | copy-start | bytes 148
  125.0 19.1 %copy-start.4 = (bf16[1,2,3072]{2,1,0:T(2,128)(2,1)S(1)}, bf16[1,2,3072]{2,1,0:T(2,128)(2,1)}, u32[]{:S(2)}) copy-start(bf16[1,2,3072]{2,1,0:T(2,128)(2,1)} %param.9) | copy-start | bytes 36868
  144.2 7.6 %collective-permute-start.1 = (bf16[2,3072]{1,0:T(2,128)(2,1)S(1)}, bf16[2,3072]{1,0:T(2,128)(2,1)S(1)}, u32[]{:S(2)}, u32[]{:S(2)}) collective-permute-start(bf16[2,3072]{1,0:T(2,128)(2,1)S(1)} %fusion.84), channel_id=1, source_target_pairs={{448,0},{0,64},{64,128},{128,192},{192,256},{256,320},{320,384},{3... | collective-permute-start | bytes 36872 | tf_op jit(solution)/shard_map/ppermute | solution.py:21
  169.4 11.0 %copy-start.3 = (bf16[1,3,48,3072]{3,2,1,0:T(8,128)(2,1)S(1)}, bf16[1,3,48,3072]{3,2,1,0:T(8,128)(2,1)}, u32[]{:S(2)}) copy-start(bf16[1,3,48,3072]{3,2,1,0:T(8,128)(2,1)} %param.10) | copy-start | bytes 2654212
  180.8 20.9 %copy-start.6 = (bf16[192,1,3,128]{3,2,1,0:T(4,128)(2,1)S(1)}, bf16[192,1,3,128]{3,2,1,0:T(4,128)(2,1)}, u32[]{:S(2)}) copy-start(bf16[192,1,3,128]{3,2,1,0:T(4,128)(2,1)} %copy-done.5) | copy-start | bytes 442372
  180.8 20.9 %copy-start.19 = (f32[128]{0:T(128)S(1)}, f32[128]{0:T(128)}, u32[]{:S(2)}) copy-start(f32[128]{0:T(128)} %copy-done.18) | copy-start | bytes 1540
  180.8 20.9 %copy-start.21 = (pred[192]{0:T(512)(128)(4,1)S(1)}, pred[192]{0:T(512)(128)(4,1)}, u32[]{:S(2)}) copy-start(pred[192]{0:T(512)(128)(4,1)} %copy-done.20) | copy-start | bytes 580
  180.8 21.2 %copy-start.17 = (f32[128]{0:T(128)S(1)}, f32[128]{0:T(128)}, u32[]{:S(2)}) copy-start(f32[128]{0:T(128)} %copy-done.16) | copy-start | bytes 1540
  180.9 21.2 %copy-start.23 = (pred[128]{0:T(512)(128)(4,1)S(1)}, pred[128]{0:T(512)(128)(4,1)}, u32[]{:S(2)}) copy-start(pred[128]{0:T(512)(128)(4,1)} %copy-done.22) | copy-start | bytes 388
  203.6 18.8 %copy-start.12 = (pred[48]{0:T(512)(128)(4,1)S(1)}, pred[48]{0:T(512)(128)(4,1)}, u32[]{:S(2)}) copy-start(pred[48]{0:T(512)(128)(4,1)} %copy-done.11) | copy-start | bytes 148
  203.6 18.8 %copy-start.14 = (pred[48]{0:T(512)(128)(4,1)S(1)}, pred[48]{0:T(512)(128)(4,1)}, u32[]{:S(2)}) copy-start(pred[48]{0:T(512)(128)(4,1)} %copy-done.13) | copy-start | bytes 148
  203.6 18.8 %all-to-all-start.9 = ((bf16[8,64,128]{2,1,0:T(8,128)(2,1)}), bf16[8,64,128]{2,1,0:T(8,128)(2,1)S(1)}, u32[]{:S(2)}, u32[]{:S(2)}) async-start(bf16[8,64,128]{2,1,0:T(8,128)(2,1)} %maximum_maximum_fusion.1), calls=%async_computation.9 | async-start | bytes 262144 | tf_op jit(solution)/shard_map/all_to_all | solution.py:146
  212.6 11.3 %copy-start.10 = (f32[1,1,3072]{2,0,1:T(1,128)S(1)}, f32[1,1,3072]{2,0,1:T(1,128)}, u32[]{:S(2)}) copy-start(f32[1,1,3072]{2,0,1:T(1,128)} %copy-done.9) | copy-start | bytes 36868
  253.7 15.8 %collective-permute-start.2 = (bf16[2,3072]{1,0:T(2,128)(2,1)S(1)}, bf16[2,3072]{1,0:T(2,128)(2,1)S(1)}, u32[]{:S(2)}, u32[]{:S(2)}) collective-permute-start(bf16[2,3072]{1,0:T(2,128)(2,1)S(1)} %fusion.78), channel_id=1, source_target_pairs={{448,0},{0,64},{64,128},{128,192},{192,256},{256,320},{320,384},{3... | collective-permute-start | bytes 36872 | tf_op jit(solution)/shard_map/ppermute | solution.py:21

commit v4 on v3

--- a/solution.py
+++ b/solution.py
@@ -1,6 +1,8 @@
 import jax
 import jax.numpy as jnp
 from jax import lax
+from jax.experimental import pallas as pl
+from jax.experimental.pallas import tpu as pltpu
 from jax.sharding import PartitionSpec as P
 
 HEADS = 24
@@ -29,9 +31,61 @@
     return (normed * (1.0 + shift_scale[1]) + shift_scale[0]).astype(bf16)
 
 
-def head_norm(values_in, gain_vector):
-    mean_square = jnp.mean(values_in * values_in, axis=-2, keepdims=True)
-    return values_in * lax.rsqrt(mean_square + eps_norm) * gain_vector[:, None]
+def attend_kernel(team_ref, cached_ref, mask_ref, gain_q_ref, gain_k_ref, out_ref, packed_ref):
+    shard = team_ref.shape[1] - 16
+    members = team_ref.shape[0]
+    lane = lax.broadcasted_iota(jnp.int32, (16, LANES), 1)
+    row = lax.broadcasted_iota(jnp.int32, (16, LANES), 0)
+    fresh = [team_ref[c, shard:, :].astype(f32) for c in range(members)]
+    features = jnp.concatenate([team_ref[c, :shard, :] for c in range(members)], axis=0)
+    open_key = mask_ref[...] > 0.0
+    sums = jnp.zeros((16, LANES), f32)
+    for h in range(TEAM_HEADS):
+        query = features[h * HEAD_DIM : (h + 1) * HEAD_DIM].astype(f32)
+        scale = lax.rsqrt(jnp.mean(query * query, axis=0, keepdims=True) + eps_norm)
+        query = (query * scale * gain_q_ref[...] * HEAD_DIM ** (-0.5)).astype(bf16)
+        key = jnp.zeros((16, LANES), f32)
+        value = jnp.zeros((16, LANES), f32)
+        for c in range(members):
+            start = c * shard - h * HEAD_DIM
+            if start <= -shard or start >= HEAD_DIM:
+                continue
+            here = (lane >= start) & (lane < start + shard)
+            key = jnp.where(here, pltpu.roll(fresh[c], start % LANES, 1), key)
+            value = jnp.where(here, pltpu.roll(fresh[c], (start - shard) % LANES, 1), value)
+        scale = lax.rsqrt(jnp.mean(key * key, axis=1, keepdims=True) + eps_norm)
+        key = (key * scale * gain_k_ref[...]).astype(bf16)
+        cached_key = cached_ref[:, h * HEAD_DIM : (h + 1) * HEAD_DIM]
+        at = (TEAM_HEADS + h) * HEAD_DIM
+        cached_value = cached_ref[:, at : at + HEAD_DIM]
+        scores = jnp.dot(cached_key, query, preferred_element_type=f32)
+        probs = jnp.exp(jnp.where(open_key, scores, -1e30))
+        fresh_probs = jnp.exp(jnp.dot(key, query, preferred_element_type=f32))
+        total = jnp.sum(probs, axis=0, keepdims=True) + jnp.sum(fresh_probs, axis=0, keepdims=True)
+        sums = jnp.where(row == h, total, sums)
+        contract = (((0,), (0,)), ((), ()))
+        weighted = lax.dot_general(
+            cached_value, probs.astype(bf16), contract, preferred_element_type=f32
+        ) + lax.dot_general(
+            value.astype(bf16), fresh_probs.astype(bf16), contract, preferred_element_type=f32
+        )
+        packed_ref[h * HEAD_DIM : (h + 1) * HEAD_DIM, :] = weighted.astype(bf16)
+    for c in range(members):
+        out_ref[c, :shard, :] = packed_ref[c * shard : (c + 1) * shard, :]
+        out_ref[c, shard:, :] = sums.astype(bf16)
+
+
+def attend(team, cached, mask, gains, interpret=False):
+    whole = pl.BlockSpec(memory_space=pltpu.VMEM)
+    return pl.pallas_call(
+        attend_kernel,
+        out_shape=jax.ShapeDtypeStruct(team.shape, bf16),
+        in_specs=[whole] * 5,
+        out_specs=whole,
+        scratch_shapes=[pltpu.VMEM((TEAM_HEADS * HEAD_DIM, LANES), bf16)],
+        compiler_params=pltpu.CompilerParams(vmem_limit_bytes=16 * 1024 * 1024),
+        interpret=interpret,
+    )(team, cached, mask, gains[0][:, None], gains[1][None, :])
 
 
 def gathered(block, groups):
@@ -67,7 +121,8 @@
     inside = [[TEAM * t + m for m in range(TEAM)] for t in range(teams)]
     shift_scale = modulation[0]
     gains = qk_gain[0]
-    weight_qkv = w_qkv[0].reshape(3 * shard, width)
+    weight_q = w_qkv[0, 0]
+    weight_kv = w_qkv[0, 1:].reshape(2 * shard, width)
     weight_mlp = w_mlp[0]
     weight_attn = w_attn_out[0]
     weight_down = w_mlp_out[0]
@@ -97,10 +152,8 @@
     within = slot % (2 * ctx_local)
     source = z_count * (slot // (2 * ctx_local)) + jnp.where(within < ctx_local, z_here, z_partner)
     position = ctx_local * source + within % ctx_local
-    cached_mask = (position >= TXT) | (position < text_len[0])
-    token = jnp.arange(tokens, dtype=jnp.int32)
-    fresh_mask = token // (tokens // TEAM) == member
-
+    cached_mask = ((position >= TXT) | (position < text_len[0])).astype(f32)
+    cached_mask = jnp.broadcast_to(cached_mask[:, None], (teams * ctx_local, LANES))
     current = in_flight[0]
     for tick_number in range(TICKS):
         normed_rows = modulated(current, shift_scale)
@@ -116,33 +169,21 @@
             both = lax.all_to_all(both, "tp", 0, 0, axis_index_groups=along_x)
             normed = both[:, : normed.shape[0]].reshape(x_count, split, -1, wide)
             normed = normed.transpose(0, 2, 1, 3).reshape(tokens, width)
-            cached = both[:, split * rows * z_count :].reshape(-1, 2, TEAM_HEADS, HEAD_DIM)
-            cached_keys, cached_values = cached[:, 0], cached[:, 1]
+            cached = both[:, split * rows * z_count :].reshape(-1, wide)
         else:
             normed = gathered(normed, along_x)
-        own = lax.dot_general(
-            weight_qkv, normed, (((1,), (1,)), ((), ())), preferred_element_type=f32
+        own_q = lax.dot_general(
+            weight_q, normed, (((1,), (1,)), ((), ())), preferred_element_type=f32
         ).astype(bf16)
-        team = gathered(own, inside).reshape(TEAM, 3, shard, tokens).transpose(1, 0, 2, 3)
-        team = team.reshape(3, TEAM_HEADS, HEAD_DIM, tokens)
-        queries = (head_norm(team[0].astype(f32), gains[0]) * HEAD_DIM ** (-0.5)).astype(bf16)
-        fresh_keys = head_norm(team[1].astype(f32), gains[1]).astype(bf16)
-        fresh_values = team[2]
-        cached_scores = jnp.einsum("khd,hdq->hkq", cached_keys, queries, preferred_element_type=f32)
-        fresh_scores = jnp.einsum("hdk,hdq->hkq", fresh_keys, queries, preferred_element_type=f32)
-        cached_probs = jnp.exp(jnp.where(cached_mask[None, :, None], cached_scores, -1e30))
-        fresh_probs = jnp.exp(jnp.where(fresh_mask[None, :, None], fresh_scores, -1e30))
-        totals = jnp.sum(cached_probs, axis=1) + jnp.sum(fresh_probs, axis=1)
-        weighted = jnp.einsum(
-            "khd,hkq->hdq", cached_values, cached_probs.astype(bf16), preferred_element_type=f32
-        ) + jnp.einsum(
-            "hdk,hkq->hdq", fresh_values, fresh_probs.astype(bf16), preferred_element_type=f32
+        own_kv = lax.dot_general(
+            normed, weight_kv, (((1,), (1,)), ((), ())), preferred_element_type=f32
+        ).astype(bf16)
+        own_kv = jnp.pad(own_kv, ((0, 0), (0, LANES - 2 * shard))).reshape(TEAM, -1, LANES)
+        team = jnp.concatenate(
+            [jnp.broadcast_to(own_q[None], (TEAM,) + own_q.shape), own_kv], axis=1
         )
-        parts = weighted.astype(bf16).reshape(TEAM, shard, tokens)
-        spread_totals = jnp.broadcast_to(totals.astype(bf16)[None], (TEAM, TEAM_HEADS, tokens))
-        parts = jnp.concatenate(
-            [parts, spread_totals, jnp.zeros((TEAM, 16 - TEAM_HEADS, tokens), bf16)], axis=1
-        )
+        team = lax.all_to_all(team, "tp", 0, 0, axis_index_groups=inside)
+        parts = attend(team, cached, cached_mask, gains)
         parts = lax.all_to_all(parts, "tp", 0, 0, axis_index_groups=inside)
         summed = jnp.sum(parts.astype(f32), axis=0)
         feature_head = (member * shard + jnp.arange(shard, dtype=jnp.int32)) // HEAD_DIM
@@ -157,10 +198,13 @@
             approximate=True,
         ).astype(bf16)
         hidden = lax.optimization_barrier(hidden)
+        forward = jnp.dot(hidden, weight_down, preferred_element_type=f32) * shift_scale[2]
+        forward = lax.optimization_barrier(forward)
         branch = lax.dot_general(
             attention, weight_attn, (((0,), (0,)), ((), ())), preferred_element_type=f32
-        ) + jnp.dot(hidden, weight_down, preferred_element_type=f32)
-        branch = summed_over(branch * shift_scale[2], along_x)
+        )
+        branch = branch * shift_scale[2] + forward
+        branch = summed_over(branch, along_x)
         branch = summed_over(branch.reshape(-1, LANES), along_z).reshape(rows, width)
         finished = (current.astype(f32) + branch).astype(bf16)
         current = shifted(finished, "pipe", 1)

time: 271 us -> 255 us (0.941)
  blocking collectives: 126 us -> 104 us
  waiting for transfers between devices: 44.6 us -> 53.7 us
  starting transfers between devices: 74.5 us -> 68.4 us
  Pallas kernels: 0 us -> 2.95 us
    all_to_all x0 -> x2, waiting for transfers between devices: none -> 22.1 us  [the longest x1 13.6 us: local(): both = lax.all_to_all(both, 'tp', 0, 0, axis_index_groups=along_x)]
    all_to_all x3 -> x2, blocking collectives: 47.8 us -> 27 us  [gathered(): spread = lax.all_to_all(spread, 'tp', 0, 0, axis_index_groups=groups)]
    all_to_all x0 -> x2, starting transfers between devices: none -> 15.1 us  [the longest x1 11.1 us: local(): team = lax.all_to_all(team, 'tp', 0, 0, axis_index_groups=inside)]
    all_to_all x2 -> x1, starting transfers between devices: 26.9 us -> 15.7 us  [gathered(): spread = lax.all_to_all(spread, 'tp', 0, 0, axis_index_groups=groups)]
    all_to_all x2, starting transfers between devices: 18.7 us -> 8.78 us  [local(): parts = lax.all_to_all(parts, 'tp', 0, 0, axis_index_groups=inside)]
    all_to_all x2 -> x1, waiting for transfers between devices: 9.69 us -> 0.01 us  [gathered(): spread = lax.all_to_all(spread, 'tp', 0, 0, axis_index_groups=groups)]
    all_to_all x2, waiting for transfers between devices: 19.5 us -> 16.2 us  [local(): parts = lax.all_to_all(parts, 'tp', 0, 0, axis_index_groups=inside)]
    pallas_call x0 -> x2, Pallas kernels: none -> 2.95 us  [attend(): pl.pallas_call(attend_kernel, out_shape=jax.ShapeDtypeStruct(team.shape,...]
  transfers between devices with their start and end apart: 7 -> 8, of which waited for: 6 -> 7; matrix products, arithmetic and copies ran while one was open for 2% -> 3% of each run, Pallas kernels for 0% -> 0%
where the time goes in v4:
time: 255 us; the launch traced here: 254 us
  blocking collectives  104 us (41%)
  starting transfers between devices  68.4 us (27%)
  waiting for transfers between devices  53.7 us (21%)
  matrix products  8.78 us (3%)
  local copies, waits for them, and re-layouts  7.86 us (3%)
  other arithmetic  7 us (3%)
  Pallas kernels  2.95 us (1%)
    all_to_all x4, blocking collectives, summed_over(): parts = lax.all_to_all(parts, 'tp', 0, 0, axis_index_groups=groups)  59.7 us
    all_to_all x2, blocking collectives, gathered(): spread = lax.all_to_all(spread, 'tp', 0, 0, axis_index_groups=groups)  27 us
    ppermute x2, starting transfers between devices, shifted(): lax.ppermute(block, axis, [((i - distance) % size, i) for i in range(size)])  21.6 us
    all_to_all x1, blocking collectives, local(): team = lax.all_to_all(team, 'tp', 0, 0, axis_index_groups=inside)  17.6 us
    all_to_all x2, waiting for transfers between devices, local(): parts = lax.all_to_all(parts, 'tp', 0, 0, axis_index_groups=inside)  16.2 us
    all_to_all x1, starting transfers between devices, gathered(): spread = lax.all_to_all(spread, 'tp', 0, 0, axis_index_groups=groups)  15.7 us
    ppermute x1, waiting for transfers between devices, local(): lax.ppermute(give, 'tp', [(z_count * x + z, z_count * x + partner[z]) for...  13.8 us
    all_to_all x1, waiting for transfers between devices, local(): both = lax.all_to_all(both, 'tp', 0, 0, axis_index_groups=along_x)  13.6 us
  transfers between devices with their start and end apart: 8, of which 7 were waited for; matrix products, arithmetic and copies ran while one was open for 3% of the time, Pallas kernels for 0%

profile of v4, /device:TPU:1, one launch (start us, length us, event | category | flops | bytes accessed | tf_op | source)
XLA Modules:
  0.0 254.2 jit_solution(17704028907880665430)
XLA Ops:
  0.0 0.9 convert_reduce_fusion.5
  0.9 0.7 reshape.219
  1.7 0.9 fusion.53
  2.9 0.8 fusion.73
  3.8 0.7 broadcast_in_dim.138
  4.5 15.7 %all-to-all-start = ((bf16[16,48,128]{2,1,0:T(8,128)(2,1)}), bf16[16,48,128]{2,1,0:T(8,128)(2,1)S(1)}, u32[]{:S(2)}, u32[]{:S(2)}) async-start(bf16[16,48,128]{2,1,0:T(8,128)(2,1)} %broadcast_in_dim.138), calls=%async_computation | async-start | bytes 393216 | tf_op jit(solution)/shard_map/all_to_all | solution.py:94
  20.2 1.2 reshape_squeeze.6
  21.4 0.7 broadcast_select_fusion.1
  22.1 7.2 %collective-permute-start = (bf16[2,24,4,384]{3,1,2,0:T(8,128)(2,1)S(1)}, bf16[2,24,4,384]{3,1,2,0:T(8,128)(2,1)S(1)}, u32[]{:S(2)}, u32[]{:S(2)}) collective-permute-start(bf16[2,24,4,384]{3,1,2,0:T(8,128)(2,1)S(1)} %bitcast.132), channel_id=1, source_target_pairs={{0,12},{1,13},{2,14},{3,15},{4,8},{5,9},{6,10},{7,11},{8,4},{9,5},... | collective-permute-start | bytes 442376 | tf_op jit(solution)/shard_map/ppermute | solution.py:146
  29.4 13.8 %collective-permute-done = bf16[2,24,4,384]{3,1,2,0:T(8,128)(2,1)S(1)} collective-permute-done((bf16[2,24,4,384]{3,1,2,0:T(8,128)(2,1)S(1)}, bf16[2,24,4,384]{3,1,2,0:T(8,128)(2,1)S(1)}, u32[]{:S(2)}, u32[]{:S(2)}) %collective-permute-start) | collective-permute-done | bytes 147488 | tf_op jit(solution)/shard_map/ppermute | solution.py:146
  43.4 1.1 pad_maximum_fusion
  44.4 4.0 %all-to-all-start.1 = ((bf16[4,176,768]{2,1,0:T(8,128)(2,1)}), bf16[4,176,768]{2,1,0:T(8,128)(2,1)S(1)}, u32[]{:S(2)}, u32[]{:S(2)}) async-start(bf16[4,176,768]{2,1,0:T(8,128)(2,1)} %pad_maximum_fusion), calls=%async_computation.1 | async-start | bytes 2162688 | tf_op jit(solution)/shard_map/all_to_all | solution.py:169
  48.5 1.1 slice.79
  49.6 13.6 %all-to-all-done.1 = bf16[4,176,768]{2,1,0:T(8,128)(2,1)S(1)} async-done(((bf16[4,176,768]{2,1,0:T(8,128)(2,1)}), bf16[4,176,768]{2,1,0:T(8,128)(2,1)S(1)}, u32[]{:S(2)}, u32[]{:S(2)}) %all-to-all-start.1) | async-done | bytes 1081376 | tf_op jit(solution)/shard_map/all_to_all | solution.py:169
  63.2 0.6 copy.45
  64.3 1.3 fusion.10
  65.6 0.4 convolution_convert_fusion.1
  66.2 0.7 pad_maximum_fusion.1
  66.8 11.1 %all-to-all-start.2 = ((bf16[8,64,128]{2,1,0:T(8,128)(2,1)}), bf16[8,64,128]{2,1,0:T(8,128)(2,1)S(1)}, u32[]{:S(2)}, u32[]{:S(2)}) async-start(bf16[8,64,128]{2,1,0:T(8,128)(2,1)} %pad_maximum_fusion.1), calls=%async_computation.2 | async-start | bytes 262144 | tf_op jit(solution)/shard_map/all_to_all | solution.py:185
  78.8 1.0 slice.96
  79.8 8.5 %all-to-all-done.2.team_ref = bf16[8,64,128]{2,1,0:T(8,128)(2,1)S(1)} async-done(((bf16[8,64,128]{2,1,0:T(8,128)(2,1)}), bf16[8,64,128]{2,1,0:T(8,128)(2,1)S(1)}, u32[]{:S(2)}, u32[]{:S(2)}) %all-to-all-start.2) | async-done | bytes 131104 | tf_op jit(solution)/shard_map/all_to_all | solution.py:185
  88.4 1.5 shard_map.91
  89.9 5.4 %all-to-all-start.3 = ((bf16[8,64,128]{2,1,0:T(8,128)(2,1)}), bf16[8,64,128]{2,1,0:T(8,128)(2,1)}, u32[]{:S(2)}, u32[]{:S(2)}) async-start(bf16[8,64,128]{2,1,0:T(8,128)(2,1)} %shard_map.91), calls=%async_computation.3 | async-start | bytes 262144 | tf_op jit(solution)/shard_map/all_to_all | solution.py:187
  95.3 1.8 fusion.27
  97.1 0.4 convolution_multiply_fusion.1
  97.5 8.2 %all-to-all-done.3 = bf16[8,64,128]{2,1,0:T(8,128)(2,1)} async-done(((bf16[8,64,128]{2,1,0:T(8,128)(2,1)}), bf16[8,64,128]{2,1,0:T(8,128)(2,1)}, u32[]{:S(2)}, u32[]{:S(2)}) %all-to-all-start.3) | async-done | bytes 131104 | tf_op jit(solution)/shard_map/all_to_all | solution.py:187
  105.7 0.9 convert_reduce_fusion.3
  106.6 0.5 fusion.2
  107.1 11.6 %all_to_all.60 = bf16[4,32,3072]{2,1,0:T(8,128)(2,1)S(1)} all-to-all(bf16[4,32,3072]{2,1,0:T(8,128)(2,1)S(1)} %bitcast.123), channel_id=1, replica_groups={{0,16,32,48},{1,17,33,49},{2,18,34,50},{3,19,35,51},{4,20,36,52},{5,21,..., dimensions={0} | all-to-all | bytes 1572864 | tf_op jit(solution)/shard_map/all_to_all | solution.py:101
  119.0 19.1 %all_to_all.61 = bf16[16,48,128]{2,1,0:T(8,128)(2,1)S(1)} all-to-all(bf16[16,48,128]{2,1,0:T(8,128)(2,1)S(1)} %convert_element_type.119), channel_id=1, replica_groups={{0,1,2,3,4,5,6,7,8,9,10,11,12,13,14,15},{16,17,18,19,20,21,22,23,24,25,..., dimensions={0} | all-to-all | bytes 393216 | tf_op jit(solution)/shard_map/all_to_all | solution.py:101
  138.3 6.8 %collective-permute-start.1 = (bf16[2,3072]{1,0:T(2,128)(2,1)S(1)}, bf16[2,3072]{1,0:T(2,128)(2,1)S(1)}, u32[]{:S(2)}, u32[]{:S(2)}) collective-permute-start(bf16[2,3072]{1,0:T(2,128)(2,1)S(1)} %fusion.54), channel_id=1, source_target_pairs={{448,0},{0,64},{64,128},{128,192},{192,256},{256,320},{320,384},{3... | collective-permute-start | bytes 36872 | tf_op jit(solution)/shard_map/ppermute | solution.py:23
  145.1 0.8 collective-permute-done.1
  146.4 16.2 %all_to_all.62 = bf16[16,48,128]{2,1,0:T(8,128)(2,1)S(1)} all-to-all(bf16[16,48,128]{2,1,0:T(8,128)(2,1)S(1)} %broadcast_in_dim.154), channel_id=1, replica_groups={{0,1,2,3,4,5,6,7,8,9,10,11,12,13,14,15},{16,17,18,19,20,21,22,23,24,25,..., dimensions={0} | all-to-all | bytes 393216 | tf_op jit(solution)/shard_map/all_to_all | solution.py:94
  162.8 10.7 %all_to_all.63 = bf16[4,32,3072]{2,1,0:T(8,128)(2,1)S(1)} all-to-all(bf16[4,32,3072]{2,1,0:T(8,128)(2,1)S(1)} %broadcast_in_dim.156), channel_id=1, replica_groups={{0,16,32,48},{1,17,33,49},{2,18,34,50},{3,19,35,51},{4,20,36,52},{5,21,..., dimensions={0} | all-to-all | bytes 1572864 | tf_op jit(solution)/shard_map/all_to_all | solution.py:94
  173.6 0.4 convolution_convert_fusion
  174.0 1.3 fusion.11
  175.5 17.6 %all_to_all.64.team_ref = bf16[8,64,128]{2,1,0:T(8,128)(2,1)S(1)} all-to-all(bf16[8,64,128]{2,1,0:T(8,128)(2,1)S(1)} %pad_maximum_fusion.2), channel_id=1, replica_groups={{0,1,2,3,4,5,6,7},{8,9,10,11,12,13,14,15},{16,17,18,19,20,21,22,23},{24..., dimensions={0} | all-to-all | bytes 262144 | tf_op jit(solution)/shard_map/all_to_all | solution.py:185
  193.1 1.5 shard_map.92
  194.6 3.4 %all-to-all-start.9 = ((bf16[8,64,128]{2,1,0:T(8,128)(2,1)}), bf16[8,64,128]{2,1,0:T(8,128)(2,1)S(1)}, u32[]{:S(2)}, u32[]{:S(2)}) async-start(bf16[8,64,128]{2,1,0:T(8,128)(2,1)} %shard_map.92), calls=%async_computation.9 | async-start | bytes 262144 | tf_op jit(solution)/shard_map/all_to_all | solution.py:187
  197.9 1.8 fusion.39
  199.7 0.4 convolution_multiply_fusion
  200.1 8.0 %all-to-all-done.9 = bf16[8,64,128]{2,1,0:T(8,128)(2,1)S(1)} async-done(((bf16[8,64,128]{2,1,0:T(8,128)(2,1)}), bf16[8,64,128]{2,1,0:T(8,128)(2,1)S(1)}, u32[]{:S(2)}, u32[]{:S(2)}) %all-to-all-start.9) | async-done | bytes 131104 | tf_op jit(solution)/shard_map/all_to_all | solution.py:187
  208.2 0.5 fusion.3
  208.7 10.7 %all_to_all.65 = bf16[4,32,3072]{2,1,0:T(8,128)(2,1)S(1)} all-to-all(bf16[4,32,3072]{2,1,0:T(8,128)(2,1)S(1)} %bitcast.122), channel_id=1, replica_groups={{0,16,32,48},{1,17,33,49},{2,18,34,50},{3,19,35,51},{4,20,36,52},{5,21,..., dimensions={0} | all-to-all | bytes 1572864 | tf_op jit(solution)/shard_map/all_to_all | solution.py:101
  219.7 18.2 %all_to_all.66 = bf16[16,48,128]{2,1,0:T(8,128)(2,1)S(1)} all-to-all(bf16[16,48,128]{2,1,0:T(8,128)(2,1)S(1)} %convert_element_type.131), channel_id=1, replica_groups={{0,1,2,3,4,5,6,7,8,9,10,11,12,13,14,15},{16,17,18,19,20,21,22,23,24,25,..., dimensions={0} | all-to-all | bytes 393216 | tf_op jit(solution)/shard_map/all_to_all | solution.py:101
  238.0 14.7 %collective-permute-start.2 = (bf16[2,3072]{1,0:T(2,128)(2,1)S(1)}, bf16[2,3072]{1,0:T(2,128)(2,1)S(1)}, u32[]{:S(2)}, u32[]{:S(2)}) collective-permute-start(bf16[2,3072]{1,0:T(2,128)(2,1)S(1)} %fusion.48), channel_id=1, source_target_pairs={{448,0},{0,64},{64,128},{128,192},{192,256},{256,320},{320,384},{3... | collective-permute-start | bytes 36872 | tf_op jit(solution)/shard_map/ppermute | solution.py:23
  252.7 0.8 collective-permute-done.2
  253.6 0.6 copy.60
  (69 shorter events, 3.0 us)
Async XLA Ops:
  0.0 97.1 %copy-start = (bf16[1,192,3072]{2,1,0:T(8,128)(2,1)S(1)}, bf16[1,192,3072]{2,1,0:T(8,128)(2,1)}, u32[]{:S(2)}) copy-start(bf16[1,192,3072]{2,1,0:T(8,128)(2,1)} %param.13) | copy-start | bytes 3538948
  3.7 25.7 %copy-start.6 = (f32[1,1,3072]{2,0,1:T(1,128)}, f32[1,1,3072]{2,0,1:T(1,128)S(1)}, u32[]{:S(2)}) copy-start(f32[1,1,3072]{2,0,1:T(1,128)S(1)} %get-tuple-element.9) | copy-start | bytes 36868
  4.5 38.7 %all-to-all-start = ((bf16[16,48,128]{2,1,0:T(8,128)(2,1)}), bf16[16,48,128]{2,1,0:T(8,128)(2,1)S(1)}, u32[]{:S(2)}, u32[]{:S(2)}) async-start(bf16[16,48,128]{2,1,0:T(8,128)(2,1)} %broadcast_in_dim.138), calls=%async_computation | async-start | bytes 393216 | tf_op jit(solution)/shard_map/all_to_all | solution.py:94
  22.1 21.0 %collective-permute-start = (bf16[2,24,4,384]{3,1,2,0:T(8,128)(2,1)S(1)}, bf16[2,24,4,384]{3,1,2,0:T(8,128)(2,1)S(1)}, u32[]{:S(2)}, u32[]{:S(2)}) collective-permute-start(bf16[2,24,4,384]{3,1,2,0:T(8,128)(2,1)S(1)} %bitcast.132), channel_id=1, source_target_pairs={{0,12},{1,13},{2,14},{3,15},{4,8},{5,9},{6,10},{7,11},{8,4},{9,5},... | collective-permute-start | bytes 442376 | tf_op jit(solution)/shard_map/ppermute | solution.py:146
  44.4 18.7 %all-to-all-start.1 = ((bf16[4,176,768]{2,1,0:T(8,128)(2,1)}), bf16[4,176,768]{2,1,0:T(8,128)(2,1)S(1)}, u32[]{:S(2)}, u32[]{:S(2)}) async-start(bf16[4,176,768]{2,1,0:T(8,128)(2,1)} %pad_maximum_fusion), calls=%async_computation.1 | async-start | bytes 2162688 | tf_op jit(solution)/shard_map/all_to_all | solution.py:169
  49.6 16.1 %copy-start.1 = (bf16[1,2,48,3072]{3,2,1,0:T(8,128)(2,1)}, bf16[1,2,48,3072]{3,2,1,0:T(8,128)(2,1)S(1)}, u32[]{:S(2)}) copy-start(bf16[1,2,48,3072]{3,2,1,0:T(8,128)(2,1)S(1)} %slice.79) | copy-start | bytes 1769476
  63.2 1.0 copy-start.3
  64.3 14.4 %copy-start.8 = (f32[1,2,128]{2,1,0:T(2,128)S(1)}, f32[1,2,128]{2,1,0:T(2,128)}, u32[]{:S(2)}) copy-start(f32[1,2,128]{2,1,0:T(2,128)} %param.15) | copy-start | bytes 3076
  66.8 21.5 %all-to-all-start.2 = ((bf16[8,64,128]{2,1,0:T(8,128)(2,1)}), bf16[8,64,128]{2,1,0:T(8,128)(2,1)S(1)}, u32[]{:S(2)}, u32[]{:S(2)}) async-start(bf16[8,64,128]{2,1,0:T(8,128)(2,1)} %pad_maximum_fusion.1), calls=%async_computation.2 | async-start | bytes 262144 | tf_op jit(solution)/shard_map/all_to_all | solution.py:185
  89.9 15.8 %all-to-all-start.3 = ((bf16[8,64,128]{2,1,0:T(8,128)(2,1)}), bf16[8,64,128]{2,1,0:T(8,128)(2,1)}, u32[]{:S(2)}, u32[]{:S(2)}) async-start(bf16[8,64,128]{2,1,0:T(8,128)(2,1)} %shard_map.91), calls=%async_computation.3 | async-start | bytes 262144 | tf_op jit(solution)/shard_map/all_to_all | solution.py:187
  97.1 9.6 %copy-start.4 = (bf16[1,48,3072]{2,1,0:T(8,128)(2,1)S(1)}, bf16[1,48,3072]{2,1,0:T(8,128)(2,1)}, u32[]{:S(2)}) copy-start(bf16[1,48,3072]{2,1,0:T(8,128)(2,1)} %param.12) | copy-start | bytes 884740
  107.1 31.1 %copy-start.5 = (bf16[1,2,3072]{2,1,0:T(2,128)(2,1)S(1)}, bf16[1,2,3072]{2,1,0:T(2,128)(2,1)}, u32[]{:S(2)}) copy-start(bf16[1,2,3072]{2,1,0:T(2,128)(2,1)} %param.9) | copy-start | bytes 36868
  107.1 39.2 %copy-start.7 = (f32[1,1,3072]{2,0,1:T(1,128)S(1)}, f32[1,1,3072]{2,0,1:T(1,128)}, u32[]{:S(2)}) copy-start(f32[1,1,3072]{2,0,1:T(1,128)} %copy-done.6) | copy-start | bytes 36868
  138.3 7.7 %collective-permute-start.1 = (bf16[2,3072]{1,0:T(2,128)(2,1)S(1)}, bf16[2,3072]{1,0:T(2,128)(2,1)S(1)}, u32[]{:S(2)}, u32[]{:S(2)}) collective-permute-start(bf16[2,3072]{1,0:T(2,128)(2,1)S(1)} %fusion.54), channel_id=1, source_target_pairs={{448,0},{0,64},{64,128},{128,192},{192,256},{256,320},{320,384},{3... | collective-permute-start | bytes 36872 | tf_op jit(solution)/shard_map/ppermute | solution.py:23
  162.7 10.9 %copy-start.2 = (bf16[1,2,48,3072]{3,2,1,0:T(8,128)(2,1)S(1)}, bf16[1,2,48,3072]{3,2,1,0:T(8,128)(2,1)}, u32[]{:S(2)}) copy-start(bf16[1,2,48,3072]{3,2,1,0:T(8,128)(2,1)} %copy-done.1) | copy-start | bytes 1769476
  194.6 13.6 %all-to-all-start.9 = ((bf16[8,64,128]{2,1,0:T(8,128)(2,1)}), bf16[8,64,128]{2,1,0:T(8,128)(2,1)S(1)}, u32[]{:S(2)}, u32[]{:S(2)}) async-start(bf16[8,64,128]{2,1,0:T(8,128)(2,1)} %shard_map.92), calls=%async_computation.9 | async-start | bytes 262144 | tf_op jit(solution)/shard_map/all_to_all | solution.py:187
  238.0 15.6 %collective-permute-start.2 = (bf16[2,3072]{1,0:T(2,128)(2,1)S(1)}, bf16[2,3072]{1,0:T(2,128)(2,1)S(1)}, u32[]{:S(2)}, u32[]{:S(2)}) collective-permute-start(bf16[2,3072]{1,0:T(2,128)(2,1)S(1)} %fusion.48), channel_id=1, source_target_pairs={{448,0},{0,64},{64,128},{128,192},{192,256},{256,320},{320,384},{3... | collective-permute-start | bytes 36872 | tf_op jit(solution)/shard_map/ppermute | solution.py:23

commit v5 on v4

--- a/solution.py
+++ b/solution.py
@@ -29,6 +29,33 @@
     row_var = jnp.mean(jnp.square(x_float - row_mean), axis=-1, keepdims=True)
     normed = (x_float - row_mean) * lax.rsqrt(row_var + eps_norm)
     return (normed * (1.0 + shift_scale[1]) + shift_scale[0]).astype(bf16)
+
+
+def project_kernel(normed_ref, weight_ref, out_ref):
+    members = out_ref.shape[0]
+    shard = weight_ref.shape[0] // 3
+    contract = (((1,), (1,)), ((), ()))
+    query = lax.dot_general(
+        weight_ref[:shard], normed_ref[...], contract, preferred_element_type=f32
+    ).astype(bf16)
+    others = lax.dot_general(
+        normed_ref[...], weight_ref[shard:], contract, preferred_element_type=f32
+    ).astype(bf16)
+    for c in range(members):
+        out_ref[c, :shard, :] = query
+        out_ref[c, shard:, : 2 * shard] = others[16 * c : 16 * c + 16]
+        out_ref[c, shard:, 2 * shard :] = jnp.zeros((16, LANES - 2 * shard), bf16)
+
+
+def project(normed, weights):
+    whole = pl.BlockSpec(memory_space=pltpu.VMEM)
+    return pl.pallas_call(
+        project_kernel,
+        out_shape=jax.ShapeDtypeStruct((TEAM, weights.shape[0] // 3 + 16, LANES), bf16),
+        in_specs=[whole] * 2,
+        out_specs=whole,
+        compiler_params=pltpu.CompilerParams(vmem_limit_bytes=16 * 1024 * 1024),
+    )(normed, weights)
 
 
 def attend_kernel(team_ref, cached_ref, mask_ref, gain_q_ref, gain_k_ref, out_ref, packed_ref):
@@ -121,8 +148,7 @@
     inside = [[TEAM * t + m for m in range(TEAM)] for t in range(teams)]
     shift_scale = modulation[0]
     gains = qk_gain[0]
-    weight_q = w_qkv[0, 0]
-    weight_kv = w_qkv[0, 1:].reshape(2 * shard, width)
+    weight_qkv = w_qkv[0].reshape(3 * shard, width)
     weight_mlp = w_mlp[0]
     weight_attn = w_attn_out[0]
     weight_down = w_mlp_out[0]
@@ -133,55 +159,57 @@
         else z - half_team if z < TEAM + half_team else z - TEAM - half_team
         for z in range(z_count)
     ]
-    z_here = tp_index % z_count
+    x_here, z_here = tp_index // z_count, tp_index % z_count
     z_partner = jnp.where(
         z_here < TEAM,
         z_here + jnp.where(z_here < half_team, TEAM + half_team, half_team),
         z_here - jnp.where(z_here < TEAM + half_team, half_team, TEAM + half_team),
     )
-    by_half = context_kv[0].reshape(2, ctx_local, x_count, 2, team_width)
     upper = z_here >= TEAM
-    keep = jnp.where(upper, by_half[:, :, :, 1], by_half[:, :, :, 0])
-    give = jnp.where(upper, by_half[:, :, :, 0], by_half[:, :, :, 1])
-    got = lax.ppermute(
-        give, "tp", [(z_count * x + z, z_count * x + partner[z]) for x in range(x_count) for z in range(z_count)]
-    )
-    cached = jnp.concatenate([keep, got], axis=1).transpose(2, 1, 0, 3)
-    cached = cached.reshape(x_count, 2 * ctx_local, 2 * team_width)
     slot = jnp.arange(teams * ctx_local, dtype=jnp.int32)
     within = slot % (2 * ctx_local)
-    source = z_count * (slot // (2 * ctx_local)) + jnp.where(within < ctx_local, z_here, z_partner)
+    source = z_count * ((x_here - slot // (2 * ctx_local)) % x_count)
+    source = source + jnp.where(within < ctx_local, z_here, z_partner)
     position = ctx_local * source + within % ctx_local
     cached_mask = ((position >= TXT) | (position < text_len[0])).astype(f32)
     cached_mask = jnp.broadcast_to(cached_mask[:, None], (teams * ctx_local, LANES))
+
     current = in_flight[0]
+    first_rows = modulated(current, shift_scale)
+    first_rows, flat = lax.optimization_barrier((first_rows, context_kv[0]))
+    flat = flat.reshape(2 * ctx_local, width)
+    by_x = []
+    for step in range(x_count):
+        block = lax.dynamic_slice_in_dim(
+            flat, (x_here + step) % x_count * 2 * team_width, 2 * team_width, 1
+        )
+        if step:
+            route = [
+                (z_count * x + z, z_count * ((x + step) % x_count) + z)
+                for x in range(x_count) for z in range(z_count)
+            ]
+            block = lax.ppermute(block, "tp", route)
+        by_x.append(block)
+    by_x = jnp.stack(by_x)
+    keep = jnp.where(upper, by_x[:, :, team_width:], by_x[:, :, :team_width])
+    give = jnp.where(upper, by_x[:, :, :team_width], by_x[:, :, team_width:])
+
     for tick_number in range(TICKS):
-        normed_rows = modulated(current, shift_scale)
+        normed_rows = modulated(current, shift_scale) if tick_number else first_rows
         normed = gathered(normed_rows.reshape(rows * width // LANES, LANES), along_z)
         normed = normed.reshape(rows * z_count, width)
         if tick_number == 0:
-            wide = 2 * team_width
-            split = width // wide
-            normed = normed.reshape(-1, split, wide).transpose(1, 0, 2).reshape(-1, wide)
-            both = jnp.concatenate(
-                [jnp.broadcast_to(normed[None], (x_count,) + normed.shape), cached], axis=1
+            normed, give = lax.optimization_barrier((normed, give))
+            got = lax.ppermute(
+                give,
+                "tp",
+                [(z_count * x + z, z_count * x + partner[z]) for x in range(x_count) for z in range(z_count)],
             )
-            both = lax.all_to_all(both, "tp", 0, 0, axis_index_groups=along_x)
-            normed = both[:, : normed.shape[0]].reshape(x_count, split, -1, wide)
-            normed = normed.transpose(0, 2, 1, 3).reshape(tokens, width)
-            cached = both[:, split * rows * z_count :].reshape(-1, wide)
-        else:
-            normed = gathered(normed, along_x)
-        own_q = lax.dot_general(
-            weight_q, normed, (((1,), (1,)), ((), ())), preferred_element_type=f32
-        ).astype(bf16)
-        own_kv = lax.dot_general(
-            normed, weight_kv, (((1,), (1,)), ((), ())), preferred_element_type=f32
-        ).astype(bf16)
-        own_kv = jnp.pad(own_kv, ((0, 0), (0, LANES - 2 * shard))).reshape(TEAM, -1, LANES)
-        team = jnp.concatenate(
-            [jnp.broadcast_to(own_q[None], (TEAM,) + own_q.shape), own_kv], axis=1
-        )
+            cached = jnp.stack([keep, got], axis=1)
+            cached = cached.reshape(x_count, 2, 2, ctx_local, team_width).transpose(0, 1, 3, 2, 4)
+            cached = cached.reshape(teams * ctx_local, 2 * team_width)
+        normed = gathered(normed, along_x)
+        team = project(normed, weight_qkv)
         team = lax.all_to_all(team, "tp", 0, 0, axis_index_groups=inside)
         parts = attend(team, cached, cached_mask, gains)
         parts = lax.all_to_all(parts, "tp", 0, 0, axis_index_groups=inside)

time: 255 us -> 249 us (0.976)
  waiting for transfers between devices: 53.7 us -> 36.4 us
  starting transfers between devices: 68.4 us -> 83.5 us
    all_to_all x1 -> x0, waiting for transfers between devices: 13.6 us -> none  [local(): both = lax.all_to_all(both, 'tp', 0, 0, axis_index_groups=along_x)]
    all_to_all x1 -> x2, waiting for transfers between devices: 0.01 us -> 9.52 us  [gathered(): spread = lax.all_to_all(spread, 'tp', 0, 0, axis_index_groups=groups)]
    ppermute x0 -> x3, starting transfers between devices: none -> 9.33 us  [local(): block = lax.ppermute(block, 'tp', route)]
    all_to_all x1, waiting for transfers between devices: 8.49 us -> 0.01 us  [local(): team = lax.all_to_all(team, 'tp', 0, 0, axis_index_groups=inside)]
    ppermute x1, waiting for transfers between devices: 13.8 us -> 5.7 us  [local(): lax.ppermute(give, 'tp', [(z_count * x + z, z_count * x + partner[z]) for...]
    all_to_all x2, starting transfers between devices: 8.78 us -> 16.8 us  [local(): parts = lax.all_to_all(parts, 'tp', 0, 0, axis_index_groups=inside)]
    ppermute x0 -> x3, waiting for transfers between devices: none -> 4.51 us  [local(): block = lax.ppermute(block, 'tp', route)]
    all_to_all x1 -> x0, starting transfers between devices: 4.01 us -> none  [local(): both = lax.all_to_all(both, 'tp', 0, 0, axis_index_groups=along_x)]
  transfers between devices with their start and end apart: 8 -> 11, of which waited for: 7 -> 8; matrix products, arithmetic and copies ran while one was open for 3% -> 4% of each run, Pallas kernels for 0% -> 0%
where the time goes in v5:
time: 249 us; the launch traced here: 248 us
  blocking collectives  103 us (41%)
  starting transfers between devices  83.5 us (34%)
  waiting for transfers between devices  36.4 us (15%)
  matrix products  7.87 us (3%)
  other arithmetic  6.83 us (3%)
  local copies, waits for them, and re-layouts  5.62 us (2%)
  Pallas kernels  4.05 us (2%)
    all_to_all x4, blocking collectives, summed_over(): parts = lax.all_to_all(parts, 'tp', 0, 0, axis_index_groups=groups)  58.3 us
    all_to_all x2, blocking collectives, gathered(): spread = lax.all_to_all(spread, 'tp', 0, 0, axis_index_groups=groups)  26.6 us
    ppermute x2, starting transfers between devices, shifted(): lax.ppermute(block, axis, [((i - distance) % size, i) for i in range(size)])  22 us
    all_to_all x2, starting transfers between devices, gathered(): spread = lax.all_to_all(spread, 'tp', 0, 0, axis_index_groups=groups)  19.4 us
    all_to_all x1, blocking collectives, local(): team = lax.all_to_all(team, 'tp', 0, 0, axis_index_groups=inside)  17.6 us
    all_to_all x2, starting transfers between devices, local(): parts = lax.all_to_all(parts, 'tp', 0, 0, axis_index_groups=inside)  16.8 us
    all_to_all x2, waiting for transfers between devices, local(): parts = lax.all_to_all(parts, 'tp', 0, 0, axis_index_groups=inside)  15 us
    all_to_all x1, starting transfers between devices, local(): team = lax.all_to_all(team, 'tp', 0, 0, axis_index_groups=inside)  9.65 us
  transfers between devices with their start and end apart: 11, of which 8 were waited for; matrix products, arithmetic and copies ran while one was open for 4% of the time, Pallas kernels for 0%

profile of v5, /device:TPU:1, one launch (start us, length us, event | category | flops | bytes accessed | tf_op | source)
XLA Modules:
  0.0 247.9 jit_solution(589041280507953075)
XLA Ops:
  0.0 0.9 convert_reduce_fusion.5
  1.0 0.9 fusion.46
  1.9 0.8 fusion.74
  2.6 0.8 fusion.49
  3.5 0.7 broadcast_in_dim.128
  4.2 15.7 %all-to-all-start = ((bf16[16,48,128]{2,1,0:T(8,128)(2,1)}), bf16[16,48,128]{2,1,0:T(8,128)(2,1)S(1)}, u32[]{:S(2)}, u32[]{:S(2)}) async-start(bf16[16,48,128]{2,1,0:T(8,128)(2,1)} %broadcast_in_dim.128), calls=%async_computation | async-start | bytes 393216 | tf_op jit(solution)/shard_map/all_to_all | solution.py:121
  20.0 1.0 dynamic-slice_bitcast_fusion
  21.0 4.4 %collective-permute-start.2 = (bf16[48,768]{1,0:T(8,128)(2,1)S(1)}, bf16[48,768]{1,0:T(8,128)(2,1)S(1)}, u32[]{:S(2)}, u32[]{:S(2)}) collective-permute-start(bf16[48,768]{1,0:T(8,128)(2,1)S(1)} %get-tuple-element.16), channel_id=1, source_target_pairs={{0,48},{1,49},{2,50},{3,51},{4,52},{5,53},{6,54},{7,55},{8,56},{9,... | collective-permute-start | bytes 221192 | tf_op jit(solution)/shard_map/ppermute | solution.py:191
  25.4 2.4 collective-permute-start.1
  27.9 2.5 %collective-permute-start = (bf16[48,768]{1,0:T(8,128)(2,1)S(1)}, bf16[48,768]{1,0:T(8,128)(2,1)S(1)}, u32[]{:S(2)}, u32[]{:S(2)}) collective-permute-start(bf16[48,768]{1,0:T(8,128)(2,1)S(1)} %get-tuple-element.18), channel_id=1, source_target_pairs={{0,16},{1,17},{2,18},{3,19},{4,20},{5,21},{6,22},{7,23},{8,24},{9,... | collective-permute-start | bytes 221192 | tf_op jit(solution)/shard_map/ppermute | solution.py:191
  30.4 1.9 collective-permute-done.1
  32.3 2.6 %collective-permute-done = bf16[48,768]{1,0:T(8,128)(2,1)S(1)} collective-permute-done((bf16[48,768]{1,0:T(8,128)(2,1)S(1)}, bf16[48,768]{1,0:T(8,128)(2,1)S(1)}, u32[]{:S(2)}, u32[]{:S(2)}) %collective-permute-start) | collective-permute-done | bytes 73760 | tf_op jit(solution)/shard_map/ppermute | solution.py:191
  35.0 0.7 broadcast_select_fusion
  35.8 1.0 broadcast_in_dim.129
  36.7 3.6 %all-to-all-start.1 = ((bf16[4,32,3072]{2,1,0:T(8,128)(2,1)}), bf16[4,32,3072]{2,1,0:T(8,128)(2,1)S(1)}, u32[]{:S(2)}, u32[]{:S(2)}) async-start(bf16[4,32,3072]{2,1,0:T(8,128)(2,1)} %broadcast_in_dim.129), calls=%async_computation.1 | async-start | bytes 1572864 | tf_op jit(solution)/shard_map/all_to_all | solution.py:121
  40.4 9.5 %all-to-all-done.1 = bf16[4,32,3072]{2,1,0:T(8,128)(2,1)S(1)} async-done(((bf16[4,32,3072]{2,1,0:T(8,128)(2,1)}), bf16[4,32,3072]{2,1,0:T(8,128)(2,1)S(1)}, u32[]{:S(2)}, u32[]{:S(2)}) %all-to-all-start.1) | async-done | bytes 786464 | tf_op jit(solution)/shard_map/all_to_all | solution.py:121
  49.9 1.2 shard_map.91
  51.1 9.6 %all-to-all-start.2 = ((bf16[8,64,128]{2,1,0:T(8,128)(2,1)}), bf16[8,64,128]{2,1,0:T(8,128)(2,1)S(1)}, u32[]{:S(2)}, u32[]{:S(2)}) async-start(bf16[8,64,128]{2,1,0:T(8,128)(2,1)} %shard_map.91), calls=%async_computation.2 | async-start | bytes 262144 | tf_op jit(solution)/shard_map/all_to_all | solution.py:213
  60.8 6.3 %collective-permute-start.3 = (bf16[4,48,384]{2,1,0:T(8,128)(2,1)S(1)}, bf16[4,48,384]{2,1,0:T(8,128)(2,1)S(1)}, u32[]{:S(2)}, u32[]{:S(2)}) collective-permute-start(bf16[4,48,384]{2,1,0:T(8,128)(2,1)S(1)} %get-tuple-element.12), channel_id=1, source_target_pairs={{0,12},{1,13},{2,14},{3,15},{4,8},{5,9},{6,10},{7,11},{8,4},{9,5},... | collective-permute-start | bytes 442376 | tf_op jit(solution)/shard_map/ppermute | solution.py:203
  67.9 5.7 %collective-permute-done.3 = bf16[4,48,384]{2,1,0:T(8,128)(2,1)S(1)} collective-permute-done((bf16[4,48,384]{2,1,0:T(8,128)(2,1)S(1)}, bf16[4,48,384]{2,1,0:T(8,128)(2,1)S(1)}, u32[]{:S(2)}, u32[]{:S(2)}) %collective-permute-start.3) | collective-permute-done | bytes 147488 | tf_op jit(solution)/shard_map/ppermute | solution.py:203
  73.6 0.6 copy-done.6
  74.3 1.0 maximum_bitcast_fusion
  75.7 0.8 shard_map.92
  76.5 0.7 copy-done.2
  77.1 13.5 %all-to-all-start.3 = ((bf16[8,64,128]{2,1,0:T(8,128)(2,1)}), bf16[8,64,128]{2,1,0:T(8,128)(2,1)S(1)}, u32[]{:S(2)}, u32[]{:S(2)}) async-start(bf16[8,64,128]{2,1,0:T(8,128)(2,1)} %copy-done.2), calls=%async_computation.3 | async-start | bytes 262144 | tf_op jit(solution)/shard_map/all_to_all | solution.py:215
  90.6 1.8 fusion.21
  92.4 1.6 convolution_multiply_fusion.1
  94.0 6.9 %all-to-all-done.3 = bf16[8,64,128]{2,1,0:T(8,128)(2,1)S(1)} async-done(((bf16[8,64,128]{2,1,0:T(8,128)(2,1)}), bf16[8,64,128]{2,1,0:T(8,128)(2,1)S(1)}, u32[]{:S(2)}, u32[]{:S(2)}) %all-to-all-start.3) | async-done | bytes 131104 | tf_op jit(solution)/shard_map/all_to_all | solution.py:215
  100.9 1.9 fusion.2
  102.8 11.4 %all_to_all.60 = bf16[4,32,3072]{2,1,0:T(8,128)(2,1)S(1)} all-to-all(bf16[4,32,3072]{2,1,0:T(8,128)(2,1)S(1)} %bitcast.97), channel_id=1, replica_groups={{0,16,32,48},{1,17,33,49},{2,18,34,50},{3,19,35,51},{4,20,36,52},{5,21,..., dimensions={0} | all-to-all | bytes 1572864 | tf_op jit(solution)/shard_map/all_to_all | solution.py:128
  114.5 17.9 %all_to_all.61 = bf16[16,48,128]{2,1,0:T(8,128)(2,1)S(1)} all-to-all(bf16[16,48,128]{2,1,0:T(8,128)(2,1)S(1)} %convert_element_type.80), channel_id=1, replica_groups={{0,1,2,3,4,5,6,7,8,9,10,11,12,13,14,15},{16,17,18,19,20,21,22,23,24,25,..., dimensions={0} | all-to-all | bytes 393216 | tf_op jit(solution)/shard_map/all_to_all | solution.py:128
  132.5 7.3 %collective-permute-start.4 = (bf16[2,3072]{1,0:T(2,128)(2,1)S(1)}, bf16[2,3072]{1,0:T(2,128)(2,1)S(1)}, u32[]{:S(2)}, u32[]{:S(2)}) collective-permute-start(bf16[2,3072]{1,0:T(2,128)(2,1)S(1)} %fusion.50), channel_id=1, source_target_pairs={{448,0},{0,64},{64,128},{128,192},{192,256},{256,320},{320,384},{3... | collective-permute-start | bytes 36872 | tf_op jit(solution)/shard_map/ppermute | solution.py:23
  139.7 0.8 collective-permute-done.4
  140.9 0.8 fusion.45
  141.8 15.9 %all_to_all.62 = bf16[16,48,128]{2,1,0:T(8,128)(2,1)S(1)} all-to-all(bf16[16,48,128]{2,1,0:T(8,128)(2,1)S(1)} %broadcast_in_dim.142), channel_id=1, replica_groups={{0,1,2,3,4,5,6,7,8,9,10,11,12,13,14,15},{16,17,18,19,20,21,22,23,24,25,..., dimensions={0} | all-to-all | bytes 393216 | tf_op jit(solution)/shard_map/all_to_all | solution.py:121
  157.9 10.7 %all_to_all.63 = bf16[4,32,3072]{2,1,0:T(8,128)(2,1)S(1)} all-to-all(bf16[4,32,3072]{2,1,0:T(8,128)(2,1)S(1)} %broadcast_in_dim.144), channel_id=1, replica_groups={{0,16,32,48},{1,17,33,49},{2,18,34,50},{3,19,35,51},{4,20,36,52},{5,21,..., dimensions={0} | all-to-all | bytes 1572864 | tf_op jit(solution)/shard_map/all_to_all | solution.py:121
  168.6 0.6 shard_map.93
  169.2 17.6 %all_to_all.64.team_ref = bf16[8,64,128]{2,1,0:T(8,128)(2,1)S(1)} all-to-all(bf16[8,64,128]{2,1,0:T(8,128)(2,1)S(1)} %shard_map.93), channel_id=1, replica_groups={{0,1,2,3,4,5,6,7},{8,9,10,11,12,13,14,15},{16,17,18,19,20,21,22,23},{24..., dimensions={0} | all-to-all | bytes 262144 | tf_op jit(solution)/shard_map/all_to_all | solution.py:213
  186.8 1.5 shard_map.94
  188.3 3.4 %all-to-all-start.9 = ((bf16[8,64,128]{2,1,0:T(8,128)(2,1)}), bf16[8,64,128]{2,1,0:T(8,128)(2,1)S(1)}, u32[]{:S(2)}, u32[]{:S(2)}) async-start(bf16[8,64,128]{2,1,0:T(8,128)(2,1)} %shard_map.94), calls=%async_computation.9 | async-start | bytes 262144 | tf_op jit(solution)/shard_map/all_to_all | solution.py:215
  191.6 1.8 fusion.33
  193.8 8.0 %all-to-all-done.9 = bf16[8,64,128]{2,1,0:T(8,128)(2,1)S(1)} async-done(((bf16[8,64,128]{2,1,0:T(8,128)(2,1)}), bf16[8,64,128]{2,1,0:T(8,128)(2,1)S(1)}, u32[]{:S(2)}, u32[]{:S(2)}) %all-to-all-start.9) | async-done | bytes 131104 | tf_op jit(solution)/shard_map/all_to_all | solution.py:215
  201.9 0.5 fusion.3
  202.4 10.7 %all_to_all.65 = bf16[4,32,3072]{2,1,0:T(8,128)(2,1)S(1)} all-to-all(bf16[4,32,3072]{2,1,0:T(8,128)(2,1)S(1)} %bitcast.96), channel_id=1, replica_groups={{0,16,32,48},{1,17,33,49},{2,18,34,50},{3,19,35,51},{4,20,36,52},{5,21,..., dimensions={0} | all-to-all | bytes 1572864 | tf_op jit(solution)/shard_map/all_to_all | solution.py:128
  213.4 18.2 %all_to_all.66 = bf16[16,48,128]{2,1,0:T(8,128)(2,1)S(1)} all-to-all(bf16[16,48,128]{2,1,0:T(8,128)(2,1)S(1)} %convert_element_type.89), channel_id=1, replica_groups={{0,1,2,3,4,5,6,7,8,9,10,11,12,13,14,15},{16,17,18,19,20,21,22,23,24,25,..., dimensions={0} | all-to-all | bytes 393216 | tf_op jit(solution)/shard_map/all_to_all | solution.py:128
  231.7 14.8 %collective-permute-start.5 = (bf16[2,3072]{1,0:T(2,128)(2,1)S(1)}, bf16[2,3072]{1,0:T(2,128)(2,1)S(1)}, u32[]{:S(2)}, u32[]{:S(2)}) collective-permute-start(bf16[2,3072]{1,0:T(2,128)(2,1)S(1)} %fusion.51), channel_id=1, source_target_pairs={{448,0},{0,64},{64,128},{128,192},{192,256},{256,320},{320,384},{3... | collective-permute-start | bytes 36872 | tf_op jit(solution)/shard_map/ppermute | solution.py:23
  246.4 0.8 collective-permute-done.5
  247.3 0.6 copy.21
  (54 shorter events, 2.3 us)
Async XLA Ops:
  0.0 92.4 %copy-start = (bf16[1,192,3072]{2,1,0:T(8,128)(2,1)S(1)}, bf16[1,192,3072]{2,1,0:T(8,128)(2,1)}, u32[]{:S(2)}) copy-start(bf16[1,192,3072]{2,1,0:T(8,128)(2,1)} %param.13) | copy-start | bytes 3538948
  2.6 34.1 %copy-start.7 = (f32[1,1,3072]{2,0,1:T(1,128)}, f32[1,1,3072]{2,0,1:T(1,128)S(1)}, u32[]{:S(2)}) copy-start(f32[1,1,3072]{2,0,1:T(1,128)S(1)} %get-tuple-element.21) | copy-start | bytes 36868
  4.2 31.5 %all-to-all-start = ((bf16[16,48,128]{2,1,0:T(8,128)(2,1)}), bf16[16,48,128]{2,1,0:T(8,128)(2,1)S(1)}, u32[]{:S(2)}, u32[]{:S(2)}) async-start(bf16[16,48,128]{2,1,0:T(8,128)(2,1)} %broadcast_in_dim.128), calls=%async_computation | async-start | bytes 393216 | tf_op jit(solution)/shard_map/all_to_all | solution.py:121
  21.0 9.4 %collective-permute-start.2 = (bf16[48,768]{1,0:T(8,128)(2,1)S(1)}, bf16[48,768]{1,0:T(8,128)(2,1)S(1)}, u32[]{:S(2)}, u32[]{:S(2)}) collective-permute-start(bf16[48,768]{1,0:T(8,128)(2,1)S(1)} %get-tuple-element.16), channel_id=1, source_target_pairs={{0,48},{1,49},{2,50},{3,51},{4,52},{5,53},{6,54},{7,55},{8,56},{9,... | collective-permute-start | bytes 221192 | tf_op jit(solution)/shard_map/ppermute | solution.py:191
  25.4 6.9 %collective-permute-start.1 = (bf16[48,768]{1,0:T(8,128)(2,1)S(1)}, bf16[48,768]{1,0:T(8,128)(2,1)S(1)}, u32[]{:S(2)}, u32[]{:S(2)}) collective-permute-start(bf16[48,768]{1,0:T(8,128)(2,1)S(1)} %get-tuple-element.17), channel_id=1, source_target_pairs={{0,32},{1,33},{2,34},{3,35},{4,36},{5,37},{6,38},{7,39},{8,40},{9,... | collective-permute-start | bytes 221192 | tf_op jit(solution)/shard_map/ppermute | solution.py:191
  27.9 7.1 %collective-permute-start = (bf16[48,768]{1,0:T(8,128)(2,1)S(1)}, bf16[48,768]{1,0:T(8,128)(2,1)S(1)}, u32[]{:S(2)}, u32[]{:S(2)}) collective-permute-start(bf16[48,768]{1,0:T(8,128)(2,1)S(1)} %get-tuple-element.18), channel_id=1, source_target_pairs={{0,16},{1,17},{2,18},{3,19},{4,20},{5,21},{6,22},{7,23},{8,24},{9,... | collective-permute-start | bytes 221192 | tf_op jit(solution)/shard_map/ppermute | solution.py:191
  35.7 14.2 %copy-start.1 = (bf16[1,3,48,3072]{3,2,1,0:T(8,128)(2,1)S(1)}, bf16[1,3,48,3072]{3,2,1,0:T(8,128)(2,1)}, u32[]{:S(2)}) copy-start(bf16[1,3,48,3072]{3,2,1,0:T(8,128)(2,1)} %param.10) | copy-start | bytes 2654212
  36.7 24.0 %copy-start.8 = (f32[1,2,128]{2,1,0:T(2,128)S(1)}, f32[1,2,128]{2,1,0:T(2,128)}, u32[]{:S(2)}) copy-start(f32[1,2,128]{2,1,0:T(2,128)} %param.15) | copy-start | bytes 3076
  36.7 13.2 %all-to-all-start.1 = ((bf16[4,32,3072]{2,1,0:T(8,128)(2,1)}), bf16[4,32,3072]{2,1,0:T(8,128)(2,1)S(1)}, u32[]{:S(2)}, u32[]{:S(2)}) async-start(bf16[4,32,3072]{2,1,0:T(8,128)(2,1)} %broadcast_in_dim.129), calls=%async_computation.1 | async-start | bytes 1572864 | tf_op jit(solution)/shard_map/all_to_all | solution.py:121
  51.1 24.5 %all-to-all-start.2 = ((bf16[8,64,128]{2,1,0:T(8,128)(2,1)}), bf16[8,64,128]{2,1,0:T(8,128)(2,1)S(1)}, u32[]{:S(2)}, u32[]{:S(2)}) async-start(bf16[8,64,128]{2,1,0:T(8,128)(2,1)} %shard_map.91), calls=%async_computation.2 | async-start | bytes 262144 | tf_op jit(solution)/shard_map/all_to_all | solution.py:213
  60.8 12.8 %collective-permute-start.3 = (bf16[4,48,384]{2,1,0:T(8,128)(2,1)S(1)}, bf16[4,48,384]{2,1,0:T(8,128)(2,1)S(1)}, u32[]{:S(2)}, u32[]{:S(2)}) collective-permute-start(bf16[4,48,384]{2,1,0:T(8,128)(2,1)S(1)} %get-tuple-element.12), channel_id=1, source_target_pairs={{0,12},{1,13},{2,14},{3,15},{4,8},{5,9},{6,10},{7,11},{8,4},{9,5},... | collective-permute-start | bytes 442376 | tf_op jit(solution)/shard_map/ppermute | solution.py:203
  73.6 0.6 copy-start.6
  76.5 0.7 copy-start.2
  77.1 23.8 %all-to-all-start.3 = ((bf16[8,64,128]{2,1,0:T(8,128)(2,1)}), bf16[8,64,128]{2,1,0:T(8,128)(2,1)S(1)}, u32[]{:S(2)}, u32[]{:S(2)}) async-start(bf16[8,64,128]{2,1,0:T(8,128)(2,1)} %copy-done.2), calls=%async_computation.3 | async-start | bytes 262144 | tf_op jit(solution)/shard_map/all_to_all | solution.py:215
  92.4 8.6 %copy-start.3 = (bf16[1,48,3072]{2,1,0:T(8,128)(2,1)S(1)}, bf16[1,48,3072]{2,1,0:T(8,128)(2,1)}, u32[]{:S(2)}) copy-start(bf16[1,48,3072]{2,1,0:T(8,128)(2,1)} %param.12) | copy-start | bytes 884740
  102.8 29.6 %copy-start.5 = (bf16[1,2,3072]{2,1,0:T(2,128)(2,1)S(1)}, bf16[1,2,3072]{2,1,0:T(2,128)(2,1)}, u32[]{:S(2)}) copy-start(bf16[1,2,3072]{2,1,0:T(2,128)(2,1)} %param.9) | copy-start | bytes 36868
  132.5 8.1 %collective-permute-start.4 = (bf16[2,3072]{1,0:T(2,128)(2,1)S(1)}, bf16[2,3072]{1,0:T(2,128)(2,1)S(1)}, u32[]{:S(2)}, u32[]{:S(2)}) collective-permute-start(bf16[2,3072]{1,0:T(2,128)(2,1)S(1)} %fusion.50), channel_id=1, source_target_pairs={{448,0},{0,64},{64,128},{128,192},{192,256},{256,320},{320,384},{3... | collective-permute-start | bytes 36872 | tf_op jit(solution)/shard_map/ppermute | solution.py:23
  188.3 13.6 %all-to-all-start.9 = ((bf16[8,64,128]{2,1,0:T(8,128)(2,1)}), bf16[8,64,128]{2,1,0:T(8,128)(2,1)S(1)}, u32[]{:S(2)}, u32[]{:S(2)}) async-start(bf16[8,64,128]{2,1,0:T(8,128)(2,1)} %shard_map.94), calls=%async_computation.9 | async-start | bytes 262144 | tf_op jit(solution)/shard_map/all_to_all | solution.py:215
  193.4 8.5 %copy-start.4 = (bf16[1,48,3072]{2,1,0:T(8,128)(2,1)S(1)}, bf16[1,48,3072]{2,1,0:T(8,128)(2,1)}, u32[]{:S(2)}) copy-start(bf16[1,48,3072]{2,1,0:T(8,128)(2,1)} %param.12) | copy-start | bytes 884740
  231.7 15.6 %collective-permute-start.5 = (bf16[2,3072]{1,0:T(2,128)(2,1)S(1)}, bf16[2,3072]{1,0:T(2,128)(2,1)S(1)}, u32[]{:S(2)}, u32[]{:S(2)}) collective-permute-start(bf16[2,3072]{1,0:T(2,128)(2,1)S(1)} %fusion.51), channel_id=1, source_target_pairs={{448,0},{0,64},{64,128},{128,192},{192,256},{256,320},{320,384},{3... | collective-permute-start | bytes 36872 | tf_op jit(solution)/shard_map/ppermute | solution.py:23

commit v6 on v5

--- a/solution.py
+++ b/solution.py
@@ -23,12 +23,61 @@
     return lax.ppermute(block, axis, [((i - distance) % size, i) for i in range(size)])
 
 
-def modulated(hidden_state, shift_scale):
-    x_float = hidden_state.astype(f32)
-    row_mean = jnp.mean(x_float, axis=-1, keepdims=True)
-    row_var = jnp.mean(jnp.square(x_float - row_mean), axis=-1, keepdims=True)
-    normed = (x_float - row_mean) * lax.rsqrt(row_var + eps_norm)
-    return (normed * (1.0 + shift_scale[1]) + shift_scale[0]).astype(bf16)
+def spread_kernel(rows_ref, modulation_ref, out_ref, block_ref):
+    x = rows_ref[...].astype(f32)
+    centred = x - jnp.mean(x, axis=1, keepdims=True)
+    variance = jnp.mean(centred * centred, axis=1, keepdims=True)
+    normed = centred * lax.rsqrt(variance + eps_norm)
+    normed = normed * (1.0 + modulation_ref[1:2, :]) + modulation_ref[0:1, :]
+    rows, width = x.shape
+    pieces = width // LANES
+    for r in range(rows):
+        for p in range(pieces):
+            at = r * pieces + p
+            block_ref[at : at + 1, :] = normed[r : r + 1, p * LANES : (p + 1) * LANES]
+    block = block_ref[...].astype(bf16)
+    for j in range(out_ref.shape[0]):
+        out_ref[j] = block
+
+
+def spread(rows, modulation, receivers):
+    whole = pl.BlockSpec(memory_space=pltpu.VMEM)
+    lines = rows.shape[0] * rows.shape[1] // LANES
+    return pl.pallas_call(
+        spread_kernel,
+        out_shape=jax.ShapeDtypeStruct((receivers, lines, LANES), bf16),
+        in_specs=[whole] * 2,
+        out_specs=whole,
+        scratch_shapes=[pltpu.VMEM((lines, LANES), f32)],
+        compiler_params=pltpu.CompilerParams(vmem_limit_bytes=16 * 1024 * 1024),
+    )(rows, modulation)
+
+
+def finish_kernel(member_ref, parts_ref, weight_ref, forward_ref, modulation_ref, out_ref):
+    shard, width = weight_ref.shape
+    summed = parts_ref[0].astype(f32)
+    for c in range(1, parts_ref.shape[0]):
+        summed = summed + parts_ref[c].astype(f32)
+    feature = member_ref[0] * shard + lax.broadcasted_iota(jnp.int32, (shard, LANES), 0)
+    total = jnp.broadcast_to(summed[shard + TEAM_HEADS - 1][None], (shard, LANES))
+    for h in range(TEAM_HEADS - 2, -1, -1):
+        total = jnp.where(feature < (h + 1) * HEAD_DIM, summed[shard + h][None], total)
+    attention = (summed[:shard] / total).astype(bf16)
+    branch = lax.dot_general(
+        attention, weight_ref[...], (((0,), (0,)), ((), ())), preferred_element_type=f32
+    )
+    out_ref[...] = ((branch + forward_ref[...]) * modulation_ref[2:3, :]).astype(bf16)
+
+
+def finish(member, parts, weights, forward, modulation):
+    whole = pl.BlockSpec(memory_space=pltpu.VMEM)
+    return pl.pallas_call(
+        finish_kernel,
+        out_shape=jax.ShapeDtypeStruct(forward.shape, bf16),
+        in_specs=[pl.BlockSpec(memory_space=pltpu.SMEM)] + [whole] * 4,
+        out_specs=whole,
+        compiler_params=pltpu.CompilerParams(vmem_limit_bytes=16 * 1024 * 1024),
+    )(member, parts, weights, forward, modulation)
 
 
 def project_kernel(normed_ref, weight_ref, out_ref):
@@ -58,7 +107,9 @@
     )(normed, weights)
 
 
-def attend_kernel(team_ref, cached_ref, mask_ref, gain_q_ref, gain_k_ref, out_ref, packed_ref):
+def attend_kernel(
+    team_ref, keep_ref, got_ref, mask_ref, gain_q_ref, gain_k_ref, out_ref, packed_ref
+):
     shard = team_ref.shape[1] - 16
     members = team_ref.shape[0]
     lane = lax.broadcasted_iota(jnp.int32, (16, LANES), 1)
@@ -66,6 +117,10 @@
     fresh = [team_ref[c, shard:, :].astype(f32) for c in range(members)]
     features = jnp.concatenate([team_ref[c, :shard, :] for c in range(members)], axis=0)
     open_key = mask_ref[...] > 0.0
+    blocks = [r[i].astype(f32) for i in range(keep_ref.shape[0]) for r in (keep_ref, got_ref)]
+    half = keep_ref.shape[1] // 2
+    cached_keys = jnp.concatenate([b[:half] for b in blocks], axis=0).astype(bf16)
+    cached_values = jnp.concatenate([b[half:] for b in blocks], axis=0).astype(bf16)
     sums = jnp.zeros((16, LANES), f32)
     for h in range(TEAM_HEADS):
         query = features[h * HEAD_DIM : (h + 1) * HEAD_DIM].astype(f32)
@@ -82,9 +137,8 @@
             value = jnp.where(here, pltpu.roll(fresh[c], (start - shard) % LANES, 1), value)
         scale = lax.rsqrt(jnp.mean(key * key, axis=1, keepdims=True) + eps_norm)
         key = (key * scale * gain_k_ref[...]).astype(bf16)
-        cached_key = cached_ref[:, h * HEAD_DIM : (h + 1) * HEAD_DIM]
-        at = (TEAM_HEADS + h) * HEAD_DIM
-        cached_value = cached_ref[:, at : at + HEAD_DIM]
+        cached_key = cached_keys[:, h * HEAD_DIM : (h + 1) * HEAD_DIM]
+        cached_value = cached_values[:, h * HEAD_DIM : (h + 1) * HEAD_DIM]
         scores = jnp.dot(cached_key, query, preferred_element_type=f32)
         probs = jnp.exp(jnp.where(open_key, scores, -1e30))
         fresh_probs = jnp.exp(jnp.dot(key, query, preferred_element_type=f32))
@@ -102,17 +156,16 @@
         out_ref[c, shard:, :] = sums.astype(bf16)
 
 
-def attend(team, cached, mask, gains, interpret=False):
+def attend(team, keep, got, mask, gains):
     whole = pl.BlockSpec(memory_space=pltpu.VMEM)
     return pl.pallas_call(
         attend_kernel,
         out_shape=jax.ShapeDtypeStruct(team.shape, bf16),
-        in_specs=[whole] * 5,
+        in_specs=[whole] * 6,
         out_specs=whole,
         scratch_shapes=[pltpu.VMEM((TEAM_HEADS * HEAD_DIM, LANES), bf16)],
         compiler_params=pltpu.CompilerParams(vmem_limit_bytes=16 * 1024 * 1024),
-        interpret=interpret,
-    )(team, cached, mask, gains[0][:, None], gains[1][None, :])
+    )(team, keep, got, mask, gains[0][:, None], gains[1][None, :])
 
 
 def gathered(block, groups):
@@ -175,12 +228,12 @@
     cached_mask = jnp.broadcast_to(cached_mask[:, None], (teams * ctx_local, LANES))
 
     current = in_flight[0]
-    first_rows = modulated(current, shift_scale)
-    first_rows, flat = lax.optimization_barrier((first_rows, context_kv[0]))
+    block = spread(current, shift_scale, z_count)
+    block, flat = lax.optimization_barrier((block, context_kv[0]))
     flat = flat.reshape(2 * ctx_local, width)
     by_x = []
     for step in range(x_count):
-        block = lax.dynamic_slice_in_dim(
+        part = lax.dynamic_slice_in_dim(
             flat, (x_here + step) % x_count * 2 * team_width, 2 * team_width, 1
         )
         if step:
@@ -188,15 +241,16 @@
                 (z_count * x + z, z_count * ((x + step) % x_count) + z)
                 for x in range(x_count) for z in range(z_count)
             ]
-            block = lax.ppermute(block, "tp", route)
-        by_x.append(block)
+            part = lax.ppermute(part, "tp", route)
+        by_x.append(part)
     by_x = jnp.stack(by_x)
     keep = jnp.where(upper, by_x[:, :, team_width:], by_x[:, :, :team_width])
     give = jnp.where(upper, by_x[:, :, :team_width], by_x[:, :, team_width:])
 
     for tick_number in range(TICKS):
-        normed_rows = modulated(current, shift_scale) if tick_number else first_rows
-        normed = gathered(normed_rows.reshape(rows * width // LANES, LANES), along_z)
+        if tick_number:
+            block = spread(current, shift_scale, z_count)
+        normed = lax.all_to_all(block, "tp", 0, 0, axis_index_groups=along_z)
         normed = normed.reshape(rows * z_count, width)
         if tick_number == 0:
             normed, give = lax.optimization_barrier((normed, give))
@@ -205,20 +259,13 @@
                 "tp",
                 [(z_count * x + z, z_count * x + partner[z]) for x in range(x_count) for z in range(z_count)],
             )
-            cached = jnp.stack([keep, got], axis=1)
-            cached = cached.reshape(x_count, 2, 2, ctx_local, team_width).transpose(0, 1, 3, 2, 4)
-            cached = cached.reshape(teams * ctx_local, 2 * team_width)
         normed = gathered(normed, along_x)
+        if tick_number == 0:
+            normed, got = lax.optimization_barrier((normed, got))
         team = project(normed, weight_qkv)
         team = lax.all_to_all(team, "tp", 0, 0, axis_index_groups=inside)
-        parts = attend(team, cached, cached_mask, gains)
+        parts = attend(team, keep, got, cached_mask, gains)
         parts = lax.all_to_all(parts, "tp", 0, 0, axis_index_groups=inside)
-        summed = jnp.sum(parts.astype(f32), axis=0)
-        feature_head = (member * shard + jnp.arange(shard, dtype=jnp.int32)) // HEAD_DIM
-        total_rows = summed[shard + TEAM_HEADS - 1][None]
-        for h in range(TEAM_HEADS - 1):
-            total_rows = jnp.where(feature_head[:, None] == h, summed[shard + h][None], total_rows)
-        attention = (summed[:shard] / total_rows).astype(bf16)
         hidden = jax.nn.gelu(
             lax.dot_general(
                 normed, weight_mlp, (((1,), (1,)), ((), ())), preferred_element_type=f32
@@ -226,12 +273,9 @@
             approximate=True,
         ).astype(bf16)
         hidden = lax.optimization_barrier(hidden)
-        forward = jnp.dot(hidden, weight_down, preferred_element_type=f32) * shift_scale[2]
+        forward = jnp.dot(hidden, weight_down, preferred_element_type=f32)
         forward = lax.optimization_barrier(forward)
-        branch = lax.dot_general(
-            attention, weight_attn, (((0,), (0,)), ((), ())), preferred_element_type=f32
-        )
-        branch = branch * shift_scale[2] + forward
+        branch = finish(member[None], parts, weight_attn, forward, shift_scale)
         branch = summed_over(branch, along_x)
         branch = summed_over(branch.reshape(-1, LANES), along_z).reshape(rows, width)
         finished = (current.astype(f32) + branch).astype(bf16)

time: 249 us -> 245 us (0.984)
  starting transfers between devices: 83.5 us -> 72.6 us
  waiting for transfers between devices: 36.4 us -> 44.9 us
  other arithmetic: 6.83 us -> 0.5 us
  blocking collectives: 103 us -> 107 us
  Pallas kernels: 4.05 us -> 7.69 us
  matrix products: 7.87 us -> 4.3 us
    all_to_all x0 -> x1, blocking collectives: none -> 16.7 us  [local(): normed = lax.all_to_all(block, 'tp', 0, 0, axis_index_groups=along_z)]
    all_to_all x2 -> x1, starting transfers between devices: 19.4 us -> 3.49 us  [gathered(): spread = lax.all_to_all(spread, 'tp', 0, 0, axis_index_groups=groups)]
    all_to_all x2 -> x1, blocking collectives: 26.6 us -> 10.9 us  [gathered(): spread = lax.all_to_all(spread, 'tp', 0, 0, axis_index_groups=groups)]
    all_to_all x0 -> x1, starting transfers between devices: none -> 15.7 us  [local(): normed = lax.all_to_all(block, 'tp', 0, 0, axis_index_groups=along_z)]
    all_to_all x1, waiting for transfers between devices: 0.01 us -> 9.55 us  [local(): team = lax.all_to_all(team, 'tp', 0, 0, axis_index_groups=inside)]
    all_to_all x2 -> x1, waiting for transfers between devices: 9.52 us -> 0.01 us  [gathered(): spread = lax.all_to_all(spread, 'tp', 0, 0, axis_index_groups=groups)]
    all_to_all x2, starting transfers between devices: 16.8 us -> 8.7 us  [local(): parts = lax.all_to_all(parts, 'tp', 0, 0, axis_index_groups=inside)]
    ppermute x1, waiting for transfers between devices: 5.7 us -> 12.9 us  [local(): lax.ppermute(give, 'tp', [(z_count * x + z, z_count * x + partner[z]) for...]
  transfers between devices with their start and end apart: 11 -> 11, of which waited for: 8 -> 8; matrix products, arithmetic and copies ran while one was open for 4% -> 2% of each run, Pallas kernels for 0% -> 0%
where the time goes in v6:
time: 245 us; the launch traced here: 244 us
  blocking collectives  107 us (44%)
  starting transfers between devices  72.6 us (30%)
  waiting for transfers between devices  44.9 us (18%)
  Pallas kernels  7.69 us (3%)
  local copies, waits for them, and re-layouts  5.48 us (2%)
  matrix products  4.3 us (2%)
    all_to_all x4, blocking collectives, summed_over(): parts = lax.all_to_all(parts, 'tp', 0, 0, axis_index_groups=groups)  62 us
    ppermute x2, starting transfers between devices, shifted(): lax.ppermute(block, axis, [((i - distance) % size, i) for i in range(size)])  21.6 us
    all_to_all x1, blocking collectives, local(): team = lax.all_to_all(team, 'tp', 0, 0, axis_index_groups=inside)  17.6 us
    all_to_all x1, blocking collectives, local(): normed = lax.all_to_all(block, 'tp', 0, 0, axis_index_groups=along_z)  16.7 us
    all_to_all x2, waiting for transfers between devices, local(): parts = lax.all_to_all(parts, 'tp', 0, 0, axis_index_groups=inside)  16.3 us
    all_to_all x1, starting transfers between devices, local(): normed = lax.all_to_all(block, 'tp', 0, 0, axis_index_groups=along_z)  15.7 us
    ppermute x1, waiting for transfers between devices, local(): lax.ppermute(give, 'tp', [(z_count * x + z, z_count * x + partner[z]) for...  12.9 us
    all_to_all x1, blocking collectives, gathered(): spread = lax.all_to_all(spread, 'tp', 0, 0, axis_index_groups=groups)  10.9 us
  transfers between devices with their start and end apart: 11, of which 8 were waited for; matrix products, arithmetic and copies ran while one was open for 2% of the time, Pallas kernels for 0%

profile of v6, /device:TPU:1, one launch (start us, length us, event | category | flops | bytes accessed | tf_op | source)
XLA Modules:
  0.0 243.8 jit_solution(5127663172080652709)
XLA Ops:
  0.0 0.9 copy.16
  0.9 0.7 copy-done.4
  1.6 0.9 shard_map.91
  2.5 15.7 %all-to-all-start = ((bf16[16,48,128]{2,1,0:T(8,128)(2,1)}), bf16[16,48,128]{2,1,0:T(8,128)(2,1)S(1)}, u32[]{:S(2)}, u32[]{:S(2)}) async-start(bf16[16,48,128]{2,1,0:T(8,128)(2,1)} %shard_map.91), calls=%async_computation | async-start | bytes 393216 | tf_op jit(solution)/shard_map/all_to_all | solution.py:253
  18.4 1.0 dynamic-slice_bitcast_fusion
  19.4 4.4 %collective-permute-start.2 = (bf16[48,768]{1,0:T(8,128)(2,1)S(1)}, bf16[48,768]{1,0:T(8,128)(2,1)S(1)}, u32[]{:S(2)}, u32[]{:S(2)}) collective-permute-start(bf16[48,768]{1,0:T(8,128)(2,1)S(1)} %get-tuple-element.20), channel_id=1, source_target_pairs={{0,48},{1,49},{2,50},{3,51},{4,52},{5,53},{6,54},{7,55},{8,56},{9,... | collective-permute-start | bytes 221192 | tf_op jit(solution)/shard_map/ppermute | solution.py:244
  23.8 2.4 collective-permute-start.1
  26.2 2.5 %collective-permute-start = (bf16[48,768]{1,0:T(8,128)(2,1)S(1)}, bf16[48,768]{1,0:T(8,128)(2,1)S(1)}, u32[]{:S(2)}, u32[]{:S(2)}) collective-permute-start(bf16[48,768]{1,0:T(8,128)(2,1)S(1)} %get-tuple-element.22), channel_id=1, source_target_pairs={{0,16},{1,17},{2,18},{3,19},{4,20},{5,21},{6,22},{7,23},{8,24},{9,... | collective-permute-start | bytes 221192 | tf_op jit(solution)/shard_map/ppermute | solution.py:244
  28.8 1.9 collective-permute-done.1
  30.7 2.6 %collective-permute-done = bf16[48,768]{1,0:T(8,128)(2,1)S(1)} collective-permute-done((bf16[48,768]{1,0:T(8,128)(2,1)S(1)}, bf16[48,768]{1,0:T(8,128)(2,1)S(1)}, u32[]{:S(2)}, u32[]{:S(2)}) %collective-permute-start) | collective-permute-done | bytes 73760 | tf_op jit(solution)/shard_map/ppermute | solution.py:244
  33.5 1.0 broadcast_in_dim.35
  34.5 3.5 %all-to-all-start.1 = ((bf16[4,32,3072]{2,1,0:T(8,128)(2,1)}), bf16[4,32,3072]{2,1,0:T(8,128)(2,1)S(1)}, u32[]{:S(2)}, u32[]{:S(2)}) async-start(bf16[4,32,3072]{2,1,0:T(8,128)(2,1)} %broadcast_in_dim.35), calls=%async_computation.1 | async-start | bytes 1572864 | tf_op jit(solution)/shard_map/all_to_all | solution.py:174
  38.0 7.2 %collective-permute-start.3 = (bf16[4,48,384]{2,1,0:T(8,128)(2,1)S(1)}, bf16[4,48,384]{2,1,0:T(8,128)(2,1)S(1)}, u32[]{:S(2)}, u32[]{:S(2)}) collective-permute-start(bf16[4,48,384]{2,1,0:T(8,128)(2,1)S(1)} %get-tuple-element.14), channel_id=1, source_target_pairs={{0,12},{1,13},{2,14},{3,15},{4,8},{5,9},{6,10},{7,11},{8,4},{9,5},... | collective-permute-start | bytes 442376 | tf_op jit(solution)/shard_map/ppermute | solution.py:257
  45.2 12.9 %collective-permute-done.3.got_ref = bf16[4,48,384]{2,1,0:T(8,128)(2,1)S(1)} collective-permute-done((bf16[4,48,384]{2,1,0:T(8,128)(2,1)S(1)}, bf16[4,48,384]{2,1,0:T(8,128)(2,1)S(1)}, u32[]{:S(2)}, u32[]{:S(2)}) %collective-permute-start.3) | collective-permute-done | bytes 147488 | tf_op jit(solution)/shard_map/ppermute | solution.py:257
  58.1 1.2 shard_map.92
  59.3 6.6 %all-to-all-start.2 = ((bf16[8,64,128]{2,1,0:T(8,128)(2,1)}), bf16[8,64,128]{2,1,0:T(8,128)(2,1)S(1)}, u32[]{:S(2)}, u32[]{:S(2)}) async-start(bf16[8,64,128]{2,1,0:T(8,128)(2,1)} %shard_map.92), calls=%async_computation.2 | async-start | bytes 262144 | tf_op jit(solution)/shard_map/all_to_all | solution.py:266
  66.6 0.1 copy.12.gain_q_ref
  66.7 9.5 %all-to-all-done.2.team_ref = bf16[8,64,128]{2,1,0:T(8,128)(2,1)S(1)} async-done(((bf16[8,64,128]{2,1,0:T(8,128)(2,1)}), bf16[8,64,128]{2,1,0:T(8,128)(2,1)S(1)}, u32[]{:S(2)}, u32[]{:S(2)}) %all-to-all-start.2) | async-done | bytes 131104 | tf_op jit(solution)/shard_map/all_to_all | solution.py:266
  76.3 1.5 shard_map.93
  77.8 5.3 %all-to-all-start.3 = ((bf16[8,64,128]{2,1,0:T(8,128)(2,1)}), bf16[8,64,128]{2,1,0:T(8,128)(2,1)}, u32[]{:S(2)}, u32[]{:S(2)}) async-start(bf16[8,64,128]{2,1,0:T(8,128)(2,1)} %shard_map.93), calls=%async_computation.3 | async-start | bytes 262144 | tf_op jit(solution)/shard_map/all_to_all | solution.py:268
  83.2 1.8 fusion.17
  85.0 0.4 fusion.2.forward_ref
  85.3 8.2 %all-to-all-done.3.parts_ref = bf16[8,64,128]{2,1,0:T(8,128)(2,1)} async-done(((bf16[8,64,128]{2,1,0:T(8,128)(2,1)}), bf16[8,64,128]{2,1,0:T(8,128)(2,1)}, u32[]{:S(2)}, u32[]{:S(2)}) %all-to-all-start.3) | async-done | bytes 131104 | tf_op jit(solution)/shard_map/all_to_all | solution.py:268
  93.5 1.3 shard_map.94
  94.9 13.4 %all_to_all.60 = bf16[4,32,3072]{2,1,0:T(8,128)(2,1)S(1)} all-to-all(bf16[4,32,3072]{2,1,0:T(8,128)(2,1)S(1)} %bitcast.55), channel_id=1, replica_groups={{0,16,32,48},{1,17,33,49},{2,18,34,50},{3,19,35,51},{4,20,36,52},{5,21,..., dimensions={0} | all-to-all | bytes 1572864 | tf_op jit(solution)/shard_map/all_to_all | solution.py:181
  108.3 0.2 reduce_sum.42
  108.4 0.1 convert_element_type.46
  108.5 19.7 %all_to_all.61 = bf16[16,48,128]{2,1,0:T(8,128)(2,1)S(1)} all-to-all(bf16[16,48,128]{2,1,0:T(8,128)(2,1)S(1)} %convert_element_type.46), channel_id=1, replica_groups={{0,1,2,3,4,5,6,7,8,9,10,11,12,13,14,15},{16,17,18,19,20,21,22,23,24,25,..., dimensions={0} | all-to-all | bytes 393216 | tf_op jit(solution)/shard_map/all_to_all | solution.py:181
  128.3 6.8 %collective-permute-start.4 = (bf16[2,3072]{1,0:T(2,128)(2,1)S(1)}, bf16[2,3072]{1,0:T(2,128)(2,1)S(1)}, u32[]{:S(2)}, u32[]{:S(2)}) collective-permute-start(bf16[2,3072]{1,0:T(2,128)(2,1)S(1)} %add_convert_fusion.1), channel_id=1, source_target_pairs={{448,0},{0,64},{64,128},{128,192},{192,256},{256,320},{320,384},{3... | collective-permute-start | bytes 36872 | tf_op jit(solution)/shard_map/ppermute | solution.py:23
  135.1 0.8 collective-permute-done.4.rows_ref
  135.9 0.3 shard_map.95
  136.2 0.6 copy-done.6
  136.8 16.7 %all_to_all.62 = bf16[16,48,128]{2,1,0:T(8,128)(2,1)S(1)} all-to-all(bf16[16,48,128]{2,1,0:T(8,128)(2,1)S(1)} %shard_map.95), channel_id=1, replica_groups={{0,1,2,3,4,5,6,7,8,9,10,11,12,13,14,15},{16,17,18,19,20,21,22,23,24,25,..., dimensions={0} | all-to-all | bytes 393216 | tf_op jit(solution)/shard_map/all_to_all | solution.py:253
  153.7 10.9 %all_to_all.63 = bf16[4,32,3072]{2,1,0:T(8,128)(2,1)S(1)} all-to-all(bf16[4,32,3072]{2,1,0:T(8,128)(2,1)S(1)} %broadcast_in_dim.40), channel_id=1, replica_groups={{0,16,32,48},{1,17,33,49},{2,18,34,50},{3,19,35,51},{4,20,36,52},{5,21,..., dimensions={0} | all-to-all | bytes 1572864 | tf_op jit(solution)/shard_map/all_to_all | solution.py:174
  164.6 0.6 shard_map.96
  165.1 17.6 %all_to_all.64.team_ref = bf16[8,64,128]{2,1,0:T(8,128)(2,1)S(1)} all-to-all(bf16[8,64,128]{2,1,0:T(8,128)(2,1)S(1)} %shard_map.96), channel_id=1, replica_groups={{0,1,2,3,4,5,6,7},{8,9,10,11,12,13,14,15},{16,17,18,19,20,21,22,23},{24..., dimensions={0} | all-to-all | bytes 262144 | tf_op jit(solution)/shard_map/all_to_all | solution.py:266
  182.7 1.5 shard_map.97
  184.2 3.4 %all-to-all-start.9 = ((bf16[8,64,128]{2,1,0:T(8,128)(2,1)}), bf16[8,64,128]{2,1,0:T(8,128)(2,1)S(1)}, u32[]{:S(2)}, u32[]{:S(2)}) async-start(bf16[8,64,128]{2,1,0:T(8,128)(2,1)} %shard_map.97), calls=%async_computation.9 | async-start | bytes 262144 | tf_op jit(solution)/shard_map/all_to_all | solution.py:268
  187.6 1.8 fusion.29
  189.4 0.4 fusion.forward_ref
  189.8 8.1 %all-to-all-done.9.parts_ref = bf16[8,64,128]{2,1,0:T(8,128)(2,1)S(1)} async-done(((bf16[8,64,128]{2,1,0:T(8,128)(2,1)}), bf16[8,64,128]{2,1,0:T(8,128)(2,1)S(1)}, u32[]{:S(2)}, u32[]{:S(2)}) %all-to-all-start.9) | async-done | bytes 131104 | tf_op jit(solution)/shard_map/all_to_all | solution.py:268
  197.8 0.4 shard_map.98
  198.3 10.7 %all_to_all.65 = bf16[4,32,3072]{2,1,0:T(8,128)(2,1)S(1)} all-to-all(bf16[4,32,3072]{2,1,0:T(8,128)(2,1)S(1)} %bitcast.54), channel_id=1, replica_groups={{0,16,32,48},{1,17,33,49},{2,18,34,50},{3,19,35,51},{4,20,36,52},{5,21,..., dimensions={0} | all-to-all | bytes 1572864 | tf_op jit(solution)/shard_map/all_to_all | solution.py:181
  209.0 0.2 reduce_sum.44
  209.3 18.2 %all_to_all.66 = bf16[16,48,128]{2,1,0:T(8,128)(2,1)S(1)} all-to-all(bf16[16,48,128]{2,1,0:T(8,128)(2,1)S(1)} %convert_element_type.51), channel_id=1, replica_groups={{0,1,2,3,4,5,6,7,8,9,10,11,12,13,14,15},{16,17,18,19,20,21,22,23,24,25,..., dimensions={0} | all-to-all | bytes 393216 | tf_op jit(solution)/shard_map/all_to_all | solution.py:181
  227.6 14.8 %collective-permute-start.5 = (bf16[2,3072]{1,0:T(2,128)(2,1)S(1)}, bf16[2,3072]{1,0:T(2,128)(2,1)S(1)}, u32[]{:S(2)}, u32[]{:S(2)}) collective-permute-start(bf16[2,3072]{1,0:T(2,128)(2,1)S(1)} %add_convert_fusion), channel_id=1, source_target_pairs={{448,0},{0,64},{64,128},{128,192},{192,256},{256,320},{320,384},{3... | collective-permute-start | bytes 36872 | tf_op jit(solution)/shard_map/ppermute | solution.py:23
  242.4 0.8 collective-permute-done.5
  243.2 0.6 copy.19
  (38 shorter events, 0.7 us)
Async XLA Ops:
  0.0 84.9 %copy-start = (bf16[1,192,3072]{2,1,0:T(8,128)(2,1)S(1)}, bf16[1,192,3072]{2,1,0:T(8,128)(2,1)}, u32[]{:S(2)}) copy-start(bf16[1,192,3072]{2,1,0:T(8,128)(2,1)} %param.13) | copy-start | bytes 3538948
  0.9 0.7 copy-start.4
  2.5 30.9 %all-to-all-start = ((bf16[16,48,128]{2,1,0:T(8,128)(2,1)}), bf16[16,48,128]{2,1,0:T(8,128)(2,1)S(1)}, u32[]{:S(2)}, u32[]{:S(2)}) async-start(bf16[16,48,128]{2,1,0:T(8,128)(2,1)} %shard_map.91), calls=%async_computation | async-start | bytes 393216 | tf_op jit(solution)/shard_map/all_to_all | solution.py:253
  19.4 9.4 %collective-permute-start.2 = (bf16[48,768]{1,0:T(8,128)(2,1)S(1)}, bf16[48,768]{1,0:T(8,128)(2,1)S(1)}, u32[]{:S(2)}, u32[]{:S(2)}) collective-permute-start(bf16[48,768]{1,0:T(8,128)(2,1)S(1)} %get-tuple-element.20), channel_id=1, source_target_pairs={{0,48},{1,49},{2,50},{3,51},{4,52},{5,53},{6,54},{7,55},{8,56},{9,... | collective-permute-start | bytes 221192 | tf_op jit(solution)/shard_map/ppermute | solution.py:244
  23.8 6.9 %collective-permute-start.1 = (bf16[48,768]{1,0:T(8,128)(2,1)S(1)}, bf16[48,768]{1,0:T(8,128)(2,1)S(1)}, u32[]{:S(2)}, u32[]{:S(2)}) collective-permute-start(bf16[48,768]{1,0:T(8,128)(2,1)S(1)} %get-tuple-element.21), channel_id=1, source_target_pairs={{0,32},{1,33},{2,34},{3,35},{4,36},{5,37},{6,38},{7,39},{8,40},{9,... | collective-permute-start | bytes 221192 | tf_op jit(solution)/shard_map/ppermute | solution.py:244
  26.2 7.1 %collective-permute-start = (bf16[48,768]{1,0:T(8,128)(2,1)S(1)}, bf16[48,768]{1,0:T(8,128)(2,1)S(1)}, u32[]{:S(2)}, u32[]{:S(2)}) collective-permute-start(bf16[48,768]{1,0:T(8,128)(2,1)S(1)} %get-tuple-element.22), channel_id=1, source_target_pairs={{0,16},{1,17},{2,18},{3,19},{4,20},{5,21},{6,22},{7,23},{8,24},{9,... | collective-permute-start | bytes 221192 | tf_op jit(solution)/shard_map/ppermute | solution.py:244
  33.5 24.6 %copy-start.1 = (bf16[1,3,48,3072]{3,2,1,0:T(8,128)(2,1)S(1)}, bf16[1,3,48,3072]{3,2,1,0:T(8,128)(2,1)}, u32[]{:S(2)}) copy-start(bf16[1,3,48,3072]{3,2,1,0:T(8,128)(2,1)} %param.10) | copy-start | bytes 2654212
  34.5 23.6 %all-to-all-start.1 = ((bf16[4,32,3072]{2,1,0:T(8,128)(2,1)}), bf16[4,32,3072]{2,1,0:T(8,128)(2,1)S(1)}, u32[]{:S(2)}, u32[]{:S(2)}) async-start(bf16[4,32,3072]{2,1,0:T(8,128)(2,1)} %broadcast_in_dim.35), calls=%async_computation.1 | async-start | bytes 1572864 | tf_op jit(solution)/shard_map/all_to_all | solution.py:174
  38.0 28.6 %copy-start.10 = (f32[1,2,128]{2,1,0:T(2,128)S(1)}, f32[1,2,128]{2,1,0:T(2,128)}, u32[]{:S(2)}) copy-start(f32[1,2,128]{2,1,0:T(2,128)} %param.15) | copy-start | bytes 3076
  38.0 20.1 %collective-permute-start.3 = (bf16[4,48,384]{2,1,0:T(8,128)(2,1)S(1)}, bf16[4,48,384]{2,1,0:T(8,128)(2,1)S(1)}, u32[]{:S(2)}, u32[]{:S(2)}) collective-permute-start(bf16[4,48,384]{2,1,0:T(8,128)(2,1)S(1)} %get-tuple-element.14), channel_id=1, source_target_pairs={{0,12},{1,13},{2,14},{3,15},{4,8},{5,9},{6,10},{7,11},{8,4},{9,5},... | collective-permute-start | bytes 442376 | tf_op jit(solution)/shard_map/ppermute | solution.py:257
  59.3 16.9 %all-to-all-start.2 = ((bf16[8,64,128]{2,1,0:T(8,128)(2,1)}), bf16[8,64,128]{2,1,0:T(8,128)(2,1)S(1)}, u32[]{:S(2)}, u32[]{:S(2)}) async-start(bf16[8,64,128]{2,1,0:T(8,128)(2,1)} %shard_map.92), calls=%async_computation.2 | async-start | bytes 262144 | tf_op jit(solution)/shard_map/all_to_all | solution.py:266
  66.5 16.6 %copy-start.8 = (f32[1,128]{1,0:T(1,128)}, f32[1,128]{1,0:T(1,128)S(1)}, u32[]{:S(2)}) copy-start(f32[1,128]{1,0:T(1,128)S(1)} %get-tuple-element.23.gain_k_ref) | copy-start | bytes 1540
  77.8 15.7 %all-to-all-start.3 = ((bf16[8,64,128]{2,1,0:T(8,128)(2,1)}), bf16[8,64,128]{2,1,0:T(8,128)(2,1)}, u32[]{:S(2)}, u32[]{:S(2)}) async-start(bf16[8,64,128]{2,1,0:T(8,128)(2,1)} %shard_map.93), calls=%async_computation.3 | async-start | bytes 262144 | tf_op jit(solution)/shard_map/all_to_all | solution.py:268
  84.9 8.6 %copy-start.3 = (bf16[1,48,3072]{2,1,0:T(8,128)(2,1)S(1)}, bf16[1,48,3072]{2,1,0:T(8,128)(2,1)}, u32[]{:S(2)}) copy-start(bf16[1,48,3072]{2,1,0:T(8,128)(2,1)} %param.12) | copy-start | bytes 884740
  108.3 20.0 %copy-start.5 = (bf16[1,2,3072]{2,1,0:T(2,128)(2,1)S(1)}, bf16[1,2,3072]{2,1,0:T(2,128)(2,1)}, u32[]{:S(2)}) copy-start(bf16[1,2,3072]{2,1,0:T(2,128)(2,1)} %param.9) | copy-start | bytes 36868
  128.3 7.6 %collective-permute-start.4 = (bf16[2,3072]{1,0:T(2,128)(2,1)S(1)}, bf16[2,3072]{1,0:T(2,128)(2,1)S(1)}, u32[]{:S(2)}, u32[]{:S(2)}) collective-permute-start(bf16[2,3072]{1,0:T(2,128)(2,1)S(1)} %add_convert_fusion.1), channel_id=1, source_target_pairs={{448,0},{0,64},{64,128},{128,192},{192,256},{256,320},{320,384},{3... | collective-permute-start | bytes 36872 | tf_op jit(solution)/shard_map/ppermute | solution.py:23
  136.2 0.6 copy-start.6
  153.6 11.0 %copy-start.2 = (bf16[1,3,48,3072]{3,2,1,0:T(8,128)(2,1)S(1)}, bf16[1,3,48,3072]{3,2,1,0:T(8,128)(2,1)}, u32[]{:S(2)}) copy-start(bf16[1,3,48,3072]{3,2,1,0:T(8,128)(2,1)} %param.10) | copy-start | bytes 2654212
  164.6 18.2 %copy-start.9 = (f32[1,128]{1,0:T(1,128)S(1)}, f32[1,128]{1,0:T(1,128)}, u32[]{:S(2)}) copy-start(f32[1,128]{1,0:T(1,128)} %copy-done.8) | copy-start | bytes 1540
  184.2 13.6 %all-to-all-start.9 = ((bf16[8,64,128]{2,1,0:T(8,128)(2,1)}), bf16[8,64,128]{2,1,0:T(8,128)(2,1)S(1)}, u32[]{:S(2)}, u32[]{:S(2)}) async-start(bf16[8,64,128]{2,1,0:T(8,128)(2,1)} %shard_map.97), calls=%async_computation.9 | async-start | bytes 262144 | tf_op jit(solution)/shard_map/all_to_all | solution.py:268
  209.0 18.5 %copy-start.7 = (bf16[2,3072]{1,0:T(2,128)(2,1)S(1)}, bf16[2,3072]{1,0:T(2,128)(2,1)}, u32[]{:S(2)}) copy-start(bf16[2,3072]{1,0:T(2,128)(2,1)} %copy-done.6) | copy-start | bytes 36868
  227.6 15.6 %collective-permute-start.5 = (bf16[2,3072]{1,0:T(2,128)(2,1)S(1)}, bf16[2,3072]{1,0:T(2,128)(2,1)S(1)}, u32[]{:S(2)}, u32[]{:S(2)}) collective-permute-start(bf16[2,3072]{1,0:T(2,128)(2,1)S(1)} %add_convert_fusion), channel_id=1, source_target_pairs={{448,0},{0,64},{64,128},{128,192},{192,256},{256,320},{320,384},{3... | collective-permute-start | bytes 36872 | tf_op jit(solution)/shard_map/ppermute | solution.py:23

commit v7 on v6

--- a/solution.py
+++ b/solution.py
@@ -28,7 +28,7 @@
     centred = x - jnp.mean(x, axis=1, keepdims=True)
     variance = jnp.mean(centred * centred, axis=1, keepdims=True)
     normed = centred * lax.rsqrt(variance + eps_norm)
-    normed = normed * (1.0 + modulation_ref[1:2, :]) + modulation_ref[0:1, :]
+    normed = normed * (1.0 + modulation_ref[1]) + modulation_ref[0]
     rows, width = x.shape
     pieces = width // LANES
     for r in range(rows):
@@ -66,7 +66,7 @@
     branch = lax.dot_general(
         attention, weight_ref[...], (((0,), (0,)), ((), ())), preferred_element_type=f32
     )
-    out_ref[...] = ((branch + forward_ref[...]) * modulation_ref[2:3, :]).astype(bf16)
+    out_ref[...] = ((branch + forward_ref[...]) * modulation_ref[2]).astype(bf16)
 
 
 def finish(member, parts, weights, forward, modulation):
@@ -107,9 +107,8 @@
     )(normed, weights)
 
 
-def attend_kernel(
-    team_ref, keep_ref, got_ref, mask_ref, gain_q_ref, gain_k_ref, out_ref, packed_ref
-):
+def attend_kernel(team_ref, mask_ref, gain_q_ref, gain_k_ref, *refs):
+    *cached_refs, out_ref, packed_ref = refs
     shard = team_ref.shape[1] - 16
     members = team_ref.shape[0]
     lane = lax.broadcasted_iota(jnp.int32, (16, LANES), 1)
@@ -117,8 +116,8 @@
     fresh = [team_ref[c, shard:, :].astype(f32) for c in range(members)]
     features = jnp.concatenate([team_ref[c, :shard, :] for c in range(members)], axis=0)
     open_key = mask_ref[...] > 0.0
-    blocks = [r[i].astype(f32) for i in range(keep_ref.shape[0]) for r in (keep_ref, got_ref)]
-    half = keep_ref.shape[1] // 2
+    blocks = [r[i].astype(f32) for r in cached_refs for i in range(r.shape[0])]
+    half = blocks[0].shape[0] // 2
     cached_keys = jnp.concatenate([b[:half] for b in blocks], axis=0).astype(bf16)
     cached_values = jnp.concatenate([b[half:] for b in blocks], axis=0).astype(bf16)
     sums = jnp.zeros((16, LANES), f32)
@@ -156,16 +155,16 @@
         out_ref[c, shard:, :] = sums.astype(bf16)
 
 
-def attend(team, keep, got, mask, gains):
+def attend(team, cached, mask, gains):
     whole = pl.BlockSpec(memory_space=pltpu.VMEM)
     return pl.pallas_call(
         attend_kernel,
         out_shape=jax.ShapeDtypeStruct(team.shape, bf16),
-        in_specs=[whole] * 6,
+        in_specs=[whole] * (4 + len(cached)),
         out_specs=whole,
         scratch_shapes=[pltpu.VMEM((TEAM_HEADS * HEAD_DIM, LANES), bf16)],
         compiler_params=pltpu.CompilerParams(vmem_limit_bytes=16 * 1024 * 1024),
-    )(team, keep, got, mask, gains[0][:, None], gains[1][None, :])
+    )(team, mask, gains[0][:, None], gains[1][None, :], *cached)
 
 
 def gathered(block, groups):
@@ -199,7 +198,7 @@
     along_z = [[z_count * x + z for z in range(z_count)] for x in range(x_count)]
     along_x = [[z_count * x + z for x in range(x_count)] for z in range(z_count)]
     inside = [[TEAM * t + m for m in range(TEAM)] for t in range(teams)]
-    shift_scale = modulation[0]
+    shift_scale = modulation.reshape(3, 1, width)
     gains = qk_gain[0]
     weight_qkv = w_qkv[0].reshape(3 * shard, width)
     weight_mlp = w_mlp[0]
@@ -230,22 +229,14 @@
     current = in_flight[0]
     block = spread(current, shift_scale, z_count)
     block, flat = lax.optimization_barrier((block, context_kv[0]))
-    flat = flat.reshape(2 * ctx_local, width)
-    by_x = []
-    for step in range(x_count):
-        part = lax.dynamic_slice_in_dim(
-            flat, (x_here + step) % x_count * 2 * team_width, 2 * team_width, 1
-        )
-        if step:
-            route = [
-                (z_count * x + z, z_count * ((x + step) % x_count) + z)
-                for x in range(x_count) for z in range(z_count)
-            ]
-            part = lax.ppermute(part, "tp", route)
-        by_x.append(part)
-    by_x = jnp.stack(by_x)
-    keep = jnp.where(upper, by_x[:, :, team_width:], by_x[:, :, :team_width])
-    give = jnp.where(upper, by_x[:, :, :team_width], by_x[:, :, team_width:])
+    by_team = flat.reshape(2 * ctx_local, x_count, 2, team_width).transpose(2, 1, 0, 3)
+    keep = jnp.where(upper, by_team[1], by_team[0])
+    give = jnp.where(upper, by_team[0], by_team[1])
+    got = lax.ppermute(
+        give,
+        "tp",
+        [(z_count * x + z, z_count * x + partner[z]) for x in range(x_count) for z in range(z_count)],
+    )
 
     for tick_number in range(TICKS):
         if tick_number:
@@ -253,18 +244,26 @@
         normed = lax.all_to_all(block, "tp", 0, 0, axis_index_groups=along_z)
         normed = normed.reshape(rows * z_count, width)
         if tick_number == 0:
-            normed, give = lax.optimization_barrier((normed, give))
-            got = lax.ppermute(
-                give,
-                "tp",
-                [(z_count * x + z, z_count * x + partner[z]) for x in range(x_count) for z in range(z_count)],
-            )
+            normed, keep, got = lax.optimization_barrier((normed, keep, got))
+            cached = []
+            for step in range(x_count):
+                target = (x_here + step) % x_count
+                part = jnp.stack(
+                    [lax.dynamic_index_in_dim(p, target, 0, keepdims=False) for p in (keep, got)]
+                )
+                if step:
+                    route = [
+                        (z_count * x + z, z_count * ((x + step) % x_count) + z)
+                        for x in range(x_count) for z in range(z_count)
+                    ]
+                    part = lax.ppermute(part, "tp", route)
+                cached.append(part)
         normed = gathered(normed, along_x)
         if tick_number == 0:
-            normed, got = lax.optimization_barrier((normed, got))
+            normed, cached = lax.optimization_barrier((normed, cached))
         team = project(normed, weight_qkv)
         team = lax.all_to_all(team, "tp", 0, 0, axis_index_groups=inside)
-        parts = attend(team, keep, got, cached_mask, gains)
+        parts = attend(team, cached, cached_mask, gains)
         parts = lax.all_to_all(parts, "tp", 0, 0, axis_index_groups=inside)
         hidden = jax.nn.gelu(
             lax.dot_general(

time: 245 us -> 248 us (1.012)
  starting transfers between devices: 72.6 us -> 79.5 us
    all_to_all x1, starting transfers between devices: 6.55 us -> 12.2 us  [local(): team = lax.all_to_all(team, 'tp', 0, 0, axis_index_groups=inside)]
    all_to_all x1, waiting for transfers between devices: 0.01 us -> 4.1 us  [local(): normed = lax.all_to_all(block, 'tp', 0, 0, axis_index_groups=along_z)]
    ppermute x1, waiting for transfers between devices: 12.9 us -> 9.27 us  [local(): lax.ppermute(give, 'tp', [(z_count * x + z, z_count * x + partner[z]) for...]
  transfers between devices with their start and end apart: 11 -> 11, of which waited for: 8 -> 8; matrix products, arithmetic and copies ran while one was open for 2% -> 3% of each run, Pallas kernels for 0% -> 0%
where the time goes in v7:
time: 248 us; the launch traced here: 247 us
  blocking collectives  106 us (43%)
  starting transfers between devices  79.5 us (32%)
  waiting for transfers between devices  43.2 us (17%)
  Pallas kernels  6.69 us (3%)
  local copies, waits for them, and re-layouts  5.91 us (2%)
  matrix products  4.3 us (2%)
    all_to_all x4, blocking collectives, summed_over(): parts = lax.all_to_all(parts, 'tp', 0, 0, axis_index_groups=groups)  61.3 us
    ppermute x2, starting transfers between devices, shifted(): lax.ppermute(block, axis, [((i - distance) % size, i) for i in range(size)])  21.6 us
    all_to_all x1, blocking collectives, local(): team = lax.all_to_all(team, 'tp', 0, 0, axis_index_groups=inside)  17.6 us
    all_to_all x1, blocking collectives, local(): normed = lax.all_to_all(block, 'tp', 0, 0, axis_index_groups=along_z)  16.2 us
    all_to_all x2, waiting for transfers between devices, local(): parts = lax.all_to_all(parts, 'tp', 0, 0, axis_index_groups=inside)  16.1 us
    all_to_all x1, starting transfers between devices, local(): normed = lax.all_to_all(block, 'tp', 0, 0, axis_index_groups=along_z)  15.7 us
    all_to_all x1, starting transfers between devices, local(): team = lax.all_to_all(team, 'tp', 0, 0, axis_index_groups=inside)  12.2 us
    all_to_all x1, blocking collectives, gathered(): spread = lax.all_to_all(spread, 'tp', 0, 0, axis_index_groups=groups)  10.9 us
  transfers between devices with their start and end apart: 11, of which 8 were waited for; matrix products, arithmetic and copies ran while one was open for 3% of the time, Pallas kernels for 0%

profile of v7, /device:TPU:1, one launch (start us, length us, event | category | flops | bytes accessed | tf_op | source)
XLA Modules:
  0.0 247.1 jit_solution(1187492020111672177)
XLA Ops:
  0.0 0.9 copy-done.4
  0.9 0.7 copy-done.10
  1.6 0.9 shard_map.91
  2.5 15.7 %all-to-all-start = ((bf16[16,48,128]{2,1,0:T(8,128)(2,1)}), bf16[16,48,128]{2,1,0:T(8,128)(2,1)S(1)}, u32[]{:S(2)}, u32[]{:S(2)}) async-start(bf16[16,48,128]{2,1,0:T(8,128)(2,1)} %shard_map.91), calls=%async_computation | async-start | bytes 393216 | tf_op jit(solution)/shard_map/all_to_all | solution.py:244
  18.3 1.2 reshape.91
  19.5 7.2 %collective-permute-start = (bf16[4,48,384]{2,1,0:T(8,128)(2,1)S(1)}, bf16[4,48,384]{2,1,0:T(8,128)(2,1)S(1)}, u32[]{:S(2)}, u32[]{:S(2)}) collective-permute-start(bf16[4,48,384]{2,1,0:T(8,128)(2,1)S(1)} %get-tuple-element.25), channel_id=1, source_target_pairs={{0,12},{1,13},{2,14},{3,15},{4,8},{5,9},{6,10},{7,11},{8,4},{9,5},... | collective-permute-start | bytes 442376 | tf_op jit(solution)/shard_map/ppermute | solution.py:235
  26.7 4.1 %all-to-all-done = bf16[16,48,128]{2,1,0:T(8,128)(2,1)S(1)} async-done(((bf16[16,48,128]{2,1,0:T(8,128)(2,1)}), bf16[16,48,128]{2,1,0:T(8,128)(2,1)S(1)}, u32[]{:S(2)}, u32[]{:S(2)}) %all-to-all-start) | async-done | bytes 196640 | tf_op jit(solution)/shard_map/all_to_all | solution.py:244
  30.9 9.3 %collective-permute-done = bf16[4,48,384]{2,1,0:T(8,128)(2,1)S(1)} collective-permute-done((bf16[4,48,384]{2,1,0:T(8,128)(2,1)S(1)}, bf16[4,48,384]{2,1,0:T(8,128)(2,1)S(1)}, u32[]{:S(2)}, u32[]{:S(2)}) %collective-permute-start) | collective-permute-done | bytes 147488 | tf_op jit(solution)/shard_map/ppermute | solution.py:235
  40.2 1.0 broadcast_in_dim.35
  41.1 4.1 %all-to-all-start.1 = ((bf16[4,32,3072]{2,1,0:T(8,128)(2,1)}), bf16[4,32,3072]{2,1,0:T(8,128)(2,1)S(1)}, u32[]{:S(2)}, u32[]{:S(2)}) async-start(bf16[4,32,3072]{2,1,0:T(8,128)(2,1)} %broadcast_in_dim.35), calls=%async_computation.1 | async-start | bytes 1572864 | tf_op jit(solution)/shard_map/all_to_all | solution.py:173
  45.3 0.9 constant_dynamic-slice_fusion
  46.2 3.4 %collective-permute-start.1 = (bf16[2,48,384]{2,1,0:T(8,128)(2,1)S(1)}, bf16[2,48,384]{2,1,0:T(8,128)(2,1)S(1)}, u32[]{:S(2)}, u32[]{:S(2)}) collective-permute-start(bf16[2,48,384]{2,1,0:T(8,128)(2,1)S(1)} %pad_maximum_fusion.1), channel_id=1, source_target_pairs={{0,16},{1,17},{2,18},{3,19},{4,20},{5,21},{6,22},{7,23},{8,24},{9,... | collective-permute-start | bytes 221192 | tf_op jit(solution)/shard_map/ppermute | solution.py:259
  49.6 4.3 %collective-permute-start.2 = (bf16[2,48,384]{2,1,0:T(8,128)(2,1)S(1)}, bf16[2,48,384]{2,1,0:T(8,128)(2,1)S(1)}, u32[]{:S(2)}, u32[]{:S(2)}) collective-permute-start(bf16[2,48,384]{2,1,0:T(8,128)(2,1)S(1)} %pad_maximum_fusion.2), channel_id=1, source_target_pairs={{0,32},{1,33},{2,34},{3,35},{4,36},{5,37},{6,38},{7,39},{8,40},{9,... | collective-permute-start | bytes 221192 | tf_op jit(solution)/shard_map/ppermute | solution.py:259
  53.9 3.1 %collective-permute-start.3 = (bf16[2,48,384]{2,1,0:T(8,128)(2,1)S(1)}, bf16[2,48,384]{2,1,0:T(8,128)(2,1)S(1)}, u32[]{:S(2)}, u32[]{:S(2)}) collective-permute-start(bf16[2,48,384]{2,1,0:T(8,128)(2,1)S(1)} %pad_maximum_fusion.3), channel_id=1, source_target_pairs={{0,48},{1,49},{2,50},{3,51},{4,52},{5,53},{6,54},{7,55},{8,56},{9,... | collective-permute-start | bytes 221192 | tf_op jit(solution)/shard_map/ppermute | solution.py:259
  57.0 2.6 %collective-permute-done.2.refs_2_ = bf16[2,48,384]{2,1,0:T(8,128)(2,1)S(1)} collective-permute-done((bf16[2,48,384]{2,1,0:T(8,128)(2,1)S(1)}, bf16[2,48,384]{2,1,0:T(8,128)(2,1)S(1)}, u32[]{:S(2)}, u32[]{:S(2)}) %collective-permute-start.2) | collective-permute-done | bytes 73760 | tf_op jit(solution)/shard_map/ppermute | solution.py:259
  59.6 1.2 shard_map.92
  60.8 12.2 %all-to-all-start.2 = ((bf16[8,64,128]{2,1,0:T(8,128)(2,1)}), bf16[8,64,128]{2,1,0:T(8,128)(2,1)S(1)}, u32[]{:S(2)}, u32[]{:S(2)}) async-start(bf16[8,64,128]{2,1,0:T(8,128)(2,1)} %shard_map.92), calls=%async_computation.2 | async-start | bytes 262144 | tf_op jit(solution)/shard_map/all_to_all | solution.py:265
  73.7 0.1 copy.16.gain_q_ref
  73.9 9.5 %all-to-all-done.2.team_ref = bf16[8,64,128]{2,1,0:T(8,128)(2,1)S(1)} async-done(((bf16[8,64,128]{2,1,0:T(8,128)(2,1)}), bf16[8,64,128]{2,1,0:T(8,128)(2,1)S(1)}, u32[]{:S(2)}, u32[]{:S(2)}) %all-to-all-start.2) | async-done | bytes 131104 | tf_op jit(solution)/shard_map/all_to_all | solution.py:265
  83.4 1.5 shard_map.93
  84.9 4.4 %all-to-all-start.3 = ((bf16[8,64,128]{2,1,0:T(8,128)(2,1)}), bf16[8,64,128]{2,1,0:T(8,128)(2,1)S(1)}, u32[]{:S(2)}, u32[]{:S(2)}) async-start(bf16[8,64,128]{2,1,0:T(8,128)(2,1)} %shard_map.93), calls=%async_computation.3 | async-start | bytes 262144 | tf_op jit(solution)/shard_map/all_to_all | solution.py:267
  89.3 1.8 fusion.17
  91.1 0.4 fusion.2.forward_ref
  91.5 8.1 %all-to-all-done.3.parts_ref = bf16[8,64,128]{2,1,0:T(8,128)(2,1)S(1)} async-done(((bf16[8,64,128]{2,1,0:T(8,128)(2,1)}), bf16[8,64,128]{2,1,0:T(8,128)(2,1)S(1)}, u32[]{:S(2)}, u32[]{:S(2)}) %all-to-all-start.3) | async-done | bytes 131104 | tf_op jit(solution)/shard_map/all_to_all | solution.py:267
  99.6 0.4 shard_map.94
  100.0 12.1 %all_to_all.60 = bf16[4,32,3072]{2,1,0:T(8,128)(2,1)S(1)} all-to-all(bf16[4,32,3072]{2,1,0:T(8,128)(2,1)S(1)} %bitcast.54), channel_id=1, replica_groups={{0,16,32,48},{1,17,33,49},{2,18,34,50},{3,19,35,51},{4,20,36,52},{5,21,..., dimensions={0} | all-to-all | bytes 1572864 | tf_op jit(solution)/shard_map/all_to_all | solution.py:180
  112.1 0.2 reduce_sum.42
  112.3 0.1 convert_element_type.46
  112.4 20.2 %all_to_all.61 = bf16[16,48,128]{2,1,0:T(8,128)(2,1)S(1)} all-to-all(bf16[16,48,128]{2,1,0:T(8,128)(2,1)S(1)} %convert_element_type.46), channel_id=1, replica_groups={{0,1,2,3,4,5,6,7,8,9,10,11,12,13,14,15},{16,17,18,19,20,21,22,23,24,25,..., dimensions={0} | all-to-all | bytes 393216 | tf_op jit(solution)/shard_map/all_to_all | solution.py:180
  132.7 6.8 %collective-permute-start.4 = (bf16[2,3072]{1,0:T(2,128)(2,1)S(1)}, bf16[2,3072]{1,0:T(2,128)(2,1)S(1)}, u32[]{:S(2)}, u32[]{:S(2)}) collective-permute-start(bf16[2,3072]{1,0:T(2,128)(2,1)S(1)} %add_convert_fusion.1), channel_id=1, source_target_pairs={{448,0},{0,64},{64,128},{128,192},{192,256},{256,320},{320,384},{3... | collective-permute-start | bytes 36872 | tf_op jit(solution)/shard_map/ppermute | solution.py:23
  139.5 0.8 collective-permute-done.4.rows_ref
  140.3 0.3 shard_map.95
  140.6 16.2 %all_to_all.62 = bf16[16,48,128]{2,1,0:T(8,128)(2,1)S(1)} all-to-all(bf16[16,48,128]{2,1,0:T(8,128)(2,1)S(1)} %shard_map.95), channel_id=1, replica_groups={{0,1,2,3,4,5,6,7,8,9,10,11,12,13,14,15},{16,17,18,19,20,21,22,23,24,25,..., dimensions={0} | all-to-all | bytes 393216 | tf_op jit(solution)/shard_map/all_to_all | solution.py:244
  157.0 10.9 %all_to_all.63 = bf16[4,32,3072]{2,1,0:T(8,128)(2,1)S(1)} all-to-all(bf16[4,32,3072]{2,1,0:T(8,128)(2,1)S(1)} %broadcast_in_dim.40), channel_id=1, replica_groups={{0,16,32,48},{1,17,33,49},{2,18,34,50},{3,19,35,51},{4,20,36,52},{5,21,..., dimensions={0} | all-to-all | bytes 1572864 | tf_op jit(solution)/shard_map/all_to_all | solution.py:173
  167.9 0.6 shard_map.96
  168.4 17.6 %all_to_all.64.team_ref = bf16[8,64,128]{2,1,0:T(8,128)(2,1)S(1)} all-to-all(bf16[8,64,128]{2,1,0:T(8,128)(2,1)S(1)} %shard_map.96), channel_id=1, replica_groups={{0,1,2,3,4,5,6,7},{8,9,10,11,12,13,14,15},{16,17,18,19,20,21,22,23},{24..., dimensions={0} | all-to-all | bytes 262144 | tf_op jit(solution)/shard_map/all_to_all | solution.py:265
  186.0 1.5 shard_map.97
  187.5 3.4 %all-to-all-start.9 = ((bf16[8,64,128]{2,1,0:T(8,128)(2,1)}), bf16[8,64,128]{2,1,0:T(8,128)(2,1)S(1)}, u32[]{:S(2)}, u32[]{:S(2)}) async-start(bf16[8,64,128]{2,1,0:T(8,128)(2,1)} %shard_map.97), calls=%async_computation.9 | async-start | bytes 262144 | tf_op jit(solution)/shard_map/all_to_all | solution.py:267
  190.9 1.8 fusion.29
  192.7 0.4 fusion.forward_ref
  193.1 8.1 %all-to-all-done.9.parts_ref = bf16[8,64,128]{2,1,0:T(8,128)(2,1)S(1)} async-done(((bf16[8,64,128]{2,1,0:T(8,128)(2,1)}), bf16[8,64,128]{2,1,0:T(8,128)(2,1)S(1)}, u32[]{:S(2)}, u32[]{:S(2)}) %all-to-all-start.9) | async-done | bytes 131104 | tf_op jit(solution)/shard_map/all_to_all | solution.py:267
  201.1 0.4 shard_map.98
  201.5 10.7 %all_to_all.65 = bf16[4,32,3072]{2,1,0:T(8,128)(2,1)S(1)} all-to-all(bf16[4,32,3072]{2,1,0:T(8,128)(2,1)S(1)} %bitcast.53), channel_id=1, replica_groups={{0,16,32,48},{1,17,33,49},{2,18,34,50},{3,19,35,51},{4,20,36,52},{5,21,..., dimensions={0} | all-to-all | bytes 1572864 | tf_op jit(solution)/shard_map/all_to_all | solution.py:180
  212.3 0.2 reduce_sum.44
  212.5 18.2 %all_to_all.66 = bf16[16,48,128]{2,1,0:T(8,128)(2,1)S(1)} all-to-all(bf16[16,48,128]{2,1,0:T(8,128)(2,1)S(1)} %convert_element_type.51), channel_id=1, replica_groups={{0,1,2,3,4,5,6,7,8,9,10,11,12,13,14,15},{16,17,18,19,20,21,22,23,24,25,..., dimensions={0} | all-to-all | bytes 393216 | tf_op jit(solution)/shard_map/all_to_all | solution.py:180
  230.9 14.8 %collective-permute-start.5 = (bf16[2,3072]{1,0:T(2,128)(2,1)S(1)}, bf16[2,3072]{1,0:T(2,128)(2,1)S(1)}, u32[]{:S(2)}, u32[]{:S(2)}) collective-permute-start(bf16[2,3072]{1,0:T(2,128)(2,1)S(1)} %add_convert_fusion), channel_id=1, source_target_pairs={{448,0},{0,64},{64,128},{128,192},{192,256},{256,320},{320,384},{3... | collective-permute-start | bytes 36872 | tf_op jit(solution)/shard_map/ppermute | solution.py:23
  245.6 0.8 collective-permute-done.5
  246.5 0.6 copy.22
  (48 shorter events, 0.8 us)
Async XLA Ops:
  0.0 91.1 %copy-start = (bf16[1,192,3072]{2,1,0:T(8,128)(2,1)S(1)}, bf16[1,192,3072]{2,1,0:T(8,128)(2,1)}, u32[]{:S(2)}) copy-start(bf16[1,192,3072]{2,1,0:T(8,128)(2,1)} %param.13) | copy-start | bytes 3538948
  0.0 0.9 copy-start.4
  0.9 0.7 copy-start.10
  2.5 28.3 %all-to-all-start = ((bf16[16,48,128]{2,1,0:T(8,128)(2,1)}), bf16[16,48,128]{2,1,0:T(8,128)(2,1)S(1)}, u32[]{:S(2)}, u32[]{:S(2)}) async-start(bf16[16,48,128]{2,1,0:T(8,128)(2,1)} %shard_map.91), calls=%async_computation | async-start | bytes 393216 | tf_op jit(solution)/shard_map/all_to_all | solution.py:244
  19.5 20.6 %collective-permute-start = (bf16[4,48,384]{2,1,0:T(8,128)(2,1)S(1)}, bf16[4,48,384]{2,1,0:T(8,128)(2,1)S(1)}, u32[]{:S(2)}, u32[]{:S(2)}) collective-permute-start(bf16[4,48,384]{2,1,0:T(8,128)(2,1)S(1)} %get-tuple-element.25), channel_id=1, source_target_pairs={{0,12},{1,13},{2,14},{3,15},{4,8},{5,9},{6,10},{7,11},{8,4},{9,5},... | collective-permute-start | bytes 442376 | tf_op jit(solution)/shard_map/ppermute | solution.py:235
  40.2 1.0 copy-start.12
  41.1 18.5 %copy-start.1 = (bf16[1,3,48,3072]{3,2,1,0:T(8,128)(2,1)S(1)}, bf16[1,3,48,3072]{3,2,1,0:T(8,128)(2,1)}, u32[]{:S(2)}) copy-start(bf16[1,3,48,3072]{3,2,1,0:T(8,128)(2,1)} %param.10) | copy-start | bytes 2654212
  41.1 18.5 %all-to-all-start.1 = ((bf16[4,32,3072]{2,1,0:T(8,128)(2,1)}), bf16[4,32,3072]{2,1,0:T(8,128)(2,1)S(1)}, u32[]{:S(2)}, u32[]{:S(2)}) async-start(bf16[4,32,3072]{2,1,0:T(8,128)(2,1)} %broadcast_in_dim.35), calls=%async_computation.1 | async-start | bytes 1572864 | tf_op jit(solution)/shard_map/all_to_all | solution.py:173
  46.2 10.9 %collective-permute-start.1 = (bf16[2,48,384]{2,1,0:T(8,128)(2,1)S(1)}, bf16[2,48,384]{2,1,0:T(8,128)(2,1)S(1)}, u32[]{:S(2)}, u32[]{:S(2)}) collective-permute-start(bf16[2,48,384]{2,1,0:T(8,128)(2,1)S(1)} %pad_maximum_fusion.1), channel_id=1, source_target_pairs={{0,16},{1,17},{2,18},{3,19},{4,20},{5,21},{6,22},{7,23},{8,24},{9,... | collective-permute-start | bytes 221192 | tf_op jit(solution)/shard_map/ppermute | solution.py:259
  49.6 10.0 %collective-permute-start.2 = (bf16[2,48,384]{2,1,0:T(8,128)(2,1)S(1)}, bf16[2,48,384]{2,1,0:T(8,128)(2,1)S(1)}, u32[]{:S(2)}, u32[]{:S(2)}) collective-permute-start(bf16[2,48,384]{2,1,0:T(8,128)(2,1)S(1)} %pad_maximum_fusion.2), channel_id=1, source_target_pairs={{0,32},{1,33},{2,34},{3,35},{4,36},{5,37},{6,38},{7,39},{8,40},{9,... | collective-permute-start | bytes 221192 | tf_op jit(solution)/shard_map/ppermute | solution.py:259
  53.9 19.9 %copy-start.13 = (f32[1,2,128]{2,1,0:T(2,128)S(1)}, f32[1,2,128]{2,1,0:T(2,128)}, u32[]{:S(2)}) copy-start(f32[1,2,128]{2,1,0:T(2,128)} %param.15) | copy-start | bytes 3076
  53.9 5.7 %collective-permute-start.3 = (bf16[2,48,384]{2,1,0:T(8,128)(2,1)S(1)}, bf16[2,48,384]{2,1,0:T(8,128)(2,1)S(1)}, u32[]{:S(2)}, u32[]{:S(2)}) collective-permute-start(bf16[2,48,384]{2,1,0:T(8,128)(2,1)S(1)} %pad_maximum_fusion.3), channel_id=1, source_target_pairs={{0,48},{1,49},{2,50},{3,51},{4,52},{5,53},{6,54},{7,55},{8,56},{9,... | collective-permute-start | bytes 221192 | tf_op jit(solution)/shard_map/ppermute | solution.py:259
  59.6 25.3 %copy-start.6 = (bf16[2,48,384]{2,1,0:T(8,128)(2,1)}, bf16[2,48,384]{2,1,0:T(8,128)(2,1)S(1)}, u32[]{:S(2)}) copy-start(bf16[2,48,384]{2,1,0:T(8,128)(2,1)S(1)} %collective-permute-done.2.refs_2_) | copy-start | bytes 221188
  59.6 25.3 %copy-start.8 = (bf16[2,48,384]{2,1,0:T(8,128)(2,1)}, bf16[2,48,384]{2,1,0:T(8,128)(2,1)S(1)}, u32[]{:S(2)}) copy-start(bf16[2,48,384]{2,1,0:T(8,128)(2,1)S(1)} %collective-permute-done.3.refs_3_) | copy-start | bytes 221188
  60.8 22.5 %all-to-all-start.2 = ((bf16[8,64,128]{2,1,0:T(8,128)(2,1)}), bf16[8,64,128]{2,1,0:T(8,128)(2,1)S(1)}, u32[]{:S(2)}, u32[]{:S(2)}) async-start(bf16[8,64,128]{2,1,0:T(8,128)(2,1)} %shard_map.92), calls=%async_computation.2 | async-start | bytes 262144 | tf_op jit(solution)/shard_map/all_to_all | solution.py:265
  84.9 14.7 %all-to-all-start.3 = ((bf16[8,64,128]{2,1,0:T(8,128)(2,1)}), bf16[8,64,128]{2,1,0:T(8,128)(2,1)S(1)}, u32[]{:S(2)}, u32[]{:S(2)}) async-start(bf16[8,64,128]{2,1,0:T(8,128)(2,1)} %shard_map.93), calls=%async_computation.3 | async-start | bytes 262144 | tf_op jit(solution)/shard_map/all_to_all | solution.py:267
  91.1 8.5 %copy-start.3 = (bf16[1,48,3072]{2,1,0:T(8,128)(2,1)S(1)}, bf16[1,48,3072]{2,1,0:T(8,128)(2,1)}, u32[]{:S(2)}) copy-start(bf16[1,48,3072]{2,1,0:T(8,128)(2,1)} %param.12) | copy-start | bytes 884740
  91.1 8.5 %copy-start.5 = (f32[1,3,3072]{2,0,1:T(1,128)S(1)}, f32[1,3,3072]{2,0,1:T(1,128)}, u32[]{:S(2)}) copy-start(f32[1,3,3072]{2,0,1:T(1,128)} %param.14) | copy-start | bytes 110596
  112.1 20.5 %copy-start.11 = (bf16[1,2,3072]{2,1,0:T(2,128)(2,1)S(1)}, bf16[1,2,3072]{2,1,0:T(2,128)(2,1)}, u32[]{:S(2)}) copy-start(bf16[1,2,3072]{2,1,0:T(2,128)(2,1)} %param.9) | copy-start | bytes 36868
  132.7 7.7 %collective-permute-start.4 = (bf16[2,3072]{1,0:T(2,128)(2,1)S(1)}, bf16[2,3072]{1,0:T(2,128)(2,1)S(1)}, u32[]{:S(2)}, u32[]{:S(2)}) collective-permute-start(bf16[2,3072]{1,0:T(2,128)(2,1)S(1)} %add_convert_fusion.1), channel_id=1, source_target_pairs={{448,0},{0,64},{64,128},{128,192},{192,256},{256,320},{320,384},{3... | collective-permute-start | bytes 36872 | tf_op jit(solution)/shard_map/ppermute | solution.py:23
  156.9 11.0 %copy-start.2 = (bf16[1,3,48,3072]{3,2,1,0:T(8,128)(2,1)S(1)}, bf16[1,3,48,3072]{3,2,1,0:T(8,128)(2,1)}, u32[]{:S(2)}) copy-start(bf16[1,3,48,3072]{3,2,1,0:T(8,128)(2,1)} %param.10) | copy-start | bytes 2654212
  167.9 18.2 %copy-start.7 = (bf16[2,48,384]{2,1,0:T(8,128)(2,1)S(1)}, bf16[2,48,384]{2,1,0:T(8,128)(2,1)}, u32[]{:S(2)}) copy-start(bf16[2,48,384]{2,1,0:T(8,128)(2,1)} %copy-done.6) | copy-start | bytes 221188
  167.9 18.2 %copy-start.9 = (bf16[2,48,384]{2,1,0:T(8,128)(2,1)S(1)}, bf16[2,48,384]{2,1,0:T(8,128)(2,1)}, u32[]{:S(2)}) copy-start(bf16[2,48,384]{2,1,0:T(8,128)(2,1)} %copy-done.8) | copy-start | bytes 221188
  187.5 13.6 %all-to-all-start.9 = ((bf16[8,64,128]{2,1,0:T(8,128)(2,1)}), bf16[8,64,128]{2,1,0:T(8,128)(2,1)S(1)}, u32[]{:S(2)}, u32[]{:S(2)}) async-start(bf16[8,64,128]{2,1,0:T(8,128)(2,1)} %shard_map.97), calls=%async_computation.9 | async-start | bytes 262144 | tf_op jit(solution)/shard_map/all_to_all | solution.py:267
  230.9 15.6 %collective-permute-start.5 = (bf16[2,3072]{1,0:T(2,128)(2,1)S(1)}, bf16[2,3072]{1,0:T(2,128)(2,1)S(1)}, u32[]{:S(2)}, u32[]{:S(2)}) collective-permute-start(bf16[2,3072]{1,0:T(2,128)(2,1)S(1)} %add_convert_fusion), channel_id=1, source_target_pairs={{448,0},{0,64},{64,128},{128,192},{192,256},{256,320},{320,384},{3... | collective-permute-start | bytes 36872 | tf_op jit(solution)/shard_map/ppermute | solution.py:23

commit v8 on v6

--- a/solution.py
+++ b/solution.py
@@ -21,36 +21,6 @@
 def shifted(block, axis, distance):
     size = lax.axis_size(axis)
     return lax.ppermute(block, axis, [((i - distance) % size, i) for i in range(size)])
-
-
-def spread_kernel(rows_ref, modulation_ref, out_ref, block_ref):
-    x = rows_ref[...].astype(f32)
-    centred = x - jnp.mean(x, axis=1, keepdims=True)
-    variance = jnp.mean(centred * centred, axis=1, keepdims=True)
-    normed = centred * lax.rsqrt(variance + eps_norm)
-    normed = normed * (1.0 + modulation_ref[1:2, :]) + modulation_ref[0:1, :]
-    rows, width = x.shape
-    pieces = width // LANES
-    for r in range(rows):
-        for p in range(pieces):
-            at = r * pieces + p
-            block_ref[at : at + 1, :] = normed[r : r + 1, p * LANES : (p + 1) * LANES]
-    block = block_ref[...].astype(bf16)
-    for j in range(out_ref.shape[0]):
-        out_ref[j] = block
-
-
-def spread(rows, modulation, receivers):
-    whole = pl.BlockSpec(memory_space=pltpu.VMEM)
-    lines = rows.shape[0] * rows.shape[1] // LANES
-    return pl.pallas_call(
-        spread_kernel,
-        out_shape=jax.ShapeDtypeStruct((receivers, lines, LANES), bf16),
-        in_specs=[whole] * 2,
-        out_specs=whole,
-        scratch_shapes=[pltpu.VMEM((lines, LANES), f32)],
-        compiler_params=pltpu.CompilerParams(vmem_limit_bytes=16 * 1024 * 1024),
-    )(rows, modulation)
 
 
 def finish_kernel(member_ref, parts_ref, weight_ref, forward_ref, modulation_ref, out_ref):
@@ -66,7 +36,7 @@
     branch = lax.dot_general(
         attention, weight_ref[...], (((0,), (0,)), ((), ())), preferred_element_type=f32
     )
-    out_ref[...] = ((branch + forward_ref[...]) * modulation_ref[2:3, :]).astype(bf16)
+    out_ref[...] = ((branch + forward_ref[...]) * modulation_ref[2]).astype(bf16)
 
 
 def finish(member, parts, weights, forward, modulation):
@@ -80,9 +50,16 @@
     )(member, parts, weights, forward, modulation)
 
 
-def project_kernel(normed_ref, weight_ref, out_ref):
+def project_kernel(rows_ref, weight_ref, modulation_ref, out_ref, normed_ref):
     members = out_ref.shape[0]
     shard = weight_ref.shape[0] // 3
+    for j in range(rows_ref.shape[0] // 16):
+        x = rows_ref[16 * j : 16 * j + 16, :].astype(f32)
+        centred = x - jnp.mean(x, axis=1, keepdims=True)
+        variance = jnp.mean(centred * centred, axis=1, keepdims=True)
+        normed = centred * lax.rsqrt(variance + eps_norm)
+        normed = normed * (1.0 + modulation_ref[1]) + modulation_ref[0]
+        normed_ref[16 * j : 16 * j + 16, :] = normed.astype(bf16)
     contract = (((1,), (1,)), ((), ()))
     query = lax.dot_general(
         weight_ref[:shard], normed_ref[...], contract, preferred_element_type=f32
@@ -96,15 +73,16 @@
         out_ref[c, shard:, 2 * shard :] = jnp.zeros((16, LANES - 2 * shard), bf16)
 
 
-def project(normed, weights):
+def project(rows, weights, modulation):
     whole = pl.BlockSpec(memory_space=pltpu.VMEM)
+    message = jax.ShapeDtypeStruct((TEAM, weights.shape[0] // 3 + 16, LANES), bf16)
     return pl.pallas_call(
         project_kernel,
-        out_shape=jax.ShapeDtypeStruct((TEAM, weights.shape[0] // 3 + 16, LANES), bf16),
-        in_specs=[whole] * 2,
-        out_specs=whole,
-        compiler_params=pltpu.CompilerParams(vmem_limit_bytes=16 * 1024 * 1024),
-    )(normed, weights)
+        out_shape=(message, jax.ShapeDtypeStruct(rows.shape, bf16)),
+        in_specs=[whole] * 3,
+        out_specs=(whole, whole),
+        compiler_params=pltpu.CompilerParams(vmem_limit_bytes=24 * 1024 * 1024),
+    )(rows, weights, modulation)
 
 
 def attend_kernel(
@@ -196,10 +174,18 @@
     team_width = TEAM * shard
     member = tp_index % TEAM
     z_count, x_count = 2 * TEAM, tp_count // (2 * TEAM)
-    along_z = [[z_count * x + z for z in range(z_count)] for x in range(x_count)]
-    along_x = [[z_count * x + z for x in range(x_count)] for z in range(z_count)]
+    quads = z_count // 4
+
+    def device(x, a, c, l):
+        return z_count * x + 4 * a + 2 * c + l
+
+    xs, quarters, two = range(x_count), range(quads), range(2)
+    far = [[device(x, a, c, l) for c in two for a in quarters] for x in xs for l in two]
+    blocks = [[device(x, a, c, l) for x in xs for l in two] for a in quarters for c in two]
+    pairs = [[device(x, a, c, l) for c in two] for x in xs for l in two for a in quarters]
+    quad = [[device(x, a, c, l) for a in quarters] for x in xs for l in two for c in two]
     inside = [[TEAM * t + m for m in range(TEAM)] for t in range(teams)]
-    shift_scale = modulation[0]
+    shift_scale = modulation.reshape(3, 1, width)
     gains = qk_gain[0]
     weight_qkv = w_qkv[0].reshape(3 * shard, width)
     weight_mlp = w_mlp[0]
@@ -228,7 +214,9 @@
     cached_mask = jnp.broadcast_to(cached_mask[:, None], (teams * ctx_local, LANES))
 
     current = in_flight[0]
-    block = spread(current, shift_scale, z_count)
+    block = jnp.broadcast_to(
+        current.reshape(1, rows * width // LANES, LANES), (2 * quads, rows * width // LANES, LANES)
+    )
     block, flat = lax.optimization_barrier((block, context_kv[0]))
     flat = flat.reshape(2 * ctx_local, width)
     by_x = []
@@ -247,22 +235,22 @@
     keep = jnp.where(upper, by_x[:, :, team_width:], by_x[:, :, :team_width])
     give = jnp.where(upper, by_x[:, :, :team_width], by_x[:, :, team_width:])
 
+    first = 2 * quads * rows * (2 * x_here + z_here % 2) + quads * rows * (z_here // 2 % 2)
+    eighth = lax.all_to_all(block, "tp", 0, 0, axis_index_groups=far).reshape(-1, width)
     for tick_number in range(TICKS):
-        if tick_number:
-            block = spread(current, shift_scale, z_count)
-        normed = lax.all_to_all(block, "tp", 0, 0, axis_index_groups=along_z)
-        normed = normed.reshape(rows * z_count, width)
         if tick_number == 0:
-            normed, give = lax.optimization_barrier((normed, give))
+            eighth, give = lax.optimization_barrier((eighth, give))
             got = lax.ppermute(
                 give,
                 "tp",
                 [(z_count * x + z, z_count * x + partner[z]) for x in range(x_count) for z in range(z_count)],
             )
-        normed = gathered(normed, along_x)
+        else:
+            eighth = gathered(current, pairs)
+        patch = gathered(eighth, blocks)
         if tick_number == 0:
-            normed, got = lax.optimization_barrier((normed, got))
-        team = project(normed, weight_qkv)
+            patch, got = lax.optimization_barrier((patch, got))
+        team, normed = project(patch, weight_qkv, shift_scale)
         team = lax.all_to_all(team, "tp", 0, 0, axis_index_groups=inside)
         parts = attend(team, keep, got, cached_mask, gains)
         parts = lax.all_to_all(parts, "tp", 0, 0, axis_index_groups=inside)
@@ -276,9 +264,19 @@
         forward = jnp.dot(hidden, weight_down, preferred_element_type=f32)
         forward = lax.optimization_barrier(forward)
         branch = finish(member[None], parts, weight_attn, forward, shift_scale)
-        branch = summed_over(branch, along_x)
-        branch = summed_over(branch.reshape(-1, LANES), along_z).reshape(rows, width)
-        finished = (current.astype(f32) + branch).astype(bf16)
+        branch = summed_over(branch, blocks).astype(bf16)
+        if tick_number < TICKS - 1:
+            branch = summed_over(branch, pairs).astype(bf16)
+            branch = lax.all_to_all(
+                jnp.broadcast_to(branch[None], (quads,) + branch.shape),
+                "tp", 0, 0, axis_index_groups=quad,
+            )
+            branch = jnp.sum(branch.astype(f32), axis=0)
+            residual = lax.dynamic_slice_in_dim(patch, first, quads * rows, 0)
+        else:
+            branch = summed_over(branch.reshape(-1, LANES), far).reshape(rows, width)
+            residual = lax.dynamic_slice_in_dim(patch, first + rows * (z_here // 4), rows, 0)
+        finished = (residual.astype(f32) + branch).astype(bf16)
         current = shifted(finished, "pipe", 1)
     return current[None]
 

time: 245 us -> 249 us (1.016)
  blocking collectives: 107 us -> 61.6 us
  waiting for transfers between devices: 44.9 us -> 75.4 us
  starting transfers between devices: 72.6 us -> 85.2 us
  local copies, waits for them, and re-layouts: 5.48 us -> 10.9 us
    all_to_all x1 -> x3, waiting for transfers between devices: 0.01 us -> 35.9 us  [the longest x1 12.4 us: local(): lax.all_to_all(jnp.broadcast_to(branch[None], (quads,) + branch.shape), '...]
    all_to_all x4 -> x3, blocking collectives: 62 us -> 29.7 us  [summed_over(): parts = lax.all_to_all(parts, 'tp', 0, 0, axis_index_groups=groups)]
    all_to_all x1 -> x0, blocking collectives: 16.7 us -> none  [local(): normed = lax.all_to_all(block, 'tp', 0, 0, axis_index_groups=along_z)]
    all_to_all x1 -> x3, starting transfers between devices: 15.7 us -> 28.1 us  [the longest x1 14.8 us: local(): lax.all_to_all(block, 'tp', 0, 0, axis_index_groups=far).reshape(-1, width)]
    all_to_all x1 -> x2, blocking collectives: 10.9 us -> 18.7 us  [gathered(): spread = lax.all_to_all(spread, 'tp', 0, 0, axis_index_groups=groups)]
    ppermute x3, waiting for transfers between devices: 4.51 us -> 0.01 us  [local(): part = lax.ppermute(part, 'tp', route)]
    all_to_all x1, blocking collectives: 17.6 us -> 13.2 us  [local(): team = lax.all_to_all(team, 'tp', 0, 0, axis_index_groups=inside)]
    ppermute x1, waiting for transfers between devices: 12.9 us -> 8.58 us  [local(): lax.ppermute(give, 'tp', [(z_count * x + z, z_count * x + partner[z]) for...]
  transfers between devices with their start and end apart: 11 -> 13, of which waited for: 8 -> 10; matrix products, arithmetic and copies ran while one was open for 2% -> 2% of each run, Pallas kernels for 0% -> 0%
where the time goes in v8:
time: 249 us; the launch traced here: 247 us
  starting transfers between devices  85.2 us (34%)
  waiting for transfers between devices  75.4 us (30%)
  blocking collectives  61.6 us (25%)
  local copies, waits for them, and re-layouts  10.9 us (4%)
  Pallas kernels  8.25 us (3%)
  matrix products  4.34 us (2%)
    all_to_all x3, blocking collectives, summed_over(): parts = lax.all_to_all(parts, 'tp', 0, 0, axis_index_groups=groups)  29.7 us
    ppermute x2, starting transfers between devices, shifted(): lax.ppermute(block, axis, [((i - distance) % size, i) for i in range(size)])  22.4 us
    all_to_all x2, blocking collectives, gathered(): spread = lax.all_to_all(spread, 'tp', 0, 0, axis_index_groups=groups)  18.7 us
    all_to_all x2, waiting for transfers between devices, local(): parts = lax.all_to_all(parts, 'tp', 0, 0, axis_index_groups=inside)  16.2 us
    all_to_all x1, starting transfers between devices, local(): lax.all_to_all(block, 'tp', 0, 0, axis_index_groups=far).reshape(-1, width)  14.8 us
    all_to_all x1, blocking collectives, local(): team = lax.all_to_all(team, 'tp', 0, 0, axis_index_groups=inside)  13.2 us
    all_to_all x1, waiting for transfers between devices, local(): lax.all_to_all(jnp.broadcast_to(branch[None], (quads,) + branch.shape), '...  12.4 us
    all_to_all x1, waiting for transfers between devices, local(): lax.all_to_all(block, 'tp', 0, 0, axis_index_groups=far).reshape(-1, width)  11.8 us
  transfers between devices with their start and end apart: 13, of which 10 were waited for; matrix products, arithmetic and copies ran while one was open for 2% of the time, Pallas kernels for 0%

profile of v8, /device:TPU:1, one launch (start us, length us, event | category | flops | bytes accessed | tf_op | source)
XLA Modules:
  0.0 247.1 jit_solution(8636793586045205384)
XLA Ops:
  0.0 0.8 broadcast_in_dim.28
  0.8 0.7 broadcast_in_dim.54
  1.5 1.0 dynamic-slice_bitcast_fusion
  2.5 5.2 %collective-permute-start.2 = (bf16[48,768]{1,0:T(8,128)(2,1)S(1)}, bf16[48,768]{1,0:T(8,128)(2,1)S(1)}, u32[]{:S(2)}, u32[]{:S(2)}) collective-permute-start(bf16[48,768]{1,0:T(8,128)(2,1)S(1)} %get-tuple-element.28), channel_id=1, source_target_pairs={{0,48},{1,49},{2,50},{3,51},{4,52},{5,53},{6,54},{7,55},{8,56},{9,... | collective-permute-start | bytes 221192 | tf_op jit(solution)/shard_map/ppermute | solution.py:232
  7.7 2.4 collective-permute-start.1
  10.2 2.5 %collective-permute-start = (bf16[48,768]{1,0:T(8,128)(2,1)S(1)}, bf16[48,768]{1,0:T(8,128)(2,1)S(1)}, u32[]{:S(2)}, u32[]{:S(2)}) collective-permute-start(bf16[48,768]{1,0:T(8,128)(2,1)S(1)} %get-tuple-element.30), channel_id=1, source_target_pairs={{0,16},{1,17},{2,18},{3,19},{4,20},{5,21},{6,22},{7,23},{8,24},{9,... | collective-permute-start | bytes 221192 | tf_op jit(solution)/shard_map/ppermute | solution.py:232
  12.7 14.8 %all-to-all-start = ((bf16[8,48,128]{2,1,0:T(8,128)(2,1)}), bf16[8,48,128]{2,1,0:T(8,128)(2,1)S(1)}, u32[]{:S(2)}, u32[]{:S(2)}) async-start(bf16[8,48,128]{2,1,0:T(8,128)(2,1)} %broadcast_in_dim.54), calls=%async_computation | async-start | bytes 196608 | tf_op jit(solution)/shard_map/all_to_all | solution.py:239
  27.6 11.8 %all-to-all-done = bf16[8,48,128]{2,1,0:T(8,128)(2,1)S(1)} async-done(((bf16[8,48,128]{2,1,0:T(8,128)(2,1)}), bf16[8,48,128]{2,1,0:T(8,128)(2,1)S(1)}, u32[]{:S(2)}, u32[]{:S(2)}) %all-to-all-start) | async-done | bytes 98336 | tf_op jit(solution)/shard_map/all_to_all | solution.py:239
  39.5 1.0 broadcast_in_dim.55
  40.5 4.1 %all-to-all-start.1 = ((bf16[8,16,3072]{2,1,0:T(8,128)(2,1)}), bf16[8,16,3072]{2,1,0:T(8,128)(2,1)S(1)}, u32[]{:S(2)}, u32[]{:S(2)}) async-start(bf16[8,16,3072]{2,1,0:T(8,128)(2,1)} %broadcast_in_dim.55), calls=%async_computation.1 | async-start | bytes 1572864 | tf_op jit(solution)/shard_map/all_to_all | solution.py:152
  44.6 2.9 %collective-permute-start.3 = (bf16[4,48,384]{2,1,0:T(8,128)(2,1)S(1)}, bf16[4,48,384]{2,1,0:T(8,128)(2,1)S(1)}, u32[]{:S(2)}, u32[]{:S(2)}) collective-permute-start(bf16[4,48,384]{2,1,0:T(8,128)(2,1)S(1)} %get-tuple-element.18), channel_id=1, source_target_pairs={{0,12},{1,13},{2,14},{3,15},{4,8},{5,9},{6,10},{7,11},{8,4},{9,5},... | collective-permute-start | bytes 442376 | tf_op jit(solution)/shard_map/ppermute | solution.py:243
  47.5 8.6 %collective-permute-done.3.got_ref = bf16[4,48,384]{2,1,0:T(8,128)(2,1)S(1)} collective-permute-done((bf16[4,48,384]{2,1,0:T(8,128)(2,1)S(1)}, bf16[4,48,384]{2,1,0:T(8,128)(2,1)S(1)}, u32[]{:S(2)}, u32[]{:S(2)}) %collective-permute-start.3) | collective-permute-done | bytes 147488 | tf_op jit(solution)/shard_map/ppermute | solution.py:243
  56.1 3.3 %all-to-all-done.1 = bf16[8,16,3072]{2,1,0:T(8,128)(2,1)S(1)} async-done(((bf16[8,16,3072]{2,1,0:T(8,128)(2,1)}), bf16[8,16,3072]{2,1,0:T(8,128)(2,1)S(1)}, u32[]{:S(2)}, u32[]{:S(2)}) %all-to-all-start.1) | async-done | bytes 786464 | tf_op jit(solution)/shard_map/all_to_all | solution.py:152
  59.3 1.7 shard_map.91
  61.0 0.9 copy-done.9
  61.9 9.5 %all-to-all-start.2 = ((bf16[8,64,128]{2,1,0:T(8,128)(2,1)}), bf16[8,64,128]{2,1,0:T(8,128)(2,1)S(1)}, u32[]{:S(2)}, u32[]{:S(2)}) async-start(bf16[8,64,128]{2,1,0:T(8,128)(2,1)} %get-tuple-element.20), calls=%async_computation.2 | async-start | bytes 262144 | tf_op jit(solution)/shard_map/all_to_all | solution.py:254
  72.2 9.4 %all-to-all-done.2.team_ref = bf16[8,64,128]{2,1,0:T(8,128)(2,1)S(1)} async-done(((bf16[8,64,128]{2,1,0:T(8,128)(2,1)}), bf16[8,64,128]{2,1,0:T(8,128)(2,1)S(1)}, u32[]{:S(2)}, u32[]{:S(2)}) %all-to-all-start.2) | async-done | bytes 131104 | tf_op jit(solution)/shard_map/all_to_all | solution.py:254
  81.8 1.5 shard_map.92
  83.9 4.0 %all-to-all-start.3 = ((bf16[8,64,128]{2,1,0:T(8,128)(2,1)}), bf16[8,64,128]{2,1,0:T(8,128)(2,1)}, u32[]{:S(2)}, u32[]{:S(2)}) async-start(bf16[8,64,128]{2,1,0:T(8,128)(2,1)} %shard_map.92), calls=%async_computation.3 | async-start | bytes 262144 | tf_op jit(solution)/shard_map/all_to_all | solution.py:256
  87.9 1.8 fusion.17
  90.1 8.1 %all-to-all-done.3.parts_ref = bf16[8,64,128]{2,1,0:T(8,128)(2,1)} async-done(((bf16[8,64,128]{2,1,0:T(8,128)(2,1)}), bf16[8,64,128]{2,1,0:T(8,128)(2,1)}, u32[]{:S(2)}, u32[]{:S(2)}) %all-to-all-start.3) | async-done | bytes 131104 | tf_op jit(solution)/shard_map/all_to_all | solution.py:256
  98.2 1.0 copy-done.5
  99.1 0.8 copy-done.16
  99.9 1.3 shard_map.93
  101.2 11.4 %all_to_all.65 = bf16[8,16,3072]{2,1,0:T(8,128)(2,1)S(1)} all-to-all(bf16[8,16,3072]{2,1,0:T(8,128)(2,1)S(1)} %bitcast.53), channel_id=1, replica_groups={{0,1,16,17,32,33,48,49},{2,3,18,19,34,35,50,51},{4,5,20,21,36,37,52,53}..., dimensions={0} | all-to-all | bytes 1572864 | tf_op jit(solution)/shard_map/all_to_all | solution.py:159
  112.7 6.9 %all_to_all.66 = bf16[2,8,3072]{2,1,0:T(8,128)(2,1)S(1)} all-to-all(bf16[2,8,3072]{2,1,0:T(8,128)(2,1)S(1)} %bitcast.60), channel_id=1, replica_groups={{0,2},{4,6},{8,10},{12,14},{1,3},{5,7},{9,11},{13,15},{16,18},{20,22},{..., dimensions={0} | all-to-all | bytes 196608 | tf_op jit(solution)/shard_map/all_to_all | solution.py:159
  119.7 0.7 broadcast_in_dim.60
  120.4 7.6 %all-to-all-start.6 = ((bf16[4,8,3072]{2,1,0:T(8,128)(2,1)}), bf16[4,8,3072]{2,1,0:T(8,128)(2,1)S(1)}, u32[]{:S(2)}, u32[]{:S(2)}) async-start(bf16[4,8,3072]{2,1,0:T(8,128)(2,1)} %broadcast_in_dim.60), calls=%async_computation.6 | async-start | bytes 393216 | tf_op jit(solution)/shard_map/all_to_all | solution.py:270
  127.9 12.4 %all-to-all-done.6 = bf16[4,8,3072]{2,1,0:T(8,128)(2,1)S(1)} async-done(((bf16[4,8,3072]{2,1,0:T(8,128)(2,1)}), bf16[4,8,3072]{2,1,0:T(8,128)(2,1)S(1)}, u32[]{:S(2)}, u32[]{:S(2)}) %all-to-all-start.6) | async-done | bytes 196640 | tf_op jit(solution)/shard_map/all_to_all | solution.py:270
  140.4 11.9 %collective-permute-start.4 = (bf16[8,3072]{1,0:T(8,128)(2,1)S(1)}, bf16[8,3072]{1,0:T(8,128)(2,1)S(1)}, u32[]{:S(2)}, u32[]{:S(2)}) collective-permute-start(bf16[8,3072]{1,0:T(8,128)(2,1)S(1)} %add_convert_fusion), channel_id=1, source_target_pairs={{448,0},{0,64},{64,128},{128,192},{192,256},{256,320},{320,384},{3... | collective-permute-start | bytes 147464 | tf_op jit(solution)/shard_map/ppermute | solution.py:23
  152.3 1.2 collective-permute-done.4
  153.5 6.4 %all_to_all.67 = bf16[2,8,3072]{2,1,0:T(8,128)(2,1)S(1)} all-to-all(bf16[2,8,3072]{2,1,0:T(8,128)(2,1)S(1)} %broadcast_in_dim.61), channel_id=1, replica_groups={{0,2},{4,6},{8,10},{12,14},{1,3},{5,7},{9,11},{13,15},{16,18},{20,22},{..., dimensions={0} | all-to-all | bytes 196608 | tf_op jit(solution)/shard_map/all_to_all | solution.py:152
  159.9 12.3 %all_to_all.68 = bf16[8,16,3072]{2,1,0:T(8,128)(2,1)S(1)} all-to-all(bf16[8,16,3072]{2,1,0:T(8,128)(2,1)S(1)} %broadcast_in_dim.63), channel_id=1, replica_groups={{0,1,16,17,32,33,48,49},{2,3,18,19,34,35,50,51},{4,5,20,21,36,37,52,53}..., dimensions={0} | all-to-all | bytes 1572864 | tf_op jit(solution)/shard_map/all_to_all | solution.py:152
  172.3 1.0 shard_map.94
  173.3 13.2 %all_to_all.69.team_ref = bf16[8,64,128]{2,1,0:T(8,128)(2,1)S(1)} all-to-all(bf16[8,64,128]{2,1,0:T(8,128)(2,1)S(1)} %get-tuple-element.23), channel_id=1, replica_groups={{0,1,2,3,4,5,6,7},{8,9,10,11,12,13,14,15},{16,17,18,19,20,21,22,23},{24..., dimensions={0} | all-to-all | bytes 262144 | tf_op jit(solution)/shard_map/all_to_all | solution.py:254
  186.6 1.5 shard_map.95
  188.1 4.0 %all-to-all-start.10 = ((bf16[8,64,128]{2,1,0:T(8,128)(2,1)}), bf16[8,64,128]{2,1,0:T(8,128)(2,1)}, u32[]{:S(2)}, u32[]{:S(2)}) async-start(bf16[8,64,128]{2,1,0:T(8,128)(2,1)} %shard_map.95), calls=%async_computation.10 | async-start | bytes 262144 | tf_op jit(solution)/shard_map/all_to_all | solution.py:256
  192.1 1.8 fusion.29
  194.2 8.1 %all-to-all-done.10.parts_ref = bf16[8,64,128]{2,1,0:T(8,128)(2,1)} async-done(((bf16[8,64,128]{2,1,0:T(8,128)(2,1)}), bf16[8,64,128]{2,1,0:T(8,128)(2,1)}, u32[]{:S(2)}, u32[]{:S(2)}) %all-to-all-start.10) | async-done | bytes 131104 | tf_op jit(solution)/shard_map/all_to_all | solution.py:256
  202.4 1.0 copy-done.6
  203.3 0.8 copy-done.18
  204.1 1.3 shard_map.96
  205.4 11.4 %all_to_all.70 = bf16[8,16,3072]{2,1,0:T(8,128)(2,1)S(1)} all-to-all(bf16[8,16,3072]{2,1,0:T(8,128)(2,1)S(1)} %bitcast.52), channel_id=1, replica_groups={{0,1,16,17,32,33,48,49},{2,3,18,19,34,35,50,51},{4,5,20,21,36,37,52,53}..., dimensions={0} | all-to-all | bytes 1572864 | tf_op jit(solution)/shard_map/all_to_all | solution.py:159
  216.9 0.7 reshape_reshape.3
  217.6 5.7 %all-to-all-start.12 = ((bf16[8,48,128]{2,1,0:T(8,128)(2,1)}), bf16[8,48,128]{2,1,0:T(8,128)(2,1)S(1)}, u32[]{:S(2)}, u32[]{:S(2)}) async-start(bf16[8,48,128]{2,1,0:T(8,128)(2,1)} %reshape_reshape.3), calls=%async_computation.12 | async-start | bytes 196608 | tf_op jit(solution)/shard_map/all_to_all | solution.py:159
  223.3 11.8 %all-to-all-done.12 = bf16[8,48,128]{2,1,0:T(8,128)(2,1)S(1)} async-done(((bf16[8,48,128]{2,1,0:T(8,128)(2,1)}), bf16[8,48,128]{2,1,0:T(8,128)(2,1)S(1)}, u32[]{:S(2)}, u32[]{:S(2)}) %all-to-all-start.12) | async-done | bytes 98336 | tf_op jit(solution)/shard_map/all_to_all | solution.py:159
  235.1 10.5 %collective-permute-start.5 = (bf16[2,3072]{1,0:T(2,128)(2,1)S(1)}, bf16[2,3072]{1,0:T(2,128)(2,1)S(1)}, u32[]{:S(2)}, u32[]{:S(2)}) collective-permute-start(bf16[2,3072]{1,0:T(2,128)(2,1)S(1)} %add_convert_fusion.1), channel_id=1, source_target_pairs={{448,0},{0,64},{64,128},{128,192},{192,256},{256,320},{320,384},{3... | collective-permute-start | bytes 36872 | tf_op jit(solution)/shard_map/ppermute | solution.py:23
  245.6 0.8 collective-permute-done.5
  (58 shorter events, 2.9 us)
Async XLA Ops:
  0.0 89.7 %copy-start = (bf16[1,192,3072]{2,1,0:T(8,128)(2,1)S(1)}, bf16[1,192,3072]{2,1,0:T(8,128)(2,1)}, u32[]{:S(2)}) copy-start(bf16[1,192,3072]{2,1,0:T(8,128)(2,1)} %param.13) | copy-start | bytes 3538948
  2.5 25.0 %collective-permute-start.2 = (bf16[48,768]{1,0:T(8,128)(2,1)S(1)}, bf16[48,768]{1,0:T(8,128)(2,1)S(1)}, u32[]{:S(2)}, u32[]{:S(2)}) collective-permute-start(bf16[48,768]{1,0:T(8,128)(2,1)S(1)} %get-tuple-element.28), channel_id=1, source_target_pairs={{0,48},{1,49},{2,50},{3,51},{4,52},{5,53},{6,54},{7,55},{8,56},{9,... | collective-permute-start | bytes 221192 | tf_op jit(solution)/shard_map/ppermute | solution.py:232
  7.7 19.8 %collective-permute-start.1 = (bf16[48,768]{1,0:T(8,128)(2,1)S(1)}, bf16[48,768]{1,0:T(8,128)(2,1)S(1)}, u32[]{:S(2)}, u32[]{:S(2)}) collective-permute-start(bf16[48,768]{1,0:T(8,128)(2,1)S(1)} %get-tuple-element.29), channel_id=1, source_target_pairs={{0,32},{1,33},{2,34},{3,35},{4,36},{5,37},{6,38},{7,39},{8,40},{9,... | collective-permute-start | bytes 221192 | tf_op jit(solution)/shard_map/ppermute | solution.py:232
  10.2 17.4 %collective-permute-start = (bf16[48,768]{1,0:T(8,128)(2,1)S(1)}, bf16[48,768]{1,0:T(8,128)(2,1)S(1)}, u32[]{:S(2)}, u32[]{:S(2)}) collective-permute-start(bf16[48,768]{1,0:T(8,128)(2,1)S(1)} %get-tuple-element.30), channel_id=1, source_target_pairs={{0,16},{1,17},{2,18},{3,19},{4,20},{5,21},{6,22},{7,23},{8,24},{9,... | collective-permute-start | bytes 221192 | tf_op jit(solution)/shard_map/ppermute | solution.py:232
  12.7 26.7 %all-to-all-start = ((bf16[8,48,128]{2,1,0:T(8,128)(2,1)}), bf16[8,48,128]{2,1,0:T(8,128)(2,1)S(1)}, u32[]{:S(2)}, u32[]{:S(2)}) async-start(bf16[8,48,128]{2,1,0:T(8,128)(2,1)} %broadcast_in_dim.54), calls=%async_computation | async-start | bytes 196608 | tf_op jit(solution)/shard_map/all_to_all | solution.py:239
  27.6 54.1 %copy-start.3 = (bf16[4,48,384]{2,1,0:T(8,128)(2,1)}, bf16[4,48,384]{2,1,0:T(8,128)(2,1)S(1)}, u32[]{:S(2)}) copy-start(bf16[4,48,384]{2,1,0:T(8,128)(2,1)S(1)} %get-tuple-element.25.keep_ref) | copy-start | bytes 442372
  39.4 19.9 %copy-start.1 = (bf16[1,3,48,3072]{3,2,1,0:T(8,128)(2,1)S(1)}, bf16[1,3,48,3072]{3,2,1,0:T(8,128)(2,1)}, u32[]{:S(2)}) copy-start(bf16[1,3,48,3072]{3,2,1,0:T(8,128)(2,1)} %param.10) | copy-start | bytes 2654212
  39.5 19.9 %copy-start.15 = (f32[1,3,3072]{2,0,1:T(1,128)S(1)}, f32[1,3,3072]{2,0,1:T(1,128)}, u32[]{:S(2)}) copy-start(f32[1,3,3072]{2,0,1:T(1,128)} %param.14) | copy-start | bytes 110596
  40.5 18.9 %all-to-all-start.1 = ((bf16[8,16,3072]{2,1,0:T(8,128)(2,1)}), bf16[8,16,3072]{2,1,0:T(8,128)(2,1)S(1)}, u32[]{:S(2)}, u32[]{:S(2)}) async-start(bf16[8,16,3072]{2,1,0:T(8,128)(2,1)} %broadcast_in_dim.55), calls=%async_computation.1 | async-start | bytes 1572864 | tf_op jit(solution)/shard_map/all_to_all | solution.py:152
  44.6 27.5 %copy-start.19 = (f32[1,2,128]{2,1,0:T(2,128)S(1)}, f32[1,2,128]{2,1,0:T(2,128)}, u32[]{:S(2)}) copy-start(f32[1,2,128]{2,1,0:T(2,128)} %param.15) | copy-start | bytes 3076
  44.6 11.5 %collective-permute-start.3 = (bf16[4,48,384]{2,1,0:T(8,128)(2,1)S(1)}, bf16[4,48,384]{2,1,0:T(8,128)(2,1)S(1)}, u32[]{:S(2)}, u32[]{:S(2)}) collective-permute-start(bf16[4,48,384]{2,1,0:T(8,128)(2,1)S(1)} %get-tuple-element.18), channel_id=1, source_target_pairs={{0,12},{1,13},{2,14},{3,15},{4,8},{5,9},{6,10},{7,11},{8,4},{9,5},... | collective-permute-start | bytes 442376 | tf_op jit(solution)/shard_map/ppermute | solution.py:243
  56.1 27.2 %copy-start.11 = (bf16[4,48,384]{2,1,0:T(8,128)(2,1)}, bf16[4,48,384]{2,1,0:T(8,128)(2,1)S(1)}, u32[]{:S(2)}) copy-start(bf16[4,48,384]{2,1,0:T(8,128)(2,1)S(1)} %collective-permute-done.3.got_ref) | copy-start | bytes 442372
  61.0 0.9 copy-start.9
  61.9 26.0 %copy-start.10 = (bf16[128,3072]{1,0:T(8,128)(2,1)S(1)}, bf16[128,3072]{1,0:T(8,128)(2,1)}, u32[]{:S(2)}) copy-start(bf16[128,3072]{1,0:T(8,128)(2,1)} %copy-done.9) | copy-start | bytes 2359300
  61.9 19.7 %all-to-all-start.2 = ((bf16[8,64,128]{2,1,0:T(8,128)(2,1)}), bf16[8,64,128]{2,1,0:T(8,128)(2,1)S(1)}, u32[]{:S(2)}, u32[]{:S(2)}) async-start(bf16[8,64,128]{2,1,0:T(8,128)(2,1)} %get-tuple-element.20), calls=%async_computation.2 | async-start | bytes 262144 | tf_op jit(solution)/shard_map/all_to_all | solution.py:254
  72.2 15.7 %copy-start.13 = (f32[128,1]{1,0:T(8,128)}, f32[128,1]{1,0:T(8,128)S(1)}, u32[]{:S(2)}) copy-start(f32[128,1]{1,0:T(8,128)S(1)} %copy.12.gain_q_ref) | copy-start | bytes 1540
  83.2 0.6 copy-start.7
  83.9 14.3 %all-to-all-start.3 = ((bf16[8,64,128]{2,1,0:T(8,128)(2,1)}), bf16[8,64,128]{2,1,0:T(8,128)(2,1)}, u32[]{:S(2)}, u32[]{:S(2)}) async-start(bf16[8,64,128]{2,1,0:T(8,128)(2,1)} %shard_map.92), calls=%async_computation.3 | async-start | bytes 262144 | tf_op jit(solution)/shard_map/all_to_all | solution.py:256
  98.2 1.0 copy-start.5
  99.1 0.8 copy-start.16
  120.4 20.0 %all-to-all-start.6 = ((bf16[4,8,3072]{2,1,0:T(8,128)(2,1)}), bf16[4,8,3072]{2,1,0:T(8,128)(2,1)S(1)}, u32[]{:S(2)}, u32[]{:S(2)}) async-start(bf16[4,8,3072]{2,1,0:T(8,128)(2,1)} %broadcast_in_dim.60), calls=%async_computation.6 | async-start | bytes 393216 | tf_op jit(solution)/shard_map/all_to_all | solution.py:270
  140.4 13.1 %collective-permute-start.4 = (bf16[8,3072]{1,0:T(8,128)(2,1)S(1)}, bf16[8,3072]{1,0:T(8,128)(2,1)S(1)}, u32[]{:S(2)}, u32[]{:S(2)}) collective-permute-start(bf16[8,3072]{1,0:T(8,128)(2,1)S(1)} %add_convert_fusion), channel_id=1, source_target_pairs={{448,0},{0,64},{64,128},{128,192},{192,256},{256,320},{320,384},{3... | collective-permute-start | bytes 147464 | tf_op jit(solution)/shard_map/ppermute | solution.py:23
  159.9 12.4 %copy-start.2 = (bf16[1,3,48,3072]{3,2,1,0:T(8,128)(2,1)S(1)}, bf16[1,3,48,3072]{3,2,1,0:T(8,128)(2,1)}, u32[]{:S(2)}) copy-start(bf16[1,3,48,3072]{3,2,1,0:T(8,128)(2,1)} %param.10) | copy-start | bytes 2654212
  159.9 12.4 %copy-start.17 = (f32[1,3,3072]{2,0,1:T(1,128)S(1)}, f32[1,3,3072]{2,0,1:T(1,128)}, u32[]{:S(2)}) copy-start(f32[1,3,3072]{2,0,1:T(1,128)} %param.14) | copy-start | bytes 110596
  172.3 14.3 %copy-start.4 = (bf16[4,48,384]{2,1,0:T(8,128)(2,1)S(1)}, bf16[4,48,384]{2,1,0:T(8,128)(2,1)}, u32[]{:S(2)}) copy-start(bf16[4,48,384]{2,1,0:T(8,128)(2,1)} %copy-done.3) | copy-start | bytes 442372
  172.3 14.3 %copy-start.8 = (f32[192,128]{1,0:T(8,128)S(1)}, f32[192,128]{1,0:T(8,128)}, u32[]{:S(2)}) copy-start(f32[192,128]{1,0:T(8,128)} %copy-done.7) | copy-start | bytes 294916
  172.3 14.3 %copy-start.12 = (bf16[4,48,384]{2,1,0:T(8,128)(2,1)S(1)}, bf16[4,48,384]{2,1,0:T(8,128)(2,1)}, u32[]{:S(2)}) copy-start(bf16[4,48,384]{2,1,0:T(8,128)(2,1)} %copy-done.11) | copy-start | bytes 442372
  172.3 14.3 %copy-start.14 = (f32[128,1]{1,0:T(8,128)S(1)}, f32[128,1]{1,0:T(8,128)}, u32[]{:S(2)}) copy-start(f32[128,1]{1,0:T(8,128)} %copy-done.13) | copy-start | bytes 1540
  188.1 14.3 %all-to-all-start.10 = ((bf16[8,64,128]{2,1,0:T(8,128)(2,1)}), bf16[8,64,128]{2,1,0:T(8,128)(2,1)}, u32[]{:S(2)}, u32[]{:S(2)}) async-start(bf16[8,64,128]{2,1,0:T(8,128)(2,1)} %shard_map.95), calls=%async_computation.10 | async-start | bytes 262144 | tf_op jit(solution)/shard_map/all_to_all | solution.py:256
  202.4 1.0 copy-start.6
  203.3 0.8 copy-start.18
  217.6 17.5 %all-to-all-start.12 = ((bf16[8,48,128]{2,1,0:T(8,128)(2,1)}), bf16[8,48,128]{2,1,0:T(8,128)(2,1)S(1)}, u32[]{:S(2)}, u32[]{:S(2)}) async-start(bf16[8,48,128]{2,1,0:T(8,128)(2,1)} %reshape_reshape.3), calls=%async_computation.12 | async-start | bytes 196608 | tf_op jit(solution)/shard_map/all_to_all | solution.py:159
  235.1 11.4 %collective-permute-start.5 = (bf16[2,3072]{1,0:T(2,128)(2,1)S(1)}, bf16[2,3072]{1,0:T(2,128)(2,1)S(1)}, u32[]{:S(2)}, u32[]{:S(2)}) collective-permute-start(bf16[2,3072]{1,0:T(2,128)(2,1)S(1)} %add_convert_fusion.1), channel_id=1, source_target_pairs={{448,0},{0,64},{64,128},{128,192},{192,256},{256,320},{320,384},{3... | collective-permute-start | bytes 36872 | tf_op jit(solution)/shard_map/ppermute | solution.py:23

commit v9 on v6

--- a/solution.py
+++ b/solution.py
@@ -28,7 +28,7 @@
     centred = x - jnp.mean(x, axis=1, keepdims=True)
     variance = jnp.mean(centred * centred, axis=1, keepdims=True)
     normed = centred * lax.rsqrt(variance + eps_norm)
-    normed = normed * (1.0 + modulation_ref[1:2, :]) + modulation_ref[0:1, :]
+    normed = normed * (1.0 + modulation_ref[1]) + modulation_ref[0]
     rows, width = x.shape
     pieces = width // LANES
     for r in range(rows):
@@ -49,7 +49,7 @@
         in_specs=[whole] * 2,
         out_specs=whole,
         scratch_shapes=[pltpu.VMEM((lines, LANES), f32)],
-        compiler_params=pltpu.CompilerParams(vmem_limit_bytes=16 * 1024 * 1024),
+        compiler_params=pltpu.CompilerParams(vmem_limit_bytes=8 * 1024 * 1024),
     )(rows, modulation)
 
 
@@ -66,7 +66,7 @@
     branch = lax.dot_general(
         attention, weight_ref[...], (((0,), (0,)), ((), ())), preferred_element_type=f32
     )
-    out_ref[...] = ((branch + forward_ref[...]) * modulation_ref[2:3, :]).astype(bf16)
+    out_ref[...] = ((branch + forward_ref[...]) * modulation_ref[2]).astype(bf16)
 
 
 def finish(member, parts, weights, forward, modulation):
@@ -76,7 +76,7 @@
         out_shape=jax.ShapeDtypeStruct(forward.shape, bf16),
         in_specs=[pl.BlockSpec(memory_space=pltpu.SMEM)] + [whole] * 4,
         out_specs=whole,
-        compiler_params=pltpu.CompilerParams(vmem_limit_bytes=16 * 1024 * 1024),
+        compiler_params=pltpu.CompilerParams(vmem_limit_bytes=8 * 1024 * 1024),
     )(member, parts, weights, forward, modulation)
 
 
@@ -103,7 +103,7 @@
         out_shape=jax.ShapeDtypeStruct((TEAM, weights.shape[0] // 3 + 16, LANES), bf16),
         in_specs=[whole] * 2,
         out_specs=whole,
-        compiler_params=pltpu.CompilerParams(vmem_limit_bytes=16 * 1024 * 1024),
+        compiler_params=pltpu.CompilerParams(vmem_limit_bytes=8 * 1024 * 1024),
     )(normed, weights)
 
 
@@ -164,7 +164,7 @@
         in_specs=[whole] * 6,
         out_specs=whole,
         scratch_shapes=[pltpu.VMEM((TEAM_HEADS * HEAD_DIM, LANES), bf16)],
-        compiler_params=pltpu.CompilerParams(vmem_limit_bytes=16 * 1024 * 1024),
+        compiler_params=pltpu.CompilerParams(vmem_limit_bytes=8 * 1024 * 1024),
     )(team, keep, got, mask, gains[0][:, None], gains[1][None, :])
 
 
@@ -196,10 +196,13 @@
     team_width = TEAM * shard
     member = tp_index % TEAM
     z_count, x_count = 2 * TEAM, tp_count // (2 * TEAM)
-    along_z = [[z_count * x + z for z in range(z_count)] for x in range(x_count)]
-    along_x = [[z_count * x + z for x in range(x_count)] for z in range(z_count)]
+    xs, hs, two = range(x_count), range(z_count // 2), range(2)
+    along_z = [[z_count * x + 2 * h + l for l in two for h in hs] for x in xs]
+    along_x = [[z_count * x + z for x in xs] for z in range(z_count)]
+    far = [[z_count * x + 2 * h + l for h in hs] for x in xs for l in two]
+    blocks = [[z_count * x + 2 * h + l for x in xs for l in two] for h in hs]
     inside = [[TEAM * t + m for m in range(TEAM)] for t in range(teams)]
-    shift_scale = modulation[0]
+    shift_scale = modulation.reshape(3, 1, width)
     gains = qk_gain[0]
     weight_qkv = w_qkv[0].reshape(3 * shard, width)
     weight_mlp = w_mlp[0]
@@ -248,20 +251,21 @@
     give = jnp.where(upper, by_x[:, :, :team_width], by_x[:, :, team_width:])
 
     for tick_number in range(TICKS):
-        if tick_number:
-            block = spread(current, shift_scale, z_count)
-        normed = lax.all_to_all(block, "tp", 0, 0, axis_index_groups=along_z)
-        normed = normed.reshape(rows * z_count, width)
         if tick_number == 0:
+            normed = lax.all_to_all(block, "tp", 0, 0, axis_index_groups=along_z)
+            normed = normed.reshape(-1, width)
             normed, give = lax.optimization_barrier((normed, give))
             got = lax.ppermute(
                 give,
                 "tp",
                 [(z_count * x + z, z_count * x + partner[z]) for x in range(x_count) for z in range(z_count)],
             )
-        normed = gathered(normed, along_x)
-        if tick_number == 0:
+            normed = gathered(normed, along_x)
             normed, got = lax.optimization_barrier((normed, got))
+        else:
+            block = spread(current, shift_scale, len(hs))
+            normed = lax.all_to_all(block, "tp", 0, 0, axis_index_groups=far)
+            normed = gathered(normed.reshape(-1, width), blocks)
         team = project(normed, weight_qkv)
         team = lax.all_to_all(team, "tp", 0, 0, axis_index_groups=inside)
         parts = attend(team, keep, got, cached_mask, gains)
@@ -276,8 +280,8 @@
         forward = jnp.dot(hidden, weight_down, preferred_element_type=f32)
         forward = lax.optimization_barrier(forward)
         branch = finish(member[None], parts, weight_attn, forward, shift_scale)
-        branch = summed_over(branch, along_x)
-        branch = summed_over(branch.reshape(-1, LANES), along_z).reshape(rows, width)
+        branch = summed_over(branch, blocks)
+        branch = summed_over(branch.reshape(-1, LANES), far).reshape(rows, width)
         finished = (current.astype(f32) + branch).astype(bf16)
         current = shifted(finished, "pipe", 1)
     return current[None]

time: 245 us -> 241 us (0.984)
    all_to_all x1, blocking collectives: 17.6 us -> 12.7 us  [local(): team = lax.all_to_all(team, 'tp', 0, 0, axis_index_groups=inside)]
    all_to_all x4, blocking collectives: 62 us -> 65.3 us  [summed_over(): parts = lax.all_to_all(parts, 'tp', 0, 0, axis_index_groups=groups)]
where the time goes in v9:
time: 241 us; the launch traced here: 240 us
  blocking collectives  105 us (44%)
  starting transfers between devices  71.7 us (30%)
  waiting for transfers between devices  45 us (19%)
  Pallas kernels  7.66 us (3%)
  local copies, waits for them, and re-layouts  4.75 us (2%)
  matrix products  4.32 us (2%)
    all_to_all x4, blocking collectives, summed_over(): parts = lax.all_to_all(parts, 'tp', 0, 0, axis_index_groups=groups)  65.3 us
    ppermute x2, starting transfers between devices, shifted(): lax.ppermute(block, axis, [((i - distance) % size, i) for i in range(size)])  20.9 us
    all_to_all x2, waiting for transfers between devices, local(): parts = lax.all_to_all(parts, 'tp', 0, 0, axis_index_groups=inside)  16.2 us
    all_to_all x1, starting transfers between devices, local(): normed = lax.all_to_all(block, 'tp', 0, 0, axis_index_groups=along_z)  15.7 us
    all_to_all x1, blocking collectives, local(): normed = lax.all_to_all(block, 'tp', 0, 0, axis_index_groups=far)  14.9 us
    ppermute x1, waiting for transfers between devices, local(): lax.ppermute(give, 'tp', [(z_count * x + z, z_count * x + partner[z]) for...  13 us
    all_to_all x1, blocking collectives, local(): team = lax.all_to_all(team, 'tp', 0, 0, axis_index_groups=inside)  12.7 us
    all_to_all x1, blocking collectives, gathered(): spread = lax.all_to_all(spread, 'tp', 0, 0, axis_index_groups=groups)  11.9 us
  transfers between devices with their start and end apart: 11, of which 8 were waited for; matrix products, arithmetic and copies ran while one was open for 2% of the time, Pallas kernels for 0%

profile of v9, /device:TPU:1, one launch (start us, length us, event | category | flops | bytes accessed | tf_op | source)
XLA Modules:
  0.0 239.7 jit_solution(8737989765326323847)
XLA Ops:
  0.0 0.9 copy-done.4
  0.9 0.7 copy-done.6
  1.6 0.9 shard_map.91
  2.5 15.7 %all-to-all-start = ((bf16[16,48,128]{2,1,0:T(8,128)(2,1)}), bf16[16,48,128]{2,1,0:T(8,128)(2,1)S(1)}, u32[]{:S(2)}, u32[]{:S(2)}) async-start(bf16[16,48,128]{2,1,0:T(8,128)(2,1)} %shard_map.91), calls=%async_computation | async-start | bytes 393216 | tf_op jit(solution)/shard_map/all_to_all | solution.py:255
  18.4 1.0 dynamic-slice_bitcast_fusion
  19.4 4.4 %collective-permute-start.2 = (bf16[48,768]{1,0:T(8,128)(2,1)S(1)}, bf16[48,768]{1,0:T(8,128)(2,1)S(1)}, u32[]{:S(2)}, u32[]{:S(2)}) collective-permute-start(bf16[48,768]{1,0:T(8,128)(2,1)S(1)} %get-tuple-element.20), channel_id=1, source_target_pairs={{0,48},{1,49},{2,50},{3,51},{4,52},{5,53},{6,54},{7,55},{8,56},{9,... | collective-permute-start | bytes 221192 | tf_op jit(solution)/shard_map/ppermute | solution.py:247
  23.8 2.4 %collective-permute-start.1 = (bf16[48,768]{1,0:T(8,128)(2,1)S(1)}, bf16[48,768]{1,0:T(8,128)(2,1)S(1)}, u32[]{:S(2)}, u32[]{:S(2)}) collective-permute-start(bf16[48,768]{1,0:T(8,128)(2,1)S(1)} %get-tuple-element.21), channel_id=1, source_target_pairs={{0,32},{1,33},{2,34},{3,35},{4,36},{5,37},{6,38},{7,39},{8,40},{9,... | collective-permute-start | bytes 221192 | tf_op jit(solution)/shard_map/ppermute | solution.py:247
  26.2 2.5 %collective-permute-start = (bf16[48,768]{1,0:T(8,128)(2,1)S(1)}, bf16[48,768]{1,0:T(8,128)(2,1)S(1)}, u32[]{:S(2)}, u32[]{:S(2)}) collective-permute-start(bf16[48,768]{1,0:T(8,128)(2,1)S(1)} %get-tuple-element.22), channel_id=1, source_target_pairs={{0,16},{1,17},{2,18},{3,19},{4,20},{5,21},{6,22},{7,23},{8,24},{9,... | collective-permute-start | bytes 221192 | tf_op jit(solution)/shard_map/ppermute | solution.py:247
  28.8 1.9 collective-permute-done.1
  30.7 2.6 %collective-permute-done = bf16[48,768]{1,0:T(8,128)(2,1)S(1)} collective-permute-done((bf16[48,768]{1,0:T(8,128)(2,1)S(1)}, bf16[48,768]{1,0:T(8,128)(2,1)S(1)}, u32[]{:S(2)}, u32[]{:S(2)}) %collective-permute-start) | collective-permute-done | bytes 73760 | tf_op jit(solution)/shard_map/ppermute | solution.py:247
  33.4 0.1 reshape.86
  33.5 1.0 broadcast_in_dim.35
  34.5 3.5 %all-to-all-start.1 = ((bf16[4,32,3072]{2,1,0:T(8,128)(2,1)}), bf16[4,32,3072]{2,1,0:T(8,128)(2,1)S(1)}, u32[]{:S(2)}, u32[]{:S(2)}) async-start(bf16[4,32,3072]{2,1,0:T(8,128)(2,1)} %broadcast_in_dim.35), calls=%async_computation.1 | async-start | bytes 1572864 | tf_op jit(solution)/shard_map/all_to_all | solution.py:174
  38.0 7.2 %collective-permute-start.3 = (bf16[4,48,384]{2,1,0:T(8,128)(2,1)S(1)}, bf16[4,48,384]{2,1,0:T(8,128)(2,1)S(1)}, u32[]{:S(2)}, u32[]{:S(2)}) collective-permute-start(bf16[4,48,384]{2,1,0:T(8,128)(2,1)S(1)} %get-tuple-element.14), channel_id=1, source_target_pairs={{0,12},{1,13},{2,14},{3,15},{4,8},{5,9},{6,10},{7,11},{8,4},{9,5},... | collective-permute-start | bytes 442376 | tf_op jit(solution)/shard_map/ppermute | solution.py:258
  45.2 13.0 %collective-permute-done.3.got_ref = bf16[4,48,384]{2,1,0:T(8,128)(2,1)S(1)} collective-permute-done((bf16[4,48,384]{2,1,0:T(8,128)(2,1)S(1)}, bf16[4,48,384]{2,1,0:T(8,128)(2,1)S(1)}, u32[]{:S(2)}, u32[]{:S(2)}) %collective-permute-start.3) | collective-permute-done | bytes 147488 | tf_op jit(solution)/shard_map/ppermute | solution.py:258
  58.2 1.2 shard_map.92
  59.4 6.4 %all-to-all-start.2 = ((bf16[8,64,128]{2,1,0:T(8,128)(2,1)}), bf16[8,64,128]{2,1,0:T(8,128)(2,1)S(1)}, u32[]{:S(2)}, u32[]{:S(2)}) async-start(bf16[8,64,128]{2,1,0:T(8,128)(2,1)} %shard_map.92), calls=%async_computation.2 | async-start | bytes 262144 | tf_op jit(solution)/shard_map/all_to_all | solution.py:270
  66.5 0.1 copy.12.gain_q_ref
  66.7 9.5 %all-to-all-done.2.team_ref = bf16[8,64,128]{2,1,0:T(8,128)(2,1)S(1)} async-done(((bf16[8,64,128]{2,1,0:T(8,128)(2,1)}), bf16[8,64,128]{2,1,0:T(8,128)(2,1)S(1)}, u32[]{:S(2)}, u32[]{:S(2)}) %all-to-all-start.2) | async-done | bytes 131104 | tf_op jit(solution)/shard_map/all_to_all | solution.py:270
  76.2 0.1 broadcast_in_dim.38.mask_ref
  76.3 1.5 shard_map.93
  77.8 5.3 %all-to-all-start.3 = ((bf16[8,64,128]{2,1,0:T(8,128)(2,1)}), bf16[8,64,128]{2,1,0:T(8,128)(2,1)}, u32[]{:S(2)}, u32[]{:S(2)}) async-start(bf16[8,64,128]{2,1,0:T(8,128)(2,1)} %shard_map.93), calls=%async_computation.3 | async-start | bytes 262144 | tf_op jit(solution)/shard_map/all_to_all | solution.py:272
  83.1 1.8 fusion.17
  84.9 0.4 fusion.2.forward_ref
  85.3 8.2 %all-to-all-done.3.parts_ref = bf16[8,64,128]{2,1,0:T(8,128)(2,1)} async-done(((bf16[8,64,128]{2,1,0:T(8,128)(2,1)}), bf16[8,64,128]{2,1,0:T(8,128)(2,1)}, u32[]{:S(2)}, u32[]{:S(2)}) %all-to-all-start.3) | async-done | bytes 131104 | tf_op jit(solution)/shard_map/all_to_all | solution.py:272
  93.5 1.3 shard_map.94
  94.9 13.5 %all_to_all.60 = bf16[8,16,3072]{2,1,0:T(8,128)(2,1)S(1)} all-to-all(bf16[8,16,3072]{2,1,0:T(8,128)(2,1)S(1)} %bitcast.53), channel_id=1, replica_groups={{0,1,16,17,32,33,48,49},{2,3,18,19,34,35,50,51},{4,5,20,21,36,37,52,53}..., dimensions={0} | all-to-all | bytes 1572864 | tf_op jit(solution)/shard_map/all_to_all | solution.py:181
  108.3 0.1 reduce_sum.42
  108.5 20.2 %all_to_all.61 = bf16[8,48,128]{2,1,0:T(8,128)(2,1)S(1)} all-to-all(bf16[8,48,128]{2,1,0:T(8,128)(2,1)S(1)} %convert_element_type.46), channel_id=1, replica_groups={{0,2,4,6,8,10,12,14},{1,3,5,7,9,11,13,15},{16,18,20,22,24,26,28,30},{17..., dimensions={0} | all-to-all | bytes 196608 | tf_op jit(solution)/shard_map/all_to_all | solution.py:181
  128.8 7.3 %collective-permute-start.4 = (bf16[2,3072]{1,0:T(2,128)(2,1)S(1)}, bf16[2,3072]{1,0:T(2,128)(2,1)S(1)}, u32[]{:S(2)}, u32[]{:S(2)}) collective-permute-start(bf16[2,3072]{1,0:T(2,128)(2,1)S(1)} %add_convert_fusion.1), channel_id=1, source_target_pairs={{448,0},{0,64},{64,128},{128,192},{192,256},{256,320},{320,384},{3... | collective-permute-start | bytes 36872 | tf_op jit(solution)/shard_map/ppermute | solution.py:23
  136.0 0.8 collective-permute-done.4.rows_ref
  136.9 0.2 shard_map.95
  137.1 14.9 %all_to_all.62 = bf16[8,48,128]{2,1,0:T(8,128)(2,1)S(1)} all-to-all(bf16[8,48,128]{2,1,0:T(8,128)(2,1)S(1)} %shard_map.95), channel_id=1, replica_groups={{0,2,4,6,8,10,12,14},{1,3,5,7,9,11,13,15},{16,18,20,22,24,26,28,30},{17..., dimensions={0} | all-to-all | bytes 196608 | tf_op jit(solution)/shard_map/all_to_all | solution.py:267
  152.2 11.9 %all_to_all.63 = bf16[8,16,3072]{2,1,0:T(8,128)(2,1)S(1)} all-to-all(bf16[8,16,3072]{2,1,0:T(8,128)(2,1)S(1)} %broadcast_in_dim.40), channel_id=1, replica_groups={{0,1,16,17,32,33,48,49},{2,3,18,19,34,35,50,51},{4,5,20,21,36,37,52,53}..., dimensions={0} | all-to-all | bytes 1572864 | tf_op jit(solution)/shard_map/all_to_all | solution.py:174
  164.1 0.6 shard_map.96
  164.6 12.7 %all_to_all.64.team_ref = bf16[8,64,128]{2,1,0:T(8,128)(2,1)S(1)} all-to-all(bf16[8,64,128]{2,1,0:T(8,128)(2,1)S(1)} %shard_map.96), channel_id=1, replica_groups={{0,1,2,3,4,5,6,7},{8,9,10,11,12,13,14,15},{16,17,18,19,20,21,22,23},{24..., dimensions={0} | all-to-all | bytes 262144 | tf_op jit(solution)/shard_map/all_to_all | solution.py:270
  177.3 1.5 shard_map.97
  178.8 3.4 %all-to-all-start.9 = ((bf16[8,64,128]{2,1,0:T(8,128)(2,1)}), bf16[8,64,128]{2,1,0:T(8,128)(2,1)S(1)}, u32[]{:S(2)}, u32[]{:S(2)}) async-start(bf16[8,64,128]{2,1,0:T(8,128)(2,1)} %shard_map.97), calls=%async_computation.9 | async-start | bytes 262144 | tf_op jit(solution)/shard_map/all_to_all | solution.py:272
  182.2 1.8 fusion.29
  183.9 0.4 fusion.forward_ref
  184.3 8.1 %all-to-all-done.9.parts_ref = bf16[8,64,128]{2,1,0:T(8,128)(2,1)S(1)} async-done(((bf16[8,64,128]{2,1,0:T(8,128)(2,1)}), bf16[8,64,128]{2,1,0:T(8,128)(2,1)S(1)}, u32[]{:S(2)}, u32[]{:S(2)}) %all-to-all-start.9) | async-done | bytes 131104 | tf_op jit(solution)/shard_map/all_to_all | solution.py:272
  192.4 0.4 shard_map.98
  192.8 11.4 %all_to_all.65 = bf16[8,16,3072]{2,1,0:T(8,128)(2,1)S(1)} all-to-all(bf16[8,16,3072]{2,1,0:T(8,128)(2,1)S(1)} %bitcast.52), channel_id=1, replica_groups={{0,1,16,17,32,33,48,49},{2,3,18,19,34,35,50,51},{4,5,20,21,36,37,52,53}..., dimensions={0} | all-to-all | bytes 1572864 | tf_op jit(solution)/shard_map/all_to_all | solution.py:181
  204.2 0.1 reduce_sum.44
  204.3 20.2 %all_to_all.66 = bf16[8,48,128]{2,1,0:T(8,128)(2,1)S(1)} all-to-all(bf16[8,48,128]{2,1,0:T(8,128)(2,1)S(1)} %convert_element_type.51), channel_id=1, replica_groups={{0,2,4,6,8,10,12,14},{1,3,5,7,9,11,13,15},{16,18,20,22,24,26,28,30},{17..., dimensions={0} | all-to-all | bytes 196608 | tf_op jit(solution)/shard_map/all_to_all | solution.py:181
  224.6 13.6 %collective-permute-start.5 = (bf16[2,3072]{1,0:T(2,128)(2,1)S(1)}, bf16[2,3072]{1,0:T(2,128)(2,1)S(1)}, u32[]{:S(2)}, u32[]{:S(2)}) collective-permute-start(bf16[2,3072]{1,0:T(2,128)(2,1)S(1)} %add_convert_fusion), channel_id=1, source_target_pairs={{448,0},{0,64},{64,128},{128,192},{192,256},{256,320},{320,384},{3... | collective-permute-start | bytes 36872 | tf_op jit(solution)/shard_map/ppermute | solution.py:23
  238.2 0.8 collective-permute-done.5
  239.1 0.6 copy.16
  (37 shorter events, 0.5 us)
Async XLA Ops:
  0.0 84.9 %copy-start = (bf16[1,192,3072]{2,1,0:T(8,128)(2,1)S(1)}, bf16[1,192,3072]{2,1,0:T(8,128)(2,1)}, u32[]{:S(2)}) copy-start(bf16[1,192,3072]{2,1,0:T(8,128)(2,1)} %param.13) | copy-start | bytes 3538948
  0.0 0.9 copy-start.4
  0.9 0.7 copy-start.6
  2.5 30.9 %all-to-all-start = ((bf16[16,48,128]{2,1,0:T(8,128)(2,1)}), bf16[16,48,128]{2,1,0:T(8,128)(2,1)S(1)}, u32[]{:S(2)}, u32[]{:S(2)}) async-start(bf16[16,48,128]{2,1,0:T(8,128)(2,1)} %shard_map.91), calls=%async_computation | async-start | bytes 393216 | tf_op jit(solution)/shard_map/all_to_all | solution.py:255
  19.4 9.4 %collective-permute-start.2 = (bf16[48,768]{1,0:T(8,128)(2,1)S(1)}, bf16[48,768]{1,0:T(8,128)(2,1)S(1)}, u32[]{:S(2)}, u32[]{:S(2)}) collective-permute-start(bf16[48,768]{1,0:T(8,128)(2,1)S(1)} %get-tuple-element.20), channel_id=1, source_target_pairs={{0,48},{1,49},{2,50},{3,51},{4,52},{5,53},{6,54},{7,55},{8,56},{9,... | collective-permute-start | bytes 221192 | tf_op jit(solution)/shard_map/ppermute | solution.py:247
  23.8 6.9 %collective-permute-start.1 = (bf16[48,768]{1,0:T(8,128)(2,1)S(1)}, bf16[48,768]{1,0:T(8,128)(2,1)S(1)}, u32[]{:S(2)}, u32[]{:S(2)}) collective-permute-start(bf16[48,768]{1,0:T(8,128)(2,1)S(1)} %get-tuple-element.21), channel_id=1, source_target_pairs={{0,32},{1,33},{2,34},{3,35},{4,36},{5,37},{6,38},{7,39},{8,40},{9,... | collective-permute-start | bytes 221192 | tf_op jit(solution)/shard_map/ppermute | solution.py:247
  26.2 7.1 %collective-permute-start = (bf16[48,768]{1,0:T(8,128)(2,1)S(1)}, bf16[48,768]{1,0:T(8,128)(2,1)S(1)}, u32[]{:S(2)}, u32[]{:S(2)}) collective-permute-start(bf16[48,768]{1,0:T(8,128)(2,1)S(1)} %get-tuple-element.22), channel_id=1, source_target_pairs={{0,16},{1,17},{2,18},{3,19},{4,20},{5,21},{6,22},{7,23},{8,24},{9,... | collective-permute-start | bytes 221192 | tf_op jit(solution)/shard_map/ppermute | solution.py:247
  33.5 24.7 %copy-start.1 = (bf16[1,3,48,3072]{3,2,1,0:T(8,128)(2,1)S(1)}, bf16[1,3,48,3072]{3,2,1,0:T(8,128)(2,1)}, u32[]{:S(2)}) copy-start(bf16[1,3,48,3072]{3,2,1,0:T(8,128)(2,1)} %param.10) | copy-start | bytes 2654212
  34.5 23.7 %all-to-all-start.1 = ((bf16[4,32,3072]{2,1,0:T(8,128)(2,1)}), bf16[4,32,3072]{2,1,0:T(8,128)(2,1)S(1)}, u32[]{:S(2)}, u32[]{:S(2)}) async-start(bf16[4,32,3072]{2,1,0:T(8,128)(2,1)} %broadcast_in_dim.35), calls=%async_computation.1 | async-start | bytes 1572864 | tf_op jit(solution)/shard_map/all_to_all | solution.py:174
  38.0 28.5 %copy-start.10 = (f32[1,2,128]{2,1,0:T(2,128)S(1)}, f32[1,2,128]{2,1,0:T(2,128)}, u32[]{:S(2)}) copy-start(f32[1,2,128]{2,1,0:T(2,128)} %param.15) | copy-start | bytes 3076
  38.0 20.2 %collective-permute-start.3 = (bf16[4,48,384]{2,1,0:T(8,128)(2,1)S(1)}, bf16[4,48,384]{2,1,0:T(8,128)(2,1)S(1)}, u32[]{:S(2)}, u32[]{:S(2)}) collective-permute-start(bf16[4,48,384]{2,1,0:T(8,128)(2,1)S(1)} %get-tuple-element.14), channel_id=1, source_target_pairs={{0,12},{1,13},{2,14},{3,15},{4,8},{5,9},{6,10},{7,11},{8,4},{9,5},... | collective-permute-start | bytes 442376 | tf_op jit(solution)/shard_map/ppermute | solution.py:258
  59.4 16.8 %all-to-all-start.2 = ((bf16[8,64,128]{2,1,0:T(8,128)(2,1)}), bf16[8,64,128]{2,1,0:T(8,128)(2,1)S(1)}, u32[]{:S(2)}, u32[]{:S(2)}) async-start(bf16[8,64,128]{2,1,0:T(8,128)(2,1)} %shard_map.92), calls=%async_computation.2 | async-start | bytes 262144 | tf_op jit(solution)/shard_map/all_to_all | solution.py:270
  66.5 16.6 %copy-start.8 = (f32[1,128]{1,0:T(1,128)}, f32[1,128]{1,0:T(1,128)S(1)}, u32[]{:S(2)}) copy-start(f32[1,128]{1,0:T(1,128)S(1)} %get-tuple-element.23.gain_k_ref) | copy-start | bytes 1540
  77.8 15.7 %all-to-all-start.3 = ((bf16[8,64,128]{2,1,0:T(8,128)(2,1)}), bf16[8,64,128]{2,1,0:T(8,128)(2,1)}, u32[]{:S(2)}, u32[]{:S(2)}) async-start(bf16[8,64,128]{2,1,0:T(8,128)(2,1)} %shard_map.93), calls=%async_computation.3 | async-start | bytes 262144 | tf_op jit(solution)/shard_map/all_to_all | solution.py:272
  84.9 8.6 %copy-start.3 = (bf16[1,48,3072]{2,1,0:T(8,128)(2,1)S(1)}, bf16[1,48,3072]{2,1,0:T(8,128)(2,1)}, u32[]{:S(2)}) copy-start(bf16[1,48,3072]{2,1,0:T(8,128)(2,1)} %param.12) | copy-start | bytes 884740
  84.9 8.6 %copy-start.5 = (f32[1,3,3072]{2,0,1:T(1,128)S(1)}, f32[1,3,3072]{2,0,1:T(1,128)}, u32[]{:S(2)}) copy-start(f32[1,3,3072]{2,0,1:T(1,128)} %param.14) | copy-start | bytes 110596
  94.8 33.9 %copy-start.7 = (bf16[1,2,3072]{2,1,0:T(2,128)(2,1)S(1)}, bf16[1,2,3072]{2,1,0:T(2,128)(2,1)}, u32[]{:S(2)}) copy-start(bf16[1,2,3072]{2,1,0:T(2,128)(2,1)} %param.9) | copy-start | bytes 36868
  128.8 8.1 %collective-permute-start.4 = (bf16[2,3072]{1,0:T(2,128)(2,1)S(1)}, bf16[2,3072]{1,0:T(2,128)(2,1)S(1)}, u32[]{:S(2)}, u32[]{:S(2)}) collective-permute-start(bf16[2,3072]{1,0:T(2,128)(2,1)S(1)} %add_convert_fusion.1), channel_id=1, source_target_pairs={{448,0},{0,64},{64,128},{128,192},{192,256},{256,320},{320,384},{3... | collective-permute-start | bytes 36872 | tf_op jit(solution)/shard_map/ppermute | solution.py:23
  152.1 12.0 %copy-start.2 = (bf16[1,3,48,3072]{3,2,1,0:T(8,128)(2,1)S(1)}, bf16[1,3,48,3072]{3,2,1,0:T(8,128)(2,1)}, u32[]{:S(2)}) copy-start(bf16[1,3,48,3072]{3,2,1,0:T(8,128)(2,1)} %param.10) | copy-start | bytes 2654212
  164.0 13.2 %copy-start.9 = (f32[1,128]{1,0:T(1,128)S(1)}, f32[1,128]{1,0:T(1,128)}, u32[]{:S(2)}) copy-start(f32[1,128]{1,0:T(1,128)} %copy-done.8) | copy-start | bytes 1540
  178.8 13.6 %all-to-all-start.9 = ((bf16[8,64,128]{2,1,0:T(8,128)(2,1)}), bf16[8,64,128]{2,1,0:T(8,128)(2,1)S(1)}, u32[]{:S(2)}, u32[]{:S(2)}) async-start(bf16[8,64,128]{2,1,0:T(8,128)(2,1)} %shard_map.97), calls=%async_computation.9 | async-start | bytes 262144 | tf_op jit(solution)/shard_map/all_to_all | solution.py:272
  224.6 14.4 %collective-permute-start.5 = (bf16[2,3072]{1,0:T(2,128)(2,1)S(1)}, bf16[2,3072]{1,0:T(2,128)(2,1)S(1)}, u32[]{:S(2)}, u32[]{:S(2)}) collective-permute-start(bf16[2,3072]{1,0:T(2,128)(2,1)S(1)} %add_convert_fusion), channel_id=1, source_target_pairs={{448,0},{0,64},{64,128},{128,192},{192,256},{256,320},{320,384},{3... | collective-permute-start | bytes 36872 | tf_op jit(solution)/shard_map/ppermute | solution.py:23

commit v10 on v9

--- a/solution.py
+++ b/solution.py
@@ -107,9 +107,8 @@
     )(normed, weights)
 
 
-def attend_kernel(
-    team_ref, keep_ref, got_ref, mask_ref, gain_q_ref, gain_k_ref, out_ref, packed_ref
-):
+def attend_kernel(team_ref, mask_ref, gain_q_ref, gain_k_ref, *refs):
+    *cached_refs, out_ref, packed_ref = refs
     shard = team_ref.shape[1] - 16
     members = team_ref.shape[0]
     lane = lax.broadcasted_iota(jnp.int32, (16, LANES), 1)
@@ -117,8 +116,8 @@
     fresh = [team_ref[c, shard:, :].astype(f32) for c in range(members)]
     features = jnp.concatenate([team_ref[c, :shard, :] for c in range(members)], axis=0)
     open_key = mask_ref[...] > 0.0
-    blocks = [r[i].astype(f32) for i in range(keep_ref.shape[0]) for r in (keep_ref, got_ref)]
-    half = keep_ref.shape[1] // 2
+    blocks = [r[i].astype(f32) for r in cached_refs for i in range(r.shape[0])]
+    half = blocks[0].shape[0] // 2
     cached_keys = jnp.concatenate([b[:half] for b in blocks], axis=0).astype(bf16)
     cached_values = jnp.concatenate([b[half:] for b in blocks], axis=0).astype(bf16)
     sums = jnp.zeros((16, LANES), f32)
@@ -156,16 +155,16 @@
         out_ref[c, shard:, :] = sums.astype(bf16)
 
 
-def attend(team, keep, got, mask, gains):
+def attend(team, cached, mask, gains):
     whole = pl.BlockSpec(memory_space=pltpu.VMEM)
     return pl.pallas_call(
         attend_kernel,
         out_shape=jax.ShapeDtypeStruct(team.shape, bf16),
-        in_specs=[whole] * 6,
+        in_specs=[whole] * (4 + len(cached)),
         out_specs=whole,
         scratch_shapes=[pltpu.VMEM((TEAM_HEADS * HEAD_DIM, LANES), bf16)],
         compiler_params=pltpu.CompilerParams(vmem_limit_bytes=8 * 1024 * 1024),
-    )(team, keep, got, mask, gains[0][:, None], gains[1][None, :])
+    )(team, mask, gains[0][:, None], gains[1][None, :], *cached)
 
 
 def gathered(block, groups):
@@ -223,10 +222,10 @@
     )
     upper = z_here >= TEAM
     slot = jnp.arange(teams * ctx_local, dtype=jnp.int32)
-    within = slot % (2 * ctx_local)
-    source = z_count * ((x_here - slot // (2 * ctx_local)) % x_count)
-    source = source + jnp.where(within < ctx_local, z_here, z_partner)
-    position = ctx_local * source + within % ctx_local
+    own_z = slot < x_count * ctx_local
+    source = z_count * ((x_here - slot // ctx_local % x_count) % x_count)
+    source = source + jnp.where(own_z, z_here, z_partner)
+    position = ctx_local * source + slot % ctx_local
     cached_mask = ((position >= TXT) | (position < text_len[0])).astype(f32)
     cached_mask = jnp.broadcast_to(cached_mask[:, None], (teams * ctx_local, LANES))
 
@@ -255,20 +254,21 @@
             normed = lax.all_to_all(block, "tp", 0, 0, axis_index_groups=along_z)
             normed = normed.reshape(-1, width)
             normed, give = lax.optimization_barrier((normed, give))
-            got = lax.ppermute(
-                give,
-                "tp",
-                [(z_count * x + z, z_count * x + partner[z]) for x in range(x_count) for z in range(z_count)],
-            )
+            route = [(z_count * x + z, z_count * x + partner[z]) for x in xs for z in range(z_count)]
+            got = [
+                lax.ppermute(part, "tp", route)
+                for part in (give[: x_count // 2], give[x_count // 2 :])
+            ]
             normed = gathered(normed, along_x)
-            normed, got = lax.optimization_barrier((normed, got))
+            normed, got[0] = lax.optimization_barrier((normed, got[0]))
+            cached = [keep] + got
         else:
             block = spread(current, shift_scale, len(hs))
             normed = lax.all_to_all(block, "tp", 0, 0, axis_index_groups=far)
             normed = gathered(normed.reshape(-1, width), blocks)
         team = project(normed, weight_qkv)
         team = lax.all_to_all(team, "tp", 0, 0, axis_index_groups=inside)
-        parts = attend(team, keep, got, cached_mask, gains)
+        parts = attend(team, cached, cached_mask, gains)
         parts = lax.all_to_all(parts, "tp", 0, 0, axis_index_groups=inside)
         hidden = jax.nn.gelu(
             lax.dot_general(

time: 241 us -> 238 us (0.988)
  waiting for transfers between devices: 45 us -> 33.9 us
  starting transfers between devices: 71.7 us -> 82 us
    all_to_all x1, waiting for transfers between devices: 9.55 us -> 0.01 us  [local(): team = lax.all_to_all(team, 'tp', 0, 0, axis_index_groups=inside)]
    ppermute x1 -> x2, starting transfers between devices: 7.2 us -> 16.6 us  [local(): lax.ppermute(part, 'tp', route)]
    ppermute x1 -> x2, waiting for transfers between devices: 13 us -> 11.6 us  [local(): lax.ppermute(part, 'tp', route)]
  transfers between devices with their start and end apart: 11 -> 12, of which waited for: 8 -> 8; matrix products, arithmetic and copies ran while one was open for 2% -> 2% of each run, Pallas kernels for 0% -> 0%
where the time goes in v10:
time: 238 us; the launch traced here: 237 us
  blocking collectives  104 us (44%)
  starting transfers between devices  82 us (34%)
  waiting for transfers between devices  33.9 us (14%)
  Pallas kernels  6.72 us (3%)
  local copies, waits for them, and re-layouts  4.77 us (2%)
  matrix products  4.3 us (2%)
    all_to_all x4, blocking collectives, summed_over(): parts = lax.all_to_all(parts, 'tp', 0, 0, axis_index_groups=groups)  64.2 us
    ppermute x2, starting transfers between devices, shifted(): lax.ppermute(block, axis, [((i - distance) % size, i) for i in range(size)])  22.8 us
    ppermute x2, starting transfers between devices, local(): lax.ppermute(part, 'tp', route)  16.6 us
    all_to_all x2, waiting for transfers between devices, local(): parts = lax.all_to_all(parts, 'tp', 0, 0, axis_index_groups=inside)  16.1 us
    all_to_all x1, starting transfers between devices, local(): normed = lax.all_to_all(block, 'tp', 0, 0, axis_index_groups=along_z)  15.7 us
    all_to_all x1, blocking collectives, local(): normed = lax.all_to_all(block, 'tp', 0, 0, axis_index_groups=far)  14.9 us
    all_to_all x1, blocking collectives, local(): team = lax.all_to_all(team, 'tp', 0, 0, axis_index_groups=inside)  12.7 us
    all_to_all x1, blocking collectives, gathered(): spread = lax.all_to_all(spread, 'tp', 0, 0, axis_index_groups=groups)  11.9 us
  transfers between devices with their start and end apart: 12, of which 8 were waited for; matrix products, arithmetic and copies ran while one was open for 2% of the time, Pallas kernels for 0%

profile of v10, /device:TPU:1, one launch (start us, length us, event | category | flops | bytes accessed | tf_op | source)
XLA Modules:
  0.0 236.8 jit_solution(6815483746150625496)
XLA Ops:
  0.0 0.9 copy-done.4
  0.9 0.7 copy-done.10
  1.6 0.9 shard_map.91
  2.5 15.7 %all-to-all-start = ((bf16[16,48,128]{2,1,0:T(8,128)(2,1)}), bf16[16,48,128]{2,1,0:T(8,128)(2,1)S(1)}, u32[]{:S(2)}, u32[]{:S(2)}) async-start(bf16[16,48,128]{2,1,0:T(8,128)(2,1)} %shard_map.91), calls=%async_computation | async-start | bytes 393216 | tf_op jit(solution)/shard_map/all_to_all | solution.py:254
  18.4 1.0 dynamic-slice_bitcast_fusion
  19.4 4.4 %collective-permute-start.2 = (bf16[48,768]{1,0:T(8,128)(2,1)S(1)}, bf16[48,768]{1,0:T(8,128)(2,1)S(1)}, u32[]{:S(2)}, u32[]{:S(2)}) collective-permute-start(bf16[48,768]{1,0:T(8,128)(2,1)S(1)} %get-tuple-element.20), channel_id=1, source_target_pairs={{0,48},{1,49},{2,50},{3,51},{4,52},{5,53},{6,54},{7,55},{8,56},{9,... | collective-permute-start | bytes 221192 | tf_op jit(solution)/shard_map/ppermute | solution.py:246
  23.8 2.4 %collective-permute-start.1 = (bf16[48,768]{1,0:T(8,128)(2,1)S(1)}, bf16[48,768]{1,0:T(8,128)(2,1)S(1)}, u32[]{:S(2)}, u32[]{:S(2)}) collective-permute-start(bf16[48,768]{1,0:T(8,128)(2,1)S(1)} %get-tuple-element.21), channel_id=1, source_target_pairs={{0,32},{1,33},{2,34},{3,35},{4,36},{5,37},{6,38},{7,39},{8,40},{9,... | collective-permute-start | bytes 221192 | tf_op jit(solution)/shard_map/ppermute | solution.py:246
  26.2 2.5 %collective-permute-start = (bf16[48,768]{1,0:T(8,128)(2,1)S(1)}, bf16[48,768]{1,0:T(8,128)(2,1)S(1)}, u32[]{:S(2)}, u32[]{:S(2)}) collective-permute-start(bf16[48,768]{1,0:T(8,128)(2,1)S(1)} %get-tuple-element.22), channel_id=1, source_target_pairs={{0,16},{1,17},{2,18},{3,19},{4,20},{5,21},{6,22},{7,23},{8,24},{9,... | collective-permute-start | bytes 221192 | tf_op jit(solution)/shard_map/ppermute | solution.py:246
  28.8 1.9 collective-permute-done.1
  30.7 2.6 %collective-permute-done = bf16[48,768]{1,0:T(8,128)(2,1)S(1)} collective-permute-done((bf16[48,768]{1,0:T(8,128)(2,1)S(1)}, bf16[48,768]{1,0:T(8,128)(2,1)S(1)}, u32[]{:S(2)}, u32[]{:S(2)}) %collective-permute-start) | collective-permute-done | bytes 73760 | tf_op jit(solution)/shard_map/ppermute | solution.py:246
  33.4 0.1 reshape.92
  33.5 1.0 broadcast_in_dim.35
  34.4 3.6 %all-to-all-start.1 = ((bf16[4,32,3072]{2,1,0:T(8,128)(2,1)}), bf16[4,32,3072]{2,1,0:T(8,128)(2,1)S(1)}, u32[]{:S(2)}, u32[]{:S(2)}) async-start(bf16[4,32,3072]{2,1,0:T(8,128)(2,1)} %broadcast_in_dim.35), calls=%async_computation.1 | async-start | bytes 1572864 | tf_op jit(solution)/shard_map/all_to_all | solution.py:173
  38.1 7.2 %collective-permute-start.3 = (bf16[2,48,384]{2,1,0:T(8,128)(2,1)S(1)}, bf16[2,48,384]{2,1,0:T(8,128)(2,1)S(1)}, u32[]{:S(2)}, u32[]{:S(2)}) collective-permute-start(bf16[2,48,384]{2,1,0:T(8,128)(2,1)S(1)} %get-tuple-element.24), channel_id=1, source_target_pairs={{0,12},{1,13},{2,14},{3,15},{4,8},{5,9},{6,10},{7,11},{8,4},{9,5},... | collective-permute-start | bytes 221192 | tf_op jit(solution)/shard_map/ppermute | solution.py:259
  45.3 6.5 %collective-permute-done.3.refs_1_ = bf16[2,48,384]{2,1,0:T(8,128)(2,1)S(1)} collective-permute-done((bf16[2,48,384]{2,1,0:T(8,128)(2,1)S(1)}, bf16[2,48,384]{2,1,0:T(8,128)(2,1)S(1)}, u32[]{:S(2)}, u32[]{:S(2)}) %collective-permute-start.3) | collective-permute-done | bytes 73760 | tf_op jit(solution)/shard_map/ppermute | solution.py:259
  51.8 1.2 shard_map.92
  53.0 5.4 %all-to-all-start.2 = ((bf16[8,64,128]{2,1,0:T(8,128)(2,1)}), bf16[8,64,128]{2,1,0:T(8,128)(2,1)S(1)}, u32[]{:S(2)}, u32[]{:S(2)}) async-start(bf16[8,64,128]{2,1,0:T(8,128)(2,1)} %shard_map.92), calls=%async_computation.2 | async-start | bytes 262144 | tf_op jit(solution)/shard_map/all_to_all | solution.py:270
  59.1 0.1 copy.12.gain_q_ref
  59.2 9.4 %collective-permute-start.4 = (bf16[2,48,384]{2,1,0:T(8,128)(2,1)S(1)}, bf16[2,48,384]{2,1,0:T(8,128)(2,1)S(1)}, u32[]{:S(2)}, u32[]{:S(2)}) collective-permute-start(bf16[2,48,384]{2,1,0:T(8,128)(2,1)S(1)} %get-tuple-element.23), channel_id=1, source_target_pairs={{0,12},{1,13},{2,14},{3,15},{4,8},{5,9},{6,10},{7,11},{8,4},{9,5},... | collective-permute-start | bytes 221192 | tf_op jit(solution)/shard_map/ppermute | solution.py:259
  68.7 5.1 %collective-permute-done.4.refs_2_ = bf16[2,48,384]{2,1,0:T(8,128)(2,1)S(1)} collective-permute-done((bf16[2,48,384]{2,1,0:T(8,128)(2,1)S(1)}, bf16[2,48,384]{2,1,0:T(8,128)(2,1)S(1)}, u32[]{:S(2)}, u32[]{:S(2)}) %collective-permute-start.4) | collective-permute-done | bytes 73760 | tf_op jit(solution)/shard_map/ppermute | solution.py:259
  73.9 1.5 shard_map.93
  75.3 5.1 %all-to-all-start.3 = ((bf16[8,64,128]{2,1,0:T(8,128)(2,1)}), bf16[8,64,128]{2,1,0:T(8,128)(2,1)S(1)}, u32[]{:S(2)}, u32[]{:S(2)}) async-start(bf16[8,64,128]{2,1,0:T(8,128)(2,1)} %shard_map.93), calls=%async_computation.3 | async-start | bytes 262144 | tf_op jit(solution)/shard_map/all_to_all | solution.py:272
  80.5 1.8 fusion.17
  82.3 0.4 fusion.2.forward_ref
  82.7 8.1 %all-to-all-done.3.parts_ref = bf16[8,64,128]{2,1,0:T(8,128)(2,1)S(1)} async-done(((bf16[8,64,128]{2,1,0:T(8,128)(2,1)}), bf16[8,64,128]{2,1,0:T(8,128)(2,1)S(1)}, u32[]{:S(2)}, u32[]{:S(2)}) %all-to-all-start.3) | async-done | bytes 131104 | tf_op jit(solution)/shard_map/all_to_all | solution.py:272
  90.8 0.4 shard_map.94
  91.2 13.0 %all_to_all.60 = bf16[8,16,3072]{2,1,0:T(8,128)(2,1)S(1)} all-to-all(bf16[8,16,3072]{2,1,0:T(8,128)(2,1)S(1)} %bitcast.53), channel_id=1, replica_groups={{0,1,16,17,32,33,48,49},{2,3,18,19,34,35,50,51},{4,5,20,21,36,37,52,53}..., dimensions={0} | all-to-all | bytes 1572864 | tf_op jit(solution)/shard_map/all_to_all | solution.py:180
  104.2 0.1 reduce_sum.42
  104.4 19.5 %all_to_all.61 = bf16[8,48,128]{2,1,0:T(8,128)(2,1)S(1)} all-to-all(bf16[8,48,128]{2,1,0:T(8,128)(2,1)S(1)} %convert_element_type.46), channel_id=1, replica_groups={{0,2,4,6,8,10,12,14},{1,3,5,7,9,11,13,15},{16,18,20,22,24,26,28,30},{17..., dimensions={0} | all-to-all | bytes 196608 | tf_op jit(solution)/shard_map/all_to_all | solution.py:180
  124.0 9.2 %collective-permute-start.5 = (bf16[2,3072]{1,0:T(2,128)(2,1)S(1)}, bf16[2,3072]{1,0:T(2,128)(2,1)S(1)}, u32[]{:S(2)}, u32[]{:S(2)}) collective-permute-start(bf16[2,3072]{1,0:T(2,128)(2,1)S(1)} %add_convert_fusion.1), channel_id=1, source_target_pairs={{448,0},{0,64},{64,128},{128,192},{192,256},{256,320},{320,384},{3... | collective-permute-start | bytes 36872 | tf_op jit(solution)/shard_map/ppermute | solution.py:23
  133.2 0.8 collective-permute-done.5.rows_ref
  134.1 0.2 shard_map.95
  134.3 14.9 %all_to_all.62 = bf16[8,48,128]{2,1,0:T(8,128)(2,1)S(1)} all-to-all(bf16[8,48,128]{2,1,0:T(8,128)(2,1)S(1)} %shard_map.95), channel_id=1, replica_groups={{0,2,4,6,8,10,12,14},{1,3,5,7,9,11,13,15},{16,18,20,22,24,26,28,30},{17..., dimensions={0} | all-to-all | bytes 196608 | tf_op jit(solution)/shard_map/all_to_all | solution.py:267
  149.4 11.9 %all_to_all.63 = bf16[8,16,3072]{2,1,0:T(8,128)(2,1)S(1)} all-to-all(bf16[8,16,3072]{2,1,0:T(8,128)(2,1)S(1)} %broadcast_in_dim.40), channel_id=1, replica_groups={{0,1,16,17,32,33,48,49},{2,3,18,19,34,35,50,51},{4,5,20,21,36,37,52,53}..., dimensions={0} | all-to-all | bytes 1572864 | tf_op jit(solution)/shard_map/all_to_all | solution.py:173
  161.2 0.6 shard_map.96
  161.8 12.7 %all_to_all.64.team_ref = bf16[8,64,128]{2,1,0:T(8,128)(2,1)S(1)} all-to-all(bf16[8,64,128]{2,1,0:T(8,128)(2,1)S(1)} %shard_map.96), channel_id=1, replica_groups={{0,1,2,3,4,5,6,7},{8,9,10,11,12,13,14,15},{16,17,18,19,20,21,22,23},{24..., dimensions={0} | all-to-all | bytes 262144 | tf_op jit(solution)/shard_map/all_to_all | solution.py:270
  174.5 1.5 shard_map.97
  176.0 3.4 %all-to-all-start.9 = ((bf16[8,64,128]{2,1,0:T(8,128)(2,1)}), bf16[8,64,128]{2,1,0:T(8,128)(2,1)S(1)}, u32[]{:S(2)}, u32[]{:S(2)}) async-start(bf16[8,64,128]{2,1,0:T(8,128)(2,1)} %shard_map.97), calls=%async_computation.9 | async-start | bytes 262144 | tf_op jit(solution)/shard_map/all_to_all | solution.py:272
  179.3 1.8 fusion.29
  181.1 0.4 fusion.forward_ref
  181.5 8.1 %all-to-all-done.9.parts_ref = bf16[8,64,128]{2,1,0:T(8,128)(2,1)S(1)} async-done(((bf16[8,64,128]{2,1,0:T(8,128)(2,1)}), bf16[8,64,128]{2,1,0:T(8,128)(2,1)S(1)}, u32[]{:S(2)}, u32[]{:S(2)}) %all-to-all-start.9) | async-done | bytes 131104 | tf_op jit(solution)/shard_map/all_to_all | solution.py:272
  189.6 0.4 shard_map.98
  190.0 11.4 %all_to_all.65 = bf16[8,16,3072]{2,1,0:T(8,128)(2,1)S(1)} all-to-all(bf16[8,16,3072]{2,1,0:T(8,128)(2,1)S(1)} %bitcast.52), channel_id=1, replica_groups={{0,1,16,17,32,33,48,49},{2,3,18,19,34,35,50,51},{4,5,20,21,36,37,52,53}..., dimensions={0} | all-to-all | bytes 1572864 | tf_op jit(solution)/shard_map/all_to_all | solution.py:180
  201.3 0.1 reduce_sum.44
  201.5 20.3 %all_to_all.66 = bf16[8,48,128]{2,1,0:T(8,128)(2,1)S(1)} all-to-all(bf16[8,48,128]{2,1,0:T(8,128)(2,1)S(1)} %convert_element_type.51), channel_id=1, replica_groups={{0,2,4,6,8,10,12,14},{1,3,5,7,9,11,13,15},{16,18,20,22,24,26,28,30},{17..., dimensions={0} | all-to-all | bytes 196608 | tf_op jit(solution)/shard_map/all_to_all | solution.py:180
  221.8 13.5 %collective-permute-start.6 = (bf16[2,3072]{1,0:T(2,128)(2,1)S(1)}, bf16[2,3072]{1,0:T(2,128)(2,1)S(1)}, u32[]{:S(2)}, u32[]{:S(2)}) collective-permute-start(bf16[2,3072]{1,0:T(2,128)(2,1)S(1)} %add_convert_fusion), channel_id=1, source_target_pairs={{448,0},{0,64},{64,128},{128,192},{192,256},{256,320},{320,384},{3... | collective-permute-start | bytes 36872 | tf_op jit(solution)/shard_map/ppermute | solution.py:23
  235.4 0.8 collective-permute-done.6
  236.2 0.6 copy.16
  (44 shorter events, 0.6 us)
Async XLA Ops:
  0.0 82.3 %copy-start = (bf16[1,192,3072]{2,1,0:T(8,128)(2,1)S(1)}, bf16[1,192,3072]{2,1,0:T(8,128)(2,1)}, u32[]{:S(2)}) copy-start(bf16[1,192,3072]{2,1,0:T(8,128)(2,1)} %param.13) | copy-start | bytes 3538948
  0.0 0.9 copy-start.4
  0.9 0.7 copy-start.10
  2.5 30.9 %all-to-all-start = ((bf16[16,48,128]{2,1,0:T(8,128)(2,1)}), bf16[16,48,128]{2,1,0:T(8,128)(2,1)S(1)}, u32[]{:S(2)}, u32[]{:S(2)}) async-start(bf16[16,48,128]{2,1,0:T(8,128)(2,1)} %shard_map.91), calls=%async_computation | async-start | bytes 393216 | tf_op jit(solution)/shard_map/all_to_all | solution.py:254
  19.4 9.4 %collective-permute-start.2 = (bf16[48,768]{1,0:T(8,128)(2,1)S(1)}, bf16[48,768]{1,0:T(8,128)(2,1)S(1)}, u32[]{:S(2)}, u32[]{:S(2)}) collective-permute-start(bf16[48,768]{1,0:T(8,128)(2,1)S(1)} %get-tuple-element.20), channel_id=1, source_target_pairs={{0,48},{1,49},{2,50},{3,51},{4,52},{5,53},{6,54},{7,55},{8,56},{9,... | collective-permute-start | bytes 221192 | tf_op jit(solution)/shard_map/ppermute | solution.py:246
  23.8 6.9 %collective-permute-start.1 = (bf16[48,768]{1,0:T(8,128)(2,1)S(1)}, bf16[48,768]{1,0:T(8,128)(2,1)S(1)}, u32[]{:S(2)}, u32[]{:S(2)}) collective-permute-start(bf16[48,768]{1,0:T(8,128)(2,1)S(1)} %get-tuple-element.21), channel_id=1, source_target_pairs={{0,32},{1,33},{2,34},{3,35},{4,36},{5,37},{6,38},{7,39},{8,40},{9,... | collective-permute-start | bytes 221192 | tf_op jit(solution)/shard_map/ppermute | solution.py:246
  26.2 7.1 %collective-permute-start = (bf16[48,768]{1,0:T(8,128)(2,1)S(1)}, bf16[48,768]{1,0:T(8,128)(2,1)S(1)}, u32[]{:S(2)}, u32[]{:S(2)}) collective-permute-start(bf16[48,768]{1,0:T(8,128)(2,1)S(1)} %get-tuple-element.22), channel_id=1, source_target_pairs={{0,16},{1,17},{2,18},{3,19},{4,20},{5,21},{6,22},{7,23},{8,24},{9,... | collective-permute-start | bytes 221192 | tf_op jit(solution)/shard_map/ppermute | solution.py:246
  34.4 17.4 %copy-start.1 = (bf16[1,3,48,3072]{3,2,1,0:T(8,128)(2,1)S(1)}, bf16[1,3,48,3072]{3,2,1,0:T(8,128)(2,1)}, u32[]{:S(2)}) copy-start(bf16[1,3,48,3072]{3,2,1,0:T(8,128)(2,1)} %param.10) | copy-start | bytes 2654212
  34.4 17.4 %all-to-all-start.1 = ((bf16[4,32,3072]{2,1,0:T(8,128)(2,1)}), bf16[4,32,3072]{2,1,0:T(8,128)(2,1)S(1)}, u32[]{:S(2)}, u32[]{:S(2)}) async-start(bf16[4,32,3072]{2,1,0:T(8,128)(2,1)} %broadcast_in_dim.35), calls=%async_computation.1 | async-start | bytes 1572864 | tf_op jit(solution)/shard_map/all_to_all | solution.py:173
  38.1 21.0 %copy-start.12 = (f32[1,2,128]{2,1,0:T(2,128)S(1)}, f32[1,2,128]{2,1,0:T(2,128)}, u32[]{:S(2)}) copy-start(f32[1,2,128]{2,1,0:T(2,128)} %param.15) | copy-start | bytes 3076
  38.1 13.7 %collective-permute-start.3 = (bf16[2,48,384]{2,1,0:T(8,128)(2,1)S(1)}, bf16[2,48,384]{2,1,0:T(8,128)(2,1)S(1)}, u32[]{:S(2)}, u32[]{:S(2)}) collective-permute-start(bf16[2,48,384]{2,1,0:T(8,128)(2,1)S(1)} %get-tuple-element.24), channel_id=1, source_target_pairs={{0,12},{1,13},{2,14},{3,15},{4,8},{5,9},{6,10},{7,11},{8,4},{9,5},... | collective-permute-start | bytes 221192 | tf_op jit(solution)/shard_map/ppermute | solution.py:259
  51.8 23.5 %copy-start.6 = (bf16[2,48,384]{2,1,0:T(8,128)(2,1)}, bf16[2,48,384]{2,1,0:T(8,128)(2,1)S(1)}, u32[]{:S(2)}) copy-start(bf16[2,48,384]{2,1,0:T(8,128)(2,1)S(1)} %collective-permute-done.3.refs_1_) | copy-start | bytes 221188
  53.0 20.7 %all-to-all-start.2 = ((bf16[8,64,128]{2,1,0:T(8,128)(2,1)}), bf16[8,64,128]{2,1,0:T(8,128)(2,1)S(1)}, u32[]{:S(2)}, u32[]{:S(2)}) async-start(bf16[8,64,128]{2,1,0:T(8,128)(2,1)} %shard_map.92), calls=%async_computation.2 | async-start | bytes 262144 | tf_op jit(solution)/shard_map/all_to_all | solution.py:270
  59.2 14.5 %collective-permute-start.4 = (bf16[2,48,384]{2,1,0:T(8,128)(2,1)S(1)}, bf16[2,48,384]{2,1,0:T(8,128)(2,1)S(1)}, u32[]{:S(2)}, u32[]{:S(2)}) collective-permute-start(bf16[2,48,384]{2,1,0:T(8,128)(2,1)S(1)} %get-tuple-element.23), channel_id=1, source_target_pairs={{0,12},{1,13},{2,14},{3,15},{4,8},{5,9},{6,10},{7,11},{8,4},{9,5},... | collective-permute-start | bytes 221192 | tf_op jit(solution)/shard_map/ppermute | solution.py:259
  73.8 6.7 %copy-start.8 = (bf16[2,48,384]{2,1,0:T(8,128)(2,1)}, bf16[2,48,384]{2,1,0:T(8,128)(2,1)S(1)}, u32[]{:S(2)}) copy-start(bf16[2,48,384]{2,1,0:T(8,128)(2,1)S(1)} %collective-permute-done.4.refs_2_) | copy-start | bytes 221188
  75.3 15.4 %all-to-all-start.3 = ((bf16[8,64,128]{2,1,0:T(8,128)(2,1)}), bf16[8,64,128]{2,1,0:T(8,128)(2,1)S(1)}, u32[]{:S(2)}, u32[]{:S(2)}) async-start(bf16[8,64,128]{2,1,0:T(8,128)(2,1)} %shard_map.93), calls=%async_computation.3 | async-start | bytes 262144 | tf_op jit(solution)/shard_map/all_to_all | solution.py:272
  82.3 8.5 %copy-start.3 = (bf16[1,48,3072]{2,1,0:T(8,128)(2,1)S(1)}, bf16[1,48,3072]{2,1,0:T(8,128)(2,1)}, u32[]{:S(2)}) copy-start(bf16[1,48,3072]{2,1,0:T(8,128)(2,1)} %param.12) | copy-start | bytes 884740
  82.3 8.5 %copy-start.5 = (f32[1,3,3072]{2,0,1:T(1,128)S(1)}, f32[1,3,3072]{2,0,1:T(1,128)}, u32[]{:S(2)}) copy-start(f32[1,3,3072]{2,0,1:T(1,128)} %param.14) | copy-start | bytes 110596
  91.2 32.8 %copy-start.11 = (bf16[1,2,3072]{2,1,0:T(2,128)(2,1)S(1)}, bf16[1,2,3072]{2,1,0:T(2,128)(2,1)}, u32[]{:S(2)}) copy-start(bf16[1,2,3072]{2,1,0:T(2,128)(2,1)} %param.9) | copy-start | bytes 36868
  124.0 10.1 %collective-permute-start.5 = (bf16[2,3072]{1,0:T(2,128)(2,1)S(1)}, bf16[2,3072]{1,0:T(2,128)(2,1)S(1)}, u32[]{:S(2)}, u32[]{:S(2)}) collective-permute-start(bf16[2,3072]{1,0:T(2,128)(2,1)S(1)} %add_convert_fusion.1), channel_id=1, source_target_pairs={{448,0},{0,64},{64,128},{128,192},{192,256},{256,320},{320,384},{3... | collective-permute-start | bytes 36872 | tf_op jit(solution)/shard_map/ppermute | solution.py:23
  149.3 12.0 %copy-start.2 = (bf16[1,3,48,3072]{3,2,1,0:T(8,128)(2,1)S(1)}, bf16[1,3,48,3072]{3,2,1,0:T(8,128)(2,1)}, u32[]{:S(2)}) copy-start(bf16[1,3,48,3072]{3,2,1,0:T(8,128)(2,1)} %param.10) | copy-start | bytes 2654212
  161.2 13.2 %copy-start.7 = (bf16[2,48,384]{2,1,0:T(8,128)(2,1)S(1)}, bf16[2,48,384]{2,1,0:T(8,128)(2,1)}, u32[]{:S(2)}) copy-start(bf16[2,48,384]{2,1,0:T(8,128)(2,1)} %copy-done.6) | copy-start | bytes 221188
  161.2 13.2 %copy-start.9 = (bf16[2,48,384]{2,1,0:T(8,128)(2,1)S(1)}, bf16[2,48,384]{2,1,0:T(8,128)(2,1)}, u32[]{:S(2)}) copy-start(bf16[2,48,384]{2,1,0:T(8,128)(2,1)} %copy-done.8) | copy-start | bytes 221188
  176.0 13.6 %all-to-all-start.9 = ((bf16[8,64,128]{2,1,0:T(8,128)(2,1)}), bf16[8,64,128]{2,1,0:T(8,128)(2,1)S(1)}, u32[]{:S(2)}, u32[]{:S(2)}) async-start(bf16[8,64,128]{2,1,0:T(8,128)(2,1)} %shard_map.97), calls=%async_computation.9 | async-start | bytes 262144 | tf_op jit(solution)/shard_map/all_to_all | solution.py:272
  221.8 14.4 %collective-permute-start.6 = (bf16[2,3072]{1,0:T(2,128)(2,1)S(1)}, bf16[2,3072]{1,0:T(2,128)(2,1)S(1)}, u32[]{:S(2)}, u32[]{:S(2)}) collective-permute-start(bf16[2,3072]{1,0:T(2,128)(2,1)S(1)} %add_convert_fusion), channel_id=1, source_target_pairs={{448,0},{0,64},{64,128},{128,192},{192,256},{256,320},{320,384},{3... | collective-permute-start | bytes 36872 | tf_op jit(solution)/shard_map/ppermute | solution.py:23

commit v11 on v10

--- a/solution.py
+++ b/solution.py
@@ -253,7 +253,6 @@
         if tick_number == 0:
             normed = lax.all_to_all(block, "tp", 0, 0, axis_index_groups=along_z)
             normed = normed.reshape(-1, width)
-            normed, give = lax.optimization_barrier((normed, give))
             route = [(z_count * x + z, z_count * x + partner[z]) for x in xs for z in range(z_count)]
             got = [
                 lax.ppermute(part, "tp", route)

time: 238 us -> 235 us (0.987)
  waiting for transfers between devices: 33.9 us -> 24.5 us
  starting transfers between devices: 82 us -> 90 us
    ppermute x2, waiting for transfers between devices: 11.6 us -> 3.76 us  [local(): lax.ppermute(part, 'tp', route)]
    all_to_all x2, starting transfers between devices: 8.51 us -> 13 us  [local(): parts = lax.all_to_all(parts, 'tp', 0, 0, axis_index_groups=inside)]
    ppermute x3, waiting for transfers between devices: 4.51 us -> 0.01 us  [local(): part = lax.ppermute(part, 'tp', route)]
    all_to_all x1, waiting for transfers between devices: 0.01 us -> 2.92 us  [local(): normed = lax.all_to_all(block, 'tp', 0, 0, axis_index_groups=along_z)]
    all_to_all x1, starting transfers between devices: 5.43 us -> 8.02 us  [local(): team = lax.all_to_all(team, 'tp', 0, 0, axis_index_groups=inside)]
  transfers between devices with their start and end apart: 12 -> 12, of which waited for: 8 -> 7; matrix products, arithmetic and copies ran while one was open for 2% -> 3% of each run, Pallas kernels for 0% -> 0%
where the time goes in v11:
time: 235 us; the launch traced here: 234 us
  blocking collectives  103 us (44%)
  starting transfers between devices  90 us (38%)
  waiting for transfers between devices  24.5 us (10%)
  Pallas kernels  6.7 us (3%)
  local copies, waits for them, and re-layouts  4.77 us (2%)
  matrix products  4.3 us (2%)
    all_to_all x4, blocking collectives, summed_over(): parts = lax.all_to_all(parts, 'tp', 0, 0, axis_index_groups=groups)  63.1 us
    ppermute x2, starting transfers between devices, shifted(): lax.ppermute(block, axis, [((i - distance) % size, i) for i in range(size)])  24.3 us
    all_to_all x2, waiting for transfers between devices, local(): parts = lax.all_to_all(parts, 'tp', 0, 0, axis_index_groups=inside)  16.1 us
    all_to_all x1, starting transfers between devices, local(): normed = lax.all_to_all(block, 'tp', 0, 0, axis_index_groups=along_z)  15.7 us
    ppermute x2, starting transfers between devices, local(): lax.ppermute(part, 'tp', route)  15.5 us
    all_to_all x1, blocking collectives, local(): normed = lax.all_to_all(block, 'tp', 0, 0, axis_index_groups=far)  14.9 us
    all_to_all x2, starting transfers between devices, local(): parts = lax.all_to_all(parts, 'tp', 0, 0, axis_index_groups=inside)  13 us
    all_to_all x1, blocking collectives, local(): team = lax.all_to_all(team, 'tp', 0, 0, axis_index_groups=inside)  12.7 us
  transfers between devices with their start and end apart: 12, of which 7 were waited for; matrix products, arithmetic and copies ran while one was open for 3% of the time, Pallas kernels for 0%

profile of v11, /device:TPU:1, one launch (start us, length us, event | category | flops | bytes accessed | tf_op | source)
XLA Modules:
  0.0 234.3 jit_solution(2971212401661702679)
XLA Ops:
  0.0 0.9 copy-done.4
  0.9 0.7 copy-done.10
  1.6 0.9 shard_map.91
  2.5 15.7 %all-to-all-start = ((bf16[16,48,128]{2,1,0:T(8,128)(2,1)}), bf16[16,48,128]{2,1,0:T(8,128)(2,1)S(1)}, u32[]{:S(2)}, u32[]{:S(2)}) async-start(bf16[16,48,128]{2,1,0:T(8,128)(2,1)} %shard_map.91), calls=%async_computation | async-start | bytes 393216 | tf_op jit(solution)/shard_map/all_to_all | solution.py:254
  18.4 1.0 dynamic-slice_bitcast_fusion
  19.4 4.4 %collective-permute-start.2 = (bf16[48,768]{1,0:T(8,128)(2,1)S(1)}, bf16[48,768]{1,0:T(8,128)(2,1)S(1)}, u32[]{:S(2)}, u32[]{:S(2)}) collective-permute-start(bf16[48,768]{1,0:T(8,128)(2,1)S(1)} %get-tuple-element.16), channel_id=1, source_target_pairs={{0,48},{1,49},{2,50},{3,51},{4,52},{5,53},{6,54},{7,55},{8,56},{9,... | collective-permute-start | bytes 221192 | tf_op jit(solution)/shard_map/ppermute | solution.py:246
  23.8 2.4 %collective-permute-start.1 = (bf16[48,768]{1,0:T(8,128)(2,1)S(1)}, bf16[48,768]{1,0:T(8,128)(2,1)S(1)}, u32[]{:S(2)}, u32[]{:S(2)}) collective-permute-start(bf16[48,768]{1,0:T(8,128)(2,1)S(1)} %get-tuple-element.17), channel_id=1, source_target_pairs={{0,32},{1,33},{2,34},{3,35},{4,36},{5,37},{6,38},{7,39},{8,40},{9,... | collective-permute-start | bytes 221192 | tf_op jit(solution)/shard_map/ppermute | solution.py:246
  26.2 2.5 %collective-permute-start = (bf16[48,768]{1,0:T(8,128)(2,1)S(1)}, bf16[48,768]{1,0:T(8,128)(2,1)S(1)}, u32[]{:S(2)}, u32[]{:S(2)}) collective-permute-start(bf16[48,768]{1,0:T(8,128)(2,1)S(1)} %get-tuple-element.18), channel_id=1, source_target_pairs={{0,16},{1,17},{2,18},{3,19},{4,20},{5,21},{6,22},{7,23},{8,24},{9,... | collective-permute-start | bytes 221192 | tf_op jit(solution)/shard_map/ppermute | solution.py:246
  28.8 2.9 %all-to-all-done = bf16[16,48,128]{2,1,0:T(8,128)(2,1)S(1)} async-done(((bf16[16,48,128]{2,1,0:T(8,128)(2,1)}), bf16[16,48,128]{2,1,0:T(8,128)(2,1)S(1)}, u32[]{:S(2)}, u32[]{:S(2)}) %all-to-all-start) | async-done | bytes 196640 | tf_op jit(solution)/shard_map/all_to_all | solution.py:254
  31.7 0.1 broadcast_in_dim.36
  31.8 1.0 broadcast_in_dim.37
  32.7 4.1 %all-to-all-start.1 = ((bf16[4,32,3072]{2,1,0:T(8,128)(2,1)}), bf16[4,32,3072]{2,1,0:T(8,128)(2,1)S(1)}, u32[]{:S(2)}, u32[]{:S(2)}) async-start(bf16[4,32,3072]{2,1,0:T(8,128)(2,1)} %broadcast_in_dim.37), calls=%async_computation.1 | async-start | bytes 1572864 | tf_op jit(solution)/shard_map/all_to_all | solution.py:173
  37.0 7.9 %collective-permute-start.3 = (bf16[2,48,384]{2,1,0:T(8,128)(2,1)S(1)}, bf16[2,48,384]{2,1,0:T(8,128)(2,1)S(1)}, u32[]{:S(2)}, u32[]{:S(2)}) collective-permute-start(bf16[2,48,384]{2,1,0:T(8,128)(2,1)S(1)} %get-tuple-element.20), channel_id=1, source_target_pairs={{0,12},{1,13},{2,14},{3,15},{4,8},{5,9},{6,10},{7,11},{8,4},{9,5},... | collective-permute-start | bytes 221192 | tf_op jit(solution)/shard_map/ppermute | solution.py:258
  44.9 1.7 collective-permute-done.3.refs_1_
  46.7 1.2 shard_map.92
  47.9 8.0 %all-to-all-start.2 = ((bf16[8,64,128]{2,1,0:T(8,128)(2,1)}), bf16[8,64,128]{2,1,0:T(8,128)(2,1)S(1)}, u32[]{:S(2)}, u32[]{:S(2)}) async-start(bf16[8,64,128]{2,1,0:T(8,128)(2,1)} %shard_map.92), calls=%async_computation.2 | async-start | bytes 262144 | tf_op jit(solution)/shard_map/all_to_all | solution.py:269
  56.6 0.1 copy.12.gain_q_ref
  56.7 7.6 %collective-permute-start.4 = (bf16[2,48,384]{2,1,0:T(8,128)(2,1)S(1)}, bf16[2,48,384]{2,1,0:T(8,128)(2,1)S(1)}, u32[]{:S(2)}, u32[]{:S(2)}) collective-permute-start(bf16[2,48,384]{2,1,0:T(8,128)(2,1)S(1)} %get-tuple-element.19), channel_id=1, source_target_pairs={{0,12},{1,13},{2,14},{3,15},{4,8},{5,9},{6,10},{7,11},{8,4},{9,5},... | collective-permute-start | bytes 221192 | tf_op jit(solution)/shard_map/ppermute | solution.py:258
  64.3 2.0 collective-permute-done.4.refs_2_
  66.3 0.1 broadcast_in_dim.40.mask_ref
  66.4 1.5 shard_map.93
  67.9 9.7 %all-to-all-start.3 = ((bf16[8,64,128]{2,1,0:T(8,128)(2,1)}), bf16[8,64,128]{2,1,0:T(8,128)(2,1)S(1)}, u32[]{:S(2)}, u32[]{:S(2)}) async-start(bf16[8,64,128]{2,1,0:T(8,128)(2,1)} %shard_map.93), calls=%async_computation.3 | async-start | bytes 262144 | tf_op jit(solution)/shard_map/all_to_all | solution.py:271
  77.6 1.8 fusion.17
  79.4 0.4 fusion.2.forward_ref
  79.8 8.1 %all-to-all-done.3.parts_ref = bf16[8,64,128]{2,1,0:T(8,128)(2,1)S(1)} async-done(((bf16[8,64,128]{2,1,0:T(8,128)(2,1)}), bf16[8,64,128]{2,1,0:T(8,128)(2,1)S(1)}, u32[]{:S(2)}, u32[]{:S(2)}) %all-to-all-start.3) | async-done | bytes 131104 | tf_op jit(solution)/shard_map/all_to_all | solution.py:271
  87.9 0.4 shard_map.94
  88.3 11.4 %all_to_all.60 = bf16[8,16,3072]{2,1,0:T(8,128)(2,1)S(1)} all-to-all(bf16[8,16,3072]{2,1,0:T(8,128)(2,1)S(1)} %bitcast.53), channel_id=1, replica_groups={{0,1,16,17,32,33,48,49},{2,3,18,19,34,35,50,51},{4,5,20,21,36,37,52,53}..., dimensions={0} | all-to-all | bytes 1572864 | tf_op jit(solution)/shard_map/all_to_all | solution.py:180
  99.6 0.1 reduce_sum.42
  99.8 20.1 %all_to_all.61 = bf16[8,48,128]{2,1,0:T(8,128)(2,1)S(1)} all-to-all(bf16[8,48,128]{2,1,0:T(8,128)(2,1)S(1)} %convert_element_type.46), channel_id=1, replica_groups={{0,2,4,6,8,10,12,14},{1,3,5,7,9,11,13,15},{16,18,20,22,24,26,28,30},{17..., dimensions={0} | all-to-all | bytes 196608 | tf_op jit(solution)/shard_map/all_to_all | solution.py:180
  120.0 10.8 %collective-permute-start.5 = (bf16[2,3072]{1,0:T(2,128)(2,1)S(1)}, bf16[2,3072]{1,0:T(2,128)(2,1)S(1)}, u32[]{:S(2)}, u32[]{:S(2)}) collective-permute-start(bf16[2,3072]{1,0:T(2,128)(2,1)S(1)} %add_convert_fusion.1), channel_id=1, source_target_pairs={{448,0},{0,64},{64,128},{128,192},{192,256},{256,320},{320,384},{3... | collective-permute-start | bytes 36872 | tf_op jit(solution)/shard_map/ppermute | solution.py:23
  130.8 0.8 collective-permute-done.5.rows_ref
  131.7 0.2 shard_map.95
  131.9 14.9 %all_to_all.62 = bf16[8,48,128]{2,1,0:T(8,128)(2,1)S(1)} all-to-all(bf16[8,48,128]{2,1,0:T(8,128)(2,1)S(1)} %shard_map.95), channel_id=1, replica_groups={{0,2,4,6,8,10,12,14},{1,3,5,7,9,11,13,15},{16,18,20,22,24,26,28,30},{17..., dimensions={0} | all-to-all | bytes 196608 | tf_op jit(solution)/shard_map/all_to_all | solution.py:266
  147.0 11.9 %all_to_all.63 = bf16[8,16,3072]{2,1,0:T(8,128)(2,1)S(1)} all-to-all(bf16[8,16,3072]{2,1,0:T(8,128)(2,1)S(1)} %broadcast_in_dim.42), channel_id=1, replica_groups={{0,1,16,17,32,33,48,49},{2,3,18,19,34,35,50,51},{4,5,20,21,36,37,52,53}..., dimensions={0} | all-to-all | bytes 1572864 | tf_op jit(solution)/shard_map/all_to_all | solution.py:173
  158.9 0.6 shard_map.96
  159.4 12.7 %all_to_all.64.team_ref = bf16[8,64,128]{2,1,0:T(8,128)(2,1)S(1)} all-to-all(bf16[8,64,128]{2,1,0:T(8,128)(2,1)S(1)} %shard_map.96), channel_id=1, replica_groups={{0,1,2,3,4,5,6,7},{8,9,10,11,12,13,14,15},{16,17,18,19,20,21,22,23},{24..., dimensions={0} | all-to-all | bytes 262144 | tf_op jit(solution)/shard_map/all_to_all | solution.py:269
  172.1 1.5 shard_map.97
  173.6 3.4 %all-to-all-start.9 = ((bf16[8,64,128]{2,1,0:T(8,128)(2,1)}), bf16[8,64,128]{2,1,0:T(8,128)(2,1)S(1)}, u32[]{:S(2)}, u32[]{:S(2)}) async-start(bf16[8,64,128]{2,1,0:T(8,128)(2,1)} %shard_map.97), calls=%async_computation.9 | async-start | bytes 262144 | tf_op jit(solution)/shard_map/all_to_all | solution.py:271
  177.0 1.8 fusion.29
  178.7 0.4 fusion.forward_ref
  179.1 8.1 %all-to-all-done.9.parts_ref = bf16[8,64,128]{2,1,0:T(8,128)(2,1)S(1)} async-done(((bf16[8,64,128]{2,1,0:T(8,128)(2,1)}), bf16[8,64,128]{2,1,0:T(8,128)(2,1)S(1)}, u32[]{:S(2)}, u32[]{:S(2)}) %all-to-all-start.9) | async-done | bytes 131104 | tf_op jit(solution)/shard_map/all_to_all | solution.py:271
  187.2 0.4 shard_map.98
  187.6 11.4 %all_to_all.65 = bf16[8,16,3072]{2,1,0:T(8,128)(2,1)S(1)} all-to-all(bf16[8,16,3072]{2,1,0:T(8,128)(2,1)S(1)} %bitcast.52), channel_id=1, replica_groups={{0,1,16,17,32,33,48,49},{2,3,18,19,34,35,50,51},{4,5,20,21,36,37,52,53}..., dimensions={0} | all-to-all | bytes 1572864 | tf_op jit(solution)/shard_map/all_to_all | solution.py:180
  199.0 0.1 reduce_sum.44
  199.1 20.2 %all_to_all.66 = bf16[8,48,128]{2,1,0:T(8,128)(2,1)S(1)} all-to-all(bf16[8,48,128]{2,1,0:T(8,128)(2,1)S(1)} %convert_element_type.51), channel_id=1, replica_groups={{0,2,4,6,8,10,12,14},{1,3,5,7,9,11,13,15},{16,18,20,22,24,26,28,30},{17..., dimensions={0} | all-to-all | bytes 196608 | tf_op jit(solution)/shard_map/all_to_all | solution.py:180
  219.4 13.5 %collective-permute-start.6 = (bf16[2,3072]{1,0:T(2,128)(2,1)S(1)}, bf16[2,3072]{1,0:T(2,128)(2,1)S(1)}, u32[]{:S(2)}, u32[]{:S(2)}) collective-permute-start(bf16[2,3072]{1,0:T(2,128)(2,1)S(1)} %add_convert_fusion), channel_id=1, source_target_pairs={{448,0},{0,64},{64,128},{128,192},{192,256},{256,320},{320,384},{3... | collective-permute-start | bytes 36872 | tf_op jit(solution)/shard_map/ppermute | solution.py:23
  232.9 0.8 collective-permute-done.6
  233.7 0.6 copy.16
  (44 shorter events, 0.5 us)
Async XLA Ops:
  0.0 79.3 %copy-start = (bf16[1,192,3072]{2,1,0:T(8,128)(2,1)S(1)}, bf16[1,192,3072]{2,1,0:T(8,128)(2,1)}, u32[]{:S(2)}) copy-start(bf16[1,192,3072]{2,1,0:T(8,128)(2,1)} %param.13) | copy-start | bytes 3538948
  0.0 0.9 copy-start.4
  0.9 0.7 copy-start.10
  2.5 29.2 %all-to-all-start = ((bf16[16,48,128]{2,1,0:T(8,128)(2,1)}), bf16[16,48,128]{2,1,0:T(8,128)(2,1)S(1)}, u32[]{:S(2)}, u32[]{:S(2)}) async-start(bf16[16,48,128]{2,1,0:T(8,128)(2,1)} %shard_map.91), calls=%async_computation | async-start | bytes 393216 | tf_op jit(solution)/shard_map/all_to_all | solution.py:254
  19.4 17.5 %collective-permute-start.2 = (bf16[48,768]{1,0:T(8,128)(2,1)S(1)}, bf16[48,768]{1,0:T(8,128)(2,1)S(1)}, u32[]{:S(2)}, u32[]{:S(2)}) collective-permute-start(bf16[48,768]{1,0:T(8,128)(2,1)S(1)} %get-tuple-element.16), channel_id=1, source_target_pairs={{0,48},{1,49},{2,50},{3,51},{4,52},{5,53},{6,54},{7,55},{8,56},{9,... | collective-permute-start | bytes 221192 | tf_op jit(solution)/shard_map/ppermute | solution.py:246
  23.8 13.1 %collective-permute-start.1 = (bf16[48,768]{1,0:T(8,128)(2,1)S(1)}, bf16[48,768]{1,0:T(8,128)(2,1)S(1)}, u32[]{:S(2)}, u32[]{:S(2)}) collective-permute-start(bf16[48,768]{1,0:T(8,128)(2,1)S(1)} %get-tuple-element.17), channel_id=1, source_target_pairs={{0,32},{1,33},{2,34},{3,35},{4,36},{5,37},{6,38},{7,39},{8,40},{9,... | collective-permute-start | bytes 221192 | tf_op jit(solution)/shard_map/ppermute | solution.py:246
  26.2 10.7 %collective-permute-start = (bf16[48,768]{1,0:T(8,128)(2,1)S(1)}, bf16[48,768]{1,0:T(8,128)(2,1)S(1)}, u32[]{:S(2)}, u32[]{:S(2)}) collective-permute-start(bf16[48,768]{1,0:T(8,128)(2,1)S(1)} %get-tuple-element.18), channel_id=1, source_target_pairs={{0,16},{1,17},{2,18},{3,19},{4,20},{5,21},{6,22},{7,23},{8,24},{9,... | collective-permute-start | bytes 221192 | tf_op jit(solution)/shard_map/ppermute | solution.py:246
  32.7 13.9 %copy-start.1 = (bf16[1,3,48,3072]{3,2,1,0:T(8,128)(2,1)S(1)}, bf16[1,3,48,3072]{3,2,1,0:T(8,128)(2,1)}, u32[]{:S(2)}) copy-start(bf16[1,3,48,3072]{3,2,1,0:T(8,128)(2,1)} %param.10) | copy-start | bytes 2654212
  32.7 13.9 %all-to-all-start.1 = ((bf16[4,32,3072]{2,1,0:T(8,128)(2,1)}), bf16[4,32,3072]{2,1,0:T(8,128)(2,1)S(1)}, u32[]{:S(2)}, u32[]{:S(2)}) async-start(bf16[4,32,3072]{2,1,0:T(8,128)(2,1)} %broadcast_in_dim.37), calls=%async_computation.1 | async-start | bytes 1572864 | tf_op jit(solution)/shard_map/all_to_all | solution.py:173
  37.0 19.6 %copy-start.12 = (f32[1,2,128]{2,1,0:T(2,128)S(1)}, f32[1,2,128]{2,1,0:T(2,128)}, u32[]{:S(2)}) copy-start(f32[1,2,128]{2,1,0:T(2,128)} %param.15) | copy-start | bytes 3076
  37.0 9.6 %collective-permute-start.3 = (bf16[2,48,384]{2,1,0:T(8,128)(2,1)S(1)}, bf16[2,48,384]{2,1,0:T(8,128)(2,1)S(1)}, u32[]{:S(2)}, u32[]{:S(2)}) collective-permute-start(bf16[2,48,384]{2,1,0:T(8,128)(2,1)S(1)} %get-tuple-element.20), channel_id=1, source_target_pairs={{0,12},{1,13},{2,14},{3,15},{4,8},{5,9},{6,10},{7,11},{8,4},{9,5},... | collective-permute-start | bytes 221192 | tf_op jit(solution)/shard_map/ppermute | solution.py:258
  46.7 21.2 %copy-start.6 = (bf16[2,48,384]{2,1,0:T(8,128)(2,1)}, bf16[2,48,384]{2,1,0:T(8,128)(2,1)S(1)}, u32[]{:S(2)}) copy-start(bf16[2,48,384]{2,1,0:T(8,128)(2,1)S(1)} %collective-permute-done.3.refs_1_) | copy-start | bytes 221188
  47.9 18.4 %all-to-all-start.2 = ((bf16[8,64,128]{2,1,0:T(8,128)(2,1)}), bf16[8,64,128]{2,1,0:T(8,128)(2,1)S(1)}, u32[]{:S(2)}, u32[]{:S(2)}) async-start(bf16[8,64,128]{2,1,0:T(8,128)(2,1)} %shard_map.92), calls=%async_computation.2 | async-start | bytes 262144 | tf_op jit(solution)/shard_map/all_to_all | solution.py:269
  56.7 9.6 %collective-permute-start.4 = (bf16[2,48,384]{2,1,0:T(8,128)(2,1)S(1)}, bf16[2,48,384]{2,1,0:T(8,128)(2,1)S(1)}, u32[]{:S(2)}, u32[]{:S(2)}) collective-permute-start(bf16[2,48,384]{2,1,0:T(8,128)(2,1)S(1)} %get-tuple-element.19), channel_id=1, source_target_pairs={{0,12},{1,13},{2,14},{3,15},{4,8},{5,9},{6,10},{7,11},{8,4},{9,5},... | collective-permute-start | bytes 221192 | tf_op jit(solution)/shard_map/ppermute | solution.py:258
  66.3 11.3 %copy-start.8 = (bf16[2,48,384]{2,1,0:T(8,128)(2,1)}, bf16[2,48,384]{2,1,0:T(8,128)(2,1)S(1)}, u32[]{:S(2)}) copy-start(bf16[2,48,384]{2,1,0:T(8,128)(2,1)S(1)} %collective-permute-done.4.refs_2_) | copy-start | bytes 221188
  67.9 20.0 %all-to-all-start.3 = ((bf16[8,64,128]{2,1,0:T(8,128)(2,1)}), bf16[8,64,128]{2,1,0:T(8,128)(2,1)S(1)}, u32[]{:S(2)}, u32[]{:S(2)}) async-start(bf16[8,64,128]{2,1,0:T(8,128)(2,1)} %shard_map.93), calls=%async_computation.3 | async-start | bytes 262144 | tf_op jit(solution)/shard_map/all_to_all | solution.py:271
  79.4 8.5 %copy-start.3 = (bf16[1,48,3072]{2,1,0:T(8,128)(2,1)S(1)}, bf16[1,48,3072]{2,1,0:T(8,128)(2,1)}, u32[]{:S(2)}) copy-start(bf16[1,48,3072]{2,1,0:T(8,128)(2,1)} %param.12) | copy-start | bytes 884740
  79.4 8.5 %copy-start.5 = (f32[1,3,3072]{2,0,1:T(1,128)S(1)}, f32[1,3,3072]{2,0,1:T(1,128)}, u32[]{:S(2)}) copy-start(f32[1,3,3072]{2,0,1:T(1,128)} %param.14) | copy-start | bytes 110596
  88.3 31.7 %copy-start.11 = (bf16[1,2,3072]{2,1,0:T(2,128)(2,1)S(1)}, bf16[1,2,3072]{2,1,0:T(2,128)(2,1)}, u32[]{:S(2)}) copy-start(bf16[1,2,3072]{2,1,0:T(2,128)(2,1)} %param.9) | copy-start | bytes 36868
  120.0 11.7 %collective-permute-start.5 = (bf16[2,3072]{1,0:T(2,128)(2,1)S(1)}, bf16[2,3072]{1,0:T(2,128)(2,1)S(1)}, u32[]{:S(2)}, u32[]{:S(2)}) collective-permute-start(bf16[2,3072]{1,0:T(2,128)(2,1)S(1)} %add_convert_fusion.1), channel_id=1, source_target_pairs={{448,0},{0,64},{64,128},{128,192},{192,256},{256,320},{320,384},{3... | collective-permute-start | bytes 36872 | tf_op jit(solution)/shard_map/ppermute | solution.py:23
  146.9 12.0 %copy-start.2 = (bf16[1,3,48,3072]{3,2,1,0:T(8,128)(2,1)S(1)}, bf16[1,3,48,3072]{3,2,1,0:T(8,128)(2,1)}, u32[]{:S(2)}) copy-start(bf16[1,3,48,3072]{3,2,1,0:T(8,128)(2,1)} %param.10) | copy-start | bytes 2654212
  158.9 13.2 %copy-start.7 = (bf16[2,48,384]{2,1,0:T(8,128)(2,1)S(1)}, bf16[2,48,384]{2,1,0:T(8,128)(2,1)}, u32[]{:S(2)}) copy-start(bf16[2,48,384]{2,1,0:T(8,128)(2,1)} %copy-done.6) | copy-start | bytes 221188
  158.9 13.2 %copy-start.9 = (bf16[2,48,384]{2,1,0:T(8,128)(2,1)S(1)}, bf16[2,48,384]{2,1,0:T(8,128)(2,1)}, u32[]{:S(2)}) copy-start(bf16[2,48,384]{2,1,0:T(8,128)(2,1)} %copy-done.8) | copy-start | bytes 221188
  173.6 13.6 %all-to-all-start.9 = ((bf16[8,64,128]{2,1,0:T(8,128)(2,1)}), bf16[8,64,128]{2,1,0:T(8,128)(2,1)S(1)}, u32[]{:S(2)}, u32[]{:S(2)}) async-start(bf16[8,64,128]{2,1,0:T(8,128)(2,1)} %shard_map.97), calls=%async_computation.9 | async-start | bytes 262144 | tf_op jit(solution)/shard_map/all_to_all | solution.py:271
  219.4 14.3 %collective-permute-start.6 = (bf16[2,3072]{1,0:T(2,128)(2,1)S(1)}, bf16[2,3072]{1,0:T(2,128)(2,1)S(1)}, u32[]{:S(2)}, u32[]{:S(2)}) collective-permute-start(bf16[2,3072]{1,0:T(2,128)(2,1)S(1)} %add_convert_fusion), channel_id=1, source_target_pairs={{448,0},{0,64},{64,128},{128,192},{192,256},{256,320},{320,384},{3... | collective-permute-start | bytes 36872 | tf_op jit(solution)/shard_map/ppermute | solution.py:23

commit v12 on v11

--- a/solution.py
+++ b/solution.py
@@ -69,10 +69,10 @@
     out_ref[...] = ((branch + forward_ref[...]) * modulation_ref[2]).astype(bf16)
 
 
-def finish(member, parts, weights, forward, modulation):
+def finish(member, parts, weights, forward, modulation, kernel=finish_kernel):
     whole = pl.BlockSpec(memory_space=pltpu.VMEM)
     return pl.pallas_call(
-        finish_kernel,
+        kernel,
         out_shape=jax.ShapeDtypeStruct(forward.shape, bf16),
         in_specs=[pl.BlockSpec(memory_space=pltpu.SMEM)] + [whole] * 4,
         out_specs=whole,
@@ -90,17 +90,21 @@
     others = lax.dot_general(
         normed_ref[...], weight_ref[shard:], contract, preferred_element_type=f32
     ).astype(bf16)
+    each = others.shape[0] // members
     for c in range(members):
         out_ref[c, :shard, :] = query
-        out_ref[c, shard:, : 2 * shard] = others[16 * c : 16 * c + 16]
-        out_ref[c, shard:, 2 * shard :] = jnp.zeros((16, LANES - 2 * shard), bf16)
-
-
-def project(normed, weights):
+        out_ref[c, shard:, : 2 * shard] = others[each * c : each * c + each]
+        if 2 * shard < LANES:
+            out_ref[c, shard:, 2 * shard :] = jnp.zeros((each, LANES - 2 * shard), bf16)
+
+
+def project(normed, weights, members):
     whole = pl.BlockSpec(memory_space=pltpu.VMEM)
     return pl.pallas_call(
         project_kernel,
-        out_shape=jax.ShapeDtypeStruct((TEAM, weights.shape[0] // 3 + 16, LANES), bf16),
+        out_shape=jax.ShapeDtypeStruct(
+            (members, weights.shape[0] // 3 + normed.shape[0] // members, LANES), bf16
+        ),
         in_specs=[whole] * 2,
         out_specs=whole,
         compiler_params=pltpu.CompilerParams(vmem_limit_bytes=8 * 1024 * 1024),
@@ -167,6 +171,101 @@
     )(team, mask, gains[0][:, None], gains[1][None, :], *cached)
 
 
+def attend_four_kernel(
+    member_ref, team_ref, mask_ref, gain_q_ref, gain_k_ref, near_ref, other_ref, out_ref, features_ref
+):
+    members = team_ref.shape[0]
+    own, more = 48, 16
+    upper = member_ref[0] >= members
+    lane = lax.broadcasted_iota(jnp.int32, (32, LANES), 1)
+    own_at = [pl.multiple_of(jnp.where(upper, 64, 0) + own * j, 16) for j in range(members)]
+    more_at = [pl.multiple_of(jnp.where(upper, 0, 192) + more * j, 16) for j in range(members)]
+    keys = [jnp.zeros((32, LANES), f32) for _ in range(2)]
+    values = [jnp.zeros((32, LANES), f32) for _ in range(2)]
+    for j in range(members):
+        features_ref[pl.ds(own_at[j], own), :] = team_ref[j, :own, :]
+        features_ref[pl.ds(more_at[j], more), :] = team_ref[j, own : own + more, :]
+        fresh = team_ref[j, own + more :, :].astype(f32)
+        for at, length, place in ((own_at[j], own, 0), (more_at[j], more, own)):
+            key = pltpu.roll(fresh, lax.rem(at - place + LANES, LANES), 1)
+            value = pltpu.roll(fresh, lax.rem(at - place - 64 + 2 * LANES, LANES), 1)
+            for h in range(2):
+                here = lane + h * HEAD_DIM - at
+                here = (here >= 0) & (here < length)
+                keys[h] = jnp.where(here, key, keys[h])
+                values[h] = jnp.where(here, value, values[h])
+    features = features_ref[...].astype(f32)
+    open_key = mask_ref[...] > 0.0
+    blocks = [r[i].astype(f32) for r in (near_ref, other_ref) for i in range(r.shape[0])]
+    half = blocks[0].shape[0] // 2
+    cached_keys = jnp.concatenate([b[:half] for b in blocks], axis=0).astype(bf16)
+    cached_values = jnp.concatenate([b[half:] for b in blocks], axis=0).astype(bf16)
+    sums = jnp.zeros((16, LANES), f32)
+    row = lax.broadcasted_iota(jnp.int32, (16, LANES), 0)
+    token = lax.broadcasted_iota(jnp.int32, (HEAD_DIM, LANES), 1)
+    contract = (((0,), (0,)), ((), ()))
+    for h in range(2):
+        query = features[h * HEAD_DIM : (h + 1) * HEAD_DIM]
+        scale = lax.rsqrt(jnp.mean(query * query, axis=0, keepdims=True) + eps_norm)
+        query = (query * scale * gain_q_ref[...] * HEAD_DIM ** (-0.5)).astype(bf16)
+        scale = lax.rsqrt(jnp.mean(keys[h] * keys[h], axis=1, keepdims=True) + eps_norm)
+        key = (keys[h] * scale * gain_k_ref[...]).astype(bf16)
+        scores = jnp.dot(
+            cached_keys[:, h * HEAD_DIM : (h + 1) * HEAD_DIM], query, preferred_element_type=f32
+        )
+        probs = jnp.exp(jnp.where(open_key, scores, -1e30))
+        fresh_probs = jnp.exp(jnp.dot(key, query, preferred_element_type=f32))
+        total = jnp.sum(probs, axis=0, keepdims=True) + jnp.sum(fresh_probs, axis=0, keepdims=True)
+        sums = jnp.where(row == h, total, sums)
+        weighted = lax.dot_general(
+            cached_values[:, h * HEAD_DIM : (h + 1) * HEAD_DIM], probs.astype(bf16), contract,
+            preferred_element_type=f32,
+        ) + lax.dot_general(
+            values[h].astype(bf16), fresh_probs.astype(bf16), contract, preferred_element_type=f32
+        )
+        shared = upper == (h == 0)
+        mine = (token >= LANES // 2) == upper
+        weighted = jnp.where(mine | jnp.logical_not(shared), weighted, 0.0)
+        features_ref[h * HEAD_DIM : (h + 1) * HEAD_DIM, :] = weighted.astype(bf16)
+    for j in range(members):
+        out_ref[j, :own, :] = features_ref[pl.ds(own_at[j], own), :]
+        out_ref[j, own : own + more, :] = features_ref[pl.ds(more_at[j], more), :]
+        out_ref[j, own + more :, :] = sums.astype(bf16)
+
+
+def attend_four(member, team, cached, mask, gains):
+    whole = pl.BlockSpec(memory_space=pltpu.VMEM)
+    return pl.pallas_call(
+        attend_four_kernel,
+        out_shape=jax.ShapeDtypeStruct((team.shape[0], 80, LANES), bf16),
+        in_specs=[pl.BlockSpec(memory_space=pltpu.SMEM)] + [whole] * 6,
+        out_specs=whole,
+        scratch_shapes=[pltpu.VMEM((2 * HEAD_DIM, LANES), bf16)],
+        compiler_params=pltpu.CompilerParams(vmem_limit_bytes=8 * 1024 * 1024),
+    )(member, team, mask, gains[0][:, None], gains[1][None, :], *cached)
+
+
+def finish_four_kernel(member_ref, parts_ref, weight_ref, forward_ref, modulation_ref, out_ref):
+    own, more = 48, 16
+    members = parts_ref.shape[0]
+    upper = member_ref[0] >= members
+    place = lax.rem(member_ref[0], members)
+    summed = parts_ref[0].astype(f32)
+    for c in range(1, members):
+        summed = summed + parts_ref[c].astype(f32)
+    row = lax.broadcasted_iota(jnp.int32, (own + more, LANES), 0)
+    own_at = jnp.where(upper, 64, 0) + own * place
+    more_at = jnp.where(upper, 0, 192) + more * place
+    feature = jnp.where(row < own, own_at + row, more_at + row - own)
+    first, second = summed[own + more][None], summed[own + more + 1][None]
+    total = jnp.where(feature < HEAD_DIM, first, second)
+    attention = (summed[: own + more] / total).astype(bf16)
+    branch = lax.dot_general(
+        attention, weight_ref[...], (((0,), (0,)), ((), ())), preferred_element_type=f32
+    )
+    out_ref[...] = ((branch + forward_ref[...]) * modulation_ref[2]).astype(bf16)
+
+
 def gathered(block, groups):
     size = len(groups[0])
     spread = jnp.broadcast_to(block[None], (size,) + block.shape)
@@ -194,6 +293,7 @@
     teams = tp_count // TEAM
     team_width = TEAM * shard
     member = tp_index % TEAM
+    half_team = TEAM // 2
     z_count, x_count = 2 * TEAM, tp_count // (2 * TEAM)
     xs, hs, two = range(x_count), range(z_count // 2), range(2)
     along_z = [[z_count * x + 2 * h + l for l in two for h in hs] for x in xs]
@@ -201,6 +301,7 @@
     far = [[z_count * x + 2 * h + l for h in hs] for x in xs for l in two]
     blocks = [[z_count * x + 2 * h + l for x in xs for l in two] for h in hs]
     inside = [[TEAM * t + m for m in range(TEAM)] for t in range(teams)]
+    fours = [[half_team * t + m for m in range(half_team)] for t in range(2 * teams)]
     shift_scale = modulation.reshape(3, 1, width)
     gains = qk_gain[0]
     weight_qkv = w_qkv[0].reshape(3 * shard, width)
@@ -208,7 +309,6 @@
     weight_attn = w_attn_out[0]
     weight_down = w_mlp_out[0]
 
-    half_team = TEAM // 2
     partner = [
         z + TEAM + half_team if z < half_team else z + half_team if z < TEAM
         else z - half_team if z < TEAM + half_team else z - TEAM - half_team
@@ -222,12 +322,18 @@
     )
     upper = z_here >= TEAM
     slot = jnp.arange(teams * ctx_local, dtype=jnp.int32)
-    own_z = slot < x_count * ctx_local
-    source = z_count * ((x_here - slot // ctx_local % x_count) % x_count)
-    source = source + jnp.where(own_z, z_here, z_partner)
-    position = ctx_local * source + slot % ctx_local
-    cached_mask = ((position >= TXT) | (position < text_len[0])).astype(f32)
-    cached_mask = jnp.broadcast_to(cached_mask[:, None], (teams * ctx_local, LANES))
+
+    def open_keys(z, z_other):
+        source = z_count * ((x_here - slot // ctx_local % x_count) % x_count)
+        source = source + jnp.where(slot < x_count * ctx_local, z, z_other)
+        position = ctx_local * source + slot % ctx_local
+        return ((position >= TXT) | (position < text_len[0])).astype(f32)
+
+    near_mask = open_keys(z_here, z_partner)
+    other_mask = open_keys(z_here ^ half_team, z_partner ^ half_team)
+    wide_mask = jnp.concatenate([near_mask, other_mask])
+    near_mask = jnp.broadcast_to(near_mask[:, None], (near_mask.shape[0], LANES))
+    wide_mask = jnp.broadcast_to(wide_mask[:, None], (wide_mask.shape[0], LANES))
 
     current = in_flight[0]
     block = spread(current, shift_scale, z_count)
@@ -265,10 +371,16 @@
             block = spread(current, shift_scale, len(hs))
             normed = lax.all_to_all(block, "tp", 0, 0, axis_index_groups=far)
             normed = gathered(normed.reshape(-1, width), blocks)
-        team = project(normed, weight_qkv)
-        team = lax.all_to_all(team, "tp", 0, 0, axis_index_groups=inside)
-        parts = attend(team, cached, cached_mask, gains)
-        parts = lax.all_to_all(parts, "tp", 0, 0, axis_index_groups=inside)
+        if tick_number == 0:
+            team = project(normed, weight_qkv, TEAM)
+            team = lax.all_to_all(team, "tp", 0, 0, axis_index_groups=inside)
+            parts = attend(team, cached, near_mask, gains)
+            parts = lax.all_to_all(parts, "tp", 0, 0, axis_index_groups=inside)
+        else:
+            team = project(normed, wide_qkv, half_team)
+            team = lax.all_to_all(team, "tp", 0, 0, axis_index_groups=fours)
+            parts = attend_four(member[None], team, wide_cached, wide_mask, gains)
+            parts = lax.all_to_all(parts, "tp", 0, 0, axis_index_groups=fours)
         hidden = jax.nn.gelu(
             lax.dot_general(
                 normed, weight_mlp, (((1,), (1,)), ((), ())), preferred_element_type=f32
@@ -278,9 +390,36 @@
         hidden = lax.optimization_barrier(hidden)
         forward = jnp.dot(hidden, weight_down, preferred_element_type=f32)
         forward = lax.optimization_barrier(forward)
-        branch = finish(member[None], parts, weight_attn, forward, shift_scale)
+        if tick_number == 0:
+            branch = finish(member[None], parts, weight_attn, forward, shift_scale)
+        else:
+            branch = finish(
+                member[None], parts, wide_attn, forward, shift_scale, finish_four_kernel
+            )
         branch = summed_over(branch, blocks)
         branch = summed_over(branch.reshape(-1, LANES), far).reshape(rows, width)
+        if tick_number == 0:
+            rows_here = jnp.concatenate([w_qkv[0], w_attn_out], axis=0)
+            more = 0
+            for offset, moves in (
+                (jnp.where(member % 2 == 0, 32, 0), ((4, 2), (5, 3), (2, 4), (3, 5))),
+                (16, ((4, 1), (3, 6))),
+                (jnp.where(member == 4, 0, 32), ((4, 0), (3, 7))),
+            ):
+                part = lax.dynamic_slice_in_dim(rows_here, offset, 16, 1)
+                more = more + lax.ppermute(
+                    part, "tp", [(TEAM * t + a, TEAM * t + b) for t in range(teams) for a, b in moves]
+                )
+            lower = member < half_team
+            all_cached = jnp.concatenate(cached, axis=0)
+            two_heads = 2 * HEAD_DIM
+            near = jnp.where(lower, all_cached[..., :two_heads], all_cached[..., HEAD_DIM:])
+            far_heads = jnp.where(lower, all_cached[..., HEAD_DIM:], all_cached[..., :two_heads])
+            other = lax.ppermute(far_heads, "tp", [(i, i ^ half_team) for i in range(tp_count)])
+            branch, more, other = lax.optimization_barrier((branch, more, other))
+            wide = jnp.concatenate([rows_here, more], axis=1)
+            wide_qkv, wide_attn = wide[:3].reshape(-1, width), wide[3]
+            wide_cached = [near, other]
         finished = (current.astype(f32) + branch).astype(bf16)
         current = shifted(finished, "pipe", 1)
     return current[None]

time: 235 us -> 258 us (1.098)
  blocking collectives: 103 us -> 47.2 us
  waiting for transfers between devices: 24.5 us -> 58.5 us
  starting transfers between devices: 90 us -> 115 us
  other arithmetic: 0.4 us -> 8.04 us
  local copies, waits for them, and re-layouts: 4.77 us -> 11.2 us
    all_to_all x4 -> x2, blocking collectives: 63.1 us -> 27.1 us  [summed_over(): parts = lax.all_to_all(parts, 'tp', 0, 0, axis_index_groups=groups)]
    ppermute x0 -> x4, waiting for transfers between devices: none -> 29.8 us  [the longest x3 29.8 us: local(): lax.ppermute(part, 'tp', [(TEAM * t + a, TEAM * t + b) for t in range(tea...]
    all_to_all x2 -> x0, blocking collectives: 24.6 us -> none  [the longest x1 12.7 us: local(): team = lax.all_to_all(team, 'tp', 0, 0, axis_index_groups=inside)]
    all_to_all x0 -> x4, starting transfers between devices: none -> 18.3 us  [the longest x2 11 us: summed_over(): parts = lax.all_to_all(parts, 'tp', 0, 0, axis_index_groups=groups)]
    ppermute x0 -> x4, starting transfers between devices: none -> 12.7 us  [the longest x1 9.36 us: local(): lax.ppermute(far_heads, 'tp', [(i, i ^ half_team) for i in range(tp_count)])]
    all_to_all x2 -> x1, waiting for transfers between devices: 16.1 us -> 6.89 us  [local(): parts = lax.all_to_all(parts, 'tp', 0, 0, axis_index_groups=inside)]
    all_to_all x0 -> x4, waiting for transfers between devices: none -> 8.49 us  [the longest x1 3.37 us: local(): parts = lax.all_to_all(parts, 'tp', 0, 0, axis_index_groups=fours)]
    ppermute x2, starting transfers between devices: 24.3 us -> 16.5 us  [shifted(): lax.ppermute(block, axis, [((i - distance) % size, i) for i in range(size)])]
  transfers between devices with their start and end apart: 12 -> 20, of which waited for: 7 -> 11; matrix products, arithmetic and copies ran while one was open for 3% -> 7% of each run, Pallas kernels for 0% -> 0%
where the time goes in v12:
time: 258 us; the launch traced here: 256 us
  starting transfers between devices  115 us (45%)
  waiting for transfers between devices  58.5 us (23%)
  blocking collectives  47.2 us (18%)
  local copies, waits for them, and re-layouts  11.2 us (4%)
  Pallas kernels  9.03 us (3%)
  other arithmetic  8.04 us (3%)
  matrix products  5.67 us (2%)
    ppermute x3, waiting for transfers between devices, local(): lax.ppermute(part, 'tp', [(TEAM * t + a, TEAM * t + b) for t in range(tea...  29.8 us
    all_to_all x2, blocking collectives, summed_over(): parts = lax.all_to_all(parts, 'tp', 0, 0, axis_index_groups=groups)  27.1 us
    all_to_all x1, blocking collectives, local(): normed = lax.all_to_all(block, 'tp', 0, 0, axis_index_groups=far)  20.1 us
    ppermute x2, starting transfers between devices, shifted(): lax.ppermute(block, axis, [((i - distance) % size, i) for i in range(size)])  16.5 us
    ppermute x2, starting transfers between devices, local(): lax.ppermute(part, 'tp', route)  15.9 us
    all_to_all x1, starting transfers between devices, local(): normed = lax.all_to_all(block, 'tp', 0, 0, axis_index_groups=along_z)  15.7 us
    all_to_all x2, starting transfers between devices, summed_over(): parts = lax.all_to_all(parts, 'tp', 0, 0, axis_index_groups=groups)  11 us
    ppermute x3, starting transfers between devices, local(): part = lax.ppermute(part, 'tp', route)  10.5 us
  transfers between devices with their start and end apart: 20, of which 11 were waited for; matrix products, arithmetic and copies ran while one was open for 7% of the time, Pallas kernels for 0%

profile of v12, /device:TPU:1, one launch (start us, length us, event | category | flops | bytes accessed | tf_op | source)
XLA Modules:
  0.0 255.8 jit_solution(17700542063147618465)
XLA Ops:
  2.5 15.7 %all-to-all-start = ((bf16[16,48,128]{2,1,0:T(8,128)(2,1)}), bf16[16,48,128]{2,1,0:T(8,128)(2,1)S(1)}, u32[]{:S(2)}, u32[]{:S(2)}) async-start(bf16[16,48,128]{2,1,0:T(8,128)(2,1)} %shard_map.91), calls=%async_computation | async-start | bytes 393216 | tf_op jit(solution)/shard_map/all_to_all | solution.py:360
  18.4 1.0 dynamic-slice_bitcast_fusion
  19.4 3.1 %collective-permute-start = (bf16[48,768]{1,0:T(8,128)(2,1)S(1)}, bf16[48,768]{1,0:T(8,128)(2,1)S(1)}, u32[]{:S(2)}, u32[]{:S(2)}) collective-permute-start(bf16[48,768]{1,0:T(8,128)(2,1)S(1)} %get-tuple-element.29), channel_id=1, source_target_pairs={{0,16},{1,17},{2,18},{3,19},{4,20},{5,21},{6,22},{7,23},{8,24},{9,... | collective-permute-start | bytes 221192 | tf_op jit(solution)/shard_map/ppermute | solution.py:352
  22.5 4.4 %collective-permute-start.1 = (bf16[48,768]{1,0:T(8,128)(2,1)S(1)}, bf16[48,768]{1,0:T(8,128)(2,1)S(1)}, u32[]{:S(2)}, u32[]{:S(2)}) collective-permute-start(bf16[48,768]{1,0:T(8,128)(2,1)S(1)} %get-tuple-element.28), channel_id=1, source_target_pairs={{0,32},{1,33},{2,34},{3,35},{4,36},{5,37},{6,38},{7,39},{8,40},{9,... | collective-permute-start | bytes 221192 | tf_op jit(solution)/shard_map/ppermute | solution.py:352
  26.9 3.1 %collective-permute-start.2 = (bf16[48,768]{1,0:T(8,128)(2,1)S(1)}, bf16[48,768]{1,0:T(8,128)(2,1)S(1)}, u32[]{:S(2)}, u32[]{:S(2)}) collective-permute-start(bf16[48,768]{1,0:T(8,128)(2,1)S(1)} %get-tuple-element.27), channel_id=1, source_target_pairs={{0,48},{1,49},{2,50},{3,51},{4,52},{5,53},{6,54},{7,55},{8,56},{9,... | collective-permute-start | bytes 221192 | tf_op jit(solution)/shard_map/ppermute | solution.py:352
  30.0 1.7 all-to-all-done
  32.7 4.1 %all-to-all-start.1 = ((bf16[4,32,3072]{2,1,0:T(8,128)(2,1)}), bf16[4,32,3072]{2,1,0:T(8,128)(2,1)S(1)}, u32[]{:S(2)}, u32[]{:S(2)}) async-start(bf16[4,32,3072]{2,1,0:T(8,128)(2,1)} %broadcast_in_dim.50), calls=%async_computation.1 | async-start | bytes 1572864 | tf_op jit(solution)/shard_map/all_to_all | solution.py:272
  37.0 7.9 %collective-permute-start.3 = (bf16[2,48,384]{2,1,0:T(8,128)(2,1)S(1)}, bf16[2,48,384]{2,1,0:T(8,128)(2,1)S(1)}, u32[]{:S(2)}, u32[]{:S(2)}) collective-permute-start(bf16[2,48,384]{2,1,0:T(8,128)(2,1)S(1)} %get-tuple-element.31), channel_id=1, source_target_pairs={{0,12},{1,13},{2,14},{3,15},{4,8},{5,9},{6,10},{7,11},{8,4},{9,5},... | collective-permute-start | bytes 221192 | tf_op jit(solution)/shard_map/ppermute | solution.py:364
  44.9 1.7 collective-permute-done.3.refs_1_
  46.7 1.2 shard_map.92
  47.9 7.5 %all-to-all-start.2 = ((bf16[8,64,128]{2,1,0:T(8,128)(2,1)}), bf16[8,64,128]{2,1,0:T(8,128)(2,1)S(1)}, u32[]{:S(2)}, u32[]{:S(2)}) async-start(bf16[8,64,128]{2,1,0:T(8,128)(2,1)} %shard_map.92), calls=%async_computation.2 | async-start | bytes 262144 | tf_op jit(solution)/shard_map/all_to_all | solution.py:376
  56.2 8.1 %collective-permute-start.4 = (bf16[2,48,384]{2,1,0:T(8,128)(2,1)S(1)}, bf16[2,48,384]{2,1,0:T(8,128)(2,1)S(1)}, u32[]{:S(2)}, u32[]{:S(2)}) collective-permute-start(bf16[2,48,384]{2,1,0:T(8,128)(2,1)S(1)} %get-tuple-element.30), channel_id=1, source_target_pairs={{0,12},{1,13},{2,14},{3,15},{4,8},{5,9},{6,10},{7,11},{8,4},{9,5},... | collective-permute-start | bytes 221192 | tf_op jit(solution)/shard_map/ppermute | solution.py:364
  64.3 2.0 collective-permute-done.4.refs_2_
  66.4 1.5 shard_map.93
  67.9 9.3 %all-to-all-start.3 = ((bf16[8,64,128]{2,1,0:T(8,128)(2,1)}), bf16[8,64,128]{2,1,0:T(8,128)(2,1)S(1)}, u32[]{:S(2)}, u32[]{:S(2)}) async-start(bf16[8,64,128]{2,1,0:T(8,128)(2,1)} %shard_map.93), calls=%async_computation.3 | async-start | bytes 262144 | tf_op jit(solution)/shard_map/all_to_all | solution.py:378
  77.2 1.8 fusion.20
  79.0 1.6 fusion.2.forward_ref
  80.6 6.9 %all-to-all-done.3.parts_ref = bf16[8,64,128]{2,1,0:T(8,128)(2,1)S(1)} async-done(((bf16[8,64,128]{2,1,0:T(8,128)(2,1)}), bf16[8,64,128]{2,1,0:T(8,128)(2,1)S(1)}, u32[]{:S(2)}, u32[]{:S(2)}) %all-to-all-start.3) | async-done | bytes 131104 | tf_op jit(solution)/shard_map/all_to_all | solution.py:378
  87.5 1.4 copy-done.2
  88.9 1.3 shard_map.94
  90.2 4.2 %all-to-all-start.4 = ((bf16[8,16,3072]{2,1,0:T(8,128)(2,1)}), bf16[8,16,3072]{2,1,0:T(8,128)(2,1)}, u32[]{:S(2)}, u32[]{:S(2)}) async-start(bf16[8,16,3072]{2,1,0:T(8,128)(2,1)} %bitcast.17), calls=%async_computation.4 | async-start | bytes 1572864 | tf_op jit(solution)/shard_map/all_to_all | solution.py:279
  94.4 1.0 fusion.10
  96.1 1.4 collective-permute-start.6
  97.6 1.3 collective-permute-start.7
  99.6 9.4 %collective-permute-start.8 = (bf16[8,48,256]{2,1,0:T(8,128)(2,1)S(1)}, bf16[8,48,256]{2,1,0:T(8,128)(2,1)S(1)}, u32[]{:S(2)}, u32[]{:S(2)}) collective-permute-start(bf16[8,48,256]{2,1,0:T(8,128)(2,1)S(1)} %get-tuple-element.23), channel_id=1, source_target_pairs={{0,4},{1,5},{2,6},{3,7},{4,0},{5,1},{6,2},{7,3},{8,12},{9,13},{10,... | collective-permute-start | bytes 589832 | tf_op jit(solution)/shard_map/ppermute | solution.py:418
  109.0 1.2 reduce_sum.42
  110.9 6.8 %all-to-all-start.5 = ((bf16[8,48,128]{2,1,0:T(8,128)(2,1)}), bf16[8,48,128]{2,1,0:T(8,128)(2,1)S(1)}, u32[]{:S(2)}, u32[]{:S(2)}) async-start(bf16[8,48,128]{2,1,0:T(8,128)(2,1)} %convert_element_type.49), calls=%async_computation.5 | async-start | bytes 196608 | tf_op jit(solution)/shard_map/all_to_all | solution.py:279
  117.8 29.8 %collective-permute-done.7 = bf16[4,16,3072]{2,1,0:T(8,128)(2,1)} collective-permute-done((bf16[4,16,3072]{2,1,0:T(8,128)(2,1)}, bf16[4,16,3072]{2,1,0:T(8,128)(2,1)}, u32[]{:S(2)}, u32[]{:S(2)}) %collective-permute-start.7) | collective-permute-done | bytes 393248 | tf_op jit(solution)/shard_map/ppermute | solution.py:410
  147.6 1.9 add_add_fusion
  149.5 2.8 %all-to-all-done.5 = bf16[8,48,128]{2,1,0:T(8,128)(2,1)S(1)} async-done(((bf16[8,48,128]{2,1,0:T(8,128)(2,1)}), bf16[8,48,128]{2,1,0:T(8,128)(2,1)S(1)}, u32[]{:S(2)}, u32[]{:S(2)}) %all-to-all-start.5) | async-done | bytes 98336 | tf_op jit(solution)/shard_map/all_to_all | solution.py:279
  153.1 5.4 %collective-permute-start.9 = (bf16[2,3072]{1,0:T(2,128)(2,1)S(1)}, bf16[2,3072]{1,0:T(2,128)(2,1)S(1)}, u32[]{:S(2)}, u32[]{:S(2)}) collective-permute-start(bf16[2,3072]{1,0:T(2,128)(2,1)S(1)} %add_convert_fusion.1), channel_id=1, source_target_pairs={{448,0},{0,64},{64,128},{128,192},{192,256},{256,320},{320,384},{3... | collective-permute-start | bytes 36872 | tf_op jit(solution)/shard_map/ppermute | solution.py:23
  159.6 20.1 %all_to_all.60 = bf16[8,48,128]{2,1,0:T(8,128)(2,1)S(1)} all-to-all(bf16[8,48,128]{2,1,0:T(8,128)(2,1)S(1)} %shard_map.95), channel_id=1, replica_groups={{0,2,4,6,8,10,12,14},{1,3,5,7,9,11,13,15},{16,18,20,22,24,26,28,30},{17..., dimensions={0} | all-to-all | bytes 196608 | tf_op jit(solution)/shard_map/all_to_all | solution.py:372
  180.7 4.4 %all-to-all-start.7 = ((bf16[8,16,3072]{2,1,0:T(8,128)(2,1)}), bf16[8,16,3072]{2,1,0:T(8,128)(2,1)S(1)}, u32[]{:S(2)}, u32[]{:S(2)}) async-start(bf16[8,16,3072]{2,1,0:T(8,128)(2,1)} %broadcast_in_dim.55), calls=%async_computation.7 | async-start | bytes 1572864 | tf_op jit(solution)/shard_map/all_to_all | solution.py:272
  185.8 1.1 pad_maximum_fusion
  186.9 1.1 slice.57
  188.0 6.2 %all-to-all-done.7 = bf16[8,16,3072]{2,1,0:T(8,128)(2,1)S(1)} async-done(((bf16[8,16,3072]{2,1,0:T(8,128)(2,1)}), bf16[8,16,3072]{2,1,0:T(8,128)(2,1)S(1)}, u32[]{:S(2)}, u32[]{:S(2)}) %all-to-all-start.7) | async-done | bytes 786464 | tf_op jit(solution)/shard_map/all_to_all | solution.py:272
  194.2 1.3 copy-done.4
  195.4 1.3 shard_map.96
  196.7 3.9 %all-to-all-start.8 = ((bf16[4,96,128]{2,1,0:T(8,128)(2,1)}), bf16[4,96,128]{2,1,0:T(8,128)(2,1)}, u32[]{:S(2)}, u32[]{:S(2)}) async-start(bf16[4,96,128]{2,1,0:T(8,128)(2,1)} %shard_map.96), calls=%async_computation.8 | async-start | bytes 196608 | tf_op jit(solution)/shard_map/all_to_all | solution.py:381
  201.9 1.1 fusion.32
  203.0 2.3 all-to-all-done.8.team_ref
  205.5 2.2 shard_map.97
  207.7 3.3 %all-to-all-start.9 = ((bf16[4,80,128]{2,1,0:T(8,128)(2,1)}), bf16[4,80,128]{2,1,0:T(8,128)(2,1)S(1)}, u32[]{:S(2)}, u32[]{:S(2)}) async-start(bf16[4,80,128]{2,1,0:T(8,128)(2,1)} %shard_map.97), calls=%async_computation.9 | async-start | bytes 163840 | tf_op jit(solution)/shard_map/all_to_all | solution.py:383
  211.0 1.2 fusion.forward_ref
  212.2 3.4 %all-to-all-done.9.parts_ref = bf16[4,80,128]{2,1,0:T(8,128)(2,1)S(1)} async-done(((bf16[4,80,128]{2,1,0:T(8,128)(2,1)}), bf16[4,80,128]{2,1,0:T(8,128)(2,1)S(1)}, u32[]{:S(2)}, u32[]{:S(2)}) %all-to-all-start.9) | async-done | bytes 81952 | tf_op jit(solution)/shard_map/all_to_all | solution.py:383
  216.0 11.4 %all_to_all.61 = bf16[8,16,3072]{2,1,0:T(8,128)(2,1)S(1)} all-to-all(bf16[8,16,3072]{2,1,0:T(8,128)(2,1)S(1)} %bitcast.61), channel_id=1, replica_groups={{0,1,16,17,32,33,48,49},{2,3,18,19,34,35,50,51},{4,5,20,21,36,37,52,53}..., dimensions={0} | all-to-all | bytes 1572864 | tf_op jit(solution)/shard_map/all_to_all | solution.py:279
  227.6 15.7 %all_to_all.62 = bf16[8,48,128]{2,1,0:T(8,128)(2,1)S(1)} all-to-all(bf16[8,48,128]{2,1,0:T(8,128)(2,1)S(1)} %convert_element_type.55), channel_id=1, replica_groups={{0,2,4,6,8,10,12,14},{1,3,5,7,9,11,13,15},{16,18,20,22,24,26,28,30},{17..., dimensions={0} | all-to-all | bytes 196608 | tf_op jit(solution)/shard_map/all_to_all | solution.py:279
  243.4 11.0 %collective-permute-start.10 = (bf16[2,3072]{1,0:T(2,128)(2,1)S(1)}, bf16[2,3072]{1,0:T(2,128)(2,1)S(1)}, u32[]{:S(2)}, u32[]{:S(2)}) collective-permute-start(bf16[2,3072]{1,0:T(2,128)(2,1)S(1)} %add_convert_fusion), channel_id=1, source_target_pairs={{448,0},{0,64},{64,128},{128,192},{192,256},{256,320},{320,384},{3... | collective-permute-start | bytes 36872 | tf_op jit(solution)/shard_map/ppermute | solution.py:23
  (84 shorter events, 13.1 us)
Async XLA Ops:
  0.0 79.0 %copy-start = (bf16[1,192,3072]{2,1,0:T(8,128)(2,1)S(1)}, bf16[1,192,3072]{2,1,0:T(8,128)(2,1)}, u32[]{:S(2)}) copy-start(bf16[1,192,3072]{2,1,0:T(8,128)(2,1)} %param.13) | copy-start | bytes 3538948
  0.0 0.9 copy-start.8
  0.9 0.7 copy-start.15
  2.5 29.2 %all-to-all-start = ((bf16[16,48,128]{2,1,0:T(8,128)(2,1)}), bf16[16,48,128]{2,1,0:T(8,128)(2,1)S(1)}, u32[]{:S(2)}, u32[]{:S(2)}) async-start(bf16[16,48,128]{2,1,0:T(8,128)(2,1)} %shard_map.91), calls=%async_computation | async-start | bytes 393216 | tf_op jit(solution)/shard_map/all_to_all | solution.py:360
  19.4 17.5 %collective-permute-start = (bf16[48,768]{1,0:T(8,128)(2,1)S(1)}, bf16[48,768]{1,0:T(8,128)(2,1)S(1)}, u32[]{:S(2)}, u32[]{:S(2)}) collective-permute-start(bf16[48,768]{1,0:T(8,128)(2,1)S(1)} %get-tuple-element.29), channel_id=1, source_target_pairs={{0,16},{1,17},{2,18},{3,19},{4,20},{5,21},{6,22},{7,23},{8,24},{9,... | collective-permute-start | bytes 221192 | tf_op jit(solution)/shard_map/ppermute | solution.py:352
  22.5 14.4 %collective-permute-start.1 = (bf16[48,768]{1,0:T(8,128)(2,1)S(1)}, bf16[48,768]{1,0:T(8,128)(2,1)S(1)}, u32[]{:S(2)}, u32[]{:S(2)}) collective-permute-start(bf16[48,768]{1,0:T(8,128)(2,1)S(1)} %get-tuple-element.28), channel_id=1, source_target_pairs={{0,32},{1,33},{2,34},{3,35},{4,36},{5,37},{6,38},{7,39},{8,40},{9,... | collective-permute-start | bytes 221192 | tf_op jit(solution)/shard_map/ppermute | solution.py:352
  26.9 10.0 %collective-permute-start.2 = (bf16[48,768]{1,0:T(8,128)(2,1)S(1)}, bf16[48,768]{1,0:T(8,128)(2,1)S(1)}, u32[]{:S(2)}, u32[]{:S(2)}) collective-permute-start(bf16[48,768]{1,0:T(8,128)(2,1)S(1)} %get-tuple-element.27), channel_id=1, source_target_pairs={{0,48},{1,49},{2,50},{3,51},{4,52},{5,53},{6,54},{7,55},{8,56},{9,... | collective-permute-start | bytes 221192 | tf_op jit(solution)/shard_map/ppermute | solution.py:352
  32.7 13.9 %copy-start.1 = (bf16[1,3,48,3072]{3,2,1,0:T(8,128)(2,1)S(1)}, bf16[1,3,48,3072]{3,2,1,0:T(8,128)(2,1)}, u32[]{:S(2)}) copy-start(bf16[1,3,48,3072]{3,2,1,0:T(8,128)(2,1)} %param.10) | copy-start | bytes 2654212
  32.7 13.9 %all-to-all-start.1 = ((bf16[4,32,3072]{2,1,0:T(8,128)(2,1)}), bf16[4,32,3072]{2,1,0:T(8,128)(2,1)S(1)}, u32[]{:S(2)}, u32[]{:S(2)}) async-start(bf16[4,32,3072]{2,1,0:T(8,128)(2,1)} %broadcast_in_dim.50), calls=%async_computation.1 | async-start | bytes 1572864 | tf_op jit(solution)/shard_map/all_to_all | solution.py:272
  37.0 19.1 %copy-start.21 = (f32[1,2,128]{2,1,0:T(2,128)S(1)}, f32[1,2,128]{2,1,0:T(2,128)}, u32[]{:S(2)}) copy-start(f32[1,2,128]{2,1,0:T(2,128)} %param.15) | copy-start | bytes 3076
  37.0 9.6 %collective-permute-start.3 = (bf16[2,48,384]{2,1,0:T(8,128)(2,1)S(1)}, bf16[2,48,384]{2,1,0:T(8,128)(2,1)S(1)}, u32[]{:S(2)}, u32[]{:S(2)}) collective-permute-start(bf16[2,48,384]{2,1,0:T(8,128)(2,1)S(1)} %get-tuple-element.31), channel_id=1, source_target_pairs={{0,12},{1,13},{2,14},{3,15},{4,8},{5,9},{6,10},{7,11},{8,4},{9,5},... | collective-permute-start | bytes 221192 | tf_op jit(solution)/shard_map/ppermute | solution.py:364
  47.9 18.5 %all-to-all-start.2 = ((bf16[8,64,128]{2,1,0:T(8,128)(2,1)}), bf16[8,64,128]{2,1,0:T(8,128)(2,1)S(1)}, u32[]{:S(2)}, u32[]{:S(2)}) async-start(bf16[8,64,128]{2,1,0:T(8,128)(2,1)} %shard_map.92), calls=%async_computation.2 | async-start | bytes 262144 | tf_op jit(solution)/shard_map/all_to_all | solution.py:376
  56.2 21.0 %copy-start.6 = (f32[128,1]{1,0:T(8,128)}, f32[128,1]{1,0:T(8,128)S(1)}, u32[]{:S(2)}) copy-start(f32[128,1]{1,0:T(8,128)S(1)} %copy.12.gain_q_ref) | copy-start | bytes 1540
  56.2 10.1 %collective-permute-start.4 = (bf16[2,48,384]{2,1,0:T(8,128)(2,1)S(1)}, bf16[2,48,384]{2,1,0:T(8,128)(2,1)S(1)}, u32[]{:S(2)}, u32[]{:S(2)}) collective-permute-start(bf16[2,48,384]{2,1,0:T(8,128)(2,1)S(1)} %get-tuple-element.30), channel_id=1, source_target_pairs={{0,12},{1,13},{2,14},{3,15},{4,8},{5,9},{6,10},{7,11},{8,4},{9,5},... | collective-permute-start | bytes 221192 | tf_op jit(solution)/shard_map/ppermute | solution.py:364
  64.3 3.6 %copy-start.18 = (f32[192]{0:T(256)}, f32[192]{0:T(256)S(1)}, u32[]{:S(2)}) copy-start(f32[192]{0:T(256)S(1)} %or_convert_fusion.1) | copy-start | bytes 2308
  66.3 1.6 copy-start.11
  67.9 19.5 %all-to-all-start.3 = ((bf16[8,64,128]{2,1,0:T(8,128)(2,1)}), bf16[8,64,128]{2,1,0:T(8,128)(2,1)S(1)}, u32[]{:S(2)}, u32[]{:S(2)}) async-start(bf16[8,64,128]{2,1,0:T(8,128)(2,1)} %shard_map.93), calls=%async_computation.3 | async-start | bytes 262144 | tf_op jit(solution)/shard_map/all_to_all | solution.py:378
  79.0 8.5 %copy-start.3 = (bf16[1,48,3072]{2,1,0:T(8,128)(2,1)S(1)}, bf16[1,48,3072]{2,1,0:T(8,128)(2,1)}, u32[]{:S(2)}) copy-start(bf16[1,48,3072]{2,1,0:T(8,128)(2,1)} %param.12) | copy-start | bytes 884740
  79.0 8.5 %copy-start.9 = (f32[1,3,3072]{2,0,1:T(1,128)S(1)}, f32[1,3,3072]{2,0,1:T(1,128)}, u32[]{:S(2)}) copy-start(f32[1,3,3072]{2,0,1:T(1,128)} %param.14) | copy-start | bytes 110596
  87.5 1.4 copy-start.2
  90.2 18.8 %all-to-all-start.4 = ((bf16[8,16,3072]{2,1,0:T(8,128)(2,1)}), bf16[8,16,3072]{2,1,0:T(8,128)(2,1)}, u32[]{:S(2)}, u32[]{:S(2)}) async-start(bf16[8,16,3072]{2,1,0:T(8,128)(2,1)} %bitcast.17), calls=%async_computation.4 | async-start | bytes 1572864 | tf_op jit(solution)/shard_map/all_to_all | solution.py:279
  94.4 4.4 %copy-start.12 = (bf16[2,48,384]{2,1,0:T(8,128)(2,1)S(1)}, bf16[2,48,384]{2,1,0:T(8,128)(2,1)}, u32[]{:S(2)}) copy-start(bf16[2,48,384]{2,1,0:T(8,128)(2,1)} %copy-done.11) | copy-start | bytes 221188
  95.5 22.3 %collective-permute-start.5 = (bf16[4,16,3072]{2,1,0:T(8,128)(2,1)}, bf16[4,16,3072]{2,1,0:T(8,128)(2,1)S(1)}, u32[]{:S(2)}, u32[]{:S(2)}) collective-permute-start(bf16[4,16,3072]{2,1,0:T(8,128)(2,1)} %get-tuple-element.20), channel_id=1, source_target_pairs={{4,2},{5,3},{2,4},{3,5},{12,10},{13,11},{10,12},{11,13},{20,18},{2... | collective-permute-start | bytes 1179656 | tf_op jit(solution)/shard_map/ppermute | solution.py:410
  96.1 21.7 %collective-permute-start.6 = (bf16[4,16,3072]{2,1,0:T(8,128)(2,1)}, bf16[4,16,3072]{2,1,0:T(8,128)(2,1)}, u32[]{:S(2)}, u32[]{:S(2)}) collective-permute-start(bf16[4,16,3072]{2,1,0:T(8,128)(2,1)} %get-tuple-element.19), channel_id=1, source_target_pairs={{4,1},{3,6},{12,9},{11,14},{20,17},{19,22},{28,25},{27,30},{36,33}... | collective-permute-start | bytes 1179656 | tf_op jit(solution)/shard_map/ppermute | solution.py:410
  97.6 50.1 %collective-permute-start.7 = (bf16[4,16,3072]{2,1,0:T(8,128)(2,1)}, bf16[4,16,3072]{2,1,0:T(8,128)(2,1)}, u32[]{:S(2)}, u32[]{:S(2)}) collective-permute-start(bf16[4,16,3072]{2,1,0:T(8,128)(2,1)} %get-tuple-element.21), channel_id=1, source_target_pairs={{4,0},{3,7},{12,8},{11,15},{20,16},{19,23},{28,24},{27,31},{36,32}... | collective-permute-start | bytes 1179656 | tf_op jit(solution)/shard_map/ppermute | solution.py:410
  99.6 52.8 %collective-permute-start.8 = (bf16[8,48,256]{2,1,0:T(8,128)(2,1)S(1)}, bf16[8,48,256]{2,1,0:T(8,128)(2,1)S(1)}, u32[]{:S(2)}, u32[]{:S(2)}) collective-permute-start(bf16[8,48,256]{2,1,0:T(8,128)(2,1)S(1)} %get-tuple-element.23), channel_id=1, source_target_pairs={{0,4},{1,5},{2,6},{3,7},{4,0},{5,1},{6,2},{7,3},{8,12},{9,13},{10,... | collective-permute-start | bytes 589832 | tf_op jit(solution)/shard_map/ppermute | solution.py:418
  110.2 42.8 %copy-start.16 = (bf16[1,2,3072]{2,1,0:T(2,128)(2,1)S(1)}, bf16[1,2,3072]{2,1,0:T(2,128)(2,1)}, u32[]{:S(2)}) copy-start(bf16[1,2,3072]{2,1,0:T(2,128)(2,1)} %param.9) | copy-start | bytes 36868
  110.9 41.4 %all-to-all-start.5 = ((bf16[8,48,128]{2,1,0:T(8,128)(2,1)}), bf16[8,48,128]{2,1,0:T(8,128)(2,1)S(1)}, u32[]{:S(2)}, u32[]{:S(2)}) async-start(bf16[8,48,128]{2,1,0:T(8,128)(2,1)} %convert_element_type.49), calls=%async_computation.5 | async-start | bytes 196608 | tf_op jit(solution)/shard_map/all_to_all | solution.py:279
  152.4 0.7 copy-start.13
  153.1 6.3 %collective-permute-start.9 = (bf16[2,3072]{1,0:T(2,128)(2,1)S(1)}, bf16[2,3072]{1,0:T(2,128)(2,1)S(1)}, u32[]{:S(2)}, u32[]{:S(2)}) collective-permute-start(bf16[2,3072]{1,0:T(2,128)(2,1)S(1)} %add_convert_fusion.1), channel_id=1, source_target_pairs={{448,0},{0,64},{64,128},{128,192},{192,256},{256,320},{320,384},{3... | collective-permute-start | bytes 36872 | tf_op jit(solution)/shard_map/ppermute | solution.py:23
  179.7 5.4 %copy-start.19 = (f32[192]{0:T(256)S(1)}, f32[192]{0:T(256)}, u32[]{:S(2)}) copy-start(f32[192]{0:T(256)} %copy-done.18) | copy-start | bytes 2308
  180.7 13.4 %all-to-all-start.7 = ((bf16[8,16,3072]{2,1,0:T(8,128)(2,1)}), bf16[8,16,3072]{2,1,0:T(8,128)(2,1)S(1)}, u32[]{:S(2)}, u32[]{:S(2)}) async-start(bf16[8,16,3072]{2,1,0:T(8,128)(2,1)} %broadcast_in_dim.55), calls=%async_computation.7 | async-start | bytes 1572864 | tf_op jit(solution)/shard_map/all_to_all | solution.py:272
  194.2 1.3 copy-start.4
  196.7 8.7 %all-to-all-start.8 = ((bf16[4,96,128]{2,1,0:T(8,128)(2,1)}), bf16[4,96,128]{2,1,0:T(8,128)(2,1)}, u32[]{:S(2)}, u32[]{:S(2)}) async-start(bf16[4,96,128]{2,1,0:T(8,128)(2,1)} %shard_map.96), calls=%async_computation.8 | async-start | bytes 196608 | tf_op jit(solution)/shard_map/all_to_all | solution.py:381
  200.6 1.3 copy-start.17
  201.9 3.4 %copy-start.20 = (f32[384]{0:T(512)S(1)}, f32[384]{0:T(512)}, u32[]{:S(2)}) copy-start(f32[384]{0:T(512)} %pad_maximum_fusion.3) | copy-start | bytes 4612
  201.9 3.5 %copy-start.5 = (bf16[8,48,256]{2,1,0:T(8,128)(2,1)S(1)}, bf16[8,48,256]{2,1,0:T(8,128)(2,1)}, u32[]{:S(2)}) copy-start(bf16[8,48,256]{2,1,0:T(8,128)(2,1)} %get-tuple-element.22.near_ref) | copy-start | bytes 589828
  201.9 3.5 %copy-start.7 = (f32[128,1]{1,0:T(8,128)S(1)}, f32[128,1]{1,0:T(8,128)}, u32[]{:S(2)}) copy-start(f32[128,1]{1,0:T(8,128)} %copy-done.6) | copy-start | bytes 1540
  201.9 3.6 %copy-start.14 = (bf16[8,48,256]{2,1,0:T(8,128)(2,1)S(1)}, bf16[8,48,256]{2,1,0:T(8,128)(2,1)}, u32[]{:S(2)}) copy-start(bf16[8,48,256]{2,1,0:T(8,128)(2,1)} %copy-done.13) | copy-start | bytes 589828
  207.7 7.9 %all-to-all-start.9 = ((bf16[4,80,128]{2,1,0:T(8,128)(2,1)}), bf16[4,80,128]{2,1,0:T(8,128)(2,1)S(1)}, u32[]{:S(2)}, u32[]{:S(2)}) async-start(bf16[4,80,128]{2,1,0:T(8,128)(2,1)} %shard_map.97), calls=%async_computation.9 | async-start | bytes 163840 | tf_op jit(solution)/shard_map/all_to_all | solution.py:383
  211.0 4.6 %copy-start.10 = (f32[1,3,3072]{2,0,1:T(1,128)S(1)}, f32[1,3,3072]{2,0,1:T(1,128)}, u32[]{:S(2)}) copy-start(f32[1,3,3072]{2,0,1:T(1,128)} %param.14) | copy-start | bytes 110596
  243.4 11.9 %collective-permute-start.10 = (bf16[2,3072]{1,0:T(2,128)(2,1)S(1)}, bf16[2,3072]{1,0:T(2,128)(2,1)S(1)}, u32[]{:S(2)}, u32[]{:S(2)}) collective-permute-start(bf16[2,3072]{1,0:T(2,128)(2,1)S(1)} %add_convert_fusion), channel_id=1, source_target_pairs={{448,0},{0,64},{64,128},{128,192},{192,256},{256,320},{320,384},{3... | collective-permute-start | bytes 36872 | tf_op jit(solution)/shard_map/ppermute | solution.py:23

commit v13 on v11

--- a/solution.py
+++ b/solution.py
@@ -245,9 +245,10 @@
             ]
             part = lax.ppermute(part, "tp", route)
         by_x.append(part)
-    by_x = jnp.stack(by_x)
-    keep = jnp.where(upper, by_x[:, :, team_width:], by_x[:, :, :team_width])
-    give = jnp.where(upper, by_x[:, :, :team_width], by_x[:, :, team_width:])
+    lower_teams = [part[:, :team_width] for part in by_x]
+    upper_teams = [part[:, team_width:] for part in by_x]
+    keep = [jnp.where(upper, u, l) for l, u in zip(lower_teams, upper_teams)]
+    give = [jnp.where(upper, l, u) for l, u in zip(lower_teams, upper_teams)]
 
     for tick_number in range(TICKS):
         if tick_number == 0:
@@ -255,12 +256,13 @@
             normed = normed.reshape(-1, width)
             route = [(z_count * x + z, z_count * x + partner[z]) for x in xs for z in range(z_count)]
             got = [
-                lax.ppermute(part, "tp", route)
-                for part in (give[: x_count // 2], give[x_count // 2 :])
+                lax.ppermute(jnp.stack(part), "tp", route)
+                for part in (give[:1], give[1:2], give[2:])
             ]
+            normed, got[0] = lax.optimization_barrier((normed, got[0]))
             normed = gathered(normed, along_x)
-            normed, got[0] = lax.optimization_barrier((normed, got[0]))
-            cached = [keep] + got
+            normed, got[1] = lax.optimization_barrier((normed, got[1]))
+            cached = [jnp.stack(keep)] + got
         else:
             block = spread(current, shift_scale, len(hs))
             normed = lax.all_to_all(block, "tp", 0, 0, axis_index_groups=far)

time: 235 us -> 252 us (1.072)
  starting transfers between devices: 90 us -> 99.5 us
  waiting for transfers between devices: 24.5 us -> 32.5 us
  blocking collectives: 103 us -> 99.6 us
    ppermute x2 -> x3, starting transfers between devices: 15.5 us -> 20.3 us  [local(): lax.ppermute(jnp.stack(part), 'tp', route)]
    ppermute x3, waiting for transfers between devices: 0.01 us -> 4.12 us  [local(): part = lax.ppermute(part, 'tp', route)]
    all_to_all x4, blocking collectives: 63.1 us -> 60.2 us  [summed_over(): parts = lax.all_to_all(parts, 'tp', 0, 0, axis_index_groups=groups)]
    ppermute x2 -> x3, waiting for transfers between devices: 3.76 us -> 5.06 us  [local(): lax.ppermute(jnp.stack(part), 'tp', route)]
  transfers between devices with their start and end apart: 12 -> 13, of which waited for: 7 -> 9; matrix products, arithmetic and copies ran while one was open for 3% -> 3% of each run, Pallas kernels for 0% -> 0%
where the time goes in v13:
time: 252 us; the launch traced here: 250 us
  blocking collectives  99.6 us (40%)
  starting transfers between devices  99.5 us (39%)
  waiting for transfers between devices  32.5 us (13%)
  Pallas kernels  6.79 us (3%)
  local copies, waits for them, and re-layouts  4.4 us (2%)
  matrix products  4.35 us (2%)
    all_to_all x4, blocking collectives, summed_over(): parts = lax.all_to_all(parts, 'tp', 0, 0, axis_index_groups=groups)  60.2 us
    ppermute x2, starting transfers between devices, shifted(): lax.ppermute(block, axis, [((i - distance) % size, i) for i in range(size)])  26.4 us
    ppermute x3, starting transfers between devices, local(): lax.ppermute(jnp.stack(part), 'tp', route)  20.3 us
    all_to_all x2, waiting for transfers between devices, local(): parts = lax.all_to_all(parts, 'tp', 0, 0, axis_index_groups=inside)  16.1 us
    all_to_all x1, starting transfers between devices, local(): normed = lax.all_to_all(block, 'tp', 0, 0, axis_index_groups=along_z)  15.7 us
    all_to_all x1, blocking collectives, local(): normed = lax.all_to_all(block, 'tp', 0, 0, axis_index_groups=far)  14.9 us
    all_to_all x2, starting transfers between devices, local(): parts = lax.all_to_all(parts, 'tp', 0, 0, axis_index_groups=inside)  12.7 us
    all_to_all x1, blocking collectives, local(): team = lax.all_to_all(team, 'tp', 0, 0, axis_index_groups=inside)  12.7 us
  transfers between devices with their start and end apart: 13, of which 9 were waited for; matrix products, arithmetic and copies ran while one was open for 3% of the time, Pallas kernels for 0%

profile of v13, /device:TPU:1, one launch (start us, length us, event | category | flops | bytes accessed | tf_op | source)
XLA Modules:
  0.0 250.3 jit_solution(13964817309236469040)
XLA Ops:
  0.0 0.9 copy-done.4
  0.9 0.7 copy-done.12
  1.6 0.9 shard_map.91
  2.5 15.7 %all-to-all-start = ((bf16[16,48,128]{2,1,0:T(8,128)(2,1)}), bf16[16,48,128]{2,1,0:T(8,128)(2,1)S(1)}, u32[]{:S(2)}, u32[]{:S(2)}) async-start(bf16[16,48,128]{2,1,0:T(8,128)(2,1)} %shard_map.91), calls=%async_computation | async-start | bytes 393216 | tf_op jit(solution)/shard_map/all_to_all | solution.py:255
  18.3 0.8 select_bitcast_fusion.5
  19.1 7.1 %collective-permute-start = (bf16[1,48,384]{2,1,0:T(8,128)(2,1)S(1)}, bf16[1,48,384]{2,1,0:T(8,128)(2,1)S(1)}, u32[]{:S(2)}, u32[]{:S(2)}) collective-permute-start(bf16[1,48,384]{2,1,0:T(8,128)(2,1)S(1)} %get-tuple-element.18), channel_id=1, source_target_pairs={{0,12},{1,13},{2,14},{3,15},{4,8},{5,9},{6,10},{7,11},{8,4},{9,5},... | collective-permute-start | bytes 110600 | tf_op jit(solution)/shard_map/ppermute | solution.py:259
  26.3 5.4 %all-to-all-done = bf16[16,48,128]{2,1,0:T(8,128)(2,1)S(1)} async-done(((bf16[16,48,128]{2,1,0:T(8,128)(2,1)}), bf16[16,48,128]{2,1,0:T(8,128)(2,1)S(1)}, u32[]{:S(2)}, u32[]{:S(2)}) %all-to-all-start) | async-done | bytes 196640 | tf_op jit(solution)/shard_map/all_to_all | solution.py:255
  31.8 1.0 broadcast_in_dim.35
  32.8 4.1 %all-to-all-start.1 = ((bf16[4,32,3072]{2,1,0:T(8,128)(2,1)}), bf16[4,32,3072]{2,1,0:T(8,128)(2,1)S(1)}, u32[]{:S(2)}, u32[]{:S(2)}) async-start(bf16[4,32,3072]{2,1,0:T(8,128)(2,1)} %broadcast_in_dim.35), calls=%async_computation.1 | async-start | bytes 1572864 | tf_op jit(solution)/shard_map/all_to_all | solution.py:173
  37.0 0.6 constant_dynamic-slice_fusion.1
  37.6 4.9 %collective-permute-start.3 = (bf16[48,768]{1,0:T(8,128)(2,1)S(1)}, bf16[48,768]{1,0:T(8,128)(2,1)}, u32[]{:S(2)}, u32[]{:S(2)}) collective-permute-start(bf16[48,768]{1,0:T(8,128)(2,1)S(1)} %get-tuple-element.19), channel_id=1, source_target_pairs={{0,32},{1,33},{2,34},{3,35},{4,36},{5,37},{6,38},{7,39},{8,40},{9,... | collective-permute-start | bytes 221192 | tf_op jit(solution)/shard_map/ppermute | solution.py:246
  42.5 2.8 %collective-permute-start.4 = (bf16[48,768]{1,0:T(8,128)(2,1)}, bf16[48,768]{1,0:T(8,128)(2,1)S(1)}, u32[]{:S(2)}, u32[]{:S(2)}) collective-permute-start(bf16[48,768]{1,0:T(8,128)(2,1)} %get-tuple-element.20), channel_id=1, source_target_pairs={{0,48},{1,49},{2,50},{3,51},{4,52},{5,53},{6,54},{7,55},{8,56},{9,... | collective-permute-start | bytes 221192 | tf_op jit(solution)/shard_map/ppermute | solution.py:246
  45.3 2.5 collective-permute-start.1
  48.5 4.1 %collective-permute-done.1 = bf16[48,768]{1,0:T(8,128)(2,1)S(1)} collective-permute-done((bf16[48,768]{1,0:T(8,128)(2,1)S(1)}, bf16[48,768]{1,0:T(8,128)(2,1)S(1)}, u32[]{:S(2)}, u32[]{:S(2)}) %collective-permute-start.1) | collective-permute-done | bytes 73760 | tf_op jit(solution)/shard_map/ppermute | solution.py:246
  52.6 7.8 %collective-permute-start.2 = (bf16[1,48,384]{2,1,0:T(8,128)(2,1)S(1)}, bf16[1,48,384]{2,1,0:T(8,128)(2,1)S(1)}, u32[]{:S(2)}, u32[]{:S(2)}) collective-permute-start(bf16[1,48,384]{2,1,0:T(8,128)(2,1)S(1)} %get-tuple-element.27), channel_id=1, source_target_pairs={{0,12},{1,13},{2,14},{3,15},{4,8},{5,9},{6,10},{7,11},{8,4},{9,5},... | collective-permute-start | bytes 110600 | tf_op jit(solution)/shard_map/ppermute | solution.py:259
  60.6 1.2 collective-permute-done.2.refs_2_
  61.8 1.2 shard_map.92
  63.0 10.1 %all-to-all-start.2 = ((bf16[8,64,128]{2,1,0:T(8,128)(2,1)}), bf16[8,64,128]{2,1,0:T(8,128)(2,1)S(1)}, u32[]{:S(2)}, u32[]{:S(2)}) async-start(bf16[8,64,128]{2,1,0:T(8,128)(2,1)} %shard_map.92), calls=%async_computation.2 | async-start | bytes 262144 | tf_op jit(solution)/shard_map/all_to_all | solution.py:271
  73.2 0.8 select_bitcast_fusion.1
  74.0 5.3 %collective-permute-start.5 = (bf16[2,48,384]{2,1,0:T(8,128)(2,1)S(1)}, bf16[2,48,384]{2,1,0:T(8,128)(2,1)S(1)}, u32[]{:S(2)}, u32[]{:S(2)}) collective-permute-start(bf16[2,48,384]{2,1,0:T(8,128)(2,1)S(1)} %pad_maximum_fusion.1), channel_id=1, source_target_pairs={{0,12},{1,13},{2,14},{3,15},{4,8},{5,9},{6,10},{7,11},{8,4},{9,5},... | collective-permute-start | bytes 221192 | tf_op jit(solution)/shard_map/ppermute | solution.py:259
  79.3 3.9 %collective-permute-done.5.refs_3_ = bf16[2,48,384]{2,1,0:T(8,128)(2,1)S(1)} collective-permute-done((bf16[2,48,384]{2,1,0:T(8,128)(2,1)S(1)}, bf16[2,48,384]{2,1,0:T(8,128)(2,1)S(1)}, u32[]{:S(2)}, u32[]{:S(2)}) %collective-permute-start.5) | collective-permute-done | bytes 73760 | tf_op jit(solution)/shard_map/ppermute | solution.py:259
  83.2 0.2 all-to-all-done.2.team_ref
  83.5 1.5 shard_map.93
  85.0 9.3 %all-to-all-start.3 = ((bf16[8,64,128]{2,1,0:T(8,128)(2,1)}), bf16[8,64,128]{2,1,0:T(8,128)(2,1)S(1)}, u32[]{:S(2)}, u32[]{:S(2)}) async-start(bf16[8,64,128]{2,1,0:T(8,128)(2,1)} %shard_map.93), calls=%async_computation.3 | async-start | bytes 262144 | tf_op jit(solution)/shard_map/all_to_all | solution.py:273
  94.4 1.8 fusion.17
  96.2 0.4 fusion.2.forward_ref
  96.6 8.1 %all-to-all-done.3.parts_ref = bf16[8,64,128]{2,1,0:T(8,128)(2,1)S(1)} async-done(((bf16[8,64,128]{2,1,0:T(8,128)(2,1)}), bf16[8,64,128]{2,1,0:T(8,128)(2,1)S(1)}, u32[]{:S(2)}, u32[]{:S(2)}) %all-to-all-start.3) | async-done | bytes 131104 | tf_op jit(solution)/shard_map/all_to_all | solution.py:273
  104.7 0.4 shard_map.94
  105.1 11.4 %all_to_all.60 = bf16[8,16,3072]{2,1,0:T(8,128)(2,1)S(1)} all-to-all(bf16[8,16,3072]{2,1,0:T(8,128)(2,1)S(1)} %bitcast.64), channel_id=1, replica_groups={{0,1,16,17,32,33,48,49},{2,3,18,19,34,35,50,51},{4,5,20,21,36,37,52,53}..., dimensions={0} | all-to-all | bytes 1572864 | tf_op jit(solution)/shard_map/all_to_all | solution.py:180
  116.6 17.2 %all_to_all.61 = bf16[8,48,128]{2,1,0:T(8,128)(2,1)S(1)} all-to-all(bf16[8,48,128]{2,1,0:T(8,128)(2,1)S(1)} %convert_element_type.46), channel_id=1, replica_groups={{0,2,4,6,8,10,12,14},{1,3,5,7,9,11,13,15},{16,18,20,22,24,26,28,30},{17..., dimensions={0} | all-to-all | bytes 196608 | tf_op jit(solution)/shard_map/all_to_all | solution.py:180
  133.9 12.8 %collective-permute-start.6 = (bf16[2,3072]{1,0:T(2,128)(2,1)S(1)}, bf16[2,3072]{1,0:T(2,128)(2,1)S(1)}, u32[]{:S(2)}, u32[]{:S(2)}) collective-permute-start(bf16[2,3072]{1,0:T(2,128)(2,1)S(1)} %add_convert_fusion.1), channel_id=1, source_target_pairs={{448,0},{0,64},{64,128},{128,192},{192,256},{256,320},{320,384},{3... | collective-permute-start | bytes 36872 | tf_op jit(solution)/shard_map/ppermute | solution.py:23
  146.7 0.8 collective-permute-done.6.rows_ref
  147.6 0.2 shard_map.95
  147.8 14.9 %all_to_all.62 = bf16[8,48,128]{2,1,0:T(8,128)(2,1)S(1)} all-to-all(bf16[8,48,128]{2,1,0:T(8,128)(2,1)S(1)} %shard_map.95), channel_id=1, replica_groups={{0,2,4,6,8,10,12,14},{1,3,5,7,9,11,13,15},{16,18,20,22,24,26,28,30},{17..., dimensions={0} | all-to-all | bytes 196608 | tf_op jit(solution)/shard_map/all_to_all | solution.py:268
  162.9 11.9 %all_to_all.63 = bf16[8,16,3072]{2,1,0:T(8,128)(2,1)S(1)} all-to-all(bf16[8,16,3072]{2,1,0:T(8,128)(2,1)S(1)} %broadcast_in_dim.40), channel_id=1, replica_groups={{0,1,16,17,32,33,48,49},{2,3,18,19,34,35,50,51},{4,5,20,21,36,37,52,53}..., dimensions={0} | all-to-all | bytes 1572864 | tf_op jit(solution)/shard_map/all_to_all | solution.py:173
  174.8 0.6 shard_map.96
  175.3 12.7 %all_to_all.64.team_ref = bf16[8,64,128]{2,1,0:T(8,128)(2,1)S(1)} all-to-all(bf16[8,64,128]{2,1,0:T(8,128)(2,1)S(1)} %shard_map.96), channel_id=1, replica_groups={{0,1,2,3,4,5,6,7},{8,9,10,11,12,13,14,15},{16,17,18,19,20,21,22,23},{24..., dimensions={0} | all-to-all | bytes 262144 | tf_op jit(solution)/shard_map/all_to_all | solution.py:271
  188.0 1.5 shard_map.97
  189.5 3.4 %all-to-all-start.9 = ((bf16[8,64,128]{2,1,0:T(8,128)(2,1)}), bf16[8,64,128]{2,1,0:T(8,128)(2,1)S(1)}, u32[]{:S(2)}, u32[]{:S(2)}) async-start(bf16[8,64,128]{2,1,0:T(8,128)(2,1)} %shard_map.97), calls=%async_computation.9 | async-start | bytes 262144 | tf_op jit(solution)/shard_map/all_to_all | solution.py:273
  192.9 1.8 fusion.29
  194.6 0.4 fusion.forward_ref
  195.0 8.0 %all-to-all-done.9.parts_ref = bf16[8,64,128]{2,1,0:T(8,128)(2,1)S(1)} async-done(((bf16[8,64,128]{2,1,0:T(8,128)(2,1)}), bf16[8,64,128]{2,1,0:T(8,128)(2,1)S(1)}, u32[]{:S(2)}, u32[]{:S(2)}) %all-to-all-start.9) | async-done | bytes 131104 | tf_op jit(solution)/shard_map/all_to_all | solution.py:273
  203.1 0.4 shard_map.98
  203.5 11.4 %all_to_all.65 = bf16[8,16,3072]{2,1,0:T(8,128)(2,1)S(1)} all-to-all(bf16[8,16,3072]{2,1,0:T(8,128)(2,1)S(1)} %bitcast.63), channel_id=1, replica_groups={{0,1,16,17,32,33,48,49},{2,3,18,19,34,35,50,51},{4,5,20,21,36,37,52,53}..., dimensions={0} | all-to-all | bytes 1572864 | tf_op jit(solution)/shard_map/all_to_all | solution.py:180
  215.1 20.2 %all_to_all.66 = bf16[8,48,128]{2,1,0:T(8,128)(2,1)S(1)} all-to-all(bf16[8,48,128]{2,1,0:T(8,128)(2,1)S(1)} %convert_element_type.51), channel_id=1, replica_groups={{0,2,4,6,8,10,12,14},{1,3,5,7,9,11,13,15},{16,18,20,22,24,26,28,30},{17..., dimensions={0} | all-to-all | bytes 196608 | tf_op jit(solution)/shard_map/all_to_all | solution.py:180
  235.4 13.5 %collective-permute-start.7 = (bf16[2,3072]{1,0:T(2,128)(2,1)S(1)}, bf16[2,3072]{1,0:T(2,128)(2,1)S(1)}, u32[]{:S(2)}, u32[]{:S(2)}) collective-permute-start(bf16[2,3072]{1,0:T(2,128)(2,1)S(1)} %add_convert_fusion), channel_id=1, source_target_pairs={{448,0},{0,64},{64,128},{128,192},{192,256},{256,320},{320,384},{3... | collective-permute-start | bytes 36872 | tf_op jit(solution)/shard_map/ppermute | solution.py:23
  248.9 0.8 collective-permute-done.7
  249.7 0.6 copy.16
  (55 shorter events, 1.0 us)
Async XLA Ops:
  0.0 96.2 %copy-start = (bf16[1,192,3072]{2,1,0:T(8,128)(2,1)S(1)}, bf16[1,192,3072]{2,1,0:T(8,128)(2,1)}, u32[]{:S(2)}) copy-start(bf16[1,192,3072]{2,1,0:T(8,128)(2,1)} %param.13) | copy-start | bytes 3538948
  0.0 0.9 copy-start.4
  0.9 0.7 copy-start.12
  2.5 29.2 %all-to-all-start = ((bf16[16,48,128]{2,1,0:T(8,128)(2,1)}), bf16[16,48,128]{2,1,0:T(8,128)(2,1)S(1)}, u32[]{:S(2)}, u32[]{:S(2)}) async-start(bf16[16,48,128]{2,1,0:T(8,128)(2,1)} %shard_map.91), calls=%async_computation | async-start | bytes 393216 | tf_op jit(solution)/shard_map/all_to_all | solution.py:255
  19.1 12.7 %collective-permute-start = (bf16[1,48,384]{2,1,0:T(8,128)(2,1)S(1)}, bf16[1,48,384]{2,1,0:T(8,128)(2,1)S(1)}, u32[]{:S(2)}, u32[]{:S(2)}) collective-permute-start(bf16[1,48,384]{2,1,0:T(8,128)(2,1)S(1)} %get-tuple-element.18), channel_id=1, source_target_pairs={{0,12},{1,13},{2,14},{3,15},{4,8},{5,9},{6,10},{7,11},{8,4},{9,5},... | collective-permute-start | bytes 110600 | tf_op jit(solution)/shard_map/ppermute | solution.py:259
  31.8 5.2 %copy-start.14 = (bf16[1,2,24,3072]{3,2,1,0:T(8,128)(2,1)S(1)}, bf16[1,2,24,3072]{3,2,1,0:T(8,128)(2,1)}, u32[]{:S(2)}) copy-start(bf16[1,2,24,3072]{3,2,1,0:T(8,128)(2,1)} %param.16) | copy-start | bytes 884740
  31.8 51.7 %copy-start.8 = (bf16[1,48,384]{2,1,0:T(8,128)(2,1)}, bf16[1,48,384]{2,1,0:T(8,128)(2,1)S(1)}, u32[]{:S(2)}) copy-start(bf16[1,48,384]{2,1,0:T(8,128)(2,1)S(1)} %collective-permute-done.refs_1_) | copy-start | bytes 110596
  32.8 15.0 %copy-start.15 = (f32[1,2,128]{2,1,0:T(2,128)S(1)}, f32[1,2,128]{2,1,0:T(2,128)}, u32[]{:S(2)}) copy-start(f32[1,2,128]{2,1,0:T(2,128)} %param.15) | copy-start | bytes 3076
  32.8 29.0 %copy-start.1 = (bf16[1,3,48,3072]{3,2,1,0:T(8,128)(2,1)S(1)}, bf16[1,3,48,3072]{3,2,1,0:T(8,128)(2,1)}, u32[]{:S(2)}) copy-start(bf16[1,3,48,3072]{3,2,1,0:T(8,128)(2,1)} %param.10) | copy-start | bytes 2654212
  32.8 29.0 %all-to-all-start.1 = ((bf16[4,32,3072]{2,1,0:T(8,128)(2,1)}), bf16[4,32,3072]{2,1,0:T(8,128)(2,1)S(1)}, u32[]{:S(2)}, u32[]{:S(2)}) async-start(bf16[4,32,3072]{2,1,0:T(8,128)(2,1)} %broadcast_in_dim.35), calls=%async_computation.1 | async-start | bytes 1572864 | tf_op jit(solution)/shard_map/all_to_all | solution.py:173
  37.6 35.6 %collective-permute-start.3 = (bf16[48,768]{1,0:T(8,128)(2,1)S(1)}, bf16[48,768]{1,0:T(8,128)(2,1)}, u32[]{:S(2)}, u32[]{:S(2)}) collective-permute-start(bf16[48,768]{1,0:T(8,128)(2,1)S(1)} %get-tuple-element.19), channel_id=1, source_target_pairs={{0,32},{1,33},{2,34},{3,35},{4,36},{5,37},{6,38},{7,39},{8,40},{9,... | collective-permute-start | bytes 221192 | tf_op jit(solution)/shard_map/ppermute | solution.py:246
  42.5 31.5 %collective-permute-start.4 = (bf16[48,768]{1,0:T(8,128)(2,1)}, bf16[48,768]{1,0:T(8,128)(2,1)S(1)}, u32[]{:S(2)}, u32[]{:S(2)}) collective-permute-start(bf16[48,768]{1,0:T(8,128)(2,1)} %get-tuple-element.20), channel_id=1, source_target_pairs={{0,48},{1,49},{2,50},{3,51},{4,52},{5,53},{6,54},{7,55},{8,56},{9,... | collective-permute-start | bytes 221192 | tf_op jit(solution)/shard_map/ppermute | solution.py:246
  45.3 7.3 %collective-permute-start.1 = (bf16[48,768]{1,0:T(8,128)(2,1)S(1)}, bf16[48,768]{1,0:T(8,128)(2,1)S(1)}, u32[]{:S(2)}, u32[]{:S(2)}) collective-permute-start(bf16[48,768]{1,0:T(8,128)(2,1)S(1)} %get-tuple-element.21), channel_id=1, source_target_pairs={{0,16},{1,17},{2,18},{3,19},{4,20},{5,21},{6,22},{7,23},{8,24},{9,... | collective-permute-start | bytes 221192 | tf_op jit(solution)/shard_map/ppermute | solution.py:246
  52.6 9.2 %collective-permute-start.2 = (bf16[1,48,384]{2,1,0:T(8,128)(2,1)S(1)}, bf16[1,48,384]{2,1,0:T(8,128)(2,1)S(1)}, u32[]{:S(2)}, u32[]{:S(2)}) collective-permute-start(bf16[1,48,384]{2,1,0:T(8,128)(2,1)S(1)} %get-tuple-element.27), channel_id=1, source_target_pairs={{0,12},{1,13},{2,14},{3,15},{4,8},{5,9},{6,10},{7,11},{8,4},{9,5},... | collective-permute-start | bytes 110600 | tf_op jit(solution)/shard_map/ppermute | solution.py:259
  61.8 21.7 %copy-start.10 = (bf16[1,48,384]{2,1,0:T(8,128)(2,1)}, bf16[1,48,384]{2,1,0:T(8,128)(2,1)S(1)}, u32[]{:S(2)}) copy-start(bf16[1,48,384]{2,1,0:T(8,128)(2,1)S(1)} %collective-permute-done.2.refs_2_) | copy-start | bytes 110596
  63.0 20.4 %all-to-all-start.2 = ((bf16[8,64,128]{2,1,0:T(8,128)(2,1)}), bf16[8,64,128]{2,1,0:T(8,128)(2,1)S(1)}, u32[]{:S(2)}, u32[]{:S(2)}) async-start(bf16[8,64,128]{2,1,0:T(8,128)(2,1)} %shard_map.92), calls=%async_computation.2 | async-start | bytes 262144 | tf_op jit(solution)/shard_map/all_to_all | solution.py:271
  74.0 9.2 %collective-permute-start.5 = (bf16[2,48,384]{2,1,0:T(8,128)(2,1)S(1)}, bf16[2,48,384]{2,1,0:T(8,128)(2,1)S(1)}, u32[]{:S(2)}, u32[]{:S(2)}) collective-permute-start(bf16[2,48,384]{2,1,0:T(8,128)(2,1)S(1)} %pad_maximum_fusion.1), channel_id=1, source_target_pairs={{0,12},{1,13},{2,14},{3,15},{4,8},{5,9},{6,10},{7,11},{8,4},{9,5},... | collective-permute-start | bytes 221192 | tf_op jit(solution)/shard_map/ppermute | solution.py:259
  83.2 11.2 %copy-start.6 = (bf16[2,48,384]{2,1,0:T(8,128)(2,1)}, bf16[2,48,384]{2,1,0:T(8,128)(2,1)S(1)}, u32[]{:S(2)}) copy-start(bf16[2,48,384]{2,1,0:T(8,128)(2,1)S(1)} %collective-permute-done.5.refs_3_) | copy-start | bytes 221188
  85.0 19.6 %all-to-all-start.3 = ((bf16[8,64,128]{2,1,0:T(8,128)(2,1)}), bf16[8,64,128]{2,1,0:T(8,128)(2,1)S(1)}, u32[]{:S(2)}, u32[]{:S(2)}) async-start(bf16[8,64,128]{2,1,0:T(8,128)(2,1)} %shard_map.93), calls=%async_computation.3 | async-start | bytes 262144 | tf_op jit(solution)/shard_map/all_to_all | solution.py:273
  96.2 8.5 %copy-start.3 = (bf16[1,48,3072]{2,1,0:T(8,128)(2,1)S(1)}, bf16[1,48,3072]{2,1,0:T(8,128)(2,1)}, u32[]{:S(2)}) copy-start(bf16[1,48,3072]{2,1,0:T(8,128)(2,1)} %param.12) | copy-start | bytes 884740
  96.2 8.5 %copy-start.5 = (f32[1,3,3072]{2,0,1:T(1,128)S(1)}, f32[1,3,3072]{2,0,1:T(1,128)}, u32[]{:S(2)}) copy-start(f32[1,3,3072]{2,0,1:T(1,128)} %param.14) | copy-start | bytes 110596
  105.1 28.8 %copy-start.13 = (bf16[1,2,3072]{2,1,0:T(2,128)(2,1)S(1)}, bf16[1,2,3072]{2,1,0:T(2,128)(2,1)}, u32[]{:S(2)}) copy-start(bf16[1,2,3072]{2,1,0:T(2,128)(2,1)} %param.9) | copy-start | bytes 36868
  133.9 13.7 %collective-permute-start.6 = (bf16[2,3072]{1,0:T(2,128)(2,1)S(1)}, bf16[2,3072]{1,0:T(2,128)(2,1)S(1)}, u32[]{:S(2)}, u32[]{:S(2)}) collective-permute-start(bf16[2,3072]{1,0:T(2,128)(2,1)S(1)} %add_convert_fusion.1), channel_id=1, source_target_pairs={{448,0},{0,64},{64,128},{128,192},{192,256},{256,320},{320,384},{3... | collective-permute-start | bytes 36872 | tf_op jit(solution)/shard_map/ppermute | solution.py:23
  162.8 12.0 %copy-start.2 = (bf16[1,3,48,3072]{3,2,1,0:T(8,128)(2,1)S(1)}, bf16[1,3,48,3072]{3,2,1,0:T(8,128)(2,1)}, u32[]{:S(2)}) copy-start(bf16[1,3,48,3072]{3,2,1,0:T(8,128)(2,1)} %param.10) | copy-start | bytes 2654212
  174.7 13.2 %copy-start.7 = (bf16[2,48,384]{2,1,0:T(8,128)(2,1)S(1)}, bf16[2,48,384]{2,1,0:T(8,128)(2,1)}, u32[]{:S(2)}) copy-start(bf16[2,48,384]{2,1,0:T(8,128)(2,1)} %copy-done.6) | copy-start | bytes 221188
  174.7 13.2 %copy-start.9 = (bf16[1,48,384]{2,1,0:T(8,128)(2,1)S(1)}, bf16[1,48,384]{2,1,0:T(8,128)(2,1)}, u32[]{:S(2)}) copy-start(bf16[1,48,384]{2,1,0:T(8,128)(2,1)} %copy-done.8) | copy-start | bytes 110596
  174.8 13.2 %copy-start.11 = (bf16[1,48,384]{2,1,0:T(8,128)(2,1)S(1)}, bf16[1,48,384]{2,1,0:T(8,128)(2,1)}, u32[]{:S(2)}) copy-start(bf16[1,48,384]{2,1,0:T(8,128)(2,1)} %copy-done.10) | copy-start | bytes 110596
  189.5 13.6 %all-to-all-start.9 = ((bf16[8,64,128]{2,1,0:T(8,128)(2,1)}), bf16[8,64,128]{2,1,0:T(8,128)(2,1)S(1)}, u32[]{:S(2)}, u32[]{:S(2)}) async-start(bf16[8,64,128]{2,1,0:T(8,128)(2,1)} %shard_map.97), calls=%async_computation.9 | async-start | bytes 262144 | tf_op jit(solution)/shard_map/all_to_all | solution.py:273
  235.4 14.4 %collective-permute-start.7 = (bf16[2,3072]{1,0:T(2,128)(2,1)S(1)}, bf16[2,3072]{1,0:T(2,128)(2,1)S(1)}, u32[]{:S(2)}, u32[]{:S(2)}) collective-permute-start(bf16[2,3072]{1,0:T(2,128)(2,1)S(1)} %add_convert_fusion), channel_id=1, source_target_pairs={{448,0},{0,64},{64,128},{128,192},{192,256},{256,320},{320,384},{3... | collective-permute-start | bytes 36872 | tf_op jit(solution)/shard_map/ppermute | solution.py:23

commit v14 on v11

--- a/solution.py
+++ b/solution.py
@@ -196,8 +196,6 @@
     member = tp_index % TEAM
     z_count, x_count = 2 * TEAM, tp_count // (2 * TEAM)
     xs, hs, two = range(x_count), range(z_count // 2), range(2)
-    along_z = [[z_count * x + 2 * h + l for l in two for h in hs] for x in xs]
-    along_x = [[z_count * x + z for x in xs] for z in range(z_count)]
     far = [[z_count * x + 2 * h + l for h in hs] for x in xs for l in two]
     blocks = [[z_count * x + 2 * h + l for x in xs for l in two] for h in hs]
     inside = [[TEAM * t + m for m in range(TEAM)] for t in range(teams)]
@@ -209,10 +207,9 @@
     weight_down = w_mlp_out[0]
 
     half_team = TEAM // 2
-    partner = [
-        z + TEAM + half_team if z < half_team else z + half_team if z < TEAM
-        else z - half_team if z < TEAM + half_team else z - TEAM - half_team
-        for z in range(z_count)
+    offset = [TEAM + half_team if m < half_team else half_team for m in range(TEAM)]
+    across = [
+        [z_count * x + m + half * offset[m] for x in xs for half in two] for m in range(TEAM)
     ]
     x_here, z_here = tp_index // z_count, tp_index % z_count
     z_partner = jnp.where(
@@ -220,51 +217,28 @@
         z_here + jnp.where(z_here < half_team, TEAM + half_team, half_team),
         z_here - jnp.where(z_here < TEAM + half_team, half_team, TEAM + half_team),
     )
-    upper = z_here >= TEAM
     slot = jnp.arange(teams * ctx_local, dtype=jnp.int32)
-    own_z = slot < x_count * ctx_local
-    source = z_count * ((x_here - slot // ctx_local % x_count) % x_count)
-    source = source + jnp.where(own_z, z_here, z_partner)
+    block = slot // ctx_local
+    z_block = jnp.where(block % 2 == 0, jnp.minimum(z_here, z_partner), jnp.maximum(z_here, z_partner))
+    source = z_count * (block // 2) + z_block
     position = ctx_local * source + slot % ctx_local
     cached_mask = ((position >= TXT) | (position < text_len[0])).astype(f32)
     cached_mask = jnp.broadcast_to(cached_mask[:, None], (teams * ctx_local, LANES))
 
     current = in_flight[0]
-    block = spread(current, shift_scale, z_count)
+    block = spread(current, shift_scale, len(hs))
     block, flat = lax.optimization_barrier((block, context_kv[0]))
-    flat = flat.reshape(2 * ctx_local, width)
-    by_x = []
-    for step in range(x_count):
-        part = lax.dynamic_slice_in_dim(
-            flat, (x_here + step) % x_count * 2 * team_width, 2 * team_width, 1
-        )
-        if step:
-            route = [
-                (z_count * x + z, z_count * ((x + step) % x_count) + z)
-                for x in range(x_count) for z in range(z_count)
-            ]
-            part = lax.ppermute(part, "tp", route)
-        by_x.append(part)
-    by_x = jnp.stack(by_x)
-    keep = jnp.where(upper, by_x[:, :, team_width:], by_x[:, :, :team_width])
-    give = jnp.where(upper, by_x[:, :, :team_width], by_x[:, :, team_width:])
+    by_team = flat.reshape(2 * ctx_local, teams, team_width).transpose(1, 0, 2)
 
     for tick_number in range(TICKS):
+        if tick_number:
+            block = spread(current, shift_scale, len(hs))
+        normed = lax.all_to_all(block, "tp", 0, 0, axis_index_groups=far).reshape(-1, width)
         if tick_number == 0:
-            normed = lax.all_to_all(block, "tp", 0, 0, axis_index_groups=along_z)
-            normed = normed.reshape(-1, width)
-            route = [(z_count * x + z, z_count * x + partner[z]) for x in xs for z in range(z_count)]
-            got = [
-                lax.ppermute(part, "tp", route)
-                for part in (give[: x_count // 2], give[x_count // 2 :])
-            ]
-            normed = gathered(normed, along_x)
-            normed, got[0] = lax.optimization_barrier((normed, got[0]))
-            cached = [keep] + got
-        else:
-            block = spread(current, shift_scale, len(hs))
-            normed = lax.all_to_all(block, "tp", 0, 0, axis_index_groups=far)
-            normed = gathered(normed.reshape(-1, width), blocks)
+            normed, by_team = lax.optimization_barrier((normed, by_team))
+            cached = [lax.all_to_all(by_team, "tp", 0, 0, axis_index_groups=across)]
+            normed, cached = lax.optimization_barrier((normed, cached))
+        normed = gathered(normed, blocks)
         team = project(normed, weight_qkv)
         team = lax.all_to_all(team, "tp", 0, 0, axis_index_groups=inside)
         parts = attend(team, cached, cached_mask, gains)

time: 235 us -> 245 us (1.043)
  starting transfers between devices: 90 us -> 53.3 us
  blocking collectives: 103 us -> 135 us
  waiting for transfers between devices: 24.5 us -> 39.1 us
    ppermute x5 -> x0, starting transfers between devices: 24.8 us -> none  [the longest x2 15.5 us: local(): lax.ppermute(part, 'tp', route)]
    all_to_all x1 -> x2, blocking collectives: 14.9 us -> 32.7 us  [the longest x1 17.7 us: local(): cached = [lax.all_to_all(by_team, 'tp', 0, 0, axis_index_groups=across)]]
    all_to_all x1 -> x2, blocking collectives: 11.9 us -> 26.9 us  [gathered(): spread = lax.all_to_all(spread, 'tp', 0, 0, axis_index_groups=groups)]
    all_to_all x1, waiting for transfers between devices: 0.01 us -> 9.48 us  [local(): team = lax.all_to_all(team, 'tp', 0, 0, axis_index_groups=inside)]
    all_to_all x2 -> x1, waiting for transfers between devices: 2.92 us -> 11.6 us  [local(): lax.all_to_all(block, 'tp', 0, 0, axis_index_groups=far).reshape(-1, width)]
    ppermute x2, starting transfers between devices: 24.3 us -> 18.6 us  [shifted(): lax.ppermute(block, axis, [((i - distance) % size, i) for i in range(size)])]
    all_to_all x2 -> x1, starting transfers between devices: 19.9 us -> 15.6 us  [local(): lax.all_to_all(block, 'tp', 0, 0, axis_index_groups=far).reshape(-1, width)]
    all_to_all x2, starting transfers between devices: 13 us -> 8.81 us  [local(): parts = lax.all_to_all(parts, 'tp', 0, 0, axis_index_groups=inside)]
  transfers between devices with their start and end apart: 12 -> 6, of which waited for: 7 -> 6; matrix products, arithmetic and copies ran while one was open for 3% -> 2% of each run, Pallas kernels for 0% -> 0%
where the time goes in v14:
time: 245 us; the launch traced here: 244 us
  blocking collectives  135 us (55%)
  starting transfers between devices  53.3 us (22%)
  waiting for transfers between devices  39.1 us (16%)
  Pallas kernels  7.58 us (3%)
  matrix products  4.33 us (2%)
  local copies, waits for them, and re-layouts  3.81 us (2%)
    all_to_all x4, blocking collectives, summed_over(): parts = lax.all_to_all(parts, 'tp', 0, 0, axis_index_groups=groups)  62.2 us
    all_to_all x2, blocking collectives, gathered(): spread = lax.all_to_all(spread, 'tp', 0, 0, axis_index_groups=groups)  26.9 us
    ppermute x2, starting transfers between devices, shifted(): lax.ppermute(block, axis, [((i - distance) % size, i) for i in range(size)])  18.6 us
    all_to_all x1, blocking collectives, local(): cached = [lax.all_to_all(by_team, 'tp', 0, 0, axis_index_groups=across)]  17.7 us
    all_to_all x2, waiting for transfers between devices, local(): parts = lax.all_to_all(parts, 'tp', 0, 0, axis_index_groups=inside)  16.3 us
    all_to_all x1, starting transfers between devices, local(): lax.all_to_all(block, 'tp', 0, 0, axis_index_groups=far).reshape(-1, width)  15.6 us
    all_to_all x1, blocking collectives, local(): lax.all_to_all(block, 'tp', 0, 0, axis_index_groups=far).reshape(-1, width)  15 us
    all_to_all x1, blocking collectives, local(): team = lax.all_to_all(team, 'tp', 0, 0, axis_index_groups=inside)  13.1 us
  transfers between devices with their start and end apart: 6, of which 6 were waited for; matrix products, arithmetic and copies ran while one was open for 2% of the time, Pallas kernels for 0%

profile of v14, /device:TPU:1, one launch (start us, length us, event | category | flops | bytes accessed | tf_op | source)
XLA Modules:
  0.0 244.2 jit_solution(11535420646860001654)
XLA Ops:
  0.0 0.9 copy-done.4
  0.9 0.7 copy-done.6
  1.6 0.9 shard_map.91
  2.5 15.6 %all-to-all-start = ((bf16[8,48,128]{2,1,0:T(8,128)(2,1)}), bf16[8,48,128]{2,1,0:T(8,128)(2,1)S(1)}, u32[]{:S(2)}, u32[]{:S(2)}) async-start(bf16[8,48,128]{2,1,0:T(8,128)(2,1)} %shard_map.91), calls=%async_computation | async-start | bytes 196608 | tf_op jit(solution)/shard_map/all_to_all | solution.py:236
  18.1 1.0 copy.18
  19.1 11.6 %all-to-all-done = bf16[8,48,128]{2,1,0:T(8,128)(2,1)S(1)} async-done(((bf16[8,48,128]{2,1,0:T(8,128)(2,1)}), bf16[8,48,128]{2,1,0:T(8,128)(2,1)S(1)}, u32[]{:S(2)}, u32[]{:S(2)}) %all-to-all-start) | async-done | bytes 98336 | tf_op jit(solution)/shard_map/all_to_all | solution.py:236
  30.8 17.7 %all_to_all.65.refs_0_ = bf16[8,48,384]{2,1,0:T(8,128)(2,1)S(1)} all-to-all(bf16[8,48,384]{2,1,0:T(8,128)(2,1)S(1)} %bitcast.61), channel_id=1, replica_groups={{0,12,16,28,32,44,48,60},{1,13,17,29,33,45,49,61},{2,14,18,30,34,46,50,..., dimensions={0} | all-to-all | bytes 589824 | tf_op jit(solution)/shard_map/all_to_all | solution.py:239
  48.5 0.1 broadcast_in_dim.35
  48.6 15.4 %all_to_all.66 = bf16[8,16,3072]{2,1,0:T(8,128)(2,1)S(1)} all-to-all(bf16[8,16,3072]{2,1,0:T(8,128)(2,1)S(1)} %broadcast_in_dim.35), channel_id=1, replica_groups={{0,1,16,17,32,33,48,49},{2,3,18,19,34,35,50,51},{4,5,20,21,36,37,52,53}..., dimensions={0} | all-to-all | bytes 1572864 | tf_op jit(solution)/shard_map/all_to_all | solution.py:173
  64.0 1.2 shard_map.92
  65.2 10.2 %all-to-all-start.3 = ((bf16[8,64,128]{2,1,0:T(8,128)(2,1)}), bf16[8,64,128]{2,1,0:T(8,128)(2,1)S(1)}, u32[]{:S(2)}, u32[]{:S(2)}) async-start(bf16[8,64,128]{2,1,0:T(8,128)(2,1)} %shard_map.92), calls=%async_computation.3 | async-start | bytes 262144 | tf_op jit(solution)/shard_map/all_to_all | solution.py:243
  76.1 0.1 copy.16.gain_q_ref
  76.2 9.5 %all-to-all-done.3.team_ref = bf16[8,64,128]{2,1,0:T(8,128)(2,1)S(1)} async-done(((bf16[8,64,128]{2,1,0:T(8,128)(2,1)}), bf16[8,64,128]{2,1,0:T(8,128)(2,1)S(1)}, u32[]{:S(2)}, u32[]{:S(2)}) %all-to-all-start.3) | async-done | bytes 131104 | tf_op jit(solution)/shard_map/all_to_all | solution.py:243
  85.7 0.1 broadcast_in_dim.38.mask_ref
  85.8 1.5 shard_map.93
  87.3 5.4 %all-to-all-start.4 = ((bf16[8,64,128]{2,1,0:T(8,128)(2,1)}), bf16[8,64,128]{2,1,0:T(8,128)(2,1)}, u32[]{:S(2)}, u32[]{:S(2)}) async-start(bf16[8,64,128]{2,1,0:T(8,128)(2,1)} %shard_map.93), calls=%async_computation.4 | async-start | bytes 262144 | tf_op jit(solution)/shard_map/all_to_all | solution.py:245
  92.7 1.8 fusion.17
  94.5 0.0 copy-start.3
  94.5 0.0 copy-start.5
  94.5 0.4 fusion.2.forward_ref
  94.9 8.3 %all-to-all-done.4.parts_ref = bf16[8,64,128]{2,1,0:T(8,128)(2,1)} async-done(((bf16[8,64,128]{2,1,0:T(8,128)(2,1)}), bf16[8,64,128]{2,1,0:T(8,128)(2,1)}, u32[]{:S(2)}, u32[]{:S(2)}) %all-to-all-start.4) | async-done | bytes 131104 | tf_op jit(solution)/shard_map/all_to_all | solution.py:245
  103.2 1.3 shard_map.94
  104.5 11.8 %all_to_all.67 = bf16[8,16,3072]{2,1,0:T(8,128)(2,1)S(1)} all-to-all(bf16[8,16,3072]{2,1,0:T(8,128)(2,1)S(1)} %bitcast.53), channel_id=1, replica_groups={{0,1,16,17,32,33,48,49},{2,3,18,19,34,35,50,51},{4,5,20,21,36,37,52,53}..., dimensions={0} | all-to-all | bytes 1572864 | tf_op jit(solution)/shard_map/all_to_all | solution.py:180
  116.3 0.1 reduce_sum.42
  116.4 0.1 convert_element_type.46
  116.5 19.4 %all_to_all.68 = bf16[8,48,128]{2,1,0:T(8,128)(2,1)S(1)} all-to-all(bf16[8,48,128]{2,1,0:T(8,128)(2,1)S(1)} %convert_element_type.46), channel_id=1, replica_groups={{0,2,4,6,8,10,12,14},{1,3,5,7,9,11,13,15},{16,18,20,22,24,26,28,30},{17..., dimensions={0} | all-to-all | bytes 196608 | tf_op jit(solution)/shard_map/all_to_all | solution.py:180
  136.0 5.3 %collective-permute-start = (bf16[2,3072]{1,0:T(2,128)(2,1)S(1)}, bf16[2,3072]{1,0:T(2,128)(2,1)S(1)}, u32[]{:S(2)}, u32[]{:S(2)}) collective-permute-start(bf16[2,3072]{1,0:T(2,128)(2,1)S(1)} %add_convert_fusion.1), channel_id=1, source_target_pairs={{448,0},{0,64},{64,128},{128,192},{192,256},{256,320},{320,384},{3... | collective-permute-start | bytes 36872 | tf_op jit(solution)/shard_map/ppermute | solution.py:23
  141.4 0.8 collective-permute-done.rows_ref
  142.2 0.2 shard_map.95
  142.4 15.0 %all_to_all.69 = bf16[8,48,128]{2,1,0:T(8,128)(2,1)S(1)} all-to-all(bf16[8,48,128]{2,1,0:T(8,128)(2,1)S(1)} %shard_map.95), channel_id=1, replica_groups={{0,2,4,6,8,10,12,14},{1,3,5,7,9,11,13,15},{16,18,20,22,24,26,28,30},{17..., dimensions={0} | all-to-all | bytes 196608 | tf_op jit(solution)/shard_map/all_to_all | solution.py:236
  157.5 0.0 copy-start.2
  157.5 0.1 broadcast_in_dim.40
  157.6 11.5 %all_to_all.70 = bf16[8,16,3072]{2,1,0:T(8,128)(2,1)S(1)} all-to-all(bf16[8,16,3072]{2,1,0:T(8,128)(2,1)S(1)} %broadcast_in_dim.40), channel_id=1, replica_groups={{0,1,16,17,32,33,48,49},{2,3,18,19,34,35,50,51},{4,5,20,21,36,37,52,53}..., dimensions={0} | all-to-all | bytes 1572864 | tf_op jit(solution)/shard_map/all_to_all | solution.py:173
  169.1 0.6 shard_map.96
  169.7 13.1 %all_to_all.71.team_ref = bf16[8,64,128]{2,1,0:T(8,128)(2,1)S(1)} all-to-all(bf16[8,64,128]{2,1,0:T(8,128)(2,1)S(1)} %shard_map.96), channel_id=1, replica_groups={{0,1,2,3,4,5,6,7},{8,9,10,11,12,13,14,15},{16,17,18,19,20,21,22,23},{24..., dimensions={0} | all-to-all | bytes 262144 | tf_op jit(solution)/shard_map/all_to_all | solution.py:243
  182.7 1.5 shard_map.97
  184.2 3.4 %all-to-all-start.10 = ((bf16[8,64,128]{2,1,0:T(8,128)(2,1)}), bf16[8,64,128]{2,1,0:T(8,128)(2,1)S(1)}, u32[]{:S(2)}, u32[]{:S(2)}) async-start(bf16[8,64,128]{2,1,0:T(8,128)(2,1)} %shard_map.97), calls=%async_computation.10 | async-start | bytes 262144 | tf_op jit(solution)/shard_map/all_to_all | solution.py:245
  187.6 1.8 fusion.29
  189.3 0.4 fusion.forward_ref
  189.7 8.1 %all-to-all-done.10.parts_ref = bf16[8,64,128]{2,1,0:T(8,128)(2,1)S(1)} async-done(((bf16[8,64,128]{2,1,0:T(8,128)(2,1)}), bf16[8,64,128]{2,1,0:T(8,128)(2,1)S(1)}, u32[]{:S(2)}, u32[]{:S(2)}) %all-to-all-start.10) | async-done | bytes 131104 | tf_op jit(solution)/shard_map/all_to_all | solution.py:245
  197.8 0.4 shard_map.98
  198.2 11.4 %all_to_all.72 = bf16[8,16,3072]{2,1,0:T(8,128)(2,1)S(1)} all-to-all(bf16[8,16,3072]{2,1,0:T(8,128)(2,1)S(1)} %bitcast.52), channel_id=1, replica_groups={{0,1,16,17,32,33,48,49},{2,3,18,19,34,35,50,51},{4,5,20,21,36,37,52,53}..., dimensions={0} | all-to-all | bytes 1572864 | tf_op jit(solution)/shard_map/all_to_all | solution.py:180
  209.6 0.1 reduce_sum.44
  209.7 0.1 convert_element_type.51
  209.8 19.7 %all_to_all.73 = bf16[8,48,128]{2,1,0:T(8,128)(2,1)S(1)} all-to-all(bf16[8,48,128]{2,1,0:T(8,128)(2,1)S(1)} %convert_element_type.51), channel_id=1, replica_groups={{0,2,4,6,8,10,12,14},{1,3,5,7,9,11,13,15},{16,18,20,22,24,26,28,30},{17..., dimensions={0} | all-to-all | bytes 196608 | tf_op jit(solution)/shard_map/all_to_all | solution.py:180
  229.5 13.3 %collective-permute-start.1 = (bf16[2,3072]{1,0:T(2,128)(2,1)S(1)}, bf16[2,3072]{1,0:T(2,128)(2,1)S(1)}, u32[]{:S(2)}, u32[]{:S(2)}) collective-permute-start(bf16[2,3072]{1,0:T(2,128)(2,1)S(1)} %add_convert_fusion), channel_id=1, source_target_pairs={{448,0},{0,64},{64,128},{128,192},{192,256},{256,320},{320,384},{3... | collective-permute-start | bytes 36872 | tf_op jit(solution)/shard_map/ppermute | solution.py:23
  242.8 0.8 collective-permute-done.1
  243.6 0.6 copy.23
  (28 shorter events, 0.3 us)
Async XLA Ops:
  0.0 94.5 %copy-start = (bf16[1,192,3072]{2,1,0:T(8,128)(2,1)S(1)}, bf16[1,192,3072]{2,1,0:T(8,128)(2,1)}, u32[]{:S(2)}) copy-start(bf16[1,192,3072]{2,1,0:T(8,128)(2,1)} %param.13) | copy-start | bytes 3538948
  0.0 0.9 copy-start.4
  0.9 0.7 copy-start.6
  2.5 28.3 %all-to-all-start = ((bf16[8,48,128]{2,1,0:T(8,128)(2,1)}), bf16[8,48,128]{2,1,0:T(8,128)(2,1)S(1)}, u32[]{:S(2)}, u32[]{:S(2)}) async-start(bf16[8,48,128]{2,1,0:T(8,128)(2,1)} %shard_map.91), calls=%async_computation | async-start | bytes 196608 | tf_op jit(solution)/shard_map/all_to_all | solution.py:236
  48.5 15.5 %copy-start.1 = (bf16[1,3,48,3072]{3,2,1,0:T(8,128)(2,1)S(1)}, bf16[1,3,48,3072]{3,2,1,0:T(8,128)(2,1)}, u32[]{:S(2)}) copy-start(bf16[1,3,48,3072]{3,2,1,0:T(8,128)(2,1)} %param.10) | copy-start | bytes 2654212
  64.0 12.1 %copy-start.10 = (f32[1,2,128]{2,1,0:T(2,128)S(1)}, f32[1,2,128]{2,1,0:T(2,128)}, u32[]{:S(2)}) copy-start(f32[1,2,128]{2,1,0:T(2,128)} %param.15) | copy-start | bytes 3076
  65.2 20.5 %all-to-all-start.3 = ((bf16[8,64,128]{2,1,0:T(8,128)(2,1)}), bf16[8,64,128]{2,1,0:T(8,128)(2,1)S(1)}, u32[]{:S(2)}, u32[]{:S(2)}) async-start(bf16[8,64,128]{2,1,0:T(8,128)(2,1)} %shard_map.92), calls=%async_computation.3 | async-start | bytes 262144 | tf_op jit(solution)/shard_map/all_to_all | solution.py:243
  76.1 16.7 %copy-start.8 = (f32[1,128]{1,0:T(1,128)}, f32[1,128]{1,0:T(1,128)S(1)}, u32[]{:S(2)}) copy-start(f32[1,128]{1,0:T(1,128)S(1)} %get-tuple-element.17.gain_k_ref) | copy-start | bytes 1540
  87.3 15.9 %all-to-all-start.4 = ((bf16[8,64,128]{2,1,0:T(8,128)(2,1)}), bf16[8,64,128]{2,1,0:T(8,128)(2,1)}, u32[]{:S(2)}, u32[]{:S(2)}) async-start(bf16[8,64,128]{2,1,0:T(8,128)(2,1)} %shard_map.93), calls=%async_computation.4 | async-start | bytes 262144 | tf_op jit(solution)/shard_map/all_to_all | solution.py:245
  94.5 8.7 %copy-start.3 = (bf16[1,48,3072]{2,1,0:T(8,128)(2,1)S(1)}, bf16[1,48,3072]{2,1,0:T(8,128)(2,1)}, u32[]{:S(2)}) copy-start(bf16[1,48,3072]{2,1,0:T(8,128)(2,1)} %param.12) | copy-start | bytes 884740
  94.5 8.7 %copy-start.5 = (f32[1,3,3072]{2,0,1:T(1,128)S(1)}, f32[1,3,3072]{2,0,1:T(1,128)}, u32[]{:S(2)}) copy-start(f32[1,3,3072]{2,0,1:T(1,128)} %param.14) | copy-start | bytes 110596
  104.5 31.4 %copy-start.7 = (bf16[1,2,3072]{2,1,0:T(2,128)(2,1)S(1)}, bf16[1,2,3072]{2,1,0:T(2,128)(2,1)}, u32[]{:S(2)}) copy-start(bf16[1,2,3072]{2,1,0:T(2,128)(2,1)} %param.9) | copy-start | bytes 36868
  136.0 6.2 %collective-permute-start = (bf16[2,3072]{1,0:T(2,128)(2,1)S(1)}, bf16[2,3072]{1,0:T(2,128)(2,1)S(1)}, u32[]{:S(2)}, u32[]{:S(2)}) collective-permute-start(bf16[2,3072]{1,0:T(2,128)(2,1)S(1)} %add_convert_fusion.1), channel_id=1, source_target_pairs={{448,0},{0,64},{64,128},{128,192},{192,256},{256,320},{320,384},{3... | collective-permute-start | bytes 36872 | tf_op jit(solution)/shard_map/ppermute | solution.py:23
  157.5 11.6 %copy-start.2 = (bf16[1,3,48,3072]{3,2,1,0:T(8,128)(2,1)S(1)}, bf16[1,3,48,3072]{3,2,1,0:T(8,128)(2,1)}, u32[]{:S(2)}) copy-start(bf16[1,3,48,3072]{3,2,1,0:T(8,128)(2,1)} %param.10) | copy-start | bytes 2654212
  169.1 13.6 %copy-start.9 = (f32[1,128]{1,0:T(1,128)S(1)}, f32[1,128]{1,0:T(1,128)}, u32[]{:S(2)}) copy-start(f32[1,128]{1,0:T(1,128)} %copy-done.8) | copy-start | bytes 1540
  184.2 13.6 %all-to-all-start.10 = ((bf16[8,64,128]{2,1,0:T(8,128)(2,1)}), bf16[8,64,128]{2,1,0:T(8,128)(2,1)S(1)}, u32[]{:S(2)}, u32[]{:S(2)}) async-start(bf16[8,64,128]{2,1,0:T(8,128)(2,1)} %shard_map.97), calls=%async_computation.10 | async-start | bytes 262144 | tf_op jit(solution)/shard_map/all_to_all | solution.py:245
  229.5 14.1 %collective-permute-start.1 = (bf16[2,3072]{1,0:T(2,128)(2,1)S(1)}, bf16[2,3072]{1,0:T(2,128)(2,1)S(1)}, u32[]{:S(2)}, u32[]{:S(2)}) collective-permute-start(bf16[2,3072]{1,0:T(2,128)(2,1)S(1)} %add_convert_fusion), channel_id=1, source_target_pairs={{448,0},{0,64},{64,128},{128,192},{192,256},{256,320},{320,384},{3... | collective-permute-start | bytes 36872 | tf_op jit(solution)/shard_map/ppermute | solution.py:23

commit v15 on v11

--- a/solution.py
+++ b/solution.py
@@ -37,16 +37,18 @@
             block_ref[at : at + 1, :] = normed[r : r + 1, p * LANES : (p + 1) * LANES]
     block = block_ref[...].astype(bf16)
     for j in range(out_ref.shape[0]):
-        out_ref[j] = block
-
-
-def spread(rows, modulation, receivers):
+        for k in range(out_ref.shape[1] // block.shape[0]):
+            out_ref[j, k * block.shape[0] : (k + 1) * block.shape[0], :] = block
+
+
+def spread(rows, modulation, receivers, copies=1):
     whole = pl.BlockSpec(memory_space=pltpu.VMEM)
+    given = whole if copies == 1 else pl.BlockSpec()
     lines = rows.shape[0] * rows.shape[1] // LANES
     return pl.pallas_call(
         spread_kernel,
-        out_shape=jax.ShapeDtypeStruct((receivers, lines, LANES), bf16),
-        in_specs=[whole] * 2,
+        out_shape=jax.ShapeDtypeStruct((receivers, copies * lines, LANES), bf16),
+        in_specs=[given] * 2,
         out_specs=whole,
         scratch_shapes=[pltpu.VMEM((lines, LANES), f32)],
         compiler_params=pltpu.CompilerParams(vmem_limit_bytes=8 * 1024 * 1024),
@@ -196,8 +198,6 @@
     member = tp_index % TEAM
     z_count, x_count = 2 * TEAM, tp_count // (2 * TEAM)
     xs, hs, two = range(x_count), range(z_count // 2), range(2)
-    along_z = [[z_count * x + 2 * h + l for l in two for h in hs] for x in xs]
-    along_x = [[z_count * x + z for x in xs] for z in range(z_count)]
     far = [[z_count * x + 2 * h + l for h in hs] for x in xs for l in two]
     blocks = [[z_count * x + 2 * h + l for x in xs for l in two] for h in hs]
     inside = [[TEAM * t + m for m in range(TEAM)] for t in range(teams)]
@@ -230,7 +230,7 @@
     cached_mask = jnp.broadcast_to(cached_mask[:, None], (teams * ctx_local, LANES))
 
     current = in_flight[0]
-    block = spread(current, shift_scale, z_count)
+    block = spread(current, shift_scale, len(hs), 2)
     block, flat = lax.optimization_barrier((block, context_kv[0]))
     flat = flat.reshape(2 * ctx_local, width)
     by_x = []
@@ -251,14 +251,14 @@
 
     for tick_number in range(TICKS):
         if tick_number == 0:
-            normed = lax.all_to_all(block, "tp", 0, 0, axis_index_groups=along_z)
-            normed = normed.reshape(-1, width)
+            normed = lax.all_to_all(block, "tp", 0, 0, axis_index_groups=far)
+            normed = normed[:, : block.shape[1] // 2].reshape(-1, width)
             route = [(z_count * x + z, z_count * x + partner[z]) for x in xs for z in range(z_count)]
             got = [
                 lax.ppermute(part, "tp", route)
                 for part in (give[: x_count // 2], give[x_count // 2 :])
             ]
-            normed = gathered(normed, along_x)
+            normed = gathered(normed, blocks)
             normed, got[0] = lax.optimization_barrier((normed, got[0]))
             cached = [keep] + got
         else:

time: 235 us -> 249 us (1.060)
  blocking collectives: 103 us -> 133 us
  starting transfers between devices: 90 us -> 66.2 us
  waiting for transfers between devices: 24.5 us -> 33.4 us
    all_to_all x1 -> x2, blocking collectives: 14.9 us -> 45.5 us  [local(): normed = lax.all_to_all(block, 'tp', 0, 0, axis_index_groups=far)]
    all_to_all x1 -> x0, starting transfers between devices: 15.7 us -> none  [local(): normed = lax.all_to_all(block, 'tp', 0, 0, axis_index_groups=along_z)]
    ppermute x2, waiting for transfers between devices: 3.76 us -> 10.1 us  [local(): lax.ppermute(part, 'tp', route)]
    ppermute x3, waiting for transfers between devices: 0.01 us -> 5.49 us  [local(): part = lax.ppermute(part, 'tp', route)]
    all_to_all x2, starting transfers between devices: 13 us -> 8.62 us  [local(): parts = lax.all_to_all(parts, 'tp', 0, 0, axis_index_groups=inside)]
    all_to_all x1 -> x0, waiting for transfers between devices: 2.92 us -> none  [local(): normed = lax.all_to_all(block, 'tp', 0, 0, axis_index_groups=along_z)]
  transfers between devices with their start and end apart: 12 -> 11, of which waited for: 7 -> 8; matrix products, arithmetic and copies ran while one was open for 3% -> 2% of each run, Pallas kernels for 0% -> 0%
where the time goes in v15:
time: 249 us; the launch traced here: 248 us
  blocking collectives  133 us (53%)
  starting transfers between devices  66.2 us (27%)
  waiting for transfers between devices  33.4 us (13%)
  Pallas kernels  6.02 us (2%)
  matrix products  4.3 us (2%)
  local copies, waits for them, and re-layouts  3.74 us (2%)
    all_to_all x4, blocking collectives, summed_over(): parts = lax.all_to_all(parts, 'tp', 0, 0, axis_index_groups=groups)  63 us
    all_to_all x2, blocking collectives, local(): normed = lax.all_to_all(block, 'tp', 0, 0, axis_index_groups=far)  45.5 us
    ppermute x2, starting transfers between devices, shifted(): lax.ppermute(block, axis, [((i - distance) % size, i) for i in range(size)])  22.2 us
    all_to_all x2, waiting for transfers between devices, local(): parts = lax.all_to_all(parts, 'tp', 0, 0, axis_index_groups=inside)  16.1 us
    ppermute x2, starting transfers between devices, local(): lax.ppermute(part, 'tp', route)  14.6 us
    all_to_all x1, blocking collectives, local(): team = lax.all_to_all(team, 'tp', 0, 0, axis_index_groups=inside)  12.7 us
    all_to_all x1, blocking collectives, gathered(): spread = lax.all_to_all(spread, 'tp', 0, 0, axis_index_groups=groups)  11.9 us
    ppermute x2, waiting for transfers between devices, local(): lax.ppermute(part, 'tp', route)  10.1 us
  transfers between devices with their start and end apart: 11, of which 8 were waited for; matrix products, arithmetic and copies ran while one was open for 2% of the time, Pallas kernels for 0%

profile of v15, /device:TPU:1, one launch (start us, length us, event | category | flops | bytes accessed | tf_op | source)
XLA Modules:
  0.0 248.1 jit_solution(17589856362502834335)
XLA Ops:
  0.0 0.9 copy-done.4
  0.9 0.7 copy-done.10
  1.6 0.3 shard_map.91
  1.8 30.6 %all_to_all.60 = bf16[8,96,128]{2,1,0:T(8,128)(2,1)S(1)} all-to-all(bf16[8,96,128]{2,1,0:T(8,128)(2,1)S(1)} %shard_map.91), channel_id=1, replica_groups={{0,2,4,6,8,10,12,14},{1,3,5,7,9,11,13,15},{16,18,20,22,24,26,28,30},{17..., dimensions={0} | all-to-all | bytes 393216 | tf_op jit(solution)/shard_map/all_to_all | solution.py:254
  32.5 1.0 broadcast_in_dim.37
  33.4 4.2 %all-to-all-start.1 = ((bf16[8,16,3072]{2,1,0:T(8,128)(2,1)}), bf16[8,16,3072]{2,1,0:T(8,128)(2,1)S(1)}, u32[]{:S(2)}, u32[]{:S(2)}) async-start(bf16[8,16,3072]{2,1,0:T(8,128)(2,1)} %broadcast_in_dim.37), calls=%async_computation.1 | async-start | bytes 1572864 | tf_op jit(solution)/shard_map/all_to_all | solution.py:175
  37.7 4.6 %collective-permute-start.2 = (bf16[48,768]{1,0:T(8,128)(2,1)S(1)}, bf16[48,768]{1,0:T(8,128)(2,1)S(1)}, u32[]{:S(2)}, u32[]{:S(2)}) collective-permute-start(bf16[48,768]{1,0:T(8,128)(2,1)S(1)} %get-tuple-element.16), channel_id=1, source_target_pairs={{0,48},{1,49},{2,50},{3,51},{4,52},{5,53},{6,54},{7,55},{8,56},{9,... | collective-permute-start | bytes 221192 | tf_op jit(solution)/shard_map/ppermute | solution.py:246
  42.4 2.5 %collective-permute-start.1 = (bf16[48,768]{1,0:T(8,128)(2,1)S(1)}, bf16[48,768]{1,0:T(8,128)(2,1)S(1)}, u32[]{:S(2)}, u32[]{:S(2)}) collective-permute-start(bf16[48,768]{1,0:T(8,128)(2,1)S(1)} %get-tuple-element.17), channel_id=1, source_target_pairs={{0,32},{1,33},{2,34},{3,35},{4,36},{5,37},{6,38},{7,39},{8,40},{9,... | collective-permute-start | bytes 221192 | tf_op jit(solution)/shard_map/ppermute | solution.py:246
  44.8 2.5 %collective-permute-start = (bf16[48,768]{1,0:T(8,128)(2,1)S(1)}, bf16[48,768]{1,0:T(8,128)(2,1)S(1)}, u32[]{:S(2)}, u32[]{:S(2)}) collective-permute-start(bf16[48,768]{1,0:T(8,128)(2,1)S(1)} %get-tuple-element.18), channel_id=1, source_target_pairs={{0,16},{1,17},{2,18},{3,19},{4,20},{5,21},{6,22},{7,23},{8,24},{9,... | collective-permute-start | bytes 221192 | tf_op jit(solution)/shard_map/ppermute | solution.py:246
  47.4 3.8 %collective-permute-done.1 = bf16[48,768]{1,0:T(8,128)(2,1)S(1)} collective-permute-done((bf16[48,768]{1,0:T(8,128)(2,1)S(1)}, bf16[48,768]{1,0:T(8,128)(2,1)S(1)}, u32[]{:S(2)}, u32[]{:S(2)}) %collective-permute-start.1) | collective-permute-done | bytes 73760 | tf_op jit(solution)/shard_map/ppermute | solution.py:246
  51.2 1.7 collective-permute-done
  53.0 5.3 %collective-permute-start.3 = (bf16[2,48,384]{2,1,0:T(8,128)(2,1)S(1)}, bf16[2,48,384]{2,1,0:T(8,128)(2,1)S(1)}, u32[]{:S(2)}, u32[]{:S(2)}) collective-permute-start(bf16[2,48,384]{2,1,0:T(8,128)(2,1)S(1)} %get-tuple-element.20), channel_id=1, source_target_pairs={{0,12},{1,13},{2,14},{3,15},{4,8},{5,9},{6,10},{7,11},{8,4},{9,5},... | collective-permute-start | bytes 221192 | tf_op jit(solution)/shard_map/ppermute | solution.py:258
  58.3 5.0 %collective-permute-done.3.refs_1_ = bf16[2,48,384]{2,1,0:T(8,128)(2,1)S(1)} collective-permute-done((bf16[2,48,384]{2,1,0:T(8,128)(2,1)S(1)}, bf16[2,48,384]{2,1,0:T(8,128)(2,1)S(1)}, u32[]{:S(2)}, u32[]{:S(2)}) %collective-permute-start.3) | collective-permute-done | bytes 73760 | tf_op jit(solution)/shard_map/ppermute | solution.py:258
  63.2 1.2 shard_map.92
  64.4 7.1 %all-to-all-start.2 = ((bf16[8,64,128]{2,1,0:T(8,128)(2,1)}), bf16[8,64,128]{2,1,0:T(8,128)(2,1)S(1)}, u32[]{:S(2)}, u32[]{:S(2)}) async-start(bf16[8,64,128]{2,1,0:T(8,128)(2,1)} %shard_map.92), calls=%async_computation.2 | async-start | bytes 262144 | tf_op jit(solution)/shard_map/all_to_all | solution.py:269
  72.2 0.1 copy.12.gain_q_ref
  72.3 9.3 %collective-permute-start.4 = (bf16[2,48,384]{2,1,0:T(8,128)(2,1)S(1)}, bf16[2,48,384]{2,1,0:T(8,128)(2,1)S(1)}, u32[]{:S(2)}, u32[]{:S(2)}) collective-permute-start(bf16[2,48,384]{2,1,0:T(8,128)(2,1)S(1)} %get-tuple-element.19), channel_id=1, source_target_pairs={{0,12},{1,13},{2,14},{3,15},{4,8},{5,9},{6,10},{7,11},{8,4},{9,5},... | collective-permute-start | bytes 221192 | tf_op jit(solution)/shard_map/ppermute | solution.py:258
  81.7 5.1 %collective-permute-done.4.refs_2_ = bf16[2,48,384]{2,1,0:T(8,128)(2,1)S(1)} collective-permute-done((bf16[2,48,384]{2,1,0:T(8,128)(2,1)S(1)}, bf16[2,48,384]{2,1,0:T(8,128)(2,1)S(1)}, u32[]{:S(2)}, u32[]{:S(2)}) %collective-permute-start.4) | collective-permute-done | bytes 73760 | tf_op jit(solution)/shard_map/ppermute | solution.py:258
  86.8 0.1 broadcast_in_dim.40.mask_ref
  86.9 1.5 shard_map.93
  88.3 5.2 %all-to-all-start.3 = ((bf16[8,64,128]{2,1,0:T(8,128)(2,1)}), bf16[8,64,128]{2,1,0:T(8,128)(2,1)S(1)}, u32[]{:S(2)}, u32[]{:S(2)}) async-start(bf16[8,64,128]{2,1,0:T(8,128)(2,1)} %shard_map.93), calls=%async_computation.3 | async-start | bytes 262144 | tf_op jit(solution)/shard_map/all_to_all | solution.py:271
  93.6 1.8 fusion.17
  95.4 0.4 fusion.2.forward_ref
  95.8 8.1 %all-to-all-done.3.parts_ref = bf16[8,64,128]{2,1,0:T(8,128)(2,1)S(1)} async-done(((bf16[8,64,128]{2,1,0:T(8,128)(2,1)}), bf16[8,64,128]{2,1,0:T(8,128)(2,1)S(1)}, u32[]{:S(2)}, u32[]{:S(2)}) %all-to-all-start.3) | async-done | bytes 131104 | tf_op jit(solution)/shard_map/all_to_all | solution.py:271
  103.9 0.4 shard_map.94
  104.3 11.4 %all_to_all.61 = bf16[8,16,3072]{2,1,0:T(8,128)(2,1)S(1)} all-to-all(bf16[8,16,3072]{2,1,0:T(8,128)(2,1)S(1)} %bitcast.53), channel_id=1, replica_groups={{0,1,16,17,32,33,48,49},{2,3,18,19,34,35,50,51},{4,5,20,21,36,37,52,53}..., dimensions={0} | all-to-all | bytes 1572864 | tf_op jit(solution)/shard_map/all_to_all | solution.py:182
  115.7 0.1 reduce_sum.42
  115.9 20.0 %all_to_all.62 = bf16[8,48,128]{2,1,0:T(8,128)(2,1)S(1)} all-to-all(bf16[8,48,128]{2,1,0:T(8,128)(2,1)S(1)} %convert_element_type.46), channel_id=1, replica_groups={{0,2,4,6,8,10,12,14},{1,3,5,7,9,11,13,15},{16,18,20,22,24,26,28,30},{17..., dimensions={0} | all-to-all | bytes 196608 | tf_op jit(solution)/shard_map/all_to_all | solution.py:182
  135.9 8.7 %collective-permute-start.5 = (bf16[2,3072]{1,0:T(2,128)(2,1)S(1)}, bf16[2,3072]{1,0:T(2,128)(2,1)S(1)}, u32[]{:S(2)}, u32[]{:S(2)}) collective-permute-start(bf16[2,3072]{1,0:T(2,128)(2,1)S(1)} %add_convert_fusion.1), channel_id=1, source_target_pairs={{448,0},{0,64},{64,128},{128,192},{192,256},{256,320},{320,384},{3... | collective-permute-start | bytes 36872 | tf_op jit(solution)/shard_map/ppermute | solution.py:23
  144.6 0.8 collective-permute-done.5.rows_ref
  145.4 0.2 shard_map.95
  145.6 14.9 %all_to_all.63 = bf16[8,48,128]{2,1,0:T(8,128)(2,1)S(1)} all-to-all(bf16[8,48,128]{2,1,0:T(8,128)(2,1)S(1)} %shard_map.95), channel_id=1, replica_groups={{0,2,4,6,8,10,12,14},{1,3,5,7,9,11,13,15},{16,18,20,22,24,26,28,30},{17..., dimensions={0} | all-to-all | bytes 196608 | tf_op jit(solution)/shard_map/all_to_all | solution.py:266
  160.6 0.1 broadcast_in_dim.42
  160.7 11.9 %all_to_all.64 = bf16[8,16,3072]{2,1,0:T(8,128)(2,1)S(1)} all-to-all(bf16[8,16,3072]{2,1,0:T(8,128)(2,1)S(1)} %broadcast_in_dim.42), channel_id=1, replica_groups={{0,1,16,17,32,33,48,49},{2,3,18,19,34,35,50,51},{4,5,20,21,36,37,52,53}..., dimensions={0} | all-to-all | bytes 1572864 | tf_op jit(solution)/shard_map/all_to_all | solution.py:175
  172.6 0.6 shard_map.96
  173.1 12.7 %all_to_all.65.team_ref = bf16[8,64,128]{2,1,0:T(8,128)(2,1)S(1)} all-to-all(bf16[8,64,128]{2,1,0:T(8,128)(2,1)S(1)} %shard_map.96), channel_id=1, replica_groups={{0,1,2,3,4,5,6,7},{8,9,10,11,12,13,14,15},{16,17,18,19,20,21,22,23},{24..., dimensions={0} | all-to-all | bytes 262144 | tf_op jit(solution)/shard_map/all_to_all | solution.py:269
  185.8 1.5 shard_map.97
  187.3 3.4 %all-to-all-start.9 = ((bf16[8,64,128]{2,1,0:T(8,128)(2,1)}), bf16[8,64,128]{2,1,0:T(8,128)(2,1)S(1)}, u32[]{:S(2)}, u32[]{:S(2)}) async-start(bf16[8,64,128]{2,1,0:T(8,128)(2,1)} %shard_map.97), calls=%async_computation.9 | async-start | bytes 262144 | tf_op jit(solution)/shard_map/all_to_all | solution.py:271
  190.6 1.8 fusion.29
  192.4 0.4 fusion.forward_ref
  192.8 8.1 %all-to-all-done.9.parts_ref = bf16[8,64,128]{2,1,0:T(8,128)(2,1)S(1)} async-done(((bf16[8,64,128]{2,1,0:T(8,128)(2,1)}), bf16[8,64,128]{2,1,0:T(8,128)(2,1)S(1)}, u32[]{:S(2)}, u32[]{:S(2)}) %all-to-all-start.9) | async-done | bytes 131104 | tf_op jit(solution)/shard_map/all_to_all | solution.py:271
  200.9 0.4 shard_map.98
  201.3 11.4 %all_to_all.66 = bf16[8,16,3072]{2,1,0:T(8,128)(2,1)S(1)} all-to-all(bf16[8,16,3072]{2,1,0:T(8,128)(2,1)S(1)} %bitcast.52), channel_id=1, replica_groups={{0,1,16,17,32,33,48,49},{2,3,18,19,34,35,50,51},{4,5,20,21,36,37,52,53}..., dimensions={0} | all-to-all | bytes 1572864 | tf_op jit(solution)/shard_map/all_to_all | solution.py:182
  212.6 0.1 reduce_sum.44
  212.8 20.3 %all_to_all.67 = bf16[8,48,128]{2,1,0:T(8,128)(2,1)S(1)} all-to-all(bf16[8,48,128]{2,1,0:T(8,128)(2,1)S(1)} %convert_element_type.51), channel_id=1, replica_groups={{0,2,4,6,8,10,12,14},{1,3,5,7,9,11,13,15},{16,18,20,22,24,26,28,30},{17..., dimensions={0} | all-to-all | bytes 196608 | tf_op jit(solution)/shard_map/all_to_all | solution.py:182
  233.1 13.5 %collective-permute-start.6 = (bf16[2,3072]{1,0:T(2,128)(2,1)S(1)}, bf16[2,3072]{1,0:T(2,128)(2,1)S(1)}, u32[]{:S(2)}, u32[]{:S(2)}) collective-permute-start(bf16[2,3072]{1,0:T(2,128)(2,1)S(1)} %add_convert_fusion), channel_id=1, source_target_pairs={{448,0},{0,64},{64,128},{128,192},{192,256},{256,320},{320,384},{3... | collective-permute-start | bytes 36872 | tf_op jit(solution)/shard_map/ppermute | solution.py:23
  246.7 0.8 collective-permute-done.6
  247.5 0.6 copy.16
  (46 shorter events, 0.5 us)
Async XLA Ops:
  0.0 95.4 %copy-start = (bf16[1,192,3072]{2,1,0:T(8,128)(2,1)S(1)}, bf16[1,192,3072]{2,1,0:T(8,128)(2,1)}, u32[]{:S(2)}) copy-start(bf16[1,192,3072]{2,1,0:T(8,128)(2,1)} %param.13) | copy-start | bytes 3538948
  0.0 0.9 copy-start.4
  0.9 0.7 copy-start.10
  32.5 5.2 %copy-start.12 = (bf16[1,2,24,3072]{3,2,1,0:T(8,128)(2,1)S(1)}, bf16[1,2,24,3072]{3,2,1,0:T(8,128)(2,1)}, u32[]{:S(2)}) copy-start(bf16[1,2,24,3072]{3,2,1,0:T(8,128)(2,1)} %param.16) | copy-start | bytes 884740
  33.4 29.8 %all-to-all-start.1 = ((bf16[8,16,3072]{2,1,0:T(8,128)(2,1)}), bf16[8,16,3072]{2,1,0:T(8,128)(2,1)S(1)}, u32[]{:S(2)}, u32[]{:S(2)}) async-start(bf16[8,16,3072]{2,1,0:T(8,128)(2,1)} %broadcast_in_dim.37), calls=%async_computation.1 | async-start | bytes 1572864 | tf_op jit(solution)/shard_map/all_to_all | solution.py:175
  37.6 25.7 %copy-start.1 = (bf16[1,3,48,3072]{3,2,1,0:T(8,128)(2,1)S(1)}, bf16[1,3,48,3072]{3,2,1,0:T(8,128)(2,1)}, u32[]{:S(2)}) copy-start(bf16[1,3,48,3072]{3,2,1,0:T(8,128)(2,1)} %param.10) | copy-start | bytes 2654212
  37.7 9.6 %collective-permute-start.2 = (bf16[48,768]{1,0:T(8,128)(2,1)S(1)}, bf16[48,768]{1,0:T(8,128)(2,1)S(1)}, u32[]{:S(2)}, u32[]{:S(2)}) collective-permute-start(bf16[48,768]{1,0:T(8,128)(2,1)S(1)} %get-tuple-element.16), channel_id=1, source_target_pairs={{0,48},{1,49},{2,50},{3,51},{4,52},{5,53},{6,54},{7,55},{8,56},{9,... | collective-permute-start | bytes 221192 | tf_op jit(solution)/shard_map/ppermute | solution.py:246
  42.4 8.8 %collective-permute-start.1 = (bf16[48,768]{1,0:T(8,128)(2,1)S(1)}, bf16[48,768]{1,0:T(8,128)(2,1)S(1)}, u32[]{:S(2)}, u32[]{:S(2)}) collective-permute-start(bf16[48,768]{1,0:T(8,128)(2,1)S(1)} %get-tuple-element.17), channel_id=1, source_target_pairs={{0,32},{1,33},{2,34},{3,35},{4,36},{5,37},{6,38},{7,39},{8,40},{9,... | collective-permute-start | bytes 221192 | tf_op jit(solution)/shard_map/ppermute | solution.py:246
  44.8 8.0 %collective-permute-start = (bf16[48,768]{1,0:T(8,128)(2,1)S(1)}, bf16[48,768]{1,0:T(8,128)(2,1)S(1)}, u32[]{:S(2)}, u32[]{:S(2)}) collective-permute-start(bf16[48,768]{1,0:T(8,128)(2,1)S(1)} %get-tuple-element.18), channel_id=1, source_target_pairs={{0,16},{1,17},{2,18},{3,19},{4,20},{5,21},{6,22},{7,23},{8,24},{9,... | collective-permute-start | bytes 221192 | tf_op jit(solution)/shard_map/ppermute | solution.py:246
  52.9 19.3 %copy-start.13 = (f32[1,2,128]{2,1,0:T(2,128)S(1)}, f32[1,2,128]{2,1,0:T(2,128)}, u32[]{:S(2)}) copy-start(f32[1,2,128]{2,1,0:T(2,128)} %param.15) | copy-start | bytes 3076
  53.0 10.3 %collective-permute-start.3 = (bf16[2,48,384]{2,1,0:T(8,128)(2,1)S(1)}, bf16[2,48,384]{2,1,0:T(8,128)(2,1)S(1)}, u32[]{:S(2)}, u32[]{:S(2)}) collective-permute-start(bf16[2,48,384]{2,1,0:T(8,128)(2,1)S(1)} %get-tuple-element.20), channel_id=1, source_target_pairs={{0,12},{1,13},{2,14},{3,15},{4,8},{5,9},{6,10},{7,11},{8,4},{9,5},... | collective-permute-start | bytes 221192 | tf_op jit(solution)/shard_map/ppermute | solution.py:258
  63.2 25.1 %copy-start.6 = (bf16[2,48,384]{2,1,0:T(8,128)(2,1)}, bf16[2,48,384]{2,1,0:T(8,128)(2,1)S(1)}, u32[]{:S(2)}) copy-start(bf16[2,48,384]{2,1,0:T(8,128)(2,1)S(1)} %collective-permute-done.3.refs_1_) | copy-start | bytes 221188
  64.4 22.3 %all-to-all-start.2 = ((bf16[8,64,128]{2,1,0:T(8,128)(2,1)}), bf16[8,64,128]{2,1,0:T(8,128)(2,1)S(1)}, u32[]{:S(2)}, u32[]{:S(2)}) async-start(bf16[8,64,128]{2,1,0:T(8,128)(2,1)} %shard_map.92), calls=%async_computation.2 | async-start | bytes 262144 | tf_op jit(solution)/shard_map/all_to_all | solution.py:269
  72.3 14.4 %collective-permute-start.4 = (bf16[2,48,384]{2,1,0:T(8,128)(2,1)S(1)}, bf16[2,48,384]{2,1,0:T(8,128)(2,1)S(1)}, u32[]{:S(2)}, u32[]{:S(2)}) collective-permute-start(bf16[2,48,384]{2,1,0:T(8,128)(2,1)S(1)} %get-tuple-element.19), channel_id=1, source_target_pairs={{0,12},{1,13},{2,14},{3,15},{4,8},{5,9},{6,10},{7,11},{8,4},{9,5},... | collective-permute-start | bytes 221192 | tf_op jit(solution)/shard_map/ppermute | solution.py:258
  86.8 6.8 %copy-start.8 = (bf16[2,48,384]{2,1,0:T(8,128)(2,1)}, bf16[2,48,384]{2,1,0:T(8,128)(2,1)S(1)}, u32[]{:S(2)}) copy-start(bf16[2,48,384]{2,1,0:T(8,128)(2,1)S(1)} %collective-permute-done.4.refs_2_) | copy-start | bytes 221188
  88.3 15.5 %all-to-all-start.3 = ((bf16[8,64,128]{2,1,0:T(8,128)(2,1)}), bf16[8,64,128]{2,1,0:T(8,128)(2,1)S(1)}, u32[]{:S(2)}, u32[]{:S(2)}) async-start(bf16[8,64,128]{2,1,0:T(8,128)(2,1)} %shard_map.93), calls=%async_computation.3 | async-start | bytes 262144 | tf_op jit(solution)/shard_map/all_to_all | solution.py:271
  95.4 8.5 %copy-start.3 = (bf16[1,48,3072]{2,1,0:T(8,128)(2,1)S(1)}, bf16[1,48,3072]{2,1,0:T(8,128)(2,1)}, u32[]{:S(2)}) copy-start(bf16[1,48,3072]{2,1,0:T(8,128)(2,1)} %param.12) | copy-start | bytes 884740
  95.4 8.5 %copy-start.5 = (f32[1,3,3072]{2,0,1:T(1,128)S(1)}, f32[1,3,3072]{2,0,1:T(1,128)}, u32[]{:S(2)}) copy-start(f32[1,3,3072]{2,0,1:T(1,128)} %param.14) | copy-start | bytes 110596
  104.3 31.6 %copy-start.11 = (bf16[1,2,3072]{2,1,0:T(2,128)(2,1)S(1)}, bf16[1,2,3072]{2,1,0:T(2,128)(2,1)}, u32[]{:S(2)}) copy-start(bf16[1,2,3072]{2,1,0:T(2,128)(2,1)} %param.9) | copy-start | bytes 36868
  135.9 9.5 %collective-permute-start.5 = (bf16[2,3072]{1,0:T(2,128)(2,1)S(1)}, bf16[2,3072]{1,0:T(2,128)(2,1)S(1)}, u32[]{:S(2)}, u32[]{:S(2)}) collective-permute-start(bf16[2,3072]{1,0:T(2,128)(2,1)S(1)} %add_convert_fusion.1), channel_id=1, source_target_pairs={{448,0},{0,64},{64,128},{128,192},{192,256},{256,320},{320,384},{3... | collective-permute-start | bytes 36872 | tf_op jit(solution)/shard_map/ppermute | solution.py:23
  160.6 12.0 %copy-start.2 = (bf16[1,3,48,3072]{3,2,1,0:T(8,128)(2,1)S(1)}, bf16[1,3,48,3072]{3,2,1,0:T(8,128)(2,1)}, u32[]{:S(2)}) copy-start(bf16[1,3,48,3072]{3,2,1,0:T(8,128)(2,1)} %param.10) | copy-start | bytes 2654212
  172.6 13.2 %copy-start.7 = (bf16[2,48,384]{2,1,0:T(8,128)(2,1)S(1)}, bf16[2,48,384]{2,1,0:T(8,128)(2,1)}, u32[]{:S(2)}) copy-start(bf16[2,48,384]{2,1,0:T(8,128)(2,1)} %copy-done.6) | copy-start | bytes 221188
  172.6 13.2 %copy-start.9 = (bf16[2,48,384]{2,1,0:T(8,128)(2,1)S(1)}, bf16[2,48,384]{2,1,0:T(8,128)(2,1)}, u32[]{:S(2)}) copy-start(bf16[2,48,384]{2,1,0:T(8,128)(2,1)} %copy-done.8) | copy-start | bytes 221188
  187.3 13.6 %all-to-all-start.9 = ((bf16[8,64,128]{2,1,0:T(8,128)(2,1)}), bf16[8,64,128]{2,1,0:T(8,128)(2,1)S(1)}, u32[]{:S(2)}, u32[]{:S(2)}) async-start(bf16[8,64,128]{2,1,0:T(8,128)(2,1)} %shard_map.97), calls=%async_computation.9 | async-start | bytes 262144 | tf_op jit(solution)/shard_map/all_to_all | solution.py:271
  233.1 14.4 %collective-permute-start.6 = (bf16[2,3072]{1,0:T(2,128)(2,1)S(1)}, bf16[2,3072]{1,0:T(2,128)(2,1)S(1)}, u32[]{:S(2)}, u32[]{:S(2)}) collective-permute-start(bf16[2,3072]{1,0:T(2,128)(2,1)S(1)} %add_convert_fusion), channel_id=1, source_target_pairs={{448,0},{0,64},{64,128},{128,192},{192,256},{256,320},{320,384},{3... | collective-permute-start | bytes 36872 | tf_op jit(solution)/shard_map/ppermute | solution.py:23

commit v16 on v11

--- a/solution.py
+++ b/solution.py
@@ -279,8 +279,8 @@
         forward = jnp.dot(hidden, weight_down, preferred_element_type=f32)
         forward = lax.optimization_barrier(forward)
         branch = finish(member[None], parts, weight_attn, forward, shift_scale)
-        branch = summed_over(branch, blocks)
-        branch = summed_over(branch.reshape(-1, LANES), far).reshape(rows, width)
+        branch = summed_over(branch, along_x)
+        branch = summed_over(branch.reshape(-1, LANES), along_z).reshape(rows, width)
         finished = (current.astype(f32) + branch).astype(bf16)
         current = shifted(finished, "pipe", 1)
     return current[None]

time: 235 us -> 235 us (level)
  no operation moved by 1% of the time
where the time goes in v16:
time: 235 us; the launch traced here: 234 us
  blocking collectives  104 us (44%)
  starting transfers between devices  88.1 us (37%)
  waiting for transfers between devices  24.5 us (10%)
  Pallas kernels  6.7 us (3%)
  local copies, waits for them, and re-layouts  4.86 us (2%)
  matrix products  4.32 us (2%)
    all_to_all x4, blocking collectives, summed_over(): parts = lax.all_to_all(parts, 'tp', 0, 0, axis_index_groups=groups)  62.9 us
    ppermute x2, starting transfers between devices, shifted(): lax.ppermute(block, axis, [((i - distance) % size, i) for i in range(size)])  22.4 us
    all_to_all x1, blocking collectives, local(): normed = lax.all_to_all(block, 'tp', 0, 0, axis_index_groups=far)  17.1 us
    all_to_all x2, waiting for transfers between devices, local(): parts = lax.all_to_all(parts, 'tp', 0, 0, axis_index_groups=inside)  16.1 us
    all_to_all x1, starting transfers between devices, local(): normed = lax.all_to_all(block, 'tp', 0, 0, axis_index_groups=along_z)  15.7 us
    ppermute x2, starting transfers between devices, local(): lax.ppermute(part, 'tp', route)  15.5 us
    all_to_all x2, starting transfers between devices, local(): parts = lax.all_to_all(parts, 'tp', 0, 0, axis_index_groups=inside)  13 us
    all_to_all x1, blocking collectives, local(): team = lax.all_to_all(team, 'tp', 0, 0, axis_index_groups=inside)  12.8 us
  transfers between devices with their start and end apart: 12, of which 7 were waited for; matrix products, arithmetic and copies ran while one was open for 3% of the time, Pallas kernels for 0%

profile of v16, /device:TPU:1, one launch (start us, length us, event | category | flops | bytes accessed | tf_op | source)
XLA Modules:
  0.0 234.3 jit_solution(6793076349335450942)
XLA Ops:
  0.0 0.9 copy-done.4
  0.9 0.7 copy-done.10
  1.6 0.9 shard_map.91
  2.5 15.7 %all-to-all-start = ((bf16[16,48,128]{2,1,0:T(8,128)(2,1)}), bf16[16,48,128]{2,1,0:T(8,128)(2,1)S(1)}, u32[]{:S(2)}, u32[]{:S(2)}) async-start(bf16[16,48,128]{2,1,0:T(8,128)(2,1)} %shard_map.91), calls=%async_computation | async-start | bytes 393216 | tf_op jit(solution)/shard_map/all_to_all | solution.py:254
  18.4 1.0 dynamic-slice_bitcast_fusion
  19.4 4.4 %collective-permute-start.2 = (bf16[48,768]{1,0:T(8,128)(2,1)S(1)}, bf16[48,768]{1,0:T(8,128)(2,1)S(1)}, u32[]{:S(2)}, u32[]{:S(2)}) collective-permute-start(bf16[48,768]{1,0:T(8,128)(2,1)S(1)} %get-tuple-element.16), channel_id=1, source_target_pairs={{0,48},{1,49},{2,50},{3,51},{4,52},{5,53},{6,54},{7,55},{8,56},{9,... | collective-permute-start | bytes 221192 | tf_op jit(solution)/shard_map/ppermute | solution.py:246
  23.8 2.4 %collective-permute-start.1 = (bf16[48,768]{1,0:T(8,128)(2,1)S(1)}, bf16[48,768]{1,0:T(8,128)(2,1)S(1)}, u32[]{:S(2)}, u32[]{:S(2)}) collective-permute-start(bf16[48,768]{1,0:T(8,128)(2,1)S(1)} %get-tuple-element.17), channel_id=1, source_target_pairs={{0,32},{1,33},{2,34},{3,35},{4,36},{5,37},{6,38},{7,39},{8,40},{9,... | collective-permute-start | bytes 221192 | tf_op jit(solution)/shard_map/ppermute | solution.py:246
  26.2 2.5 %collective-permute-start = (bf16[48,768]{1,0:T(8,128)(2,1)S(1)}, bf16[48,768]{1,0:T(8,128)(2,1)S(1)}, u32[]{:S(2)}, u32[]{:S(2)}) collective-permute-start(bf16[48,768]{1,0:T(8,128)(2,1)S(1)} %get-tuple-element.18), channel_id=1, source_target_pairs={{0,16},{1,17},{2,18},{3,19},{4,20},{5,21},{6,22},{7,23},{8,24},{9,... | collective-permute-start | bytes 221192 | tf_op jit(solution)/shard_map/ppermute | solution.py:246
  28.8 2.9 %all-to-all-done = bf16[16,48,128]{2,1,0:T(8,128)(2,1)S(1)} async-done(((bf16[16,48,128]{2,1,0:T(8,128)(2,1)}), bf16[16,48,128]{2,1,0:T(8,128)(2,1)S(1)}, u32[]{:S(2)}, u32[]{:S(2)}) %all-to-all-start) | async-done | bytes 196640 | tf_op jit(solution)/shard_map/all_to_all | solution.py:254
  31.8 1.0 broadcast_in_dim.37
  32.7 4.1 %all-to-all-start.1 = ((bf16[4,32,3072]{2,1,0:T(8,128)(2,1)}), bf16[4,32,3072]{2,1,0:T(8,128)(2,1)S(1)}, u32[]{:S(2)}, u32[]{:S(2)}) async-start(bf16[4,32,3072]{2,1,0:T(8,128)(2,1)} %broadcast_in_dim.37), calls=%async_computation.1 | async-start | bytes 1572864 | tf_op jit(solution)/shard_map/all_to_all | solution.py:173
  37.0 7.9 %collective-permute-start.3 = (bf16[2,48,384]{2,1,0:T(8,128)(2,1)S(1)}, bf16[2,48,384]{2,1,0:T(8,128)(2,1)S(1)}, u32[]{:S(2)}, u32[]{:S(2)}) collective-permute-start(bf16[2,48,384]{2,1,0:T(8,128)(2,1)S(1)} %get-tuple-element.20), channel_id=1, source_target_pairs={{0,12},{1,13},{2,14},{3,15},{4,8},{5,9},{6,10},{7,11},{8,4},{9,5},... | collective-permute-start | bytes 221192 | tf_op jit(solution)/shard_map/ppermute | solution.py:258
  44.9 1.7 collective-permute-done.3.refs_1_
  46.7 1.2 shard_map.92
  47.9 8.0 %all-to-all-start.2 = ((bf16[8,64,128]{2,1,0:T(8,128)(2,1)}), bf16[8,64,128]{2,1,0:T(8,128)(2,1)S(1)}, u32[]{:S(2)}, u32[]{:S(2)}) async-start(bf16[8,64,128]{2,1,0:T(8,128)(2,1)} %shard_map.92), calls=%async_computation.2 | async-start | bytes 262144 | tf_op jit(solution)/shard_map/all_to_all | solution.py:269
  56.6 0.1 copy.12.gain_q_ref
  56.7 7.6 %collective-permute-start.4 = (bf16[2,48,384]{2,1,0:T(8,128)(2,1)S(1)}, bf16[2,48,384]{2,1,0:T(8,128)(2,1)S(1)}, u32[]{:S(2)}, u32[]{:S(2)}) collective-permute-start(bf16[2,48,384]{2,1,0:T(8,128)(2,1)S(1)} %get-tuple-element.19), channel_id=1, source_target_pairs={{0,12},{1,13},{2,14},{3,15},{4,8},{5,9},{6,10},{7,11},{8,4},{9,5},... | collective-permute-start | bytes 221192 | tf_op jit(solution)/shard_map/ppermute | solution.py:258
  64.3 2.0 collective-permute-done.4.refs_2_
  66.4 1.5 shard_map.93
  67.9 9.7 %all-to-all-start.3 = ((bf16[8,64,128]{2,1,0:T(8,128)(2,1)}), bf16[8,64,128]{2,1,0:T(8,128)(2,1)S(1)}, u32[]{:S(2)}, u32[]{:S(2)}) async-start(bf16[8,64,128]{2,1,0:T(8,128)(2,1)} %shard_map.93), calls=%async_computation.3 | async-start | bytes 262144 | tf_op jit(solution)/shard_map/all_to_all | solution.py:271
  77.6 1.8 fusion.17
  79.4 0.4 fusion.2.forward_ref
  79.8 8.1 %all-to-all-done.3.parts_ref = bf16[8,64,128]{2,1,0:T(8,128)(2,1)S(1)} async-done(((bf16[8,64,128]{2,1,0:T(8,128)(2,1)}), bf16[8,64,128]{2,1,0:T(8,128)(2,1)S(1)}, u32[]{:S(2)}, u32[]{:S(2)}) %all-to-all-start.3) | async-done | bytes 131104 | tf_op jit(solution)/shard_map/all_to_all | solution.py:271
  87.9 0.4 shard_map.94
  88.3 10.7 %all_to_all.60 = bf16[4,32,3072]{2,1,0:T(8,128)(2,1)S(1)} all-to-all(bf16[4,32,3072]{2,1,0:T(8,128)(2,1)S(1)} %bitcast.53), channel_id=1, replica_groups={{0,16,32,48},{1,17,33,49},{2,18,34,50},{3,19,35,51},{4,20,36,52},{5,21,..., dimensions={0} | all-to-all | bytes 1572864 | tf_op jit(solution)/shard_map/all_to_all | solution.py:180
  99.0 0.2 reduce_sum.42
  99.2 0.1 convert_element_type.46
  99.3 20.7 %all_to_all.61 = bf16[16,48,128]{2,1,0:T(8,128)(2,1)S(1)} all-to-all(bf16[16,48,128]{2,1,0:T(8,128)(2,1)S(1)} %convert_element_type.46), channel_id=1, replica_groups={{0,2,4,6,8,10,12,14,1,3,5,7,9,11,13,15},{16,18,20,22,24,26,28,30,17,19,..., dimensions={0} | all-to-all | bytes 393216 | tf_op jit(solution)/shard_map/all_to_all | solution.py:180
  120.1 10.4 %collective-permute-start.5 = (bf16[2,3072]{1,0:T(2,128)(2,1)S(1)}, bf16[2,3072]{1,0:T(2,128)(2,1)S(1)}, u32[]{:S(2)}, u32[]{:S(2)}) collective-permute-start(bf16[2,3072]{1,0:T(2,128)(2,1)S(1)} %add_convert_fusion.1), channel_id=1, source_target_pairs={{448,0},{0,64},{64,128},{128,192},{192,256},{256,320},{320,384},{3... | collective-permute-start | bytes 36872 | tf_op jit(solution)/shard_map/ppermute | solution.py:23
  130.5 0.8 collective-permute-done.5.rows_ref
  131.3 0.2 shard_map.95
  131.6 17.1 %all_to_all.62 = bf16[8,48,128]{2,1,0:T(8,128)(2,1)S(1)} all-to-all(bf16[8,48,128]{2,1,0:T(8,128)(2,1)S(1)} %shard_map.95), channel_id=1, replica_groups={{0,2,4,6,8,10,12,14},{1,3,5,7,9,11,13,15},{16,18,20,22,24,26,28,30},{17..., dimensions={0} | all-to-all | bytes 196608 | tf_op jit(solution)/shard_map/all_to_all | solution.py:266
  148.8 11.5 %all_to_all.63 = bf16[8,16,3072]{2,1,0:T(8,128)(2,1)S(1)} all-to-all(bf16[8,16,3072]{2,1,0:T(8,128)(2,1)S(1)} %broadcast_in_dim.42), channel_id=1, replica_groups={{0,1,16,17,32,33,48,49},{2,3,18,19,34,35,50,51},{4,5,20,21,36,37,52,53}..., dimensions={0} | all-to-all | bytes 1572864 | tf_op jit(solution)/shard_map/all_to_all | solution.py:173
  160.4 0.6 shard_map.96
  160.9 12.8 %all_to_all.64.team_ref = bf16[8,64,128]{2,1,0:T(8,128)(2,1)S(1)} all-to-all(bf16[8,64,128]{2,1,0:T(8,128)(2,1)S(1)} %shard_map.96), channel_id=1, replica_groups={{0,1,2,3,4,5,6,7},{8,9,10,11,12,13,14,15},{16,17,18,19,20,21,22,23},{24..., dimensions={0} | all-to-all | bytes 262144 | tf_op jit(solution)/shard_map/all_to_all | solution.py:269
  173.7 1.5 shard_map.97
  175.2 3.4 %all-to-all-start.9 = ((bf16[8,64,128]{2,1,0:T(8,128)(2,1)}), bf16[8,64,128]{2,1,0:T(8,128)(2,1)S(1)}, u32[]{:S(2)}, u32[]{:S(2)}) async-start(bf16[8,64,128]{2,1,0:T(8,128)(2,1)} %shard_map.97), calls=%async_computation.9 | async-start | bytes 262144 | tf_op jit(solution)/shard_map/all_to_all | solution.py:271
  178.6 1.8 fusion.29
  180.3 0.4 fusion.forward_ref
  180.7 8.1 %all-to-all-done.9.parts_ref = bf16[8,64,128]{2,1,0:T(8,128)(2,1)S(1)} async-done(((bf16[8,64,128]{2,1,0:T(8,128)(2,1)}), bf16[8,64,128]{2,1,0:T(8,128)(2,1)S(1)}, u32[]{:S(2)}, u32[]{:S(2)}) %all-to-all-start.9) | async-done | bytes 131104 | tf_op jit(solution)/shard_map/all_to_all | solution.py:271
  188.8 0.4 shard_map.98
  189.2 10.7 %all_to_all.65 = bf16[4,32,3072]{2,1,0:T(8,128)(2,1)S(1)} all-to-all(bf16[4,32,3072]{2,1,0:T(8,128)(2,1)S(1)} %bitcast.52), channel_id=1, replica_groups={{0,16,32,48},{1,17,33,49},{2,18,34,50},{3,19,35,51},{4,20,36,52},{5,21,..., dimensions={0} | all-to-all | bytes 1572864 | tf_op jit(solution)/shard_map/all_to_all | solution.py:180
  199.9 0.2 reduce_sum.44
  200.1 0.1 convert_element_type.51
  200.2 20.7 %all_to_all.66 = bf16[16,48,128]{2,1,0:T(8,128)(2,1)S(1)} all-to-all(bf16[16,48,128]{2,1,0:T(8,128)(2,1)S(1)} %convert_element_type.51), channel_id=1, replica_groups={{0,2,4,6,8,10,12,14,1,3,5,7,9,11,13,15},{16,18,20,22,24,26,28,30,17,19,..., dimensions={0} | all-to-all | bytes 393216 | tf_op jit(solution)/shard_map/all_to_all | solution.py:180
  221.0 11.9 %collective-permute-start.6 = (bf16[2,3072]{1,0:T(2,128)(2,1)S(1)}, bf16[2,3072]{1,0:T(2,128)(2,1)S(1)}, u32[]{:S(2)}, u32[]{:S(2)}) collective-permute-start(bf16[2,3072]{1,0:T(2,128)(2,1)S(1)} %add_convert_fusion), channel_id=1, source_target_pairs={{448,0},{0,64},{64,128},{128,192},{192,256},{256,320},{320,384},{3... | collective-permute-start | bytes 36872 | tf_op jit(solution)/shard_map/ppermute | solution.py:23
  232.9 0.8 collective-permute-done.6
  233.7 0.6 copy.16
  (44 shorter events, 0.6 us)
Async XLA Ops:
  0.0 79.3 %copy-start = (bf16[1,192,3072]{2,1,0:T(8,128)(2,1)S(1)}, bf16[1,192,3072]{2,1,0:T(8,128)(2,1)}, u32[]{:S(2)}) copy-start(bf16[1,192,3072]{2,1,0:T(8,128)(2,1)} %param.13) | copy-start | bytes 3538948
  0.0 0.9 copy-start.4
  0.9 0.7 copy-start.10
  2.5 29.2 %all-to-all-start = ((bf16[16,48,128]{2,1,0:T(8,128)(2,1)}), bf16[16,48,128]{2,1,0:T(8,128)(2,1)S(1)}, u32[]{:S(2)}, u32[]{:S(2)}) async-start(bf16[16,48,128]{2,1,0:T(8,128)(2,1)} %shard_map.91), calls=%async_computation | async-start | bytes 393216 | tf_op jit(solution)/shard_map/all_to_all | solution.py:254
  19.4 17.5 %collective-permute-start.2 = (bf16[48,768]{1,0:T(8,128)(2,1)S(1)}, bf16[48,768]{1,0:T(8,128)(2,1)S(1)}, u32[]{:S(2)}, u32[]{:S(2)}) collective-permute-start(bf16[48,768]{1,0:T(8,128)(2,1)S(1)} %get-tuple-element.16), channel_id=1, source_target_pairs={{0,48},{1,49},{2,50},{3,51},{4,52},{5,53},{6,54},{7,55},{8,56},{9,... | collective-permute-start | bytes 221192 | tf_op jit(solution)/shard_map/ppermute | solution.py:246
  23.8 13.1 %collective-permute-start.1 = (bf16[48,768]{1,0:T(8,128)(2,1)S(1)}, bf16[48,768]{1,0:T(8,128)(2,1)S(1)}, u32[]{:S(2)}, u32[]{:S(2)}) collective-permute-start(bf16[48,768]{1,0:T(8,128)(2,1)S(1)} %get-tuple-element.17), channel_id=1, source_target_pairs={{0,32},{1,33},{2,34},{3,35},{4,36},{5,37},{6,38},{7,39},{8,40},{9,... | collective-permute-start | bytes 221192 | tf_op jit(solution)/shard_map/ppermute | solution.py:246
  26.2 10.7 %collective-permute-start = (bf16[48,768]{1,0:T(8,128)(2,1)S(1)}, bf16[48,768]{1,0:T(8,128)(2,1)S(1)}, u32[]{:S(2)}, u32[]{:S(2)}) collective-permute-start(bf16[48,768]{1,0:T(8,128)(2,1)S(1)} %get-tuple-element.18), channel_id=1, source_target_pairs={{0,16},{1,17},{2,18},{3,19},{4,20},{5,21},{6,22},{7,23},{8,24},{9,... | collective-permute-start | bytes 221192 | tf_op jit(solution)/shard_map/ppermute | solution.py:246
  32.7 13.9 %copy-start.1 = (bf16[1,3,48,3072]{3,2,1,0:T(8,128)(2,1)S(1)}, bf16[1,3,48,3072]{3,2,1,0:T(8,128)(2,1)}, u32[]{:S(2)}) copy-start(bf16[1,3,48,3072]{3,2,1,0:T(8,128)(2,1)} %param.10) | copy-start | bytes 2654212
  32.7 13.9 %all-to-all-start.1 = ((bf16[4,32,3072]{2,1,0:T(8,128)(2,1)}), bf16[4,32,3072]{2,1,0:T(8,128)(2,1)S(1)}, u32[]{:S(2)}, u32[]{:S(2)}) async-start(bf16[4,32,3072]{2,1,0:T(8,128)(2,1)} %broadcast_in_dim.37), calls=%async_computation.1 | async-start | bytes 1572864 | tf_op jit(solution)/shard_map/all_to_all | solution.py:173
  37.0 19.6 %copy-start.12 = (f32[1,2,128]{2,1,0:T(2,128)S(1)}, f32[1,2,128]{2,1,0:T(2,128)}, u32[]{:S(2)}) copy-start(f32[1,2,128]{2,1,0:T(2,128)} %param.15) | copy-start | bytes 3076
  37.0 9.6 %collective-permute-start.3 = (bf16[2,48,384]{2,1,0:T(8,128)(2,1)S(1)}, bf16[2,48,384]{2,1,0:T(8,128)(2,1)S(1)}, u32[]{:S(2)}, u32[]{:S(2)}) collective-permute-start(bf16[2,48,384]{2,1,0:T(8,128)(2,1)S(1)} %get-tuple-element.20), channel_id=1, source_target_pairs={{0,12},{1,13},{2,14},{3,15},{4,8},{5,9},{6,10},{7,11},{8,4},{9,5},... | collective-permute-start | bytes 221192 | tf_op jit(solution)/shard_map/ppermute | solution.py:258
  46.7 21.2 %copy-start.6 = (bf16[2,48,384]{2,1,0:T(8,128)(2,1)}, bf16[2,48,384]{2,1,0:T(8,128)(2,1)S(1)}, u32[]{:S(2)}) copy-start(bf16[2,48,384]{2,1,0:T(8,128)(2,1)S(1)} %collective-permute-done.3.refs_1_) | copy-start | bytes 221188
  47.9 18.4 %all-to-all-start.2 = ((bf16[8,64,128]{2,1,0:T(8,128)(2,1)}), bf16[8,64,128]{2,1,0:T(8,128)(2,1)S(1)}, u32[]{:S(2)}, u32[]{:S(2)}) async-start(bf16[8,64,128]{2,1,0:T(8,128)(2,1)} %shard_map.92), calls=%async_computation.2 | async-start | bytes 262144 | tf_op jit(solution)/shard_map/all_to_all | solution.py:269
  56.7 9.6 %collective-permute-start.4 = (bf16[2,48,384]{2,1,0:T(8,128)(2,1)S(1)}, bf16[2,48,384]{2,1,0:T(8,128)(2,1)S(1)}, u32[]{:S(2)}, u32[]{:S(2)}) collective-permute-start(bf16[2,48,384]{2,1,0:T(8,128)(2,1)S(1)} %get-tuple-element.19), channel_id=1, source_target_pairs={{0,12},{1,13},{2,14},{3,15},{4,8},{5,9},{6,10},{7,11},{8,4},{9,5},... | collective-permute-start | bytes 221192 | tf_op jit(solution)/shard_map/ppermute | solution.py:258
  66.3 11.3 %copy-start.8 = (bf16[2,48,384]{2,1,0:T(8,128)(2,1)}, bf16[2,48,384]{2,1,0:T(8,128)(2,1)S(1)}, u32[]{:S(2)}) copy-start(bf16[2,48,384]{2,1,0:T(8,128)(2,1)S(1)} %collective-permute-done.4.refs_2_) | copy-start | bytes 221188
  67.9 20.0 %all-to-all-start.3 = ((bf16[8,64,128]{2,1,0:T(8,128)(2,1)}), bf16[8,64,128]{2,1,0:T(8,128)(2,1)S(1)}, u32[]{:S(2)}, u32[]{:S(2)}) async-start(bf16[8,64,128]{2,1,0:T(8,128)(2,1)} %shard_map.93), calls=%async_computation.3 | async-start | bytes 262144 | tf_op jit(solution)/shard_map/all_to_all | solution.py:271
  79.4 8.5 %copy-start.3 = (bf16[1,48,3072]{2,1,0:T(8,128)(2,1)S(1)}, bf16[1,48,3072]{2,1,0:T(8,128)(2,1)}, u32[]{:S(2)}) copy-start(bf16[1,48,3072]{2,1,0:T(8,128)(2,1)} %param.12) | copy-start | bytes 884740
  79.4 8.5 %copy-start.5 = (f32[1,3,3072]{2,0,1:T(1,128)S(1)}, f32[1,3,3072]{2,0,1:T(1,128)}, u32[]{:S(2)}) copy-start(f32[1,3,3072]{2,0,1:T(1,128)} %param.14) | copy-start | bytes 110596
  99.0 21.0 %copy-start.11 = (bf16[1,2,3072]{2,1,0:T(2,128)(2,1)S(1)}, bf16[1,2,3072]{2,1,0:T(2,128)(2,1)}, u32[]{:S(2)}) copy-start(bf16[1,2,3072]{2,1,0:T(2,128)(2,1)} %param.9) | copy-start | bytes 36868
  120.1 11.3 %collective-permute-start.5 = (bf16[2,3072]{1,0:T(2,128)(2,1)S(1)}, bf16[2,3072]{1,0:T(2,128)(2,1)S(1)}, u32[]{:S(2)}, u32[]{:S(2)}) collective-permute-start(bf16[2,3072]{1,0:T(2,128)(2,1)S(1)} %add_convert_fusion.1), channel_id=1, source_target_pairs={{448,0},{0,64},{64,128},{128,192},{192,256},{256,320},{320,384},{3... | collective-permute-start | bytes 36872 | tf_op jit(solution)/shard_map/ppermute | solution.py:23
  148.7 11.6 %copy-start.2 = (bf16[1,3,48,3072]{3,2,1,0:T(8,128)(2,1)S(1)}, bf16[1,3,48,3072]{3,2,1,0:T(8,128)(2,1)}, u32[]{:S(2)}) copy-start(bf16[1,3,48,3072]{3,2,1,0:T(8,128)(2,1)} %param.10) | copy-start | bytes 2654212
  160.4 13.3 %copy-start.7 = (bf16[2,48,384]{2,1,0:T(8,128)(2,1)S(1)}, bf16[2,48,384]{2,1,0:T(8,128)(2,1)}, u32[]{:S(2)}) copy-start(bf16[2,48,384]{2,1,0:T(8,128)(2,1)} %copy-done.6) | copy-start | bytes 221188
  160.4 13.3 %copy-start.9 = (bf16[2,48,384]{2,1,0:T(8,128)(2,1)S(1)}, bf16[2,48,384]{2,1,0:T(8,128)(2,1)}, u32[]{:S(2)}) copy-start(bf16[2,48,384]{2,1,0:T(8,128)(2,1)} %copy-done.8) | copy-start | bytes 221188
  175.2 13.6 %all-to-all-start.9 = ((bf16[8,64,128]{2,1,0:T(8,128)(2,1)}), bf16[8,64,128]{2,1,0:T(8,128)(2,1)S(1)}, u32[]{:S(2)}, u32[]{:S(2)}) async-start(bf16[8,64,128]{2,1,0:T(8,128)(2,1)} %shard_map.97), calls=%async_computation.9 | async-start | bytes 262144 | tf_op jit(solution)/shard_map/all_to_all | solution.py:271
  221.0 12.8 %collective-permute-start.6 = (bf16[2,3072]{1,0:T(2,128)(2,1)S(1)}, bf16[2,3072]{1,0:T(2,128)(2,1)S(1)}, u32[]{:S(2)}, u32[]{:S(2)}) collective-permute-start(bf16[2,3072]{1,0:T(2,128)(2,1)S(1)} %add_convert_fusion), channel_id=1, source_target_pairs={{448,0},{0,64},{64,128},{128,192},{192,256},{256,320},{320,384},{3... | collective-permute-start | bytes 36872 | tf_op jit(solution)/shard_map/ppermute | solution.py:23

commit v17 on v16

--- a/solution.py
+++ b/solution.py
@@ -199,7 +199,10 @@
     along_z = [[z_count * x + 2 * h + l for l in two for h in hs] for x in xs]
     along_x = [[z_count * x + z for x in xs] for z in range(z_count)]
     far = [[z_count * x + 2 * h + l for h in hs] for x in xs for l in two]
-    blocks = [[z_count * x + 2 * h + l for x in xs for l in two] for h in hs]
+    blocks = [
+        [z_count * x + 2 * h for x in xs] + [z_count * x + 2 * h + 1 for x in reversed(xs)]
+        for h in hs
+    ]
     inside = [[TEAM * t + m for m in range(TEAM)] for t in range(teams)]
     shift_scale = modulation.reshape(3, 1, width)
     gains = qk_gain[0]
@@ -279,8 +282,9 @@
         forward = jnp.dot(hidden, weight_down, preferred_element_type=f32)
         forward = lax.optimization_barrier(forward)
         branch = finish(member[None], parts, weight_attn, forward, shift_scale)
-        branch = summed_over(branch, along_x)
-        branch = summed_over(branch.reshape(-1, LANES), along_z).reshape(rows, width)
+        near_groups, far_groups = (blocks, far) if tick_number else (along_x, along_z)
+        branch = summed_over(branch, near_groups)
+        branch = summed_over(branch.reshape(-1, LANES), far_groups).reshape(rows, width)
         finished = (current.astype(f32) + branch).astype(bf16)
         current = shifted(finished, "pipe", 1)
     return current[None]

time: 235 us -> 236 us (level)
  no operation moved by 1% of the time
where the time goes in v17:
time: 236 us; the launch traced here: 235 us
  blocking collectives  105 us (44%)
  starting transfers between devices  88.4 us (37%)
  waiting for transfers between devices  24.5 us (10%)
  Pallas kernels  6.7 us (3%)
  local copies, waits for them, and re-layouts  4.81 us (2%)
  matrix products  4.32 us (2%)
    all_to_all x4, blocking collectives, summed_over(): parts = lax.all_to_all(parts, 'tp', 0, 0, axis_index_groups=groups)  63.3 us
    ppermute x2, starting transfers between devices, shifted(): lax.ppermute(block, axis, [((i - distance) % size, i) for i in range(size)])  22.7 us
    all_to_all x1, blocking collectives, local(): normed = lax.all_to_all(block, 'tp', 0, 0, axis_index_groups=far)  17.1 us
    all_to_all x2, waiting for transfers between devices, local(): parts = lax.all_to_all(parts, 'tp', 0, 0, axis_index_groups=inside)  16.1 us
    all_to_all x1, starting transfers between devices, local(): normed = lax.all_to_all(block, 'tp', 0, 0, axis_index_groups=along_z)  15.7 us
    ppermute x2, starting transfers between devices, local(): lax.ppermute(part, 'tp', route)  15.5 us
    all_to_all x2, starting transfers between devices, local(): parts = lax.all_to_all(parts, 'tp', 0, 0, axis_index_groups=inside)  13 us
    all_to_all x1, blocking collectives, local(): team = lax.all_to_all(team, 'tp', 0, 0, axis_index_groups=inside)  12.7 us
  transfers between devices with their start and end apart: 12, of which 7 were waited for; matrix products, arithmetic and copies ran while one was open for 3% of the time, Pallas kernels for 0%

profile of v17, /device:TPU:1, one launch (start us, length us, event | category | flops | bytes accessed | tf_op | source)
XLA Modules:
  0.0 235.1 jit_solution(17165513011720437046)
XLA Ops:
  0.0 0.9 copy-done.4
  0.9 0.7 copy-done.10
  1.6 0.9 shard_map.91
  2.5 15.7 %all-to-all-start = ((bf16[16,48,128]{2,1,0:T(8,128)(2,1)}), bf16[16,48,128]{2,1,0:T(8,128)(2,1)S(1)}, u32[]{:S(2)}, u32[]{:S(2)}) async-start(bf16[16,48,128]{2,1,0:T(8,128)(2,1)} %shard_map.91), calls=%async_computation | async-start | bytes 393216 | tf_op jit(solution)/shard_map/all_to_all | solution.py:257
  18.4 1.0 dynamic-slice_bitcast_fusion
  19.4 4.4 %collective-permute-start.2 = (bf16[48,768]{1,0:T(8,128)(2,1)S(1)}, bf16[48,768]{1,0:T(8,128)(2,1)S(1)}, u32[]{:S(2)}, u32[]{:S(2)}) collective-permute-start(bf16[48,768]{1,0:T(8,128)(2,1)S(1)} %get-tuple-element.16), channel_id=1, source_target_pairs={{0,48},{1,49},{2,50},{3,51},{4,52},{5,53},{6,54},{7,55},{8,56},{9,... | collective-permute-start | bytes 221192 | tf_op jit(solution)/shard_map/ppermute | solution.py:249
  23.8 2.4 %collective-permute-start.1 = (bf16[48,768]{1,0:T(8,128)(2,1)S(1)}, bf16[48,768]{1,0:T(8,128)(2,1)S(1)}, u32[]{:S(2)}, u32[]{:S(2)}) collective-permute-start(bf16[48,768]{1,0:T(8,128)(2,1)S(1)} %get-tuple-element.17), channel_id=1, source_target_pairs={{0,32},{1,33},{2,34},{3,35},{4,36},{5,37},{6,38},{7,39},{8,40},{9,... | collective-permute-start | bytes 221192 | tf_op jit(solution)/shard_map/ppermute | solution.py:249
  26.2 2.5 %collective-permute-start = (bf16[48,768]{1,0:T(8,128)(2,1)S(1)}, bf16[48,768]{1,0:T(8,128)(2,1)S(1)}, u32[]{:S(2)}, u32[]{:S(2)}) collective-permute-start(bf16[48,768]{1,0:T(8,128)(2,1)S(1)} %get-tuple-element.18), channel_id=1, source_target_pairs={{0,16},{1,17},{2,18},{3,19},{4,20},{5,21},{6,22},{7,23},{8,24},{9,... | collective-permute-start | bytes 221192 | tf_op jit(solution)/shard_map/ppermute | solution.py:249
  28.8 2.9 %all-to-all-done = bf16[16,48,128]{2,1,0:T(8,128)(2,1)S(1)} async-done(((bf16[16,48,128]{2,1,0:T(8,128)(2,1)}), bf16[16,48,128]{2,1,0:T(8,128)(2,1)S(1)}, u32[]{:S(2)}, u32[]{:S(2)}) %all-to-all-start) | async-done | bytes 196640 | tf_op jit(solution)/shard_map/all_to_all | solution.py:257
  31.7 0.1 broadcast_in_dim.36
  31.8 1.0 broadcast_in_dim.37
  32.7 4.1 %all-to-all-start.1 = ((bf16[4,32,3072]{2,1,0:T(8,128)(2,1)}), bf16[4,32,3072]{2,1,0:T(8,128)(2,1)S(1)}, u32[]{:S(2)}, u32[]{:S(2)}) async-start(bf16[4,32,3072]{2,1,0:T(8,128)(2,1)} %broadcast_in_dim.37), calls=%async_computation.1 | async-start | bytes 1572864 | tf_op jit(solution)/shard_map/all_to_all | solution.py:173
  37.0 7.9 %collective-permute-start.3 = (bf16[2,48,384]{2,1,0:T(8,128)(2,1)S(1)}, bf16[2,48,384]{2,1,0:T(8,128)(2,1)S(1)}, u32[]{:S(2)}, u32[]{:S(2)}) collective-permute-start(bf16[2,48,384]{2,1,0:T(8,128)(2,1)S(1)} %get-tuple-element.20), channel_id=1, source_target_pairs={{0,12},{1,13},{2,14},{3,15},{4,8},{5,9},{6,10},{7,11},{8,4},{9,5},... | collective-permute-start | bytes 221192 | tf_op jit(solution)/shard_map/ppermute | solution.py:261
  44.9 1.7 collective-permute-done.3.refs_1_
  46.7 1.2 shard_map.92
  47.9 8.0 %all-to-all-start.2 = ((bf16[8,64,128]{2,1,0:T(8,128)(2,1)}), bf16[8,64,128]{2,1,0:T(8,128)(2,1)S(1)}, u32[]{:S(2)}, u32[]{:S(2)}) async-start(bf16[8,64,128]{2,1,0:T(8,128)(2,1)} %shard_map.92), calls=%async_computation.2 | async-start | bytes 262144 | tf_op jit(solution)/shard_map/all_to_all | solution.py:272
  56.6 0.1 copy.12.gain_q_ref
  56.7 7.6 %collective-permute-start.4 = (bf16[2,48,384]{2,1,0:T(8,128)(2,1)S(1)}, bf16[2,48,384]{2,1,0:T(8,128)(2,1)S(1)}, u32[]{:S(2)}, u32[]{:S(2)}) collective-permute-start(bf16[2,48,384]{2,1,0:T(8,128)(2,1)S(1)} %get-tuple-element.19), channel_id=1, source_target_pairs={{0,12},{1,13},{2,14},{3,15},{4,8},{5,9},{6,10},{7,11},{8,4},{9,5},... | collective-permute-start | bytes 221192 | tf_op jit(solution)/shard_map/ppermute | solution.py:261
  64.3 2.0 collective-permute-done.4.refs_2_
  66.4 1.5 shard_map.93
  67.9 9.7 %all-to-all-start.3 = ((bf16[8,64,128]{2,1,0:T(8,128)(2,1)}), bf16[8,64,128]{2,1,0:T(8,128)(2,1)S(1)}, u32[]{:S(2)}, u32[]{:S(2)}) async-start(bf16[8,64,128]{2,1,0:T(8,128)(2,1)} %shard_map.93), calls=%async_computation.3 | async-start | bytes 262144 | tf_op jit(solution)/shard_map/all_to_all | solution.py:274
  77.6 1.8 fusion.17
  79.4 0.4 fusion.2.forward_ref
  79.8 8.1 %all-to-all-done.3.parts_ref = bf16[8,64,128]{2,1,0:T(8,128)(2,1)S(1)} async-done(((bf16[8,64,128]{2,1,0:T(8,128)(2,1)}), bf16[8,64,128]{2,1,0:T(8,128)(2,1)S(1)}, u32[]{:S(2)}, u32[]{:S(2)}) %all-to-all-start.3) | async-done | bytes 131104 | tf_op jit(solution)/shard_map/all_to_all | solution.py:274
  87.9 0.4 shard_map.94
  88.3 10.7 %all_to_all.60 = bf16[4,32,3072]{2,1,0:T(8,128)(2,1)S(1)} all-to-all(bf16[4,32,3072]{2,1,0:T(8,128)(2,1)S(1)} %bitcast.53), channel_id=1, replica_groups={{0,16,32,48},{1,17,33,49},{2,18,34,50},{3,19,35,51},{4,20,36,52},{5,21,..., dimensions={0} | all-to-all | bytes 1572864 | tf_op jit(solution)/shard_map/all_to_all | solution.py:180
  99.0 0.2 reduce_sum.42
  99.2 0.1 convert_element_type.46
  99.3 20.7 %all_to_all.61 = bf16[16,48,128]{2,1,0:T(8,128)(2,1)S(1)} all-to-all(bf16[16,48,128]{2,1,0:T(8,128)(2,1)S(1)} %convert_element_type.46), channel_id=1, replica_groups={{0,2,4,6,8,10,12,14,1,3,5,7,9,11,13,15},{16,18,20,22,24,26,28,30,17,19,..., dimensions={0} | all-to-all | bytes 393216 | tf_op jit(solution)/shard_map/all_to_all | solution.py:180
  120.1 10.4 %collective-permute-start.5 = (bf16[2,3072]{1,0:T(2,128)(2,1)S(1)}, bf16[2,3072]{1,0:T(2,128)(2,1)S(1)}, u32[]{:S(2)}, u32[]{:S(2)}) collective-permute-start(bf16[2,3072]{1,0:T(2,128)(2,1)S(1)} %add_convert_fusion.1), channel_id=1, source_target_pairs={{448,0},{0,64},{64,128},{128,192},{192,256},{256,320},{320,384},{3... | collective-permute-start | bytes 36872 | tf_op jit(solution)/shard_map/ppermute | solution.py:23
  130.5 0.8 collective-permute-done.5.rows_ref
  131.3 0.2 shard_map.95
  131.6 17.1 %all_to_all.62 = bf16[8,48,128]{2,1,0:T(8,128)(2,1)S(1)} all-to-all(bf16[8,48,128]{2,1,0:T(8,128)(2,1)S(1)} %shard_map.95), channel_id=1, replica_groups={{0,2,4,6,8,10,12,14},{1,3,5,7,9,11,13,15},{16,18,20,22,24,26,28,30},{17..., dimensions={0} | all-to-all | bytes 196608 | tf_op jit(solution)/shard_map/all_to_all | solution.py:269
  148.8 11.8 %all_to_all.63 = bf16[8,16,3072]{2,1,0:T(8,128)(2,1)S(1)} all-to-all(bf16[8,16,3072]{2,1,0:T(8,128)(2,1)S(1)} %broadcast_in_dim.42), channel_id=1, replica_groups={{0,16,32,48,49,33,17,1},{2,18,34,50,51,35,19,3},{4,20,36,52,53,37,21,5}..., dimensions={0} | all-to-all | bytes 1572864 | tf_op jit(solution)/shard_map/all_to_all | solution.py:173
  160.7 0.6 shard_map.96
  161.2 12.7 %all_to_all.64.team_ref = bf16[8,64,128]{2,1,0:T(8,128)(2,1)S(1)} all-to-all(bf16[8,64,128]{2,1,0:T(8,128)(2,1)S(1)} %shard_map.96), channel_id=1, replica_groups={{0,1,2,3,4,5,6,7},{8,9,10,11,12,13,14,15},{16,17,18,19,20,21,22,23},{24..., dimensions={0} | all-to-all | bytes 262144 | tf_op jit(solution)/shard_map/all_to_all | solution.py:272
  173.9 1.5 shard_map.97
  175.4 3.4 %all-to-all-start.9 = ((bf16[8,64,128]{2,1,0:T(8,128)(2,1)}), bf16[8,64,128]{2,1,0:T(8,128)(2,1)S(1)}, u32[]{:S(2)}, u32[]{:S(2)}) async-start(bf16[8,64,128]{2,1,0:T(8,128)(2,1)} %shard_map.97), calls=%async_computation.9 | async-start | bytes 262144 | tf_op jit(solution)/shard_map/all_to_all | solution.py:274
  178.7 1.8 fusion.29
  180.5 0.4 fusion.forward_ref
  180.9 8.0 %all-to-all-done.9.parts_ref = bf16[8,64,128]{2,1,0:T(8,128)(2,1)S(1)} async-done(((bf16[8,64,128]{2,1,0:T(8,128)(2,1)}), bf16[8,64,128]{2,1,0:T(8,128)(2,1)S(1)}, u32[]{:S(2)}, u32[]{:S(2)}) %all-to-all-start.9) | async-done | bytes 131104 | tf_op jit(solution)/shard_map/all_to_all | solution.py:274
  189.0 0.4 shard_map.98
  189.4 11.4 %all_to_all.65 = bf16[8,16,3072]{2,1,0:T(8,128)(2,1)S(1)} all-to-all(bf16[8,16,3072]{2,1,0:T(8,128)(2,1)S(1)} %bitcast.52), channel_id=1, replica_groups={{0,16,32,48,49,33,17,1},{2,18,34,50,51,35,19,3},{4,20,36,52,53,37,21,5}..., dimensions={0} | all-to-all | bytes 1572864 | tf_op jit(solution)/shard_map/all_to_all | solution.py:180
  200.7 0.1 reduce_sum.44
  200.9 20.5 %all_to_all.66 = bf16[8,48,128]{2,1,0:T(8,128)(2,1)S(1)} all-to-all(bf16[8,48,128]{2,1,0:T(8,128)(2,1)S(1)} %convert_element_type.51), channel_id=1, replica_groups={{0,2,4,6,8,10,12,14},{1,3,5,7,9,11,13,15},{16,18,20,22,24,26,28,30},{17..., dimensions={0} | all-to-all | bytes 196608 | tf_op jit(solution)/shard_map/all_to_all | solution.py:180
  221.4 12.3 %collective-permute-start.6 = (bf16[2,3072]{1,0:T(2,128)(2,1)S(1)}, bf16[2,3072]{1,0:T(2,128)(2,1)S(1)}, u32[]{:S(2)}, u32[]{:S(2)}) collective-permute-start(bf16[2,3072]{1,0:T(2,128)(2,1)S(1)} %add_convert_fusion), channel_id=1, source_target_pairs={{448,0},{0,64},{64,128},{128,192},{192,256},{256,320},{320,384},{3... | collective-permute-start | bytes 36872 | tf_op jit(solution)/shard_map/ppermute | solution.py:23
  233.7 0.8 collective-permute-done.6
  234.5 0.6 copy.16
  (44 shorter events, 0.6 us)
Async XLA Ops:
  0.0 79.3 %copy-start = (bf16[1,192,3072]{2,1,0:T(8,128)(2,1)S(1)}, bf16[1,192,3072]{2,1,0:T(8,128)(2,1)}, u32[]{:S(2)}) copy-start(bf16[1,192,3072]{2,1,0:T(8,128)(2,1)} %param.13) | copy-start | bytes 3538948
  0.0 0.9 copy-start.4
  0.9 0.7 copy-start.10
  2.5 29.2 %all-to-all-start = ((bf16[16,48,128]{2,1,0:T(8,128)(2,1)}), bf16[16,48,128]{2,1,0:T(8,128)(2,1)S(1)}, u32[]{:S(2)}, u32[]{:S(2)}) async-start(bf16[16,48,128]{2,1,0:T(8,128)(2,1)} %shard_map.91), calls=%async_computation | async-start | bytes 393216 | tf_op jit(solution)/shard_map/all_to_all | solution.py:257
  19.4 17.5 %collective-permute-start.2 = (bf16[48,768]{1,0:T(8,128)(2,1)S(1)}, bf16[48,768]{1,0:T(8,128)(2,1)S(1)}, u32[]{:S(2)}, u32[]{:S(2)}) collective-permute-start(bf16[48,768]{1,0:T(8,128)(2,1)S(1)} %get-tuple-element.16), channel_id=1, source_target_pairs={{0,48},{1,49},{2,50},{3,51},{4,52},{5,53},{6,54},{7,55},{8,56},{9,... | collective-permute-start | bytes 221192 | tf_op jit(solution)/shard_map/ppermute | solution.py:249
  23.8 13.1 %collective-permute-start.1 = (bf16[48,768]{1,0:T(8,128)(2,1)S(1)}, bf16[48,768]{1,0:T(8,128)(2,1)S(1)}, u32[]{:S(2)}, u32[]{:S(2)}) collective-permute-start(bf16[48,768]{1,0:T(8,128)(2,1)S(1)} %get-tuple-element.17), channel_id=1, source_target_pairs={{0,32},{1,33},{2,34},{3,35},{4,36},{5,37},{6,38},{7,39},{8,40},{9,... | collective-permute-start | bytes 221192 | tf_op jit(solution)/shard_map/ppermute | solution.py:249
  26.2 10.7 %collective-permute-start = (bf16[48,768]{1,0:T(8,128)(2,1)S(1)}, bf16[48,768]{1,0:T(8,128)(2,1)S(1)}, u32[]{:S(2)}, u32[]{:S(2)}) collective-permute-start(bf16[48,768]{1,0:T(8,128)(2,1)S(1)} %get-tuple-element.18), channel_id=1, source_target_pairs={{0,16},{1,17},{2,18},{3,19},{4,20},{5,21},{6,22},{7,23},{8,24},{9,... | collective-permute-start | bytes 221192 | tf_op jit(solution)/shard_map/ppermute | solution.py:249
  32.7 13.9 %copy-start.1 = (bf16[1,3,48,3072]{3,2,1,0:T(8,128)(2,1)S(1)}, bf16[1,3,48,3072]{3,2,1,0:T(8,128)(2,1)}, u32[]{:S(2)}) copy-start(bf16[1,3,48,3072]{3,2,1,0:T(8,128)(2,1)} %param.10) | copy-start | bytes 2654212
  32.7 13.9 %all-to-all-start.1 = ((bf16[4,32,3072]{2,1,0:T(8,128)(2,1)}), bf16[4,32,3072]{2,1,0:T(8,128)(2,1)S(1)}, u32[]{:S(2)}, u32[]{:S(2)}) async-start(bf16[4,32,3072]{2,1,0:T(8,128)(2,1)} %broadcast_in_dim.37), calls=%async_computation.1 | async-start | bytes 1572864 | tf_op jit(solution)/shard_map/all_to_all | solution.py:173
  37.0 19.6 %copy-start.12 = (f32[1,2,128]{2,1,0:T(2,128)S(1)}, f32[1,2,128]{2,1,0:T(2,128)}, u32[]{:S(2)}) copy-start(f32[1,2,128]{2,1,0:T(2,128)} %param.15) | copy-start | bytes 3076
  37.0 9.6 %collective-permute-start.3 = (bf16[2,48,384]{2,1,0:T(8,128)(2,1)S(1)}, bf16[2,48,384]{2,1,0:T(8,128)(2,1)S(1)}, u32[]{:S(2)}, u32[]{:S(2)}) collective-permute-start(bf16[2,48,384]{2,1,0:T(8,128)(2,1)S(1)} %get-tuple-element.20), channel_id=1, source_target_pairs={{0,12},{1,13},{2,14},{3,15},{4,8},{5,9},{6,10},{7,11},{8,4},{9,5},... | collective-permute-start | bytes 221192 | tf_op jit(solution)/shard_map/ppermute | solution.py:261
  46.7 21.2 %copy-start.6 = (bf16[2,48,384]{2,1,0:T(8,128)(2,1)}, bf16[2,48,384]{2,1,0:T(8,128)(2,1)S(1)}, u32[]{:S(2)}) copy-start(bf16[2,48,384]{2,1,0:T(8,128)(2,1)S(1)} %collective-permute-done.3.refs_1_) | copy-start | bytes 221188
  47.9 18.4 %all-to-all-start.2 = ((bf16[8,64,128]{2,1,0:T(8,128)(2,1)}), bf16[8,64,128]{2,1,0:T(8,128)(2,1)S(1)}, u32[]{:S(2)}, u32[]{:S(2)}) async-start(bf16[8,64,128]{2,1,0:T(8,128)(2,1)} %shard_map.92), calls=%async_computation.2 | async-start | bytes 262144 | tf_op jit(solution)/shard_map/all_to_all | solution.py:272
  56.7 9.6 %collective-permute-start.4 = (bf16[2,48,384]{2,1,0:T(8,128)(2,1)S(1)}, bf16[2,48,384]{2,1,0:T(8,128)(2,1)S(1)}, u32[]{:S(2)}, u32[]{:S(2)}) collective-permute-start(bf16[2,48,384]{2,1,0:T(8,128)(2,1)S(1)} %get-tuple-element.19), channel_id=1, source_target_pairs={{0,12},{1,13},{2,14},{3,15},{4,8},{5,9},{6,10},{7,11},{8,4},{9,5},... | collective-permute-start | bytes 221192 | tf_op jit(solution)/shard_map/ppermute | solution.py:261
  66.3 11.3 %copy-start.8 = (bf16[2,48,384]{2,1,0:T(8,128)(2,1)}, bf16[2,48,384]{2,1,0:T(8,128)(2,1)S(1)}, u32[]{:S(2)}) copy-start(bf16[2,48,384]{2,1,0:T(8,128)(2,1)S(1)} %collective-permute-done.4.refs_2_) | copy-start | bytes 221188
  67.9 20.0 %all-to-all-start.3 = ((bf16[8,64,128]{2,1,0:T(8,128)(2,1)}), bf16[8,64,128]{2,1,0:T(8,128)(2,1)S(1)}, u32[]{:S(2)}, u32[]{:S(2)}) async-start(bf16[8,64,128]{2,1,0:T(8,128)(2,1)} %shard_map.93), calls=%async_computation.3 | async-start | bytes 262144 | tf_op jit(solution)/shard_map/all_to_all | solution.py:274
  79.4 8.5 %copy-start.3 = (bf16[1,48,3072]{2,1,0:T(8,128)(2,1)S(1)}, bf16[1,48,3072]{2,1,0:T(8,128)(2,1)}, u32[]{:S(2)}) copy-start(bf16[1,48,3072]{2,1,0:T(8,128)(2,1)} %param.12) | copy-start | bytes 884740
  79.4 8.5 %copy-start.5 = (f32[1,3,3072]{2,0,1:T(1,128)S(1)}, f32[1,3,3072]{2,0,1:T(1,128)}, u32[]{:S(2)}) copy-start(f32[1,3,3072]{2,0,1:T(1,128)} %param.14) | copy-start | bytes 110596
  99.0 21.0 %copy-start.11 = (bf16[1,2,3072]{2,1,0:T(2,128)(2,1)S(1)}, bf16[1,2,3072]{2,1,0:T(2,128)(2,1)}, u32[]{:S(2)}) copy-start(bf16[1,2,3072]{2,1,0:T(2,128)(2,1)} %param.9) | copy-start | bytes 36868
  120.1 11.3 %collective-permute-start.5 = (bf16[2,3072]{1,0:T(2,128)(2,1)S(1)}, bf16[2,3072]{1,0:T(2,128)(2,1)S(1)}, u32[]{:S(2)}, u32[]{:S(2)}) collective-permute-start(bf16[2,3072]{1,0:T(2,128)(2,1)S(1)} %add_convert_fusion.1), channel_id=1, source_target_pairs={{448,0},{0,64},{64,128},{128,192},{192,256},{256,320},{320,384},{3... | collective-permute-start | bytes 36872 | tf_op jit(solution)/shard_map/ppermute | solution.py:23
  148.7 11.9 %copy-start.2 = (bf16[1,3,48,3072]{3,2,1,0:T(8,128)(2,1)S(1)}, bf16[1,3,48,3072]{3,2,1,0:T(8,128)(2,1)}, u32[]{:S(2)}) copy-start(bf16[1,3,48,3072]{3,2,1,0:T(8,128)(2,1)} %param.10) | copy-start | bytes 2654212
  160.6 13.2 %copy-start.7 = (bf16[2,48,384]{2,1,0:T(8,128)(2,1)S(1)}, bf16[2,48,384]{2,1,0:T(8,128)(2,1)}, u32[]{:S(2)}) copy-start(bf16[2,48,384]{2,1,0:T(8,128)(2,1)} %copy-done.6) | copy-start | bytes 221188
  160.6 13.2 %copy-start.9 = (bf16[2,48,384]{2,1,0:T(8,128)(2,1)S(1)}, bf16[2,48,384]{2,1,0:T(8,128)(2,1)}, u32[]{:S(2)}) copy-start(bf16[2,48,384]{2,1,0:T(8,128)(2,1)} %copy-done.8) | copy-start | bytes 221188
  175.4 13.6 %all-to-all-start.9 = ((bf16[8,64,128]{2,1,0:T(8,128)(2,1)}), bf16[8,64,128]{2,1,0:T(8,128)(2,1)S(1)}, u32[]{:S(2)}, u32[]{:S(2)}) async-start(bf16[8,64,128]{2,1,0:T(8,128)(2,1)} %shard_map.97), calls=%async_computation.9 | async-start | bytes 262144 | tf_op jit(solution)/shard_map/all_to_all | solution.py:274
  221.4 13.1 %collective-permute-start.6 = (bf16[2,3072]{1,0:T(2,128)(2,1)S(1)}, bf16[2,3072]{1,0:T(2,128)(2,1)S(1)}, u32[]{:S(2)}, u32[]{:S(2)}) collective-permute-start(bf16[2,3072]{1,0:T(2,128)(2,1)S(1)} %add_convert_fusion), channel_id=1, source_target_pairs={{448,0},{0,64},{64,128},{128,192},{192,256},{256,320},{320,384},{3... | collective-permute-start | bytes 36872 | tf_op jit(solution)/shard_map/ppermute | solution.py:23

commit v18 on v16

--- a/solution.py
+++ b/solution.py
@@ -256,7 +256,7 @@
             route = [(z_count * x + z, z_count * x + partner[z]) for x in xs for z in range(z_count)]
             got = [
                 lax.ppermute(part, "tp", route)
-                for part in (give[: x_count // 2], give[x_count // 2 :])
+                for part in (give[: x_count - 1], give[x_count - 1 :])
             ]
             normed = gathered(normed, along_x)
             normed, got[0] = lax.optimization_barrier((normed, got[0]))

time: 235 us -> 250 us (1.064)
  waiting for transfers between devices: 24.5 us -> 46 us
  starting transfers between devices: 88.1 us -> 79.7 us
    all_to_all x1, waiting for transfers between devices: 2.92 us -> 13.3 us  [local(): normed = lax.all_to_all(block, 'tp', 0, 0, axis_index_groups=along_z)]
    ppermute x2, waiting for transfers between devices: 3.76 us -> 10.3 us  [local(): lax.ppermute(part, 'tp', route)]
    all_to_all x2, starting transfers between devices: 13 us -> 6.74 us  [local(): parts = lax.all_to_all(parts, 'tp', 0, 0, axis_index_groups=inside)]
    ppermute x3, waiting for transfers between devices: 0.01 us -> 4.64 us  [local(): part = lax.ppermute(part, 'tp', route)]
    ppermute x2, starting transfers between devices: 15.5 us -> 19.7 us  [local(): lax.ppermute(part, 'tp', route)]
    all_to_all x1, starting transfers between devices: 8.02 us -> 4.33 us  [local(): team = lax.all_to_all(team, 'tp', 0, 0, axis_index_groups=inside)]
    ppermute x2, starting transfers between devices: 22.4 us -> 19.5 us  [shifted(): lax.ppermute(block, axis, [((i - distance) % size, i) for i in range(size)])]
  transfers between devices with their start and end apart: 12 -> 12, of which waited for: 7 -> 9; matrix products, arithmetic and copies ran while one was open for 3% -> 2% of each run, Pallas kernels for 0% -> 0%
where the time goes in v18:
time: 250 us; the launch traced here: 249 us
  blocking collectives  106 us (42%)
  starting transfers between devices  79.7 us (32%)
  waiting for transfers between devices  46 us (18%)
  Pallas kernels  6.71 us (3%)
  matrix products  4.34 us (2%)
  local copies, waits for them, and re-layouts  3.87 us (2%)
    all_to_all x4, blocking collectives, summed_over(): parts = lax.all_to_all(parts, 'tp', 0, 0, axis_index_groups=groups)  65 us
    ppermute x2, starting transfers between devices, local(): lax.ppermute(part, 'tp', route)  19.7 us
    ppermute x2, starting transfers between devices, shifted(): lax.ppermute(block, axis, [((i - distance) % size, i) for i in range(size)])  19.5 us
    all_to_all x1, blocking collectives, local(): normed = lax.all_to_all(block, 'tp', 0, 0, axis_index_groups=far)  17.2 us
    all_to_all x2, waiting for transfers between devices, local(): parts = lax.all_to_all(parts, 'tp', 0, 0, axis_index_groups=inside)  16.1 us
    all_to_all x1, starting transfers between devices, local(): normed = lax.all_to_all(block, 'tp', 0, 0, axis_index_groups=along_z)  15.7 us
    all_to_all x1, waiting for transfers between devices, local(): normed = lax.all_to_all(block, 'tp', 0, 0, axis_index_groups=along_z)  13.3 us
    all_to_all x1, blocking collectives, local(): team = lax.all_to_all(team, 'tp', 0, 0, axis_index_groups=inside)  12.8 us
  transfers between devices with their start and end apart: 12, of which 9 were waited for; matrix products, arithmetic and copies ran while one was open for 2% of the time, Pallas kernels for 0%

profile of v18, /device:TPU:1, one launch (start us, length us, event | category | flops | bytes accessed | tf_op | source)
XLA Modules:
  0.0 248.7 jit_solution(6509410671467160891)
XLA Ops:
  0.0 0.9 copy-done.4
  0.9 0.7 copy-done.10
  1.6 0.9 shard_map.91
  2.5 15.7 %all-to-all-start = ((bf16[16,48,128]{2,1,0:T(8,128)(2,1)}), bf16[16,48,128]{2,1,0:T(8,128)(2,1)S(1)}, u32[]{:S(2)}, u32[]{:S(2)}) async-start(bf16[16,48,128]{2,1,0:T(8,128)(2,1)} %shard_map.91), calls=%async_computation | async-start | bytes 393216 | tf_op jit(solution)/shard_map/all_to_all | solution.py:254
  18.4 13.3 %all-to-all-done = bf16[16,48,128]{2,1,0:T(8,128)(2,1)S(1)} async-done(((bf16[16,48,128]{2,1,0:T(8,128)(2,1)}), bf16[16,48,128]{2,1,0:T(8,128)(2,1)S(1)}, u32[]{:S(2)}, u32[]{:S(2)}) %all-to-all-start) | async-done | bytes 196640 | tf_op jit(solution)/shard_map/all_to_all | solution.py:254
  31.8 1.0 broadcast_in_dim.37
  32.7 4.0 %all-to-all-start.1 = ((bf16[4,32,3072]{2,1,0:T(8,128)(2,1)}), bf16[4,32,3072]{2,1,0:T(8,128)(2,1)S(1)}, u32[]{:S(2)}, u32[]{:S(2)}) async-start(bf16[4,32,3072]{2,1,0:T(8,128)(2,1)} %broadcast_in_dim.37), calls=%async_computation.1 | async-start | bytes 1572864 | tf_op jit(solution)/shard_map/all_to_all | solution.py:173
  36.8 4.7 %collective-permute-start.2 = (bf16[48,768]{1,0:T(8,128)(2,1)S(1)}, bf16[48,768]{1,0:T(8,128)(2,1)S(1)}, u32[]{:S(2)}, u32[]{:S(2)}) collective-permute-start(bf16[48,768]{1,0:T(8,128)(2,1)S(1)} %get-tuple-element.16), channel_id=1, source_target_pairs={{0,48},{1,49},{2,50},{3,51},{4,52},{5,53},{6,54},{7,55},{8,56},{9,... | collective-permute-start | bytes 221192 | tf_op jit(solution)/shard_map/ppermute | solution.py:246
  41.5 2.5 collective-permute-start.1
  44.0 2.5 collective-permute-start
  46.5 2.7 %collective-permute-done.1 = bf16[48,768]{1,0:T(8,128)(2,1)S(1)} collective-permute-done((bf16[48,768]{1,0:T(8,128)(2,1)S(1)}, bf16[48,768]{1,0:T(8,128)(2,1)S(1)}, u32[]{:S(2)}, u32[]{:S(2)}) %collective-permute-start.1) | collective-permute-done | bytes 73760 | tf_op jit(solution)/shard_map/ppermute | solution.py:246
  49.3 1.9 collective-permute-done
  51.3 8.0 %collective-permute-start.3 = (bf16[3,48,384]{2,1,0:T(8,128)(2,1)S(1)}, bf16[3,48,384]{2,1,0:T(8,128)(2,1)S(1)}, u32[]{:S(2)}, u32[]{:S(2)}) collective-permute-start(bf16[3,48,384]{2,1,0:T(8,128)(2,1)S(1)} %slice.35), channel_id=1, source_target_pairs={{0,12},{1,13},{2,14},{3,15},{4,8},{5,9},{6,10},{7,11},{8,4},{9,5},... | collective-permute-start | bytes 331784 | tf_op jit(solution)/shard_map/ppermute | solution.py:258
  59.3 6.1 %collective-permute-done.3.refs_1_ = bf16[3,48,384]{2,1,0:T(8,128)(2,1)S(1)} collective-permute-done((bf16[3,48,384]{2,1,0:T(8,128)(2,1)S(1)}, bf16[3,48,384]{2,1,0:T(8,128)(2,1)S(1)}, u32[]{:S(2)}, u32[]{:S(2)}) %collective-permute-start.3) | collective-permute-done | bytes 110624 | tf_op jit(solution)/shard_map/ppermute | solution.py:258
  65.5 1.2 shard_map.92
  66.7 4.3 %all-to-all-start.2 = ((bf16[8,64,128]{2,1,0:T(8,128)(2,1)}), bf16[8,64,128]{2,1,0:T(8,128)(2,1)S(1)}, u32[]{:S(2)}, u32[]{:S(2)}) async-start(bf16[8,64,128]{2,1,0:T(8,128)(2,1)} %shard_map.92), calls=%async_computation.2 | async-start | bytes 262144 | tf_op jit(solution)/shard_map/all_to_all | solution.py:269
  71.7 11.7 %collective-permute-start.4 = (bf16[1,48,384]{2,1,0:T(8,128)(2,1)S(1)}, bf16[1,48,384]{2,1,0:T(8,128)(2,1)S(1)}, u32[]{:S(2)}, u32[]{:S(2)}) collective-permute-start(bf16[1,48,384]{2,1,0:T(8,128)(2,1)S(1)} %slice.36), channel_id=1, source_target_pairs={{0,12},{1,13},{2,14},{3,15},{4,8},{5,9},{6,10},{7,11},{8,4},{9,5},... | collective-permute-start | bytes 110600 | tf_op jit(solution)/shard_map/ppermute | solution.py:258
  83.4 0.1 copy.12.gain_q_ref
  83.5 4.1 %collective-permute-done.4.refs_2_ = bf16[1,48,384]{2,1,0:T(8,128)(2,1)S(1)} collective-permute-done((bf16[1,48,384]{2,1,0:T(8,128)(2,1)S(1)}, bf16[1,48,384]{2,1,0:T(8,128)(2,1)S(1)}, u32[]{:S(2)}, u32[]{:S(2)}) %collective-permute-start.4) | collective-permute-done | bytes 36896 | tf_op jit(solution)/shard_map/ppermute | solution.py:258
  87.8 1.5 shard_map.93
  89.3 3.4 %all-to-all-start.3 = ((bf16[8,64,128]{2,1,0:T(8,128)(2,1)}), bf16[8,64,128]{2,1,0:T(8,128)(2,1)S(1)}, u32[]{:S(2)}, u32[]{:S(2)}) async-start(bf16[8,64,128]{2,1,0:T(8,128)(2,1)} %shard_map.93), calls=%async_computation.3 | async-start | bytes 262144 | tf_op jit(solution)/shard_map/all_to_all | solution.py:271
  92.6 1.8 fusion.17
  94.4 0.4 fusion.2.forward_ref
  94.8 8.0 %all-to-all-done.3.parts_ref = bf16[8,64,128]{2,1,0:T(8,128)(2,1)S(1)} async-done(((bf16[8,64,128]{2,1,0:T(8,128)(2,1)}), bf16[8,64,128]{2,1,0:T(8,128)(2,1)S(1)}, u32[]{:S(2)}, u32[]{:S(2)}) %all-to-all-start.3) | async-done | bytes 131104 | tf_op jit(solution)/shard_map/all_to_all | solution.py:271
  102.9 0.4 shard_map.94
  103.3 12.5 %all_to_all.60 = bf16[4,32,3072]{2,1,0:T(8,128)(2,1)S(1)} all-to-all(bf16[4,32,3072]{2,1,0:T(8,128)(2,1)S(1)} %bitcast.53), channel_id=1, replica_groups={{0,16,32,48},{1,17,33,49},{2,18,34,50},{3,19,35,51},{4,20,36,52},{5,21,..., dimensions={0} | all-to-all | bytes 1572864 | tf_op jit(solution)/shard_map/all_to_all | solution.py:180
  115.7 0.2 reduce_sum.42
  115.9 0.1 convert_element_type.46
  116.0 21.1 %all_to_all.61 = bf16[16,48,128]{2,1,0:T(8,128)(2,1)S(1)} all-to-all(bf16[16,48,128]{2,1,0:T(8,128)(2,1)S(1)} %convert_element_type.46), channel_id=1, replica_groups={{0,2,4,6,8,10,12,14,1,3,5,7,9,11,13,15},{16,18,20,22,24,26,28,30,17,19,..., dimensions={0} | all-to-all | bytes 393216 | tf_op jit(solution)/shard_map/all_to_all | solution.py:180
  137.2 7.6 %collective-permute-start.5 = (bf16[2,3072]{1,0:T(2,128)(2,1)S(1)}, bf16[2,3072]{1,0:T(2,128)(2,1)S(1)}, u32[]{:S(2)}, u32[]{:S(2)}) collective-permute-start(bf16[2,3072]{1,0:T(2,128)(2,1)S(1)} %add_convert_fusion.1), channel_id=1, source_target_pairs={{448,0},{0,64},{64,128},{128,192},{192,256},{256,320},{320,384},{3... | collective-permute-start | bytes 36872 | tf_op jit(solution)/shard_map/ppermute | solution.py:23
  144.7 0.8 collective-permute-done.5.rows_ref
  145.6 0.2 shard_map.95
  145.8 17.2 %all_to_all.62 = bf16[8,48,128]{2,1,0:T(8,128)(2,1)S(1)} all-to-all(bf16[8,48,128]{2,1,0:T(8,128)(2,1)S(1)} %shard_map.95), channel_id=1, replica_groups={{0,2,4,6,8,10,12,14},{1,3,5,7,9,11,13,15},{16,18,20,22,24,26,28,30},{17..., dimensions={0} | all-to-all | bytes 196608 | tf_op jit(solution)/shard_map/all_to_all | solution.py:266
  163.2 11.5 %all_to_all.63 = bf16[8,16,3072]{2,1,0:T(8,128)(2,1)S(1)} all-to-all(bf16[8,16,3072]{2,1,0:T(8,128)(2,1)S(1)} %broadcast_in_dim.42), channel_id=1, replica_groups={{0,1,16,17,32,33,48,49},{2,3,18,19,34,35,50,51},{4,5,20,21,36,37,52,53}..., dimensions={0} | all-to-all | bytes 1572864 | tf_op jit(solution)/shard_map/all_to_all | solution.py:173
  174.7 0.6 shard_map.96
  175.3 12.8 %all_to_all.64.team_ref = bf16[8,64,128]{2,1,0:T(8,128)(2,1)S(1)} all-to-all(bf16[8,64,128]{2,1,0:T(8,128)(2,1)S(1)} %shard_map.96), channel_id=1, replica_groups={{0,1,2,3,4,5,6,7},{8,9,10,11,12,13,14,15},{16,17,18,19,20,21,22,23},{24..., dimensions={0} | all-to-all | bytes 262144 | tf_op jit(solution)/shard_map/all_to_all | solution.py:269
  188.1 1.5 shard_map.97
  189.5 3.4 %all-to-all-start.9 = ((bf16[8,64,128]{2,1,0:T(8,128)(2,1)}), bf16[8,64,128]{2,1,0:T(8,128)(2,1)S(1)}, u32[]{:S(2)}, u32[]{:S(2)}) async-start(bf16[8,64,128]{2,1,0:T(8,128)(2,1)} %shard_map.97), calls=%async_computation.9 | async-start | bytes 262144 | tf_op jit(solution)/shard_map/all_to_all | solution.py:271
  192.9 1.8 fusion.29
  194.7 0.4 fusion.forward_ref
  195.1 8.1 %all-to-all-done.9.parts_ref = bf16[8,64,128]{2,1,0:T(8,128)(2,1)S(1)} async-done(((bf16[8,64,128]{2,1,0:T(8,128)(2,1)}), bf16[8,64,128]{2,1,0:T(8,128)(2,1)S(1)}, u32[]{:S(2)}, u32[]{:S(2)}) %all-to-all-start.9) | async-done | bytes 131104 | tf_op jit(solution)/shard_map/all_to_all | solution.py:271
  203.1 0.4 shard_map.98
  203.6 10.7 %all_to_all.65 = bf16[4,32,3072]{2,1,0:T(8,128)(2,1)S(1)} all-to-all(bf16[4,32,3072]{2,1,0:T(8,128)(2,1)S(1)} %bitcast.52), channel_id=1, replica_groups={{0,16,32,48},{1,17,33,49},{2,18,34,50},{3,19,35,51},{4,20,36,52},{5,21,..., dimensions={0} | all-to-all | bytes 1572864 | tf_op jit(solution)/shard_map/all_to_all | solution.py:180
  214.3 0.2 reduce_sum.44
  214.6 20.7 %all_to_all.66 = bf16[16,48,128]{2,1,0:T(8,128)(2,1)S(1)} all-to-all(bf16[16,48,128]{2,1,0:T(8,128)(2,1)S(1)} %convert_element_type.51), channel_id=1, replica_groups={{0,2,4,6,8,10,12,14,1,3,5,7,9,11,13,15},{16,18,20,22,24,26,28,30,17,19,..., dimensions={0} | all-to-all | bytes 393216 | tf_op jit(solution)/shard_map/all_to_all | solution.py:180
  235.3 12.0 %collective-permute-start.6 = (bf16[2,3072]{1,0:T(2,128)(2,1)S(1)}, bf16[2,3072]{1,0:T(2,128)(2,1)S(1)}, u32[]{:S(2)}, u32[]{:S(2)}) collective-permute-start(bf16[2,3072]{1,0:T(2,128)(2,1)S(1)} %add_convert_fusion), channel_id=1, source_target_pairs={{448,0},{0,64},{64,128},{128,192},{192,256},{256,320},{320,384},{3... | collective-permute-start | bytes 36872 | tf_op jit(solution)/shard_map/ppermute | solution.py:23
  247.3 0.8 collective-permute-done.6
  248.1 0.6 copy.16
  (47 shorter events, 0.7 us)
Async XLA Ops:
  0.0 94.4 %copy-start = (bf16[1,192,3072]{2,1,0:T(8,128)(2,1)S(1)}, bf16[1,192,3072]{2,1,0:T(8,128)(2,1)}, u32[]{:S(2)}) copy-start(bf16[1,192,3072]{2,1,0:T(8,128)(2,1)} %param.13) | copy-start | bytes 3538948
  0.0 0.9 copy-start.4
  0.9 0.7 copy-start.10
  2.5 29.2 %all-to-all-start = ((bf16[16,48,128]{2,1,0:T(8,128)(2,1)}), bf16[16,48,128]{2,1,0:T(8,128)(2,1)S(1)}, u32[]{:S(2)}, u32[]{:S(2)}) async-start(bf16[16,48,128]{2,1,0:T(8,128)(2,1)} %shard_map.91), calls=%async_computation | async-start | bytes 393216 | tf_op jit(solution)/shard_map/all_to_all | solution.py:254
  31.8 5.0 %copy-start.12 = (bf16[1,2,24,3072]{3,2,1,0:T(8,128)(2,1)S(1)}, bf16[1,2,24,3072]{3,2,1,0:T(8,128)(2,1)}, u32[]{:S(2)}) copy-start(bf16[1,2,24,3072]{3,2,1,0:T(8,128)(2,1)} %param.16) | copy-start | bytes 884740
  32.7 32.7 %all-to-all-start.1 = ((bf16[4,32,3072]{2,1,0:T(8,128)(2,1)}), bf16[4,32,3072]{2,1,0:T(8,128)(2,1)S(1)}, u32[]{:S(2)}, u32[]{:S(2)}) async-start(bf16[4,32,3072]{2,1,0:T(8,128)(2,1)} %broadcast_in_dim.37), calls=%async_computation.1 | async-start | bytes 1572864 | tf_op jit(solution)/shard_map/all_to_all | solution.py:173
  36.8 28.7 %copy-start.1 = (bf16[1,3,48,3072]{3,2,1,0:T(8,128)(2,1)S(1)}, bf16[1,3,48,3072]{3,2,1,0:T(8,128)(2,1)}, u32[]{:S(2)}) copy-start(bf16[1,3,48,3072]{3,2,1,0:T(8,128)(2,1)} %param.10) | copy-start | bytes 2654212
  36.8 9.7 %collective-permute-start.2 = (bf16[48,768]{1,0:T(8,128)(2,1)S(1)}, bf16[48,768]{1,0:T(8,128)(2,1)S(1)}, u32[]{:S(2)}, u32[]{:S(2)}) collective-permute-start(bf16[48,768]{1,0:T(8,128)(2,1)S(1)} %get-tuple-element.16), channel_id=1, source_target_pairs={{0,48},{1,49},{2,50},{3,51},{4,52},{5,53},{6,54},{7,55},{8,56},{9,... | collective-permute-start | bytes 221192 | tf_op jit(solution)/shard_map/ppermute | solution.py:246
  41.5 7.7 %collective-permute-start.1 = (bf16[48,768]{1,0:T(8,128)(2,1)S(1)}, bf16[48,768]{1,0:T(8,128)(2,1)S(1)}, u32[]{:S(2)}, u32[]{:S(2)}) collective-permute-start(bf16[48,768]{1,0:T(8,128)(2,1)S(1)} %get-tuple-element.17), channel_id=1, source_target_pairs={{0,32},{1,33},{2,34},{3,35},{4,36},{5,37},{6,38},{7,39},{8,40},{9,... | collective-permute-start | bytes 221192 | tf_op jit(solution)/shard_map/ppermute | solution.py:246
  44.0 7.2 %collective-permute-start = (bf16[48,768]{1,0:T(8,128)(2,1)S(1)}, bf16[48,768]{1,0:T(8,128)(2,1)S(1)}, u32[]{:S(2)}, u32[]{:S(2)}) collective-permute-start(bf16[48,768]{1,0:T(8,128)(2,1)S(1)} %get-tuple-element.18), channel_id=1, source_target_pairs={{0,16},{1,17},{2,18},{3,19},{4,20},{5,21},{6,22},{7,23},{8,24},{9,... | collective-permute-start | bytes 221192 | tf_op jit(solution)/shard_map/ppermute | solution.py:246
  51.3 20.4 %copy-start.13 = (f32[1,2,128]{2,1,0:T(2,128)S(1)}, f32[1,2,128]{2,1,0:T(2,128)}, u32[]{:S(2)}) copy-start(f32[1,2,128]{2,1,0:T(2,128)} %param.15) | copy-start | bytes 3076
  51.3 14.2 %collective-permute-start.3 = (bf16[3,48,384]{2,1,0:T(8,128)(2,1)S(1)}, bf16[3,48,384]{2,1,0:T(8,128)(2,1)S(1)}, u32[]{:S(2)}, u32[]{:S(2)}) collective-permute-start(bf16[3,48,384]{2,1,0:T(8,128)(2,1)S(1)} %slice.35), channel_id=1, source_target_pairs={{0,12},{1,13},{2,14},{3,15},{4,8},{5,9},{6,10},{7,11},{8,4},{9,5},... | collective-permute-start | bytes 331784 | tf_op jit(solution)/shard_map/ppermute | solution.py:258
  65.5 23.8 %copy-start.6 = (bf16[3,48,384]{2,1,0:T(8,128)(2,1)}, bf16[3,48,384]{2,1,0:T(8,128)(2,1)S(1)}, u32[]{:S(2)}) copy-start(bf16[3,48,384]{2,1,0:T(8,128)(2,1)S(1)} %collective-permute-done.3.refs_1_) | copy-start | bytes 331780
  66.7 21.0 %all-to-all-start.2 = ((bf16[8,64,128]{2,1,0:T(8,128)(2,1)}), bf16[8,64,128]{2,1,0:T(8,128)(2,1)S(1)}, u32[]{:S(2)}, u32[]{:S(2)}) async-start(bf16[8,64,128]{2,1,0:T(8,128)(2,1)} %shard_map.92), calls=%async_computation.2 | async-start | bytes 262144 | tf_op jit(solution)/shard_map/all_to_all | solution.py:269
  71.7 16.0 %collective-permute-start.4 = (bf16[1,48,384]{2,1,0:T(8,128)(2,1)S(1)}, bf16[1,48,384]{2,1,0:T(8,128)(2,1)S(1)}, u32[]{:S(2)}, u32[]{:S(2)}) collective-permute-start(bf16[1,48,384]{2,1,0:T(8,128)(2,1)S(1)} %slice.36), channel_id=1, source_target_pairs={{0,12},{1,13},{2,14},{3,15},{4,8},{5,9},{6,10},{7,11},{8,4},{9,5},... | collective-permute-start | bytes 110600 | tf_op jit(solution)/shard_map/ppermute | solution.py:258
  87.7 5.0 %copy-start.8 = (bf16[1,48,384]{2,1,0:T(8,128)(2,1)}, bf16[1,48,384]{2,1,0:T(8,128)(2,1)S(1)}, u32[]{:S(2)}) copy-start(bf16[1,48,384]{2,1,0:T(8,128)(2,1)S(1)} %collective-permute-done.4.refs_2_) | copy-start | bytes 110596
  89.3 13.6 %all-to-all-start.3 = ((bf16[8,64,128]{2,1,0:T(8,128)(2,1)}), bf16[8,64,128]{2,1,0:T(8,128)(2,1)S(1)}, u32[]{:S(2)}, u32[]{:S(2)}) async-start(bf16[8,64,128]{2,1,0:T(8,128)(2,1)} %shard_map.93), calls=%async_computation.3 | async-start | bytes 262144 | tf_op jit(solution)/shard_map/all_to_all | solution.py:271
  94.4 8.4 %copy-start.3 = (bf16[1,48,3072]{2,1,0:T(8,128)(2,1)S(1)}, bf16[1,48,3072]{2,1,0:T(8,128)(2,1)}, u32[]{:S(2)}) copy-start(bf16[1,48,3072]{2,1,0:T(8,128)(2,1)} %param.12) | copy-start | bytes 884740
  94.4 8.4 %copy-start.5 = (f32[1,3,3072]{2,0,1:T(1,128)S(1)}, f32[1,3,3072]{2,0,1:T(1,128)}, u32[]{:S(2)}) copy-start(f32[1,3,3072]{2,0,1:T(1,128)} %param.14) | copy-start | bytes 110596
  115.7 21.4 %copy-start.11 = (bf16[1,2,3072]{2,1,0:T(2,128)(2,1)S(1)}, bf16[1,2,3072]{2,1,0:T(2,128)(2,1)}, u32[]{:S(2)}) copy-start(bf16[1,2,3072]{2,1,0:T(2,128)(2,1)} %param.9) | copy-start | bytes 36868
  137.2 8.4 %collective-permute-start.5 = (bf16[2,3072]{1,0:T(2,128)(2,1)S(1)}, bf16[2,3072]{1,0:T(2,128)(2,1)S(1)}, u32[]{:S(2)}, u32[]{:S(2)}) collective-permute-start(bf16[2,3072]{1,0:T(2,128)(2,1)S(1)} %add_convert_fusion.1), channel_id=1, source_target_pairs={{448,0},{0,64},{64,128},{128,192},{192,256},{256,320},{320,384},{3... | collective-permute-start | bytes 36872 | tf_op jit(solution)/shard_map/ppermute | solution.py:23
  163.1 11.6 %copy-start.2 = (bf16[1,3,48,3072]{3,2,1,0:T(8,128)(2,1)S(1)}, bf16[1,3,48,3072]{3,2,1,0:T(8,128)(2,1)}, u32[]{:S(2)}) copy-start(bf16[1,3,48,3072]{3,2,1,0:T(8,128)(2,1)} %param.10) | copy-start | bytes 2654212
  174.7 13.3 %copy-start.7 = (bf16[3,48,384]{2,1,0:T(8,128)(2,1)S(1)}, bf16[3,48,384]{2,1,0:T(8,128)(2,1)}, u32[]{:S(2)}) copy-start(bf16[3,48,384]{2,1,0:T(8,128)(2,1)} %copy-done.6) | copy-start | bytes 331780
  174.7 13.3 %copy-start.9 = (bf16[1,48,384]{2,1,0:T(8,128)(2,1)S(1)}, bf16[1,48,384]{2,1,0:T(8,128)(2,1)}, u32[]{:S(2)}) copy-start(bf16[1,48,384]{2,1,0:T(8,128)(2,1)} %copy-done.8) | copy-start | bytes 110596
  189.5 13.6 %all-to-all-start.9 = ((bf16[8,64,128]{2,1,0:T(8,128)(2,1)}), bf16[8,64,128]{2,1,0:T(8,128)(2,1)S(1)}, u32[]{:S(2)}, u32[]{:S(2)}) async-start(bf16[8,64,128]{2,1,0:T(8,128)(2,1)} %shard_map.97), calls=%async_computation.9 | async-start | bytes 262144 | tf_op jit(solution)/shard_map/all_to_all | solution.py:271
  235.3 12.8 %collective-permute-start.6 = (bf16[2,3072]{1,0:T(2,128)(2,1)S(1)}, bf16[2,3072]{1,0:T(2,128)(2,1)S(1)}, u32[]{:S(2)}, u32[]{:S(2)}) collective-permute-start(bf16[2,3072]{1,0:T(2,128)(2,1)S(1)} %add_convert_fusion), channel_id=1, source_target_pairs={{448,0},{0,64},{64,128},{128,192},{192,256},{256,320},{320,384},{3... | collective-permute-start | bytes 36872 | tf_op jit(solution)/shard_map/ppermute | solution.py:23

commit v19 on v16

--- a/solution.py
+++ b/solution.py
@@ -116,10 +116,11 @@
     fresh = [team_ref[c, shard:, :].astype(f32) for c in range(members)]
     features = jnp.concatenate([team_ref[c, :shard, :] for c in range(members)], axis=0)
     open_key = mask_ref[...] > 0.0
-    blocks = [r[i].astype(f32) for r in cached_refs for i in range(r.shape[0])]
-    half = blocks[0].shape[0] // 2
-    cached_keys = jnp.concatenate([b[:half] for b in blocks], axis=0).astype(bf16)
-    cached_values = jnp.concatenate([b[half:] for b in blocks], axis=0).astype(bf16)
+    count = sum(r.shape[0] for r in cached_refs)
+    half = cached_refs[0].shape[1] // 2
+    cached = jnp.concatenate(
+        [r[...].reshape(2 * half * r.shape[0], r.shape[2]) for r in cached_refs], axis=0
+    )
     sums = jnp.zeros((16, LANES), f32)
     for h in range(TEAM_HEADS):
         query = features[h * HEAD_DIM : (h + 1) * HEAD_DIM].astype(f32)
@@ -136,16 +137,19 @@
             value = jnp.where(here, pltpu.roll(fresh[c], (start - shard) % LANES, 1), value)
         scale = lax.rsqrt(jnp.mean(key * key, axis=1, keepdims=True) + eps_norm)
         key = (key * scale * gain_k_ref[...]).astype(bf16)
-        cached_key = cached_keys[:, h * HEAD_DIM : (h + 1) * HEAD_DIM]
-        cached_value = cached_values[:, h * HEAD_DIM : (h + 1) * HEAD_DIM]
-        scores = jnp.dot(cached_key, query, preferred_element_type=f32)
+        both = cached[:, h * HEAD_DIM : (h + 1) * HEAD_DIM]
+        scores = jnp.dot(both, query, preferred_element_type=f32)
+        scores = scores.reshape(count, 2 * half, LANES)[:, :half].reshape(count * half, LANES)
         probs = jnp.exp(jnp.where(open_key, scores, -1e30))
+        at_values = probs.reshape(count, half, LANES)
+        at_values = jnp.concatenate([jnp.zeros_like(at_values), at_values], axis=1)
+        at_values = at_values.reshape(2 * half * count, LANES)
         fresh_probs = jnp.exp(jnp.dot(key, query, preferred_element_type=f32))
         total = jnp.sum(probs, axis=0, keepdims=True) + jnp.sum(fresh_probs, axis=0, keepdims=True)
         sums = jnp.where(row == h, total, sums)
         contract = (((0,), (0,)), ((), ()))
         weighted = lax.dot_general(
-            cached_value, probs.astype(bf16), contract, preferred_element_type=f32
+            both, at_values.astype(bf16), contract, preferred_element_type=f32
         ) + lax.dot_general(
             value.astype(bf16), fresh_probs.astype(bf16), contract, preferred_element_type=f32
         )

time: 235 us -> 236 us (level)
  no operation moved by 1% of the time
where the time goes in v19:
time: 236 us; the launch traced here: 235 us
  blocking collectives  104 us (44%)
  starting transfers between devices  88.1 us (37%)
  waiting for transfers between devices  24.5 us (10%)
  Pallas kernels  6.9 us (3%)
  local copies, waits for them, and re-layouts  4.86 us (2%)
  matrix products  4.33 us (2%)
    all_to_all x4, blocking collectives, summed_over(): parts = lax.all_to_all(parts, 'tp', 0, 0, axis_index_groups=groups)  62.9 us
    ppermute x2, starting transfers between devices, shifted(): lax.ppermute(block, axis, [((i - distance) % size, i) for i in range(size)])  22.4 us
    all_to_all x1, blocking collectives, local(): normed = lax.all_to_all(block, 'tp', 0, 0, axis_index_groups=far)  17.1 us
    all_to_all x2, waiting for transfers between devices, local(): parts = lax.all_to_all(parts, 'tp', 0, 0, axis_index_groups=inside)  16.1 us
    all_to_all x1, starting transfers between devices, local(): normed = lax.all_to_all(block, 'tp', 0, 0, axis_index_groups=along_z)  15.7 us
    ppermute x2, starting transfers between devices, local(): lax.ppermute(part, 'tp', route)  15.5 us
    all_to_all x2, starting transfers between devices, local(): parts = lax.all_to_all(parts, 'tp', 0, 0, axis_index_groups=inside)  13 us
    all_to_all x1, blocking collectives, local(): team = lax.all_to_all(team, 'tp', 0, 0, axis_index_groups=inside)  12.8 us
  transfers between devices with their start and end apart: 12, of which 7 were waited for; matrix products, arithmetic and copies ran while one was open for 3% of the time, Pallas kernels for 0%

profile of v19, /device:TPU:1, one launch (start us, length us, event | category | flops | bytes accessed | tf_op | source)
XLA Modules:
  0.0 234.5 jit_solution(1973442577630231960)
XLA Ops:
  0.0 0.9 copy-done.4
  0.9 0.7 copy-done.10
  1.6 0.9 shard_map.91
  2.5 15.7 %all-to-all-start = ((bf16[16,48,128]{2,1,0:T(8,128)(2,1)}), bf16[16,48,128]{2,1,0:T(8,128)(2,1)S(1)}, u32[]{:S(2)}, u32[]{:S(2)}) async-start(bf16[16,48,128]{2,1,0:T(8,128)(2,1)} %shard_map.91), calls=%async_computation | async-start | bytes 393216 | tf_op jit(solution)/shard_map/all_to_all | solution.py:258
  18.4 1.0 dynamic-slice_bitcast_fusion
  19.4 4.4 %collective-permute-start.2 = (bf16[48,768]{1,0:T(8,128)(2,1)S(1)}, bf16[48,768]{1,0:T(8,128)(2,1)S(1)}, u32[]{:S(2)}, u32[]{:S(2)}) collective-permute-start(bf16[48,768]{1,0:T(8,128)(2,1)S(1)} %get-tuple-element.16), channel_id=1, source_target_pairs={{0,48},{1,49},{2,50},{3,51},{4,52},{5,53},{6,54},{7,55},{8,56},{9,... | collective-permute-start | bytes 221192 | tf_op jit(solution)/shard_map/ppermute | solution.py:250
  23.8 2.4 %collective-permute-start.1 = (bf16[48,768]{1,0:T(8,128)(2,1)S(1)}, bf16[48,768]{1,0:T(8,128)(2,1)S(1)}, u32[]{:S(2)}, u32[]{:S(2)}) collective-permute-start(bf16[48,768]{1,0:T(8,128)(2,1)S(1)} %get-tuple-element.17), channel_id=1, source_target_pairs={{0,32},{1,33},{2,34},{3,35},{4,36},{5,37},{6,38},{7,39},{8,40},{9,... | collective-permute-start | bytes 221192 | tf_op jit(solution)/shard_map/ppermute | solution.py:250
  26.2 2.5 %collective-permute-start = (bf16[48,768]{1,0:T(8,128)(2,1)S(1)}, bf16[48,768]{1,0:T(8,128)(2,1)S(1)}, u32[]{:S(2)}, u32[]{:S(2)}) collective-permute-start(bf16[48,768]{1,0:T(8,128)(2,1)S(1)} %get-tuple-element.18), channel_id=1, source_target_pairs={{0,16},{1,17},{2,18},{3,19},{4,20},{5,21},{6,22},{7,23},{8,24},{9,... | collective-permute-start | bytes 221192 | tf_op jit(solution)/shard_map/ppermute | solution.py:250
  28.8 2.9 %all-to-all-done = bf16[16,48,128]{2,1,0:T(8,128)(2,1)S(1)} async-done(((bf16[16,48,128]{2,1,0:T(8,128)(2,1)}), bf16[16,48,128]{2,1,0:T(8,128)(2,1)S(1)}, u32[]{:S(2)}, u32[]{:S(2)}) %all-to-all-start) | async-done | bytes 196640 | tf_op jit(solution)/shard_map/all_to_all | solution.py:258
  31.8 1.0 broadcast_in_dim.37
  32.7 4.1 %all-to-all-start.1 = ((bf16[4,32,3072]{2,1,0:T(8,128)(2,1)}), bf16[4,32,3072]{2,1,0:T(8,128)(2,1)S(1)}, u32[]{:S(2)}, u32[]{:S(2)}) async-start(bf16[4,32,3072]{2,1,0:T(8,128)(2,1)} %broadcast_in_dim.37), calls=%async_computation.1 | async-start | bytes 1572864 | tf_op jit(solution)/shard_map/all_to_all | solution.py:177
  37.0 7.9 %collective-permute-start.3 = (bf16[2,48,384]{2,1,0:T(8,128)(2,1)S(1)}, bf16[2,48,384]{2,1,0:T(8,128)(2,1)S(1)}, u32[]{:S(2)}, u32[]{:S(2)}) collective-permute-start(bf16[2,48,384]{2,1,0:T(8,128)(2,1)S(1)} %get-tuple-element.20), channel_id=1, source_target_pairs={{0,12},{1,13},{2,14},{3,15},{4,8},{5,9},{6,10},{7,11},{8,4},{9,5},... | collective-permute-start | bytes 221192 | tf_op jit(solution)/shard_map/ppermute | solution.py:262
  44.9 1.7 collective-permute-done.3.refs_1_
  46.7 1.2 shard_map.92
  47.9 8.0 %all-to-all-start.2 = ((bf16[8,64,128]{2,1,0:T(8,128)(2,1)}), bf16[8,64,128]{2,1,0:T(8,128)(2,1)S(1)}, u32[]{:S(2)}, u32[]{:S(2)}) async-start(bf16[8,64,128]{2,1,0:T(8,128)(2,1)} %shard_map.92), calls=%async_computation.2 | async-start | bytes 262144 | tf_op jit(solution)/shard_map/all_to_all | solution.py:273
  56.6 0.1 copy.12.gain_q_ref
  56.7 7.6 %collective-permute-start.4 = (bf16[2,48,384]{2,1,0:T(8,128)(2,1)S(1)}, bf16[2,48,384]{2,1,0:T(8,128)(2,1)S(1)}, u32[]{:S(2)}, u32[]{:S(2)}) collective-permute-start(bf16[2,48,384]{2,1,0:T(8,128)(2,1)S(1)} %get-tuple-element.19), channel_id=1, source_target_pairs={{0,12},{1,13},{2,14},{3,15},{4,8},{5,9},{6,10},{7,11},{8,4},{9,5},... | collective-permute-start | bytes 221192 | tf_op jit(solution)/shard_map/ppermute | solution.py:262
  64.3 2.0 collective-permute-done.4.refs_2_
  66.4 1.6 shard_map.93
  68.0 9.7 %all-to-all-start.3 = ((bf16[8,64,128]{2,1,0:T(8,128)(2,1)}), bf16[8,64,128]{2,1,0:T(8,128)(2,1)S(1)}, u32[]{:S(2)}, u32[]{:S(2)}) async-start(bf16[8,64,128]{2,1,0:T(8,128)(2,1)} %shard_map.93), calls=%async_computation.3 | async-start | bytes 262144 | tf_op jit(solution)/shard_map/all_to_all | solution.py:275
  77.7 1.8 fusion.17
  79.5 0.4 fusion.2.forward_ref
  79.9 8.0 %all-to-all-done.3.parts_ref = bf16[8,64,128]{2,1,0:T(8,128)(2,1)S(1)} async-done(((bf16[8,64,128]{2,1,0:T(8,128)(2,1)}), bf16[8,64,128]{2,1,0:T(8,128)(2,1)S(1)}, u32[]{:S(2)}, u32[]{:S(2)}) %all-to-all-start.3) | async-done | bytes 131104 | tf_op jit(solution)/shard_map/all_to_all | solution.py:275
  87.9 0.4 shard_map.94
  88.4 10.7 %all_to_all.60 = bf16[4,32,3072]{2,1,0:T(8,128)(2,1)S(1)} all-to-all(bf16[4,32,3072]{2,1,0:T(8,128)(2,1)S(1)} %bitcast.53), channel_id=1, replica_groups={{0,16,32,48},{1,17,33,49},{2,18,34,50},{3,19,35,51},{4,20,36,52},{5,21,..., dimensions={0} | all-to-all | bytes 1572864 | tf_op jit(solution)/shard_map/all_to_all | solution.py:184
  99.1 0.2 reduce_sum.42
  99.3 0.1 convert_element_type.46
  99.4 20.7 %all_to_all.61 = bf16[16,48,128]{2,1,0:T(8,128)(2,1)S(1)} all-to-all(bf16[16,48,128]{2,1,0:T(8,128)(2,1)S(1)} %convert_element_type.46), channel_id=1, replica_groups={{0,2,4,6,8,10,12,14,1,3,5,7,9,11,13,15},{16,18,20,22,24,26,28,30,17,19,..., dimensions={0} | all-to-all | bytes 393216 | tf_op jit(solution)/shard_map/all_to_all | solution.py:184
  120.1 10.4 %collective-permute-start.5 = (bf16[2,3072]{1,0:T(2,128)(2,1)S(1)}, bf16[2,3072]{1,0:T(2,128)(2,1)S(1)}, u32[]{:S(2)}, u32[]{:S(2)}) collective-permute-start(bf16[2,3072]{1,0:T(2,128)(2,1)S(1)} %add_convert_fusion.1), channel_id=1, source_target_pairs={{448,0},{0,64},{64,128},{128,192},{192,256},{256,320},{320,384},{3... | collective-permute-start | bytes 36872 | tf_op jit(solution)/shard_map/ppermute | solution.py:23
  130.6 0.8 collective-permute-done.5.rows_ref
  131.4 0.2 shard_map.95
  131.7 17.1 %all_to_all.62 = bf16[8,48,128]{2,1,0:T(8,128)(2,1)S(1)} all-to-all(bf16[8,48,128]{2,1,0:T(8,128)(2,1)S(1)} %shard_map.95), channel_id=1, replica_groups={{0,2,4,6,8,10,12,14},{1,3,5,7,9,11,13,15},{16,18,20,22,24,26,28,30},{17..., dimensions={0} | all-to-all | bytes 196608 | tf_op jit(solution)/shard_map/all_to_all | solution.py:270
  148.9 11.5 %all_to_all.63 = bf16[8,16,3072]{2,1,0:T(8,128)(2,1)S(1)} all-to-all(bf16[8,16,3072]{2,1,0:T(8,128)(2,1)S(1)} %broadcast_in_dim.42), channel_id=1, replica_groups={{0,1,16,17,32,33,48,49},{2,3,18,19,34,35,50,51},{4,5,20,21,36,37,52,53}..., dimensions={0} | all-to-all | bytes 1572864 | tf_op jit(solution)/shard_map/all_to_all | solution.py:177
  160.5 0.6 shard_map.96
  161.0 12.8 %all_to_all.64.team_ref = bf16[8,64,128]{2,1,0:T(8,128)(2,1)S(1)} all-to-all(bf16[8,64,128]{2,1,0:T(8,128)(2,1)S(1)} %shard_map.96), channel_id=1, replica_groups={{0,1,2,3,4,5,6,7},{8,9,10,11,12,13,14,15},{16,17,18,19,20,21,22,23},{24..., dimensions={0} | all-to-all | bytes 262144 | tf_op jit(solution)/shard_map/all_to_all | solution.py:273
  173.8 1.6 shard_map.97
  175.4 3.4 %all-to-all-start.9 = ((bf16[8,64,128]{2,1,0:T(8,128)(2,1)}), bf16[8,64,128]{2,1,0:T(8,128)(2,1)S(1)}, u32[]{:S(2)}, u32[]{:S(2)}) async-start(bf16[8,64,128]{2,1,0:T(8,128)(2,1)} %shard_map.97), calls=%async_computation.9 | async-start | bytes 262144 | tf_op jit(solution)/shard_map/all_to_all | solution.py:275
  178.7 1.8 fusion.29
  180.5 0.4 fusion.forward_ref
  180.9 8.1 %all-to-all-done.9.parts_ref = bf16[8,64,128]{2,1,0:T(8,128)(2,1)S(1)} async-done(((bf16[8,64,128]{2,1,0:T(8,128)(2,1)}), bf16[8,64,128]{2,1,0:T(8,128)(2,1)S(1)}, u32[]{:S(2)}, u32[]{:S(2)}) %all-to-all-start.9) | async-done | bytes 131104 | tf_op jit(solution)/shard_map/all_to_all | solution.py:275
  189.0 0.4 shard_map.98
  189.4 10.7 %all_to_all.65 = bf16[4,32,3072]{2,1,0:T(8,128)(2,1)S(1)} all-to-all(bf16[4,32,3072]{2,1,0:T(8,128)(2,1)S(1)} %bitcast.52), channel_id=1, replica_groups={{0,16,32,48},{1,17,33,49},{2,18,34,50},{3,19,35,51},{4,20,36,52},{5,21,..., dimensions={0} | all-to-all | bytes 1572864 | tf_op jit(solution)/shard_map/all_to_all | solution.py:184
  200.1 0.2 reduce_sum.44
  200.3 0.1 convert_element_type.51
  200.4 20.7 %all_to_all.66 = bf16[16,48,128]{2,1,0:T(8,128)(2,1)S(1)} all-to-all(bf16[16,48,128]{2,1,0:T(8,128)(2,1)S(1)} %convert_element_type.51), channel_id=1, replica_groups={{0,2,4,6,8,10,12,14,1,3,5,7,9,11,13,15},{16,18,20,22,24,26,28,30,17,19,..., dimensions={0} | all-to-all | bytes 393216 | tf_op jit(solution)/shard_map/all_to_all | solution.py:184
  221.1 11.9 %collective-permute-start.6 = (bf16[2,3072]{1,0:T(2,128)(2,1)S(1)}, bf16[2,3072]{1,0:T(2,128)(2,1)S(1)}, u32[]{:S(2)}, u32[]{:S(2)}) collective-permute-start(bf16[2,3072]{1,0:T(2,128)(2,1)S(1)} %add_convert_fusion), channel_id=1, source_target_pairs={{448,0},{0,64},{64,128},{128,192},{192,256},{256,320},{320,384},{3... | collective-permute-start | bytes 36872 | tf_op jit(solution)/shard_map/ppermute | solution.py:23
  233.1 0.8 collective-permute-done.6
  233.9 0.6 copy.16
  (44 shorter events, 0.6 us)
Async XLA Ops:
  0.0 79.4 %copy-start = (bf16[1,192,3072]{2,1,0:T(8,128)(2,1)S(1)}, bf16[1,192,3072]{2,1,0:T(8,128)(2,1)}, u32[]{:S(2)}) copy-start(bf16[1,192,3072]{2,1,0:T(8,128)(2,1)} %param.13) | copy-start | bytes 3538948
  0.0 0.9 copy-start.4
  0.9 0.7 copy-start.10
  2.5 29.2 %all-to-all-start = ((bf16[16,48,128]{2,1,0:T(8,128)(2,1)}), bf16[16,48,128]{2,1,0:T(8,128)(2,1)S(1)}, u32[]{:S(2)}, u32[]{:S(2)}) async-start(bf16[16,48,128]{2,1,0:T(8,128)(2,1)} %shard_map.91), calls=%async_computation | async-start | bytes 393216 | tf_op jit(solution)/shard_map/all_to_all | solution.py:258
  19.4 17.5 %collective-permute-start.2 = (bf16[48,768]{1,0:T(8,128)(2,1)S(1)}, bf16[48,768]{1,0:T(8,128)(2,1)S(1)}, u32[]{:S(2)}, u32[]{:S(2)}) collective-permute-start(bf16[48,768]{1,0:T(8,128)(2,1)S(1)} %get-tuple-element.16), channel_id=1, source_target_pairs={{0,48},{1,49},{2,50},{3,51},{4,52},{5,53},{6,54},{7,55},{8,56},{9,... | collective-permute-start | bytes 221192 | tf_op jit(solution)/shard_map/ppermute | solution.py:250
  23.8 13.1 %collective-permute-start.1 = (bf16[48,768]{1,0:T(8,128)(2,1)S(1)}, bf16[48,768]{1,0:T(8,128)(2,1)S(1)}, u32[]{:S(2)}, u32[]{:S(2)}) collective-permute-start(bf16[48,768]{1,0:T(8,128)(2,1)S(1)} %get-tuple-element.17), channel_id=1, source_target_pairs={{0,32},{1,33},{2,34},{3,35},{4,36},{5,37},{6,38},{7,39},{8,40},{9,... | collective-permute-start | bytes 221192 | tf_op jit(solution)/shard_map/ppermute | solution.py:250
  26.2 10.7 %collective-permute-start = (bf16[48,768]{1,0:T(8,128)(2,1)S(1)}, bf16[48,768]{1,0:T(8,128)(2,1)S(1)}, u32[]{:S(2)}, u32[]{:S(2)}) collective-permute-start(bf16[48,768]{1,0:T(8,128)(2,1)S(1)} %get-tuple-element.18), channel_id=1, source_target_pairs={{0,16},{1,17},{2,18},{3,19},{4,20},{5,21},{6,22},{7,23},{8,24},{9,... | collective-permute-start | bytes 221192 | tf_op jit(solution)/shard_map/ppermute | solution.py:250
  32.7 13.9 %copy-start.1 = (bf16[1,3,48,3072]{3,2,1,0:T(8,128)(2,1)S(1)}, bf16[1,3,48,3072]{3,2,1,0:T(8,128)(2,1)}, u32[]{:S(2)}) copy-start(bf16[1,3,48,3072]{3,2,1,0:T(8,128)(2,1)} %param.10) | copy-start | bytes 2654212
  32.7 13.9 %all-to-all-start.1 = ((bf16[4,32,3072]{2,1,0:T(8,128)(2,1)}), bf16[4,32,3072]{2,1,0:T(8,128)(2,1)S(1)}, u32[]{:S(2)}, u32[]{:S(2)}) async-start(bf16[4,32,3072]{2,1,0:T(8,128)(2,1)} %broadcast_in_dim.37), calls=%async_computation.1 | async-start | bytes 1572864 | tf_op jit(solution)/shard_map/all_to_all | solution.py:177
  37.0 19.6 %copy-start.12 = (f32[1,2,128]{2,1,0:T(2,128)S(1)}, f32[1,2,128]{2,1,0:T(2,128)}, u32[]{:S(2)}) copy-start(f32[1,2,128]{2,1,0:T(2,128)} %param.15) | copy-start | bytes 3076
  37.0 9.6 %collective-permute-start.3 = (bf16[2,48,384]{2,1,0:T(8,128)(2,1)S(1)}, bf16[2,48,384]{2,1,0:T(8,128)(2,1)S(1)}, u32[]{:S(2)}, u32[]{:S(2)}) collective-permute-start(bf16[2,48,384]{2,1,0:T(8,128)(2,1)S(1)} %get-tuple-element.20), channel_id=1, source_target_pairs={{0,12},{1,13},{2,14},{3,15},{4,8},{5,9},{6,10},{7,11},{8,4},{9,5},... | collective-permute-start | bytes 221192 | tf_op jit(solution)/shard_map/ppermute | solution.py:262
  46.7 21.3 %copy-start.6 = (bf16[2,48,384]{2,1,0:T(8,128)(2,1)}, bf16[2,48,384]{2,1,0:T(8,128)(2,1)S(1)}, u32[]{:S(2)}) copy-start(bf16[2,48,384]{2,1,0:T(8,128)(2,1)S(1)} %collective-permute-done.3.refs_1_) | copy-start | bytes 221188
  47.9 18.4 %all-to-all-start.2 = ((bf16[8,64,128]{2,1,0:T(8,128)(2,1)}), bf16[8,64,128]{2,1,0:T(8,128)(2,1)S(1)}, u32[]{:S(2)}, u32[]{:S(2)}) async-start(bf16[8,64,128]{2,1,0:T(8,128)(2,1)} %shard_map.92), calls=%async_computation.2 | async-start | bytes 262144 | tf_op jit(solution)/shard_map/all_to_all | solution.py:273
  56.7 9.6 %collective-permute-start.4 = (bf16[2,48,384]{2,1,0:T(8,128)(2,1)S(1)}, bf16[2,48,384]{2,1,0:T(8,128)(2,1)S(1)}, u32[]{:S(2)}, u32[]{:S(2)}) collective-permute-start(bf16[2,48,384]{2,1,0:T(8,128)(2,1)S(1)} %get-tuple-element.19), channel_id=1, source_target_pairs={{0,12},{1,13},{2,14},{3,15},{4,8},{5,9},{6,10},{7,11},{8,4},{9,5},... | collective-permute-start | bytes 221192 | tf_op jit(solution)/shard_map/ppermute | solution.py:262
  66.3 11.3 %copy-start.8 = (bf16[2,48,384]{2,1,0:T(8,128)(2,1)}, bf16[2,48,384]{2,1,0:T(8,128)(2,1)S(1)}, u32[]{:S(2)}) copy-start(bf16[2,48,384]{2,1,0:T(8,128)(2,1)S(1)} %collective-permute-done.4.refs_2_) | copy-start | bytes 221188
  68.0 20.0 %all-to-all-start.3 = ((bf16[8,64,128]{2,1,0:T(8,128)(2,1)}), bf16[8,64,128]{2,1,0:T(8,128)(2,1)S(1)}, u32[]{:S(2)}, u32[]{:S(2)}) async-start(bf16[8,64,128]{2,1,0:T(8,128)(2,1)} %shard_map.93), calls=%async_computation.3 | async-start | bytes 262144 | tf_op jit(solution)/shard_map/all_to_all | solution.py:275
  79.4 8.5 %copy-start.3 = (bf16[1,48,3072]{2,1,0:T(8,128)(2,1)S(1)}, bf16[1,48,3072]{2,1,0:T(8,128)(2,1)}, u32[]{:S(2)}) copy-start(bf16[1,48,3072]{2,1,0:T(8,128)(2,1)} %param.12) | copy-start | bytes 884740
  79.5 8.5 %copy-start.5 = (f32[1,3,3072]{2,0,1:T(1,128)S(1)}, f32[1,3,3072]{2,0,1:T(1,128)}, u32[]{:S(2)}) copy-start(f32[1,3,3072]{2,0,1:T(1,128)} %param.14) | copy-start | bytes 110596
  99.1 21.0 %copy-start.11 = (bf16[1,2,3072]{2,1,0:T(2,128)(2,1)S(1)}, bf16[1,2,3072]{2,1,0:T(2,128)(2,1)}, u32[]{:S(2)}) copy-start(bf16[1,2,3072]{2,1,0:T(2,128)(2,1)} %param.9) | copy-start | bytes 36868
  120.1 11.3 %collective-permute-start.5 = (bf16[2,3072]{1,0:T(2,128)(2,1)S(1)}, bf16[2,3072]{1,0:T(2,128)(2,1)S(1)}, u32[]{:S(2)}, u32[]{:S(2)}) collective-permute-start(bf16[2,3072]{1,0:T(2,128)(2,1)S(1)} %add_convert_fusion.1), channel_id=1, source_target_pairs={{448,0},{0,64},{64,128},{128,192},{192,256},{256,320},{320,384},{3... | collective-permute-start | bytes 36872 | tf_op jit(solution)/shard_map/ppermute | solution.py:23
  148.8 11.6 %copy-start.2 = (bf16[1,3,48,3072]{3,2,1,0:T(8,128)(2,1)S(1)}, bf16[1,3,48,3072]{3,2,1,0:T(8,128)(2,1)}, u32[]{:S(2)}) copy-start(bf16[1,3,48,3072]{3,2,1,0:T(8,128)(2,1)} %param.10) | copy-start | bytes 2654212
  160.4 13.3 %copy-start.7 = (bf16[2,48,384]{2,1,0:T(8,128)(2,1)S(1)}, bf16[2,48,384]{2,1,0:T(8,128)(2,1)}, u32[]{:S(2)}) copy-start(bf16[2,48,384]{2,1,0:T(8,128)(2,1)} %copy-done.6) | copy-start | bytes 221188
  160.4 13.3 %copy-start.9 = (bf16[2,48,384]{2,1,0:T(8,128)(2,1)S(1)}, bf16[2,48,384]{2,1,0:T(8,128)(2,1)}, u32[]{:S(2)}) copy-start(bf16[2,48,384]{2,1,0:T(8,128)(2,1)} %copy-done.8) | copy-start | bytes 221188
  175.4 13.6 %all-to-all-start.9 = ((bf16[8,64,128]{2,1,0:T(8,128)(2,1)}), bf16[8,64,128]{2,1,0:T(8,128)(2,1)S(1)}, u32[]{:S(2)}, u32[]{:S(2)}) async-start(bf16[8,64,128]{2,1,0:T(8,128)(2,1)} %shard_map.97), calls=%async_computation.9 | async-start | bytes 262144 | tf_op jit(solution)/shard_map/all_to_all | solution.py:275
  221.1 12.8 %collective-permute-start.6 = (bf16[2,3072]{1,0:T(2,128)(2,1)S(1)}, bf16[2,3072]{1,0:T(2,128)(2,1)S(1)}, u32[]{:S(2)}, u32[]{:S(2)}) collective-permute-start(bf16[2,3072]{1,0:T(2,128)(2,1)S(1)} %add_convert_fusion), channel_id=1, source_target_pairs={{448,0},{0,64},{64,128},{128,192},{192,256},{256,320},{320,384},{3... | collective-permute-start | bytes 36872 | tf_op jit(solution)/shard_map/ppermute | solution.py:23
